TPU v7x, 32 devices: a whole 2x2x4 slice. The times are simulated.
32 devices in a mesh: seq: 32 (over z, y, x, core).
Axes of the slice: x: 2, y: 2, z: 4, core: 2. Of those that a mesh axis runs over, the one named last changes fastest.
Arguments:
- saved_input: bfloat16 [8192, 192], P('seq'), may hold values from -6 to 6
- cotangent: bfloat16 [8192, 192], P('seq'), may hold values from -15 to 15
- w_in: bfloat16 [384, 768], replicated, may hold values from -0.3125 to 0.3125
- bias_in: float32 [768], replicated, may hold values from -4 to 4
- w_out: bfloat16 [768, 384], replicated, may hold values from -0.21875 to 0.21875
- residual_logit: float32 [384], replicated, may hold values from -1 to 2
- branch_scale: float32 [384], replicated, may hold values from 0.1 to 1
Outputs:
- grad_input: bfloat16 [8192, 192], P('seq')
- grad_w_in: float32 [384, 768], replicated
- grad_w_out: float32 [768, 384], replicated
All inputs are finite; a program needn't handle non-finite values.
Results may differ from a plain program's by a relative error of at most 0.02.
Values may be sent and summed in bfloat16 or wider, within the bound.
No kernel may reach another device: no remote copies, remote signals or barrier semaphores. Data moves between devices by JAX's collectives and lax.ppermute only.
A program may use at most 64 MiB of HBM per device.

v0:
```python
import jax
import jax.numpy as jnp
from jax import lax
from jax.sharding import PartitionSpec as P

epsilon = 1e-05
tanh_scale = 0.7978845608028654
cubic_coef = 0.044715


def gelu_slope(preact):
    inner = tanh_scale * (preact + cubic_coef * preact * preact * preact)
    tangent = jnp.tanh(inner)
    return 0.5 * (1.0 + tangent) + 0.5 * preact * (1.0 - tangent * tangent) * tanh_scale * (
        1.0 + 3.0 * cubic_coef * preact * preact
    )


def contract_rows(left, right):
    return lax.dot_general(
        left, right, (((0,), (0,)), ((), ())), preferred_element_type=jnp.float32
    )


def switch_parts(paired, w_in, bias_in):
    values = paired.astype(jnp.float32)
    average = jnp.mean(values, axis=-1, keepdims=True)
    centered = values - average
    inverse = lax.rsqrt(jnp.mean(centered * centered, axis=-1, keepdims=True) + epsilon)
    normed = centered * inverse
    normed_low = normed.astype(jnp.bfloat16)
    preact = jnp.dot(normed_low, w_in, preferred_element_type=jnp.float32) + bias_in
    activated = jax.nn.gelu(preact, approximate=True).astype(jnp.bfloat16)
    return (normed, normed_low, inverse, preact, activated)


def switch_result(paired, parts, w_out, keep_gate, branch_scale):
    branch = jnp.dot(parts[4], w_out, preferred_element_type=jnp.float32)
    return (keep_gate * paired.astype(jnp.float32) + branch_scale * branch).astype(jnp.bfloat16)


def switch_backward(pair_grad, parts, w_in, w_out, keep_gate, branch_scale):
    normed, normed_low, inverse, preact, activated = parts
    upstream = pair_grad.astype(jnp.float32)
    branch_grad = (branch_scale * upstream).astype(jnp.bfloat16)
    act_grad = lax.dot_general(
        branch_grad, w_out, (((1,), (1,)), ((), ())), preferred_element_type=jnp.float32
    )
    preact_grad = (act_grad * gelu_slope(preact)).astype(jnp.bfloat16)
    normed_grad = lax.dot_general(
        preact_grad, w_in, (((1,), (1,)), ((), ())), preferred_element_type=jnp.float32
    )
    centered_grad = (
        normed_grad
        - jnp.mean(normed_grad, axis=-1, keepdims=True)
        - normed * jnp.mean(normed_grad * normed, axis=-1, keepdims=True)
    )
    input_grad = (keep_gate * upstream + inverse * centered_grad).astype(jnp.bfloat16)
    return (input_grad, normed_low, preact_grad, activated, branch_grad)


def local_pairs(state, stride, width):
    groups = state.shape[0] // (2 * stride)
    viewed = state.reshape(groups, 2, stride, width)
    return jnp.concatenate([viewed[:, 0], viewed[:, 1]], axis=-1).reshape(
        groups * stride, 2 * width
    )


def local_unpair(paired, stride, width):
    groups = paired.shape[0] // stride
    viewed = paired.reshape(groups, stride, 2 * width)
    return jnp.stack([viewed[:, :, :width], viewed[:, :, width:]], axis=1).reshape(
        groups * 2 * stride, width
    )


def shards(saved_input, cotangent, w_in, bias_in, w_out, residual_logit, branch_scale):
    width = saved_input.shape[1]
    rows_here = saved_input.shape[0]
    levels = lax.axis_size("seq").bit_length() - 1
    keep_gate = jax.nn.sigmoid(residual_logit)
    units = w_in.shape[1]
    grad_in = jnp.zeros((2 * width, units), jnp.float32)
    grad_out = jnp.zeros((units, 2 * width), jnp.float32)
    block = rows_here // lax.axis_size("seq")
    current, grad_state = (
        lax.all_to_all(saved_input, "seq", split_axis=0, concat_axis=0, tiled=True),
        lax.all_to_all(cotangent, "seq", split_axis=0, concat_axis=0, tiled=True),
    )
    stored = []
    kept = []
    for level in range(levels):
        stride = block * 2**level
        paired = local_pairs(current, stride, width)
        parts = switch_parts(paired, w_in, bias_in)
        current = local_unpair(
            switch_result(paired, parts, w_out, keep_gate, branch_scale), stride, width
        )
        stored.append(paired)
        kept.append(parts)
    for level in reversed(range(levels)):
        stride = block * 2**level
        parts = kept[level]
        input_grad, normed_low, preact_grad, activated, branch_grad = switch_backward(
            local_pairs(grad_state, stride, width), parts, w_in, w_out, keep_gate, branch_scale
        )
        grad_state = local_unpair(input_grad, stride, width)
        grad_in = grad_in + contract_rows(normed_low, preact_grad)
        grad_out = grad_out + contract_rows(activated, branch_grad)
    grad_state = lax.all_to_all(grad_state, "seq", split_axis=0, concat_axis=0, tiled=True)
    totals = lax.psum((grad_in, grad_out), "seq")
    grad_scale = float(rows_here * lax.axis_size("seq")) ** (-0.5)
    return (grad_state, totals[0] * grad_scale, totals[1] * grad_scale)


def solution(mesh):
    in_specs = (P("seq", None), P("seq", None), P(), P(), P(), P(), P())
    out_specs = (P("seq", None), P(), P())
    return jax.shard_map(shards, mesh=mesh, in_specs=in_specs, out_specs=out_specs, check_vma=False)
```

profile of v0, /device:TPU:0, one launch (start us, length us, event | category | flops | bytes accessed | tf_op | source)
XLA Modules:
  0.0 193.5 jit_solution(7987699696650660033)
XLA Ops:
  7.2 1.7 copy.15
  8.9 7.3 %all-to-all-start.1 = ((bf16[32,8,192]{2,1,0:T(8,128)(2,1)}), bf16[32,8,192]{2,1,0:T(8,128)(2,1)S(1)}, u32[]{:S(2)}, u32[]{:S(2)}) async-start(bf16[32,8,192]{2,1,0:T(8,128)(2,1)} %bitcast.5), calls=%async_computation.1 | async-start | bytes 262144 | tf_op jit(solution)/shard_map/all_to_all | solution.py:88
  16.2 1.7 copy.14
  17.9 0.7 add_divide_fusion
  18.6 5.9 %all-to-all-done.1 = bf16[32,8,192]{2,1,0:T(8,128)(2,1)S(1)} async-done(((bf16[32,8,192]{2,1,0:T(8,128)(2,1)}), bf16[32,8,192]{2,1,0:T(8,128)(2,1)S(1)}, u32[]{:S(2)}, u32[]{:S(2)}) %all-to-all-start.1) | async-done | bytes 98336 | tf_op jit(solution)/shard_map/all_to_all | solution.py:88
  24.4 2.6 %all-to-all-start = ((bf16[32,8,192]{2,1,0:T(8,128)(2,1)}), bf16[32,8,192]{2,1,0:T(8,128)(2,1)S(1)}, u32[]{:S(2)}, u32[]{:S(2)}) async-start(bf16[32,8,192]{2,1,0:T(8,128)(2,1)} %bitcast), calls=%async_computation | async-start | bytes 262144 | tf_op jit(solution)/shard_map/all_to_all | solution.py:89
  32.8 2.4 %all-to-all-done = bf16[32,8,192]{2,1,0:T(8,128)(2,1)S(1)} async-done(((bf16[32,8,192]{2,1,0:T(8,128)(2,1)}), bf16[32,8,192]{2,1,0:T(8,128)(2,1)S(1)}, u32[]{:S(2)}, u32[]{:S(2)}) %all-to-all-start) | async-done | bytes 98336 | tf_op jit(solution)/shard_map/all_to_all | solution.py:89
  35.7 0.6 copy-done.6
  36.3 0.4 fusion
  37.2 0.4 fusion.163
  38.0 0.4 fusion.1
  39.6 0.4 fusion.2
  41.3 0.4 fusion.3
  43.0 0.4 fusion.4
  43.4 1.4 convolution_add_fusion
  44.8 0.4 convolution_add_fusion.7
  45.3 0.4 convolution_add_fusion.6
  45.7 0.4 convolution_add_fusion.5
  46.6 1.5 convolution_add_fusion.4
  48.5 12.5 %all_to_all.30 = bf16[32,8,192]{2,1,0:T(8,128)(2,1)S(1)} all-to-all(bf16[32,8,192]{2,1,0:T(8,128)(2,1)S(1)} %bitcast.248), channel_id=1, replica_groups=mesh['seq'=32] {'seq'}, dimensions={0} | all-to-all | bytes 196608 | tf_op jit(solution)/shard_map/all_to_all | solution.py:111
  60.9 0.7 copy.26
  61.7 121.4 %all-reduce.3.cloned.1.call-done = (f32[384,768]{1,0:T(8,128)}, f32[768,384]{1,0:T(8,128)}) async-done(((f32[384,768]{1,0:T(8,128)}, f32[768,384]{1,0:T(8,128)}), (f32[384,768]{1,0:T(8,128)}, f32[768,384]{1,0:T(8,128)})) %all-reduce.3.cloned.1.call-update) | async-done | bytes 2359312 | tf_op jit(solution)/shard_map/psum | solution.py:112
  183.1 2.5 %broadcast_multiply_fusion = f32[768,384]{1,0:T(8,128)} fusion(f32[768,384]{1,0:T(8,128)} %get-tuple-element.17), kind=kLoop, calls=%fused_computation.51 | loop fusion | flops 294912 | bytes 2359296 | tf_op jit(solution)/shard_map/mul | solution.py:114
  185.6 1.1 broadcast_multiply_fusion.1
  (95 shorter events, 11.0 us)
Async XLA Ops:
  7.2 20.3 %copy-start = (bf16[384,768]{1,0:T(8,128)(2,1)S(1)}, bf16[384,768]{1,0:T(8,128)(2,1)}, u32[]{:S(2)}) copy-start(bf16[384,768]{1,0:T(8,128)(2,1)} %param.9) | copy-start | bytes 1769476
  7.2 20.3 %copy-start.2 = (f32[768]{0:T(1024)S(1)}, f32[768]{0:T(1024)}, u32[]{:S(2)}) copy-start(f32[768]{0:T(1024)} %param.10) | copy-start | bytes 9220
  8.9 18.9 %copy-start.3 = (f32[384]{0:T(512)S(1)}, f32[384]{0:T(512)}, u32[]{:S(2)}) copy-start(f32[384]{0:T(512)} %param.13) | copy-start | bytes 4612
  8.9 19.0 %copy-start.4 = (bf16[768,384]{1,0:T(8,128)(2,1)S(1)}, bf16[768,384]{1,0:T(8,128)(2,1)}, u32[]{:S(2)}) copy-start(bf16[768,384]{1,0:T(8,128)(2,1)} %param.11) | copy-start | bytes 1769476
  8.9 15.5 %all-to-all-start.1 = ((bf16[32,8,192]{2,1,0:T(8,128)(2,1)}), bf16[32,8,192]{2,1,0:T(8,128)(2,1)S(1)}, u32[]{:S(2)}, u32[]{:S(2)}) async-start(bf16[32,8,192]{2,1,0:T(8,128)(2,1)} %bitcast.5), calls=%async_computation.1 | async-start | bytes 262144 | tf_op jit(solution)/shard_map/all_to_all | solution.py:88
  24.4 10.8 %all-to-all-start = ((bf16[32,8,192]{2,1,0:T(8,128)(2,1)}), bf16[32,8,192]{2,1,0:T(8,128)(2,1)S(1)}, u32[]{:S(2)}, u32[]{:S(2)}) async-start(bf16[32,8,192]{2,1,0:T(8,128)(2,1)} %bitcast), calls=%async_computation | async-start | bytes 262144 | tf_op jit(solution)/shard_map/all_to_all | solution.py:89
  27.0 156.1 %all-reduce.3.cloned.1.call-start = ((), (), s32[]{:S(2)}) async-start(), calls=%async_computation.3 | async-start | bytes 4718592 | tf_op jit(solution)/shard_map/psum | solution.py:112
  30.5 1.1 copy-start.5
  35.3 1.1 copy-start.6
  183.1 2.5 %copy-start.1 = (f32[384,768]{1,0:T(8,128)S(1)}, f32[384,768]{1,0:T(8,128)}, u32[]{:S(2)}) copy-start(f32[384,768]{1,0:T(8,128)} %get-tuple-element.16) | copy-start | bytes 3538948
Sparse Core Ops, SparseCore 0:
  48.2 134.8 all-reduce.2
where the time goes:
time: 194 us
  waiting for transfers between devices  130 us (67%)
  between operations  14.6 us (8%)
  matrix products  13.4 us (7%)
  blocking collectives  12.5 us (6%)
  starting transfers between devices  9.91 us (5%)
  other arithmetic  7.49 us (4%)
  local copies, waits for them, and re-layouts  5.85 us (3%)
    psum x1, waiting for transfers between devices, shards(): totals = lax.psum((grad_in, grad_out), 'seq')  121 us
    all_to_all x1, blocking collectives, shards(): lax.all_to_all(grad_state, 'seq', split_axis=0, concat_axis=0, tiled=True)  12.5 us
    all_to_all x1, starting transfers between devices, shards(): lax.all_to_all(saved_input, 'seq', split_axis=0, concat_axis=0, tiled=True)  7.3 us
    dot_general x10, matrix products, contract_rows(): lax.dot_general(left, right, (((0,), (0,)), ((), ())), preferred_element_...  6.3 us
    all_to_all x1, waiting for transfers between devices, shards(): lax.all_to_all(saved_input, 'seq', split_axis=0, concat_axis=0, tiled=True)  5.89 us
    unnamed x17, local copies, waits for them, and re-layouts  4.94 us
  transfers between devices with their start and end apart: 3, of which 3 were waited for; matrix products, arithmetic and copies ran while one was open for 4% of the time, Pallas kernels for 0%

commit v1 on v0

v1 whole, which is shorter than its diff:
```python
import functools

import jax
import jax.numpy as jnp
from jax import lax
from jax.experimental import pallas as pl
from jax.experimental.pallas import tpu as pltpu
from jax.sharding import PartitionSpec as P

epsilon = 1e-05
tanh_scale = 0.7978845608028654
cubic_coef = 0.044715
f32 = jnp.float32
bf16 = jnp.bfloat16
VMEM = pl.BlockSpec(memory_space=pltpu.VMEM)
SMEM = pl.BlockSpec(memory_space=pltpu.SMEM)
tile = 16


def dot(left, right, contract):
    return lax.dot_general(left, right, ((contract[:1], contract[1:]), ((), ())), preferred_element_type=f32)


def pair_rows(state, stride):
    rows, width = state.shape
    groups = rows // (2 * stride)
    if stride >= 8:
        viewed = state.reshape(groups, 2, stride, width)
        halves = [viewed[:, side].reshape(rows // 2, width) for side in (0, 1)]
    else:
        halves = []
        for side in (0, 1):
            row = lax.broadcasted_iota(jnp.int32, (rows // 2, rows), 0)
            col = lax.broadcasted_iota(jnp.int32, (rows // 2, rows), 1)
            pick = (row // stride) * (2 * stride) + row % stride + side * stride
            halves.append(dot((col == pick).astype(bf16), state.astype(bf16), (1, 0)))
    return jnp.concatenate(halves, axis=1)


def unpair_rows(paired, stride):
    half, double = paired.shape
    width = double // 2
    groups = half // stride
    first, second = paired[:, :width], paired[:, width:]
    if stride >= 8:
        parts = [part.reshape(groups, 1, stride, width) for part in (first, second)]
        return jnp.concatenate(parts, axis=1).reshape(2 * half, width)
    total = jnp.zeros((2 * half, width), f32)
    for side, part in enumerate((first, second)):
        row = lax.broadcasted_iota(jnp.int32, (2 * half, half), 0)
        col = lax.broadcasted_iota(jnp.int32, (2 * half, half), 1)
        place = (col // stride) * (2 * stride) + col % stride + side * stride
        total = total + dot((row == place).astype(bf16), part.astype(bf16), (1, 0))
    return total


def switch_kernel(
    levels, block, me_ref, x_ref, g_ref, w_in_ref, bias_ref, w_out_ref, logit_ref, scale_ref,
    grad_ref, keep_ref, send_ref,
    low_s, act_s, slope_s, normed_s, inverse_s, pre_s, bg_s,
):
    rows, width = x_ref.shape
    half = rows // 2
    gate = jax.nn.sigmoid(logit_ref[...])
    scale = scale_ref[...]
    state = x_ref[...].astype(f32)
    for level in range(levels):
        at = pl.ds(level * half, half)
        paired = pair_rows(state, block * 2**level)
        centered = paired - jnp.mean(paired, axis=-1, keepdims=True)
        inverse = lax.rsqrt(jnp.mean(centered * centered, axis=-1, keepdims=True) + epsilon)
        normed = centered * inverse
        low = normed.astype(bf16)
        normed_s[at, :] = normed
        inverse_s[at, :] = inverse
        low_s[at, :] = low
        u = dot(low, w_in_ref[...], (1, 0)) + bias_ref[...]
        square = u * u
        tangent = jnp.tanh(tanh_scale * (u + cubic_coef * square * u))
        rise = 0.5 * (1.0 + tangent)
        act = (u * rise).astype(bf16)
        slope_s[at, :] = rise + 0.5 * u * (1.0 - tangent * tangent) * tanh_scale * (
            1.0 + 3.0 * cubic_coef * square
        )
        act_s[at, :] = act
        if level < levels - 1:
            branch = dot(act, w_out_ref[...], (1, 0))
            result = (gate * paired + scale * branch).astype(bf16).astype(f32)
            state = unpair_rows(result, block * 2**level)
    grad = g_ref[...].astype(f32)
    for level in reversed(range(levels)):
        at = pl.ds(level * half, half)
        upstream = pair_rows(grad, block * 2**level)
        branch_grad = (scale * upstream).astype(bf16)
        bg_s[at, :] = branch_grad
        act_grad = dot(branch_grad, w_out_ref[...], (1, 1))
        pre_grad = (act_grad * slope_s[at, :]).astype(bf16)
        pre_s[at, :] = pre_grad
        normed_grad = dot(pre_grad, w_in_ref[...], (1, 1))
        normed = normed_s[at, :]
        moved = (
            normed_grad
            - jnp.mean(normed_grad, axis=-1, keepdims=True)
            - normed * jnp.mean(normed_grad * normed, axis=-1, keepdims=True)
        )
        result = (gate * upstream + inverse_s[at, :] * moved).astype(bf16).astype(f32)
        grad = unpair_rows(result, block * 2**level)
    grad_ref[...] = grad.astype(bf16)
    grad_in = dot(low_s[...], pre_s[...], (0, 0))
    grad_out = dot(act_s[...], bg_s[...], (0, 0))
    double, units = grad_in.shape
    step = units // 16

    def put_in(ref):
        for piece in range(16):
            row, lane = (piece // 2) * step, (piece % 2) * double
            ref[piece * step : (piece + 1) * step, :] = grad_in[row : row + step, lane : lane + double].astype(
                ref.dtype
            )

    def put_out(ref):
        ref[...] = grad_out.astype(ref.dtype)

    core = me_ref[0] % 2

    @pl.when(core == 0)
    def _():
        put_in(keep_ref)
        put_out(send_ref)

    @pl.when(core == 1)
    def _():
        put_in(send_ref)
        put_out(keep_ref)


def split_kernel(radix, shift, me_ref, *refs):
    count = len(refs) - radix
    parts, outs = refs[:count], refs[count:]
    rows = parts[0].shape[0] // radix
    place = (me_ref[0] >> shift) & (radix - 1)
    for other in range(radix):
        at = pl.ds(pl.multiple_of((place ^ other) * rows, tile), rows)
        total = parts[0][at, :].astype(f32)
        for part in parts[1:]:
            total = total + part[at, :].astype(f32)
        outs[other][...] = total.astype(outs[other].dtype)


def total_kernel(factor, *refs):
    total = refs[0][...].astype(f32)
    for part in refs[1:-1]:
        total = total + part[...].astype(f32)
    refs[-1][...] = (total * factor).astype(refs[-1].dtype)


def place_kernel(phases, step, me_ref, mine_ref, other_ref, in_ref, out_ref):
    me = me_ref[0]
    core = me % 2
    double = mine_ref.shape[1]
    pieces = mine_ref.shape[0] // step
    base = 0
    for bit, radix in phases:
        base = base * radix + ((me >> bit) & (radix - 1))

    def write(first_ref, second_ref):
        for slot in range(pieces):
            piece = slot ^ base
            rows = pl.ds(slot * step, step)
            to = pl.ds(pl.multiple_of((piece // 2) * step, tile), step)
            lane = pl.ds(pl.multiple_of((piece % 2) * double, 128), double)
            in_ref[to, lane] = first_ref[rows, :].astype(f32)
            out_ref[pl.ds(pl.multiple_of(piece * step, tile), step), :] = second_ref[rows, :].astype(f32)

    @pl.when(core == 0)
    def _():
        write(mine_ref, other_ref)

    @pl.when(core == 1)
    def _():
        write(other_ref, mine_ref)


def call(kernel, outs, scratch=(), specs=None, count=0):
    return pl.pallas_call(
        kernel,
        out_shape=outs,
        in_specs=specs if specs is not None else [VMEM] * count,
        out_specs=jax.tree.map(lambda _: VMEM, outs),
        scratch_shapes=list(scratch),
        compiler_params=pltpu.CompilerParams(vmem_limit_bytes=40 * 2**20),
    )


def struct(shape, dtype):
    return jax.ShapeDtypeStruct(shape, dtype)


def exchange(value, masks, size):
    return [lax.ppermute(value if not isinstance(value, list) else value[i], "seq",
                         [(d, d ^ mask) for d in range(size)]) for i, mask in enumerate(masks)]


def sum_over_devices(me, keep, send, size, factor):
    bits = size.bit_length() - 1
    rows, double = keep.shape
    arrived = exchange([send], [1], size)
    parts = [keep] + arrived
    bit = 1
    phases = []
    while bit < bits and bit < 5:
        radix = 4 if bit + 1 < min(bits, 5) else 2
        phases.append((bit, radix))
        bit += 2 if radix == 4 else 1
    for bit, radix in phases:
        rows = rows // radix
        outs = [struct((rows, double), f32)] + [struct((rows, double), bf16)] * (radix - 1)
        pieces = call(
            functools.partial(split_kernel, radix, bit), outs, specs=[SMEM] + [VMEM] * len(parts)
        )(me, *parts)
        parts = [pieces[0]] + exchange(list(pieces[1:]), [m << bit for m in range(1, radix)], size)
    bit = phases[-1][0] + phases[-1][1].bit_length() - 1
    for rest in range(bit, bits):
        total = call(functools.partial(total_kernel, 1.0), struct((rows, double), bf16), count=len(parts))(*parts)
        parts = [total] + exchange([total], [1 << rest], size)
    mine = call(functools.partial(total_kernel, factor), struct((rows, double), bf16), count=len(parts))(*parts)
    for bit, radix in reversed(phases):
        got = exchange([mine] * (radix - 1), [m << bit for m in range(1, radix)], size)
        mine = jnp.concatenate([mine] + got, axis=0)
    (other,) = exchange([mine], [1], size)
    return mine, other, rows, phases


def shards(saved_input, cotangent, w_in, bias_in, w_out, residual_logit, branch_scale):
    size = lax.axis_size("seq")
    levels = size.bit_length() - 1
    rows, width = saved_input.shape
    double, units = w_in.shape
    block = rows // size
    half = rows // 2
    me = lax.axis_index("seq").astype(jnp.int32).reshape(1)
    both = jnp.concatenate(
        [saved_input.reshape(size, block, width), cotangent.reshape(size, block, width)], axis=1
    )
    both = lax.all_to_all(both, "seq", split_axis=0, concat_axis=0, tiled=True)
    state = both[:, :block].reshape(rows, width)
    grads = both[:, block:].reshape(rows, width)
    total = levels * half
    grad_state, keep, send = call(
        functools.partial(switch_kernel, levels, block),
        [struct((rows, width), bf16), struct((units, double), f32), struct((units, double), bf16)],
        scratch=[
            pltpu.VMEM((total, double), bf16),
            pltpu.VMEM((total, units), bf16),
            pltpu.VMEM((total, units), f32),
            pltpu.VMEM((total, double), f32),
            pltpu.VMEM((total, 1), f32),
            pltpu.VMEM((total, units), bf16),
            pltpu.VMEM((total, double), bf16),
        ],
        specs=[SMEM] + [VMEM] * 7,
    )(me, state, grads, w_in, bias_in.reshape(1, units), w_out, residual_logit.reshape(1, double),
      branch_scale.reshape(1, double))
    factor = float(rows * size) ** (-0.5)
    mine, other, step, phases = sum_over_devices(me, keep, send, size, factor)
    grad_state = lax.all_to_all(
        grad_state.reshape(size, block, width), "seq", split_axis=0, concat_axis=0, tiled=True
    ).reshape(rows, width)
    grad_in, grad_out = call(
        functools.partial(place_kernel, phases, step),
        [struct((double, units), f32), struct((units, double), f32)],
        specs=[SMEM, VMEM, VMEM],
    )(me, mine, other)
    return (grad_state, grad_in, grad_out)


def solution(mesh):
    in_specs = (P("seq", None), P("seq", None), P(), P(), P(), P(), P())
    out_specs = (P("seq", None), P(), P())
    return jax.shard_map(shards, mesh=mesh, in_specs=in_specs, out_specs=out_specs, check_vma=False)
```

time: 194 us -> 78.6 us (0.41)
  waiting for transfers between devices: 130 us -> 29.1 us
  between operations: 14.6 us -> 0.86 us
  starting transfers between devices: 9.91 us -> 23.5 us
  matrix products: 13.4 us -> 0 us
  Pallas kernels: 0 us -> 9.91 us
  other arithmetic: 7.49 us -> 0.76 us
  local copies, waits for them, and re-layouts: 5.85 us -> 2.99 us
    psum x1 -> x0, waiting for transfers between devices: 121 us -> none  [shards(): totals = lax.psum((grad_in, grad_out), 'seq')]
    ppermute x0 -> x14, waiting for transfers between devices: none -> 18.6 us  [exchange(): lax.ppermute(value if not isinstance(value, list) else value[i], 'seq', [...]
    ppermute x0 -> x14, starting transfers between devices: none -> 16.2 us  [exchange(): lax.ppermute(value if not isinstance(value, list) else value[i], 'seq', [...]
    dot_general x29 -> x0, matrix products: 13.4 us -> none  [the longest x10 6.3 us: contract_rows(): lax.dot_general(left, right, (((0,), (0,)), ((), ())), preferred_element_...]
    pallas_call x0 -> x5, Pallas kernels: none -> 9.91 us  [the longest x1 8.12 us: shards(): call(functools.partial(switch_kernel, levels, block), [struct((rows, widt...]
    mul x2 -> x0, other arithmetic: 3.61 us -> none  [shards(): return (grad_state, totals[0] * grad_scale, totals[1] * grad_scale)]
    all_to_all x2 -> x1, starting transfers between devices: 9.87 us -> 7.3 us  [shards(): both = lax.all_to_all(both, 'seq', split_axis=0, concat_axis=0, tiled=True)]
    all_to_all x2 -> x1, waiting for transfers between devices: 8.33 us -> 10.5 us  [shards(): both = lax.all_to_all(both, 'seq', split_axis=0, concat_axis=0, tiled=True)]
  transfers between devices with their start and end apart: 3 -> 15, of which waited for: 3 -> 10; matrix products, arithmetic and copies ran while one was open for 4% -> 1% of each run, Pallas kernels for 0% -> 0%
where the time goes in v1:
time: 78.6 us; the launch traced here: 78.3 us
  waiting for transfers between devices  29.1 us (37%)
  starting transfers between devices  23.5 us (30%)
  blocking collectives  11.2 us (14%)
  Pallas kernels  9.91 us (13%)
  local copies, waits for them, and re-layouts  2.99 us (4%)
  between operations  0.86 us (1%)
    ppermute x14, waiting for transfers between devices, exchange(): lax.ppermute(value if not isinstance(value, list) else value[i], 'seq', [...  18.6 us
    ppermute x14, starting transfers between devices, exchange(): lax.ppermute(value if not isinstance(value, list) else value[i], 'seq', [...  16.2 us
    all_to_all x1, blocking collectives, shards(): lax.all_to_all(grad_state.reshape(size, block, width), 'seq', split_axis=...  11.2 us
    all_to_all x1, waiting for transfers between devices, shards(): both = lax.all_to_all(both, 'seq', split_axis=0, concat_axis=0, tiled=True)  10.5 us
    pallas_call x1, Pallas kernels, shards(): call(functools.partial(switch_kernel, levels, block), [struct((rows, widt...  8.12 us
    all_to_all x1, starting transfers between devices, shards(): both = lax.all_to_all(both, 'seq', split_axis=0, concat_axis=0, tiled=True)  7.3 us
    unnamed x19, local copies, waits for them, and re-layouts  2.93 us
  transfers between devices with their start and end apart: 15, of which 10 were waited for; matrix products, arithmetic and copies ran while one was open for 1% of the time, Pallas kernels for 0%

profile of v1, /device:TPU:0, one launch (start us, length us, event | category | flops | bytes accessed | tf_op | source)
XLA Modules:
  0.0 78.3 jit_solution(15030582898220141132)
XLA Ops:
  0.7 1.1 %copy.13 = bf16[256,192]{1,0:T(8,128)(2,1)S(1)} copy(bf16[256,192]{0,1:T(8,128)(2,1)} %param.7) | data formatting | bytes 196608 | tf_op args[0]
  1.8 1.0 %copy.14 = bf16[256,192]{1,0:T(8,128)(2,1)S(1)} copy(bf16[256,192]{0,1:T(8,128)(2,1)} %param.8) | data formatting | bytes 196608 | tf_op args[1]
  3.5 7.3 %all-to-all-start = ((bf16[32,16,192]{2,1,0:T(8,128)(2,1)}), bf16[32,16,192]{2,1,0:T(8,128)(2,1)S(1)}, u32[]{:S(2)}, u32[]{:S(2)}) async-start(bf16[32,16,192]{2,1,0:T(8,128)(2,1)} %pad_maximum_fusion), calls=%async_computation | async-start | bytes 524288 | tf_op jit(solution)/shard_map/all_to_all | solution.py:245
  10.9 10.5 %all-to-all-done = bf16[32,16,192]{2,1,0:T(8,128)(2,1)S(1)} async-done(((bf16[32,16,192]{2,1,0:T(8,128)(2,1)}), bf16[32,16,192]{2,1,0:T(8,128)(2,1)S(1)}, u32[]{:S(2)}, u32[]{:S(2)}) %all-to-all-start) | async-done | bytes 196640 | tf_op jit(solution)/shard_map/all_to_all | solution.py:245
  21.5 8.1 %shard_map.94 = (bf16[256,192]{1,0:T(8,128)(2,1)S(1)}, f32[768,384]{1,0:T(8,128)S(1)}, bf16[768,384]{1,0:T(8,128)(2,1)S(1)}) custom-call(s32[1]{0:T(128)} %bitcast.me_ref, bf16[256,192]{1,0:T(8,128)(2,1)S(1)} %get-tuple-element.33.x_ref, bf16[256,192]{1,0:T(8,128)(2,1)S(1)} %get-tuple-element.32.g_ref, bf16[384,768]{1,0:T(8,128)(2,1)S(1)} %copy-done, ...), custom_call_target="tpu_custom_call" | custom-call | tf_op jit(solution)/shard_map/pallas_call | solution.py:249
  29.7 2.0 %collective-permute-done.refs_1_ = bf16[768,384]{1,0:T(8,128)(2,1)S(1)} collective-permute-done((bf16[768,384]{1,0:T(8,128)(2,1)S(1)}, bf16[768,384]{1,0:T(8,128)(2,1)S(1)}, u32[]{:S(2)}, u32[]{:S(2)}) %collective-permute-start) | collective-permute-done | bytes 589856 | tf_op jit(solution)/shard_map/ppermute | solution.py:200
  32.3 1.3 %collective-permute-start.2 = (bf16[192,384]{1,0:T(8,128)(2,1)S(1)}, bf16[192,384]{1,0:T(8,128)(2,1)S(1)}, u32[]{:S(2)}, u32[]{:S(2)}) collective-permute-start(bf16[192,384]{1,0:T(8,128)(2,1)S(1)} %get-tuple-element.21), channel_id=1, source_target_pairs={{0,4},{1,5},{2,6},{3,7},{4,0},{5,1},{6,2},{7,3},{8,12},{9,13},{10,... | collective-permute-start | bytes 442376 | tf_op jit(solution)/shard_map/ppermute | solution.py:200
  33.6 1.7 %collective-permute-start.3 = (bf16[192,384]{1,0:T(8,128)(2,1)S(1)}, bf16[192,384]{1,0:T(8,128)(2,1)S(1)}, u32[]{:S(2)}, u32[]{:S(2)}) collective-permute-start(bf16[192,384]{1,0:T(8,128)(2,1)S(1)} %get-tuple-element.22), channel_id=1, source_target_pairs={{0,6},{1,7},{2,4},{3,5},{4,2},{5,3},{6,0},{7,1},{8,14},{9,15},{10,... | collective-permute-start | bytes 442376 | tf_op jit(solution)/shard_map/ppermute | solution.py:200
  35.3 3.2 %collective-permute-done.1.refs_1_ = bf16[192,384]{1,0:T(8,128)(2,1)S(1)} collective-permute-done((bf16[192,384]{1,0:T(8,128)(2,1)S(1)}, bf16[192,384]{1,0:T(8,128)(2,1)S(1)}, u32[]{:S(2)}, u32[]{:S(2)}) %collective-permute-start.1) | collective-permute-done | bytes 147488 | tf_op jit(solution)/shard_map/ppermute | solution.py:200
  39.0 2.3 %collective-permute-done.3.refs_3_ = bf16[192,384]{1,0:T(8,128)(2,1)S(1)} collective-permute-done((bf16[192,384]{1,0:T(8,128)(2,1)S(1)}, bf16[192,384]{1,0:T(8,128)(2,1)S(1)}, u32[]{:S(2)}, u32[]{:S(2)}) %collective-permute-start.3) | collective-permute-done | bytes 147488 | tf_op jit(solution)/shard_map/ppermute | solution.py:200
  42.1 1.2 %collective-permute-start.5 = (bf16[48,384]{1,0:T(8,128)(2,1)S(1)}, bf16[48,384]{1,0:T(8,128)(2,1)S(1)}, u32[]{:S(2)}, u32[]{:S(2)}) collective-permute-start(bf16[48,384]{1,0:T(8,128)(2,1)S(1)} %get-tuple-element.25), channel_id=1, source_target_pairs={{0,16},{1,17},{2,18},{3,19},{4,20},{5,21},{6,22},{7,23},{8,24},{9,... | collective-permute-start | bytes 110600 | tf_op jit(solution)/shard_map/ppermute | solution.py:200
  43.3 2.6 %collective-permute-start.6 = (bf16[48,384]{1,0:T(8,128)(2,1)S(1)}, bf16[48,384]{1,0:T(8,128)(2,1)S(1)}, u32[]{:S(2)}, u32[]{:S(2)}) collective-permute-start(bf16[48,384]{1,0:T(8,128)(2,1)S(1)} %get-tuple-element.26), channel_id=1, source_target_pairs={{0,24},{1,25},{2,26},{3,27},{4,28},{5,29},{6,30},{7,31},{8,16},{9,... | collective-permute-start | bytes 110600 | tf_op jit(solution)/shard_map/ppermute | solution.py:200
  45.9 1.3 %collective-permute-done.5.refs_2_ = bf16[48,384]{1,0:T(8,128)(2,1)S(1)} collective-permute-done((bf16[48,384]{1,0:T(8,128)(2,1)S(1)}, bf16[48,384]{1,0:T(8,128)(2,1)S(1)}, u32[]{:S(2)}, u32[]{:S(2)}) %collective-permute-start.5) | collective-permute-done | bytes 36896 | tf_op jit(solution)/shard_map/ppermute | solution.py:200
  47.1 2.0 %collective-permute-done.6.refs_3_ = bf16[48,384]{1,0:T(8,128)(2,1)S(1)} collective-permute-done((bf16[48,384]{1,0:T(8,128)(2,1)S(1)}, bf16[48,384]{1,0:T(8,128)(2,1)S(1)}, u32[]{:S(2)}, u32[]{:S(2)}) %collective-permute-start.6) | collective-permute-done | bytes 36896 | tf_op jit(solution)/shard_map/ppermute | solution.py:200
  49.2 2.5 %collective-permute-start.9 = (bf16[48,384]{1,0:T(8,128)(2,1)S(1)}, bf16[48,384]{1,0:T(8,128)(2,1)S(1)}, u32[]{:S(2)}, u32[]{:S(2)}) collective-permute-start(bf16[48,384]{1,0:T(8,128)(2,1)S(1)} %shard_map.97), channel_id=1, source_target_pairs={{0,24},{1,25},{2,26},{3,27},{4,28},{5,29},{6,30},{7,31},{8,16},{9,... | collective-permute-start | bytes 110600 | tf_op jit(solution)/shard_map/ppermute | solution.py:200
  51.7 1.9 %collective-permute-start.7 = (bf16[48,384]{1,0:T(8,128)(2,1)S(1)}, bf16[48,384]{1,0:T(8,128)(2,1)S(1)}, u32[]{:S(2)}, u32[]{:S(2)}) collective-permute-start(bf16[48,384]{1,0:T(8,128)(2,1)S(1)} %shard_map.97), channel_id=1, source_target_pairs={{0,8},{1,9},{2,10},{3,11},{4,12},{5,13},{6,14},{7,15},{8,0},{9,1},... | collective-permute-start | bytes 110600 | tf_op jit(solution)/shard_map/ppermute | solution.py:200
  53.6 1.4 %collective-permute-done.9 = bf16[48,384]{1,0:T(8,128)(2,1)S(1)} collective-permute-done((bf16[48,384]{1,0:T(8,128)(2,1)S(1)}, bf16[48,384]{1,0:T(8,128)(2,1)S(1)}, u32[]{:S(2)}, u32[]{:S(2)}) %collective-permute-start.9) | collective-permute-done | bytes 36896 | tf_op jit(solution)/shard_map/ppermute | solution.py:200
  55.0 1.6 %collective-permute-done.8 = bf16[48,384]{1,0:T(8,128)(2,1)S(1)} collective-permute-done((bf16[48,384]{1,0:T(8,128)(2,1)S(1)}, bf16[48,384]{1,0:T(8,128)(2,1)S(1)}, u32[]{:S(2)}, u32[]{:S(2)}) %collective-permute-start.8) | collective-permute-done | bytes 36896 | tf_op jit(solution)/shard_map/ppermute | solution.py:200
  56.6 1.7 %collective-permute-start.12 = (bf16[192,384]{1,0:T(8,128)(2,1)S(1)}, bf16[192,384]{1,0:T(8,128)(2,1)S(1)}, u32[]{:S(2)}, u32[]{:S(2)}) collective-permute-start(bf16[192,384]{1,0:T(8,128)(2,1)S(1)} %pad_maximum_fusion.1), channel_id=1, source_target_pairs={{0,6},{1,7},{2,4},{3,5},{4,2},{5,3},{6,0},{7,1},{8,14},{9,15},{10,... | collective-permute-start | bytes 442376 | tf_op jit(solution)/shard_map/ppermute | solution.py:200
  58.3 1.1 %collective-permute-start.11 = (bf16[192,384]{1,0:T(8,128)(2,1)S(1)}, bf16[192,384]{1,0:T(8,128)(2,1)S(1)}, u32[]{:S(2)}, u32[]{:S(2)}) collective-permute-start(bf16[192,384]{1,0:T(8,128)(2,1)S(1)} %pad_maximum_fusion.1), channel_id=1, source_target_pairs={{0,4},{1,5},{2,6},{3,7},{4,0},{5,1},{6,2},{7,3},{8,12},{9,13},{10,... | collective-permute-start | bytes 442376 | tf_op jit(solution)/shard_map/ppermute | solution.py:200
  60.2 4.4 %collective-permute-done.10 = bf16[192,384]{1,0:T(8,128)(2,1)S(1)} collective-permute-done((bf16[192,384]{1,0:T(8,128)(2,1)S(1)}, bf16[192,384]{1,0:T(8,128)(2,1)S(1)}, u32[]{:S(2)}, u32[]{:S(2)}) %collective-permute-start.10) | collective-permute-done | bytes 147488 | tf_op jit(solution)/shard_map/ppermute | solution.py:200
  64.8 11.2 %all_to_all.10 = bf16[32,8,192]{2,1,0:T(8,128)(2,1)S(1)} all-to-all(bf16[32,8,192]{2,1,0:T(8,128)(2,1)S(1)} %bitcast.9), channel_id=1, replica_groups=mesh['seq'=32] {'seq'}, dimensions={0} | all-to-all | bytes 196608 | tf_op jit(solution)/shard_map/all_to_all | solution.py:266
  76.0 0.7 copy.15
  76.8 1.6 %shard_map.98 = (f32[384,768]{1,0:T(8,128)}, f32[768,384]{1,0:T(8,128)}) custom-call(s32[1]{0:T(128)} %bitcast.me_ref, bf16[768,384]{1,0:T(8,128)(2,1)S(1)} %constant_dynamic-update-slice_fusion.mine_ref, bf16[768,384]{1,0:T(8,128)(2,1)S(1)} %collective-permute-done.13.other_ref), custom_call_target="tpu_custom_call" | custom-call | tf_op jit(solution)/shard_map/pallas_call | solution.py:269
  (38 shorter events, 3.7 us)
Async XLA Ops:
  0.6 10.2 %copy-start.3 = (f32[384]{0:T(512)S(1)}, f32[384]{0:T(512)}, u32[]{:S(2)}) copy-start(f32[384]{0:T(512)} %param.12) | copy-start | bytes 4612
  0.6 10.2 %copy-start.4 = (f32[384]{0:T(512)S(1)}, f32[384]{0:T(512)}, u32[]{:S(2)}) copy-start(f32[384]{0:T(512)} %param.13) | copy-start | bytes 4612
  0.7 10.2 %copy-start.2 = (f32[768]{0:T(1024)S(1)}, f32[768]{0:T(1024)}, u32[]{:S(2)}) copy-start(f32[768]{0:T(1024)} %param.10) | copy-start | bytes 9220
  0.7 20.8 %copy-start.1 = (bf16[768,384]{1,0:T(8,128)(2,1)S(1)}, bf16[768,384]{1,0:T(8,128)(2,1)}, u32[]{:S(2)}) copy-start(bf16[768,384]{1,0:T(8,128)(2,1)} %w_out_ref.1) | copy-start | bytes 1769476
  0.7 20.8 %copy-start = (bf16[384,768]{1,0:T(8,128)(2,1)S(1)}, bf16[384,768]{1,0:T(8,128)(2,1)}, u32[]{:S(2)}) copy-start(bf16[384,768]{1,0:T(8,128)(2,1)} %w_in_ref.1) | copy-start | bytes 1769476
  3.5 17.9 %all-to-all-start = ((bf16[32,16,192]{2,1,0:T(8,128)(2,1)}), bf16[32,16,192]{2,1,0:T(8,128)(2,1)S(1)}, u32[]{:S(2)}, u32[]{:S(2)}) async-start(bf16[32,16,192]{2,1,0:T(8,128)(2,1)} %pad_maximum_fusion), calls=%async_computation | async-start | bytes 524288 | tf_op jit(solution)/shard_map/all_to_all | solution.py:245
  29.6 2.1 %collective-permute-start = (bf16[768,384]{1,0:T(8,128)(2,1)S(1)}, bf16[768,384]{1,0:T(8,128)(2,1)S(1)}, u32[]{:S(2)}, u32[]{:S(2)}) collective-permute-start(bf16[768,384]{1,0:T(8,128)(2,1)S(1)} %get-tuple-element.18), channel_id=1, source_target_pairs={{0,1},{1,0},{2,3},{3,2},{4,5},{5,4},{6,7},{7,6},{8,9},{9,8},{10,11... | collective-permute-start | bytes 1769480 | tf_op jit(solution)/shard_map/ppermute | solution.py:200
  31.8 6.8 %collective-permute-start.1 = (bf16[192,384]{1,0:T(8,128)(2,1)S(1)}, bf16[192,384]{1,0:T(8,128)(2,1)S(1)}, u32[]{:S(2)}, u32[]{:S(2)}) collective-permute-start(bf16[192,384]{1,0:T(8,128)(2,1)S(1)} %get-tuple-element.20), channel_id=1, source_target_pairs={{0,2},{1,3},{2,0},{3,1},{4,6},{5,7},{6,4},{7,5},{8,10},{9,11},{10,... | collective-permute-start | bytes 442376 | tf_op jit(solution)/shard_map/ppermute | solution.py:200
  32.3 6.6 %collective-permute-start.2 = (bf16[192,384]{1,0:T(8,128)(2,1)S(1)}, bf16[192,384]{1,0:T(8,128)(2,1)S(1)}, u32[]{:S(2)}, u32[]{:S(2)}) collective-permute-start(bf16[192,384]{1,0:T(8,128)(2,1)S(1)} %get-tuple-element.21), channel_id=1, source_target_pairs={{0,4},{1,5},{2,6},{3,7},{4,0},{5,1},{6,2},{7,3},{8,12},{9,13},{10,... | collective-permute-start | bytes 442376 | tf_op jit(solution)/shard_map/ppermute | solution.py:200
  33.6 7.7 %collective-permute-start.3 = (bf16[192,384]{1,0:T(8,128)(2,1)S(1)}, bf16[192,384]{1,0:T(8,128)(2,1)S(1)}, u32[]{:S(2)}, u32[]{:S(2)}) collective-permute-start(bf16[192,384]{1,0:T(8,128)(2,1)S(1)} %get-tuple-element.22), channel_id=1, source_target_pairs={{0,6},{1,7},{2,4},{3,5},{4,2},{5,3},{6,0},{7,1},{8,14},{9,15},{10,... | collective-permute-start | bytes 442376 | tf_op jit(solution)/shard_map/ppermute | solution.py:200
  41.4 4.5 %collective-permute-start.4 = (bf16[48,384]{1,0:T(8,128)(2,1)S(1)}, bf16[48,384]{1,0:T(8,128)(2,1)S(1)}, u32[]{:S(2)}, u32[]{:S(2)}) collective-permute-start(bf16[48,384]{1,0:T(8,128)(2,1)S(1)} %get-tuple-element.24), channel_id=1, source_target_pairs={{0,8},{1,9},{2,10},{3,11},{4,12},{5,13},{6,14},{7,15},{8,0},{9,1},... | collective-permute-start | bytes 110600 | tf_op jit(solution)/shard_map/ppermute | solution.py:200
  42.1 5.0 %collective-permute-start.5 = (bf16[48,384]{1,0:T(8,128)(2,1)S(1)}, bf16[48,384]{1,0:T(8,128)(2,1)S(1)}, u32[]{:S(2)}, u32[]{:S(2)}) collective-permute-start(bf16[48,384]{1,0:T(8,128)(2,1)S(1)} %get-tuple-element.25), channel_id=1, source_target_pairs={{0,16},{1,17},{2,18},{3,19},{4,20},{5,21},{6,22},{7,23},{8,24},{9,... | collective-permute-start | bytes 110600 | tf_op jit(solution)/shard_map/ppermute | solution.py:200
  43.3 5.9 %collective-permute-start.6 = (bf16[48,384]{1,0:T(8,128)(2,1)S(1)}, bf16[48,384]{1,0:T(8,128)(2,1)S(1)}, u32[]{:S(2)}, u32[]{:S(2)}) collective-permute-start(bf16[48,384]{1,0:T(8,128)(2,1)S(1)} %get-tuple-element.26), channel_id=1, source_target_pairs={{0,24},{1,25},{2,26},{3,27},{4,28},{5,29},{6,30},{7,31},{8,16},{9,... | collective-permute-start | bytes 110600 | tf_op jit(solution)/shard_map/ppermute | solution.py:200
  49.2 5.8 %collective-permute-start.9 = (bf16[48,384]{1,0:T(8,128)(2,1)S(1)}, bf16[48,384]{1,0:T(8,128)(2,1)S(1)}, u32[]{:S(2)}, u32[]{:S(2)}) collective-permute-start(bf16[48,384]{1,0:T(8,128)(2,1)S(1)} %shard_map.97), channel_id=1, source_target_pairs={{0,24},{1,25},{2,26},{3,27},{4,28},{5,29},{6,30},{7,31},{8,16},{9,... | collective-permute-start | bytes 110600 | tf_op jit(solution)/shard_map/ppermute | solution.py:200
  51.7 4.9 %collective-permute-start.8 = (bf16[48,384]{1,0:T(8,128)(2,1)S(1)}, bf16[48,384]{1,0:T(8,128)(2,1)S(1)}, u32[]{:S(2)}, u32[]{:S(2)}) collective-permute-start(bf16[48,384]{1,0:T(8,128)(2,1)S(1)} %shard_map.97), channel_id=1, source_target_pairs={{0,16},{1,17},{2,18},{3,19},{4,20},{5,21},{6,22},{7,23},{8,24},{9,... | collective-permute-start | bytes 110600 | tf_op jit(solution)/shard_map/ppermute | solution.py:200
  51.7 4.9 %collective-permute-start.7 = (bf16[48,384]{1,0:T(8,128)(2,1)S(1)}, bf16[48,384]{1,0:T(8,128)(2,1)S(1)}, u32[]{:S(2)}, u32[]{:S(2)}) collective-permute-start(bf16[48,384]{1,0:T(8,128)(2,1)S(1)} %shard_map.97), channel_id=1, source_target_pairs={{0,8},{1,9},{2,10},{3,11},{4,12},{5,13},{6,14},{7,15},{8,0},{9,1},... | collective-permute-start | bytes 110600 | tf_op jit(solution)/shard_map/ppermute | solution.py:200
  56.6 8.1 %collective-permute-start.12 = (bf16[192,384]{1,0:T(8,128)(2,1)S(1)}, bf16[192,384]{1,0:T(8,128)(2,1)S(1)}, u32[]{:S(2)}, u32[]{:S(2)}) collective-permute-start(bf16[192,384]{1,0:T(8,128)(2,1)S(1)} %pad_maximum_fusion.1), channel_id=1, source_target_pairs={{0,6},{1,7},{2,4},{3,5},{4,2},{5,3},{6,0},{7,1},{8,14},{9,15},{10,... | collective-permute-start | bytes 442376 | tf_op jit(solution)/shard_map/ppermute | solution.py:200
  58.3 6.3 %collective-permute-start.11 = (bf16[192,384]{1,0:T(8,128)(2,1)S(1)}, bf16[192,384]{1,0:T(8,128)(2,1)S(1)}, u32[]{:S(2)}, u32[]{:S(2)}) collective-permute-start(bf16[192,384]{1,0:T(8,128)(2,1)S(1)} %pad_maximum_fusion.1), channel_id=1, source_target_pairs={{0,4},{1,5},{2,6},{3,7},{4,0},{5,1},{6,2},{7,3},{8,12},{9,13},{10,... | collective-permute-start | bytes 442376 | tf_op jit(solution)/shard_map/ppermute | solution.py:200
  59.4 5.1 %collective-permute-start.10 = (bf16[192,384]{1,0:T(8,128)(2,1)S(1)}, bf16[192,384]{1,0:T(8,128)(2,1)S(1)}, u32[]{:S(2)}, u32[]{:S(2)}) collective-permute-start(bf16[192,384]{1,0:T(8,128)(2,1)S(1)} %pad_maximum_fusion.1), channel_id=1, source_target_pairs={{0,2},{1,3},{2,0},{3,1},{4,6},{5,7},{6,4},{7,5},{8,10},{9,11},{10,... | collective-permute-start | bytes 442376 | tf_op jit(solution)/shard_map/ppermute | solution.py:200
  64.7 12.1 %collective-permute-start.13 = (bf16[768,384]{1,0:T(8,128)(2,1)S(1)}, bf16[768,384]{1,0:T(8,128)(2,1)S(1)}, u32[]{:S(2)}, u32[]{:S(2)}) collective-permute-start(bf16[768,384]{1,0:T(8,128)(2,1)S(1)} %constant_dynamic-update-slice_fusion.mine_ref), channel_id=1, source_target_pairs={{0,1},{1,0},{2,3},{3,2},{4,5},{5,4},{6,7},{7,6},{8,9},{9,8},{10,11... | collective-permute-start | bytes 1769480 | tf_op jit(solution)/shard_map/ppermute | solution.py:200

commit v2 on v1

--- a/solution.py
+++ b/solution.py
@@ -54,16 +54,27 @@
     return total
 
 
+def pack_kernel(x_ref, g_ref, out_ref):
+    size, both, width = out_ref.shape
+    for side, ref in enumerate((x_ref, g_ref)):
+        rows = ref[...].astype(f32).reshape(size, both // 2, width)
+        if side == 0:
+            first = rows
+        else:
+            out_ref[...] = jnp.concatenate([first, rows], axis=1).astype(bf16)
+
+
 def switch_kernel(
-    levels, block, me_ref, x_ref, g_ref, w_in_ref, bias_ref, w_out_ref, logit_ref, scale_ref,
+    levels, block, me_ref, both_ref, w_in_ref, bias_ref, w_out_ref, logit_ref, scale_ref,
     grad_ref, keep_ref, send_ref,
     low_s, act_s, slope_s, normed_s, inverse_s, pre_s, bg_s,
 ):
-    rows, width = x_ref.shape
+    rows, width = grad_ref.shape
     half = rows // 2
+    both = both_ref[...].astype(f32)
     gate = jax.nn.sigmoid(logit_ref[...])
     scale = scale_ref[...]
-    state = x_ref[...].astype(f32)
+    state = both[:, :block].reshape(rows, width)
     for level in range(levels):
         at = pl.ds(level * half, half)
         paired = pair_rows(state, block * 2**level)
@@ -87,7 +98,7 @@
             branch = dot(act, w_out_ref[...], (1, 0))
             result = (gate * paired + scale * branch).astype(bf16).astype(f32)
             state = unpair_rows(result, block * 2**level)
-    grad = g_ref[...].astype(f32)
+    grad = both[:, block:].reshape(rows, width)
     for level in reversed(range(levels)):
         at = pl.ds(level * half, half)
         upstream = pair_rows(grad, block * 2**level)
@@ -201,7 +212,7 @@
                          [(d, d ^ mask) for d in range(size)]) for i, mask in enumerate(masks)]
 
 
-def sum_over_devices(me, keep, send, size, factor):
+def sum_over_devices(me, keep, send, size, factor, beside):
     bits = size.bit_length() - 1
     rows, double = keep.shape
     arrived = exchange([send], [1], size)
@@ -224,11 +235,12 @@
         total = call(functools.partial(total_kernel, 1.0), struct((rows, double), bf16), count=len(parts))(*parts)
         parts = [total] + exchange([total], [1 << rest], size)
     mine = call(functools.partial(total_kernel, factor), struct((rows, double), bf16), count=len(parts))(*parts)
+    mine, beside = lax.optimization_barrier((mine, beside))
     for bit, radix in reversed(phases):
         got = exchange([mine] * (radix - 1), [m << bit for m in range(1, radix)], size)
         mine = jnp.concatenate([mine] + got, axis=0)
     (other,) = exchange([mine], [1], size)
-    return mine, other, rows, phases
+    return mine, other, rows, phases, beside
 
 
 def shards(saved_input, cotangent, w_in, bias_in, w_out, residual_logit, branch_scale):
@@ -239,12 +251,13 @@
     block = rows // size
     half = rows // 2
     me = lax.axis_index("seq").astype(jnp.int32).reshape(1)
-    both = jnp.concatenate(
-        [saved_input.reshape(size, block, width), cotangent.reshape(size, block, width)], axis=1
-    )
+    if block % 8 == 0:
+        both = call(pack_kernel, struct((size, 2 * block, width), bf16), count=2)(saved_input, cotangent)
+    else:
+        both = jnp.concatenate(
+            [saved_input.reshape(size, block, width), cotangent.reshape(size, block, width)], axis=1
+        )
     both = lax.all_to_all(both, "seq", split_axis=0, concat_axis=0, tiled=True)
-    state = both[:, :block].reshape(rows, width)
-    grads = both[:, block:].reshape(rows, width)
     total = levels * half
     grad_state, keep, send = call(
         functools.partial(switch_kernel, levels, block),
@@ -258,14 +271,14 @@
             pltpu.VMEM((total, units), bf16),
             pltpu.VMEM((total, double), bf16),
         ],
-        specs=[SMEM] + [VMEM] * 7,
-    )(me, state, grads, w_in, bias_in.reshape(1, units), w_out, residual_logit.reshape(1, double),
+        specs=[SMEM] + [VMEM] * 6,
+    )(me, both, w_in, bias_in.reshape(1, units), w_out, residual_logit.reshape(1, double),
       branch_scale.reshape(1, double))
     factor = float(rows * size) ** (-0.5)
-    mine, other, step, phases = sum_over_devices(me, keep, send, size, factor)
     grad_state = lax.all_to_all(
         grad_state.reshape(size, block, width), "seq", split_axis=0, concat_axis=0, tiled=True
     ).reshape(rows, width)
+    mine, other, step, phases, grad_state = sum_over_devices(me, keep, send, size, factor, grad_state)
     grad_in, grad_out = call(
         functools.partial(place_kernel, phases, step),
         [struct((double, units), f32), struct((units, double), f32)],

time: 78.6 us -> 72.5 us (0.922)
  blocking collectives: 11.2 us -> 0 us
  starting transfers between devices: 23.5 us -> 26 us
  waiting for transfers between devices: 29.1 us -> 31.2 us
  Pallas kernels: 9.91 us -> 11.3 us
    all_to_all x1 -> x0, blocking collectives: 11.2 us -> none  [shards(): lax.all_to_all(grad_state.reshape(size, block, width), 'seq', split_axis=...]
    all_to_all x0 -> x1, starting transfers between devices: none -> 2.58 us  [shards(): lax.all_to_all(grad_state.reshape(size, block, width), 'seq', split_axis=...]
    ppermute x14, waiting for transfers between devices: 18.6 us -> 20.6 us  [exchange(): lax.ppermute(value if not isinstance(value, list) else value[i], 'seq', [...]
    unnamed x19 -> x18, local copies, waits for them, and re-layouts: 2.93 us -> 2.93 us
  transfers between devices with their start and end apart: 15 -> 16, of which waited for: 10 -> 10; matrix products, arithmetic and copies ran while one was open for 1% -> 1% of each run, Pallas kernels for 0% -> 0%
where the time goes in v2:
time: 72.5 us; the launch traced here: 72.2 us
  waiting for transfers between devices  31.2 us (43%)
  starting transfers between devices  26 us (36%)
  Pallas kernels  11.3 us (16%)
  local copies, waits for them, and re-layouts  2.98 us (4%)
  between operations  0.85 us (1%)
    ppermute x14, waiting for transfers between devices, exchange(): lax.ppermute(value if not isinstance(value, list) else value[i], 'seq', [...  20.6 us
    ppermute x14, starting transfers between devices, exchange(): lax.ppermute(value if not isinstance(value, list) else value[i], 'seq', [...  16.1 us
    all_to_all x1, waiting for transfers between devices, shards(): both = lax.all_to_all(both, 'seq', split_axis=0, concat_axis=0, tiled=True)  10.5 us
    pallas_call x1, Pallas kernels, shards(): call(functools.partial(switch_kernel, levels, block), [struct((rows, widt...  8.78 us
    all_to_all x1, starting transfers between devices, shards(): both = lax.all_to_all(both, 'seq', split_axis=0, concat_axis=0, tiled=True)  7.3 us
    unnamed x18, local copies, waits for them, and re-layouts  2.93 us
    all_to_all x1, starting transfers between devices, shards(): lax.all_to_all(grad_state.reshape(size, block, width), 'seq', split_axis=...  2.58 us
    pallas_call x1, Pallas kernels, shards(): call(functools.partial(place_kernel, phases, step), [struct((double, unit...  1.56 us
  transfers between devices with their start and end apart: 16, of which 10 were waited for; matrix products, arithmetic and copies ran while one was open for 1% of the time, Pallas kernels for 0%

profile of v2, /device:TPU:0, one launch (start us, length us, event | category | flops | bytes accessed | tf_op | source)
XLA Modules:
  0.0 72.2 jit_solution(8291289642755871209)
XLA Ops:
  0.7 1.1 %copy.13.x_ref = bf16[256,192]{1,0:T(8,128)(2,1)S(1)} copy(bf16[256,192]{0,1:T(8,128)(2,1)} %param.7) | data formatting | bytes 196608 | tf_op args[0]
  1.8 1.0 %copy.14.g_ref = bf16[256,192]{1,0:T(8,128)(2,1)S(1)} copy(bf16[256,192]{0,1:T(8,128)(2,1)} %param.8) | data formatting | bytes 196608 | tf_op args[1]
  3.5 7.3 %all-to-all-start = ((bf16[32,16,192]{2,1,0:T(8,128)(2,1)}), bf16[32,16,192]{2,1,0:T(8,128)(2,1)S(1)}, u32[]{:S(2)}, u32[]{:S(2)}) async-start(bf16[32,16,192]{2,1,0:T(8,128)(2,1)} %shard_map.94), calls=%async_computation | async-start | bytes 524288 | tf_op jit(solution)/shard_map/all_to_all | solution.py:260
  10.9 10.5 %all-to-all-done.both_ref = bf16[32,16,192]{2,1,0:T(8,128)(2,1)S(1)} async-done(((bf16[32,16,192]{2,1,0:T(8,128)(2,1)}), bf16[32,16,192]{2,1,0:T(8,128)(2,1)S(1)}, u32[]{:S(2)}, u32[]{:S(2)}) %all-to-all-start) | async-done | bytes 196640 | tf_op jit(solution)/shard_map/all_to_all | solution.py:260
  21.4 8.8 %shard_map.95 = (bf16[256,192]{1,0:T(8,128)(2,1)}, f32[768,384]{1,0:T(8,128)S(1)}, bf16[768,384]{1,0:T(8,128)(2,1)S(1)}) custom-call(s32[1]{0:T(128)} %bitcast.me_ref, bf16[32,16,192]{2,1,0:T(8,128)(2,1)S(1)} %all-to-all-done.both_ref, bf16[384,768]{1,0:T(8,128)(2,1)S(1)} %copy-done, f32[1,768]{1,0:T(1,128)S(1)} %reshape.25.bias_ref, ...), custom_call_target="tpu_custom_call" | custom-call | tf_op jit(solution)/shard_map/pallas_call | solution.py:262
  30.2 2.6 %all-to-all-start.1 = ((bf16[32,8,192]{2,1,0:T(8,128)(2,1)}), bf16[32,8,192]{2,1,0:T(8,128)(2,1)S(1)}, u32[]{:S(2)}, u32[]{:S(2)}) async-start(bf16[32,8,192]{2,1,0:T(8,128)(2,1)} %bitcast.1), calls=%async_computation.1 | async-start | bytes 262144 | tf_op jit(solution)/shard_map/all_to_all | solution.py:278
  32.9 1.8 %collective-permute-start.1 = (bf16[192,384]{1,0:T(8,128)(2,1)S(1)}, bf16[192,384]{1,0:T(8,128)(2,1)S(1)}, u32[]{:S(2)}, u32[]{:S(2)}) collective-permute-start(bf16[192,384]{1,0:T(8,128)(2,1)S(1)} %get-tuple-element.21), channel_id=1, source_target_pairs={{0,2},{1,3},{2,0},{3,1},{4,6},{5,7},{6,4},{7,5},{8,10},{9,11},{10,... | collective-permute-start | bytes 442376 | tf_op jit(solution)/shard_map/ppermute | solution.py:211
  34.7 1.5 %collective-permute-start.2 = (bf16[192,384]{1,0:T(8,128)(2,1)S(1)}, bf16[192,384]{1,0:T(8,128)(2,1)S(1)}, u32[]{:S(2)}, u32[]{:S(2)}) collective-permute-start(bf16[192,384]{1,0:T(8,128)(2,1)S(1)} %get-tuple-element.22), channel_id=1, source_target_pairs={{0,4},{1,5},{2,6},{3,7},{4,0},{5,1},{6,2},{7,3},{8,12},{9,13},{10,... | collective-permute-start | bytes 442376 | tf_op jit(solution)/shard_map/ppermute | solution.py:211
  36.5 4.2 %collective-permute-done.1.refs_1_ = bf16[192,384]{1,0:T(8,128)(2,1)S(1)} collective-permute-done((bf16[192,384]{1,0:T(8,128)(2,1)S(1)}, bf16[192,384]{1,0:T(8,128)(2,1)S(1)}, u32[]{:S(2)}, u32[]{:S(2)}) %collective-permute-start.1) | collective-permute-done | bytes 147488 | tf_op jit(solution)/shard_map/ppermute | solution.py:211
  40.7 3.8 %collective-permute-done.2.refs_2_ = bf16[192,384]{1,0:T(8,128)(2,1)S(1)} collective-permute-done((bf16[192,384]{1,0:T(8,128)(2,1)S(1)}, bf16[192,384]{1,0:T(8,128)(2,1)S(1)}, u32[]{:S(2)}, u32[]{:S(2)}) %collective-permute-start.2) | collective-permute-done | bytes 147488 | tf_op jit(solution)/shard_map/ppermute | solution.py:211
  44.6 1.4 %collective-permute-start.4 = (bf16[48,384]{1,0:T(8,128)(2,1)S(1)}, bf16[48,384]{1,0:T(8,128)(2,1)S(1)}, u32[]{:S(2)}, u32[]{:S(2)}) collective-permute-start(bf16[48,384]{1,0:T(8,128)(2,1)S(1)} %get-tuple-element.25), channel_id=1, source_target_pairs={{0,8},{1,9},{2,10},{3,11},{4,12},{5,13},{6,14},{7,15},{8,0},{9,1},... | collective-permute-start | bytes 110600 | tf_op jit(solution)/shard_map/ppermute | solution.py:211
  45.9 2.4 %collective-permute-start.5 = (bf16[48,384]{1,0:T(8,128)(2,1)S(1)}, bf16[48,384]{1,0:T(8,128)(2,1)S(1)}, u32[]{:S(2)}, u32[]{:S(2)}) collective-permute-start(bf16[48,384]{1,0:T(8,128)(2,1)S(1)} %get-tuple-element.26), channel_id=1, source_target_pairs={{0,16},{1,17},{2,18},{3,19},{4,20},{5,21},{6,22},{7,23},{8,24},{9,... | collective-permute-start | bytes 110600 | tf_op jit(solution)/shard_map/ppermute | solution.py:211
  49.0 2.3 %collective-permute-done.5.refs_2_ = bf16[48,384]{1,0:T(8,128)(2,1)S(1)} collective-permute-done((bf16[48,384]{1,0:T(8,128)(2,1)S(1)}, bf16[48,384]{1,0:T(8,128)(2,1)S(1)}, u32[]{:S(2)}, u32[]{:S(2)}) %collective-permute-start.5) | collective-permute-done | bytes 36896 | tf_op jit(solution)/shard_map/ppermute | solution.py:211
  51.3 2.9 %collective-permute-done.6.refs_3_ = bf16[48,384]{1,0:T(8,128)(2,1)S(1)} collective-permute-done((bf16[48,384]{1,0:T(8,128)(2,1)S(1)}, bf16[48,384]{1,0:T(8,128)(2,1)S(1)}, u32[]{:S(2)}, u32[]{:S(2)}) %collective-permute-start.6) | collective-permute-done | bytes 36896 | tf_op jit(solution)/shard_map/ppermute | solution.py:211
  54.9 3.8 %collective-permute-start.7 = (bf16[48,384]{1,0:T(8,128)(2,1)S(1)}, bf16[48,384]{1,0:T(8,128)(2,1)S(1)}, u32[]{:S(2)}, u32[]{:S(2)}) collective-permute-start(bf16[48,384]{1,0:T(8,128)(2,1)S(1)} %shard_map.98), channel_id=1, source_target_pairs={{0,8},{1,9},{2,10},{3,11},{4,12},{5,13},{6,14},{7,15},{8,0},{9,1},... | collective-permute-start | bytes 110600 | tf_op jit(solution)/shard_map/ppermute | solution.py:211
  58.6 1.9 %collective-permute-done.7 = bf16[48,384]{1,0:T(8,128)(2,1)S(1)} collective-permute-done((bf16[48,384]{1,0:T(8,128)(2,1)S(1)}, bf16[48,384]{1,0:T(8,128)(2,1)S(1)}, u32[]{:S(2)}, u32[]{:S(2)}) %collective-permute-start.7) | collective-permute-done | bytes 36896 | tf_op jit(solution)/shard_map/ppermute | solution.py:211
  60.7 1.1 %collective-permute-start.10 = (bf16[192,384]{1,0:T(8,128)(2,1)S(1)}, bf16[192,384]{1,0:T(8,128)(2,1)S(1)}, u32[]{:S(2)}, u32[]{:S(2)}) collective-permute-start(bf16[192,384]{1,0:T(8,128)(2,1)S(1)} %get-tuple-element.36), channel_id=1, source_target_pairs={{0,2},{1,3},{2,0},{3,1},{4,6},{5,7},{6,4},{7,5},{8,10},{9,11},{10,... | collective-permute-start | bytes 442376 | tf_op jit(solution)/shard_map/ppermute | solution.py:211
  61.8 0.8 %collective-permute-start.11 = (bf16[192,384]{1,0:T(8,128)(2,1)S(1)}, bf16[192,384]{1,0:T(8,128)(2,1)S(1)}, u32[]{:S(2)}, u32[]{:S(2)}) collective-permute-start(bf16[192,384]{1,0:T(8,128)(2,1)S(1)} %get-tuple-element.36), channel_id=1, source_target_pairs={{0,4},{1,5},{2,6},{3,7},{4,0},{5,1},{6,2},{7,3},{8,12},{9,13},{10,... | collective-permute-start | bytes 442376 | tf_op jit(solution)/shard_map/ppermute | solution.py:211
  62.5 1.7 %collective-permute-start.12 = (bf16[192,384]{1,0:T(8,128)(2,1)S(1)}, bf16[192,384]{1,0:T(8,128)(2,1)S(1)}, u32[]{:S(2)}, u32[]{:S(2)}) collective-permute-start(bf16[192,384]{1,0:T(8,128)(2,1)S(1)} %get-tuple-element.36), channel_id=1, source_target_pairs={{0,6},{1,7},{2,4},{3,5},{4,2},{5,3},{6,0},{7,1},{8,14},{9,15},{10,... | collective-permute-start | bytes 442376 | tf_op jit(solution)/shard_map/ppermute | solution.py:211
  64.2 1.7 %collective-permute-done.10 = bf16[192,384]{1,0:T(8,128)(2,1)S(1)} collective-permute-done((bf16[192,384]{1,0:T(8,128)(2,1)S(1)}, bf16[192,384]{1,0:T(8,128)(2,1)S(1)}, u32[]{:S(2)}, u32[]{:S(2)}) %collective-permute-start.10) | collective-permute-done | bytes 147488 | tf_op jit(solution)/shard_map/ppermute | solution.py:211
  65.9 1.0 %collective-permute-done.11 = bf16[192,384]{1,0:T(8,128)(2,1)S(1)} collective-permute-done((bf16[192,384]{1,0:T(8,128)(2,1)S(1)}, bf16[192,384]{1,0:T(8,128)(2,1)S(1)}, u32[]{:S(2)}, u32[]{:S(2)}) %collective-permute-start.11) | collective-permute-done | bytes 147488 | tf_op jit(solution)/shard_map/ppermute | solution.py:211
  66.9 1.6 %collective-permute-done.12 = bf16[192,384]{1,0:T(8,128)(2,1)S(1)} collective-permute-done((bf16[192,384]{1,0:T(8,128)(2,1)S(1)}, bf16[192,384]{1,0:T(8,128)(2,1)S(1)}, u32[]{:S(2)}, u32[]{:S(2)}) %collective-permute-start.12) | collective-permute-done | bytes 147488 | tf_op jit(solution)/shard_map/ppermute | solution.py:211
  69.4 1.2 %collective-permute-done.13.other_ref = bf16[768,384]{1,0:T(8,128)(2,1)S(1)} collective-permute-done((bf16[768,384]{1,0:T(8,128)(2,1)S(1)}, bf16[768,384]{1,0:T(8,128)(2,1)S(1)}, u32[]{:S(2)}, u32[]{:S(2)}) %collective-permute-start.13) | collective-permute-done | bytes 589856 | tf_op jit(solution)/shard_map/ppermute | solution.py:211
  70.7 1.6 %shard_map.99 = (f32[384,768]{1,0:T(8,128)}, f32[768,384]{1,0:T(8,128)}) custom-call(s32[1]{0:T(128)} %bitcast.me_ref, bf16[768,384]{1,0:T(8,128)(2,1)S(1)} %constant_dynamic-update-slice_fusion.4.mine_ref, bf16[768,384]{1,0:T(8,128)(2,1)S(1)} %collective-permute-done.13.other_ref), custom_call_target="tpu_custom_call" | custom-call | tf_op jit(solution)/shard_map/pallas_call | solution.py:282
  (37 shorter events, 3.6 us)
Async XLA Ops:
  0.6 10.2 %copy-start.3 = (f32[384]{0:T(512)S(1)}, f32[384]{0:T(512)}, u32[]{:S(2)}) copy-start(f32[384]{0:T(512)} %param.12) | copy-start | bytes 4612
  0.6 10.2 %copy-start.4 = (f32[384]{0:T(512)S(1)}, f32[384]{0:T(512)}, u32[]{:S(2)}) copy-start(f32[384]{0:T(512)} %param.13) | copy-start | bytes 4612
  0.7 10.2 %copy-start.2 = (f32[768]{0:T(1024)S(1)}, f32[768]{0:T(1024)}, u32[]{:S(2)}) copy-start(f32[768]{0:T(1024)} %param.10) | copy-start | bytes 9220
  0.7 20.7 %copy-start.1 = (bf16[768,384]{1,0:T(8,128)(2,1)S(1)}, bf16[768,384]{1,0:T(8,128)(2,1)}, u32[]{:S(2)}) copy-start(bf16[768,384]{1,0:T(8,128)(2,1)} %w_out_ref.1) | copy-start | bytes 1769476
  0.7 20.7 %copy-start = (bf16[384,768]{1,0:T(8,128)(2,1)S(1)}, bf16[384,768]{1,0:T(8,128)(2,1)}, u32[]{:S(2)}) copy-start(bf16[384,768]{1,0:T(8,128)(2,1)} %w_in_ref.1) | copy-start | bytes 1769476
  3.5 17.9 %all-to-all-start = ((bf16[32,16,192]{2,1,0:T(8,128)(2,1)}), bf16[32,16,192]{2,1,0:T(8,128)(2,1)S(1)}, u32[]{:S(2)}, u32[]{:S(2)}) async-start(bf16[32,16,192]{2,1,0:T(8,128)(2,1)} %shard_map.94), calls=%async_computation | async-start | bytes 524288 | tf_op jit(solution)/shard_map/all_to_all | solution.py:260
  30.2 2.6 %collective-permute-start = (bf16[768,384]{1,0:T(8,128)(2,1)S(1)}, bf16[768,384]{1,0:T(8,128)(2,1)S(1)}, u32[]{:S(2)}, u32[]{:S(2)}) collective-permute-start(bf16[768,384]{1,0:T(8,128)(2,1)S(1)} %get-tuple-element.19), channel_id=1, source_target_pairs={{0,1},{1,0},{2,3},{3,2},{4,5},{5,4},{6,7},{7,6},{8,9},{9,8},{10,11... | collective-permute-start | bytes 1769480 | tf_op jit(solution)/shard_map/ppermute | solution.py:211
  30.2 24.0 %all-to-all-start.1 = ((bf16[32,8,192]{2,1,0:T(8,128)(2,1)}), bf16[32,8,192]{2,1,0:T(8,128)(2,1)S(1)}, u32[]{:S(2)}, u32[]{:S(2)}) async-start(bf16[32,8,192]{2,1,0:T(8,128)(2,1)} %bitcast.1), calls=%async_computation.1 | async-start | bytes 262144 | tf_op jit(solution)/shard_map/all_to_all | solution.py:278
  32.9 7.8 %collective-permute-start.1 = (bf16[192,384]{1,0:T(8,128)(2,1)S(1)}, bf16[192,384]{1,0:T(8,128)(2,1)S(1)}, u32[]{:S(2)}, u32[]{:S(2)}) collective-permute-start(bf16[192,384]{1,0:T(8,128)(2,1)S(1)} %get-tuple-element.21), channel_id=1, source_target_pairs={{0,2},{1,3},{2,0},{3,1},{4,6},{5,7},{6,4},{7,5},{8,10},{9,11},{10,... | collective-permute-start | bytes 442376 | tf_op jit(solution)/shard_map/ppermute | solution.py:211
  34.7 9.8 %collective-permute-start.2 = (bf16[192,384]{1,0:T(8,128)(2,1)S(1)}, bf16[192,384]{1,0:T(8,128)(2,1)S(1)}, u32[]{:S(2)}, u32[]{:S(2)}) collective-permute-start(bf16[192,384]{1,0:T(8,128)(2,1)S(1)} %get-tuple-element.22), channel_id=1, source_target_pairs={{0,4},{1,5},{2,6},{3,7},{4,0},{5,1},{6,2},{7,3},{8,12},{9,13},{10,... | collective-permute-start | bytes 442376 | tf_op jit(solution)/shard_map/ppermute | solution.py:211
  36.1 8.3 %collective-permute-start.3 = (bf16[192,384]{1,0:T(8,128)(2,1)S(1)}, bf16[192,384]{1,0:T(8,128)(2,1)S(1)}, u32[]{:S(2)}, u32[]{:S(2)}) collective-permute-start(bf16[192,384]{1,0:T(8,128)(2,1)S(1)} %get-tuple-element.23), channel_id=1, source_target_pairs={{0,6},{1,7},{2,4},{3,5},{4,2},{5,3},{6,0},{7,1},{8,14},{9,15},{10,... | collective-permute-start | bytes 442376 | tf_op jit(solution)/shard_map/ppermute | solution.py:211
  44.6 4.5 %collective-permute-start.4 = (bf16[48,384]{1,0:T(8,128)(2,1)S(1)}, bf16[48,384]{1,0:T(8,128)(2,1)S(1)}, u32[]{:S(2)}, u32[]{:S(2)}) collective-permute-start(bf16[48,384]{1,0:T(8,128)(2,1)S(1)} %get-tuple-element.25), channel_id=1, source_target_pairs={{0,8},{1,9},{2,10},{3,11},{4,12},{5,13},{6,14},{7,15},{8,0},{9,1},... | collective-permute-start | bytes 110600 | tf_op jit(solution)/shard_map/ppermute | solution.py:211
  45.9 5.3 %collective-permute-start.5 = (bf16[48,384]{1,0:T(8,128)(2,1)S(1)}, bf16[48,384]{1,0:T(8,128)(2,1)S(1)}, u32[]{:S(2)}, u32[]{:S(2)}) collective-permute-start(bf16[48,384]{1,0:T(8,128)(2,1)S(1)} %get-tuple-element.26), channel_id=1, source_target_pairs={{0,16},{1,17},{2,18},{3,19},{4,20},{5,21},{6,22},{7,23},{8,24},{9,... | collective-permute-start | bytes 110600 | tf_op jit(solution)/shard_map/ppermute | solution.py:211
  48.3 5.8 %collective-permute-start.6 = (bf16[48,384]{1,0:T(8,128)(2,1)S(1)}, bf16[48,384]{1,0:T(8,128)(2,1)S(1)}, u32[]{:S(2)}, u32[]{:S(2)}) collective-permute-start(bf16[48,384]{1,0:T(8,128)(2,1)S(1)} %get-tuple-element.27), channel_id=1, source_target_pairs={{0,24},{1,25},{2,26},{3,27},{4,28},{5,29},{6,30},{7,31},{8,16},{9,... | collective-permute-start | bytes 110600 | tf_op jit(solution)/shard_map/ppermute | solution.py:211
  54.2 6.5 %collective-permute-start.9 = (bf16[48,384]{1,0:T(8,128)(2,1)S(1)}, bf16[48,384]{1,0:T(8,128)(2,1)S(1)}, u32[]{:S(2)}, u32[]{:S(2)}) collective-permute-start(bf16[48,384]{1,0:T(8,128)(2,1)S(1)} %shard_map.98), channel_id=1, source_target_pairs={{0,24},{1,25},{2,26},{3,27},{4,28},{5,29},{6,30},{7,31},{8,16},{9,... | collective-permute-start | bytes 110600 | tf_op jit(solution)/shard_map/ppermute | solution.py:211
  54.9 5.7 %collective-permute-start.8 = (bf16[48,384]{1,0:T(8,128)(2,1)S(1)}, bf16[48,384]{1,0:T(8,128)(2,1)S(1)}, u32[]{:S(2)}, u32[]{:S(2)}) collective-permute-start(bf16[48,384]{1,0:T(8,128)(2,1)S(1)} %shard_map.98), channel_id=1, source_target_pairs={{0,16},{1,17},{2,18},{3,19},{4,20},{5,21},{6,22},{7,23},{8,24},{9,... | collective-permute-start | bytes 110600 | tf_op jit(solution)/shard_map/ppermute | solution.py:211
  54.9 5.7 %collective-permute-start.7 = (bf16[48,384]{1,0:T(8,128)(2,1)S(1)}, bf16[48,384]{1,0:T(8,128)(2,1)S(1)}, u32[]{:S(2)}, u32[]{:S(2)}) collective-permute-start(bf16[48,384]{1,0:T(8,128)(2,1)S(1)} %shard_map.98), channel_id=1, source_target_pairs={{0,8},{1,9},{2,10},{3,11},{4,12},{5,13},{6,14},{7,15},{8,0},{9,1},... | collective-permute-start | bytes 110600 | tf_op jit(solution)/shard_map/ppermute | solution.py:211
  60.7 5.2 %collective-permute-start.10 = (bf16[192,384]{1,0:T(8,128)(2,1)S(1)}, bf16[192,384]{1,0:T(8,128)(2,1)S(1)}, u32[]{:S(2)}, u32[]{:S(2)}) collective-permute-start(bf16[192,384]{1,0:T(8,128)(2,1)S(1)} %get-tuple-element.36), channel_id=1, source_target_pairs={{0,2},{1,3},{2,0},{3,1},{4,6},{5,7},{6,4},{7,5},{8,10},{9,11},{10,... | collective-permute-start | bytes 442376 | tf_op jit(solution)/shard_map/ppermute | solution.py:211
  61.8 5.1 %collective-permute-start.11 = (bf16[192,384]{1,0:T(8,128)(2,1)S(1)}, bf16[192,384]{1,0:T(8,128)(2,1)S(1)}, u32[]{:S(2)}, u32[]{:S(2)}) collective-permute-start(bf16[192,384]{1,0:T(8,128)(2,1)S(1)} %get-tuple-element.36), channel_id=1, source_target_pairs={{0,4},{1,5},{2,6},{3,7},{4,0},{5,1},{6,2},{7,3},{8,12},{9,13},{10,... | collective-permute-start | bytes 442376 | tf_op jit(solution)/shard_map/ppermute | solution.py:211
  62.5 6.0 %collective-permute-start.12 = (bf16[192,384]{1,0:T(8,128)(2,1)S(1)}, bf16[192,384]{1,0:T(8,128)(2,1)S(1)}, u32[]{:S(2)}, u32[]{:S(2)}) collective-permute-start(bf16[192,384]{1,0:T(8,128)(2,1)S(1)} %get-tuple-element.36), channel_id=1, source_target_pairs={{0,6},{1,7},{2,4},{3,5},{4,2},{5,3},{6,0},{7,1},{8,14},{9,15},{10,... | collective-permute-start | bytes 442376 | tf_op jit(solution)/shard_map/ppermute | solution.py:211
  68.6 2.1 %collective-permute-start.13 = (bf16[768,384]{1,0:T(8,128)(2,1)S(1)}, bf16[768,384]{1,0:T(8,128)(2,1)S(1)}, u32[]{:S(2)}, u32[]{:S(2)}) collective-permute-start(bf16[768,384]{1,0:T(8,128)(2,1)S(1)} %constant_dynamic-update-slice_fusion.4.mine_ref), channel_id=1, source_target_pairs={{0,1},{1,0},{2,3},{3,2},{4,5},{5,4},{6,7},{7,6},{8,9},{9,8},{10,11... | collective-permute-start | bytes 1769480 | tf_op jit(solution)/shard_map/ppermute | solution.py:211

commit v3 on v2

--- a/solution.py
+++ b/solution.py
@@ -57,7 +57,7 @@
 def pack_kernel(x_ref, g_ref, out_ref):
     size, both, width = out_ref.shape
     for side, ref in enumerate((x_ref, g_ref)):
-        rows = ref[...].astype(f32).reshape(size, both // 2, width)
+        rows = ref[...].astype(f32).T.reshape(size, both // 2, width)
         if side == 0:
             first = rows
         else:
@@ -67,10 +67,13 @@
 def switch_kernel(
     levels, block, me_ref, both_ref, w_in_ref, bias_ref, w_out_ref, logit_ref, scale_ref,
     grad_ref, keep_ref, send_ref,
-    low_s, act_s, slope_s, normed_s, inverse_s, pre_s, bg_s,
+    low_s, act_s, slope_s, normed_s, inverse_s, pre_s, bg_s, paired_s,
 ):
-    rows, width = grad_ref.shape
-    half = rows // 2
+    half, double = paired_s.shape
+    rows, width = 2 * half, double // 2
+    units = bias_ref.shape[1]
+    riding = send_ref.shape[0] > units
+    core = me_ref[0] % 2
     both = both_ref[...].astype(f32)
     gate = jax.nn.sigmoid(logit_ref[...])
     scale = scale_ref[...]
@@ -115,11 +118,27 @@
             - normed * jnp.mean(normed_grad * normed, axis=-1, keepdims=True)
         )
         result = (gate * upstream + inverse_s[at, :] * moved).astype(bf16).astype(f32)
-        grad = unpair_rows(result, block * 2**level)
-    grad_ref[...] = grad.astype(bf16)
+        if level > 0 or not riding:
+            grad = unpair_rows(result, block * 2**level)
+    if riding:
+        turned = jnp.concatenate([result[:, width:], result[:, :width]], axis=1)
+        paired_s[...] = jnp.where(core == 0, result, turned)
+        pairs = half // block
+        kept, sent = [], []
+        for plane in range(4):
+            for low in range(pairs // 8):
+                sides = []
+                for high in range(2):
+                    chip = ((high * (pairs // 8) + low) * 4 + plane) ^ (me_ref[0] >> 1)
+                    sides.append(paired_s[pl.ds(pl.multiple_of(chip * block, 8), block), :])
+                kept.append(jnp.concatenate([side[:, :width] for side in sides], axis=1))
+                sent.append(jnp.concatenate([side[:, width:] for side in sides], axis=1))
+        grad_ref[...] = jnp.concatenate(kept, axis=0).astype(bf16)
+        send_ref[units:, :] = jnp.concatenate(sent, axis=0).astype(bf16)
+    else:
+        grad_ref[...] = grad.astype(bf16)
     grad_in = dot(low_s[...], pre_s[...], (0, 0))
     grad_out = dot(act_s[...], bg_s[...], (0, 0))
-    double, units = grad_in.shape
     step = units // 16
 
     def put_in(ref):
@@ -130,9 +149,7 @@
             )
 
     def put_out(ref):
-        ref[...] = grad_out.astype(ref.dtype)
-
-    core = me_ref[0] % 2
+        ref[0:units, :] = grad_out.astype(ref.dtype)
 
     @pl.when(core == 0)
     def _():
@@ -145,23 +162,71 @@
         put_out(keep_ref)
 
 
-def split_kernel(radix, shift, me_ref, *refs):
-    count = len(refs) - radix
+def split_kernel(radix, shift, cut, me_ref, *refs):
+    count = len(refs) - radix - (cut is not None)
     parts, outs = refs[:count], refs[count:]
-    rows = parts[0].shape[0] // radix
+    rows = outs[0].shape[0]
+    if cut is not None:
+        ride_ref, parts = parts[0], parts[1:]
+        riders = cut(ride_ref, [part.at[rows * radix :, :] for part in parts[1:]])
+        outs[-1][...] = riders[0]
+        for other in range(1, radix):
+            outs[other][rows:, :] = riders[other]
     place = (me_ref[0] >> shift) & (radix - 1)
     for other in range(radix):
         at = pl.ds(pl.multiple_of((place ^ other) * rows, tile), rows)
         total = parts[0][at, :].astype(f32)
         for part in parts[1:]:
             total = total + part[at, :].astype(f32)
-        outs[other][...] = total.astype(outs[other].dtype)
+        outs[other][0:rows, :] = total.astype(outs[other].dtype)
+
+
+def cut_planes(kept_ref, arrived):
+    rows = kept_ref.shape[0] // 4
+    sources = [kept_ref[...], arrived[0][...]]
+    return [jnp.concatenate([source[m * rows : (m + 1) * rows] for source in sources], axis=0) for m in range(4)]
+
+
+def cut_lines(kept_ref, arrived):
+    sources = [ref[...].astype(f32) for ref in [kept_ref] + arrived]
+    rows, double = sources[0].shape
+    width, block = double // 2, rows // 4
+    pieces = []
+    for high in range(2):
+        for low in range(2):
+            sides = []
+            for side in range(2):
+                blocks = []
+                for source in sources[2 * side : 2 * side + 2]:
+                    for core in range(2):
+                        first = (core * 2 + low) * block
+                        blocks.append(source[first : first + block, high * width : (high + 1) * width])
+                sides.append(jnp.concatenate(blocks, axis=0))
+            pieces.append(jnp.concatenate(sides, axis=1).astype(bf16))
+    return pieces
+
+
+def unpack_kernel(block, me_ref, *refs):
+    parts, out_ref, rows_s = refs[:-2], refs[-2], refs[-1]
+    width = rows_s.shape[1]
+    for line, part in enumerate(parts):
+        values = part[part.shape[0] - 4 * block :, :].astype(f32)
+        for plane in range(4):
+            for core in range(2):
+                source = me_ref[0] ^ (line * 8 + plane * 2 + core)
+                first = ((plane % 2) * 2 + core) * block
+                side = plane // 2
+                rows_s[pl.ds(pl.multiple_of(source * block, 8), block), :] = values[
+                    first : first + block, side * width : (side + 1) * width
+                ]
+    out_ref[...] = rows_s[...].T.astype(bf16)
 
 
 def total_kernel(factor, *refs):
+    rows = refs[0].shape[0]
     total = refs[0][...].astype(f32)
     for part in refs[1:-1]:
-        total = total + part[...].astype(f32)
+        total = total + part[0:rows, :].astype(f32)
     refs[-1][...] = (total * factor).astype(refs[-1].dtype)
 
 
@@ -212,35 +277,48 @@
                          [(d, d ^ mask) for d in range(size)]) for i, mask in enumerate(masks)]
 
 
-def sum_over_devices(me, keep, send, size, factor, beside):
+def phases_of(size, units):
+    bits = size.bit_length() - 1
+    phases, bit, rows = [], 1, units
+    while bit < bits and rows % (2 * tile) == 0:
+        radix = 4 if bit + 1 < bits and rows % (4 * tile) == 0 else 2
+        phases.append((bit, radix))
+        rows //= radix
+        bit += radix.bit_length() - 1
+    return phases, bit
+
+
+def sum_over_devices(me, ride, keep, send, size, factor, riding):
     bits = size.bit_length() - 1
     rows, double = keep.shape
-    arrived = exchange([send], [1], size)
-    parts = [keep] + arrived
-    bit = 1
-    phases = []
-    while bit < bits and bit < 5:
-        radix = 4 if bit + 1 < min(bits, 5) else 2
-        phases.append((bit, radix))
-        bit += 2 if radix == 4 else 1
-    for bit, radix in phases:
+    phases, bit = phases_of(size, rows)
+    riding_rows = ride.shape[0] // 2
+    parts = [keep] + exchange([send], [1], size)
+    for phase, (low, radix) in enumerate(phases):
         rows = rows // radix
-        outs = [struct((rows, double), f32)] + [struct((rows, double), bf16)] * (radix - 1)
+        cut = (cut_planes, cut_lines)[phase] if riding else None
+        extra = riding_rows if riding else 0
+        outs = [struct((rows, double), f32)] + [struct((rows + extra, double), bf16)] * (radix - 1)
+        if riding:
+            outs.append(struct((extra, double), bf16))
+            parts = [ride] + parts
         pieces = call(
-            functools.partial(split_kernel, radix, bit), outs, specs=[SMEM] + [VMEM] * len(parts)
+            functools.partial(split_kernel, radix, low, cut), outs, specs=[SMEM] + [VMEM] * len(parts)
         )(me, *parts)
-        parts = [pieces[0]] + exchange(list(pieces[1:]), [m << bit for m in range(1, radix)], size)
-    bit = phases[-1][0] + phases[-1][1].bit_length() - 1
+        ride = pieces[-1] if riding else ride
+        parts = [pieces[0]] + exchange(list(pieces[1:radix]), [m << low for m in range(1, radix)], size)
+    riders = [ride] + parts[1:]
     for rest in range(bit, bits):
         total = call(functools.partial(total_kernel, 1.0), struct((rows, double), bf16), count=len(parts))(*parts)
         parts = [total] + exchange([total], [1 << rest], size)
     mine = call(functools.partial(total_kernel, factor), struct((rows, double), bf16), count=len(parts))(*parts)
-    mine, beside = lax.optimization_barrier((mine, beside))
-    for bit, radix in reversed(phases):
-        got = exchange([mine] * (radix - 1), [m << bit for m in range(1, radix)], size)
+    if not riding:
+        mine, ride = lax.optimization_barrier((mine, ride))
+    for low, radix in reversed(phases):
+        got = exchange([mine] * (radix - 1), [m << low for m in range(1, radix)], size)
         mine = jnp.concatenate([mine] + got, axis=0)
     (other,) = exchange([mine], [1], size)
-    return mine, other, rows, phases, beside
+    return mine, other, rows, phases, riders if riding else ride
 
 
 def shards(saved_input, cotangent, w_in, bias_in, w_out, residual_logit, branch_scale):
@@ -252,16 +330,23 @@
     half = rows // 2
     me = lax.axis_index("seq").astype(jnp.int32).reshape(1)
     if block % 8 == 0:
-        both = call(pack_kernel, struct((size, 2 * block, width), bf16), count=2)(saved_input, cotangent)
+        both = call(pack_kernel, struct((size, 2 * block, width), bf16), count=2)(saved_input.T, cotangent.T)
     else:
         both = jnp.concatenate(
             [saved_input.reshape(size, block, width), cotangent.reshape(size, block, width)], axis=1
         )
     both = lax.all_to_all(both, "seq", split_axis=0, concat_axis=0, tiled=True)
     total = levels * half
+    phases, bit = phases_of(size, units)
+    riding = block % 8 == 0 and [radix for _, radix in phases] == [4, 4] and bit == levels
+    rider = struct((rows // 4, double), bf16)
     grad_state, keep, send = call(
         functools.partial(switch_kernel, levels, block),
-        [struct((rows, width), bf16), struct((units, double), f32), struct((units, double), bf16)],
+        [
+            rider if riding else struct((rows, width), bf16),
+            struct((units, double), f32),
+            struct((units + rider.shape[0] * riding, double), bf16),
+        ],
         scratch=[
             pltpu.VMEM((total, double), bf16),
             pltpu.VMEM((total, units), bf16),
@@ -270,15 +355,24 @@
             pltpu.VMEM((total, 1), f32),
             pltpu.VMEM((total, units), bf16),
             pltpu.VMEM((total, double), bf16),
+            pltpu.VMEM((half, double), f32),
         ],
         specs=[SMEM] + [VMEM] * 6,
     )(me, both, w_in, bias_in.reshape(1, units), w_out, residual_logit.reshape(1, double),
       branch_scale.reshape(1, double))
     factor = float(rows * size) ** (-0.5)
-    grad_state = lax.all_to_all(
-        grad_state.reshape(size, block, width), "seq", split_axis=0, concat_axis=0, tiled=True
-    ).reshape(rows, width)
-    mine, other, step, phases, grad_state = sum_over_devices(me, keep, send, size, factor, grad_state)
+    if not riding:
+        grad_state = lax.all_to_all(
+            grad_state.reshape(size, block, width), "seq", split_axis=0, concat_axis=0, tiled=True
+        ).reshape(rows, width)
+    mine, other, step, phases, grad_state = sum_over_devices(me, grad_state, keep, send, size, factor, riding)
+    if riding:
+        grad_state = call(
+            functools.partial(unpack_kernel, block),
+            struct((width, rows), bf16),
+            scratch=[pltpu.VMEM((rows, width), f32)],
+            specs=[SMEM] + [VMEM] * len(grad_state),
+        )(me, *grad_state).T
     grad_in, grad_out = call(
         functools.partial(place_kernel, phases, step),
         [struct((double, units), f32), struct((units, double), f32)],

time: 72.5 us -> 71 us (0.979)
  starting transfers between devices: 26 us -> 23.4 us
  local copies, waits for them, and re-layouts: 2.98 us -> 5.08 us
  waiting for transfers between devices: 31.2 us -> 29.7 us
    all_to_all x1 -> x0, starting transfers between devices: 2.58 us -> none  [shards(): lax.all_to_all(grad_state.reshape(size, block, width), 'seq', split_axis=...]
    all_to_all x1, waiting for transfers between devices: 10.5 us -> 8.53 us  [shards(): both = lax.all_to_all(both, 'seq', split_axis=0, concat_axis=0, tiled=True)]
    pallas_call x3 -> x4, Pallas kernels: 8.97 us -> 9.32 us  [the longest x1 8.17 us: shards(): call(functools.partial(switch_kernel, levels, block), [rider if riding el...]
    unnamed x18 -> x14, local copies, waits for them, and re-layouts: 2.93 us -> 3 us
  transfers between devices with their start and end apart: 16 -> 15, of which waited for: 10 -> 11; matrix products, arithmetic and copies ran while one was open for 1% -> 3% of each run, Pallas kernels for 0% -> 1%
where the time goes in v3:
time: 71 us; the launch traced here: 70.7 us
  waiting for transfers between devices  29.7 us (42%)
  starting transfers between devices  23.4 us (33%)
  Pallas kernels  11.8 us (17%)
  local copies, waits for them, and re-layouts  5.08 us (7%)
  between operations  0.75 us (1%)
    ppermute x14, waiting for transfers between devices, exchange(): lax.ppermute(value if not isinstance(value, list) else value[i], 'seq', [...  21.1 us
    ppermute x14, starting transfers between devices, exchange(): lax.ppermute(value if not isinstance(value, list) else value[i], 'seq', [...  16.1 us
    all_to_all x1, waiting for transfers between devices, shards(): both = lax.all_to_all(both, 'seq', split_axis=0, concat_axis=0, tiled=True)  8.53 us
    pallas_call x1, Pallas kernels, shards(): call(functools.partial(switch_kernel, levels, block), [rider if riding el...  8.17 us
    all_to_all x1, starting transfers between devices, shards(): both = lax.all_to_all(both, 'seq', split_axis=0, concat_axis=0, tiled=True)  7.3 us
    unnamed x14, local copies, waits for them, and re-layouts  3 us
    pallas_call x1, Pallas kernels, shards(): call(functools.partial(place_kernel, phases, step), [struct((double, unit...  1.56 us
  transfers between devices with their start and end apart: 15, of which 11 were waited for; matrix products, arithmetic and copies ran while one was open for 3% of the time, Pallas kernels for 1%

profile of v3, /device:TPU:0, one launch (start us, length us, event | category | flops | bytes accessed | tf_op | source)
XLA Modules:
  0.0 70.7 jit_solution(11112291243351205540)
XLA Ops:
  0.7 0.9 %copy-done.2 = bf16[256,192]{0,1:T(8,128)(2,1)S(1)} copy-done((bf16[256,192]{0,1:T(8,128)(2,1)S(1)}, bf16[256,192]{0,1:T(8,128)(2,1)}, u32[]{:S(2)}) %copy-start.2) | copy-done | bytes 98328
  1.6 0.9 %copy-done.3 = bf16[256,192]{0,1:T(8,128)(2,1)S(1)} copy-done((bf16[256,192]{0,1:T(8,128)(2,1)S(1)}, bf16[256,192]{0,1:T(8,128)(2,1)}, u32[]{:S(2)}) %copy-start.3) | copy-done | bytes 98328
  3.3 7.3 %all-to-all-start = ((bf16[32,16,192]{2,1,0:T(8,128)(2,1)}), bf16[32,16,192]{2,1,0:T(8,128)(2,1)S(1)}, u32[]{:S(2)}, u32[]{:S(2)}) async-start(bf16[32,16,192]{2,1,0:T(8,128)(2,1)} %shard_map.94), calls=%async_computation | async-start | bytes 524288 | tf_op jit(solution)/shard_map/all_to_all | solution.py:338
  12.7 8.5 %all-to-all-done.both_ref = bf16[32,16,192]{2,1,0:T(8,128)(2,1)S(1)} async-done(((bf16[32,16,192]{2,1,0:T(8,128)(2,1)}), bf16[32,16,192]{2,1,0:T(8,128)(2,1)S(1)}, u32[]{:S(2)}, u32[]{:S(2)}) %all-to-all-start) | async-done | bytes 196640 | tf_op jit(solution)/shard_map/all_to_all | solution.py:338
  21.2 1.1 %copy-done.1 = bf16[768,384]{1,0:T(8,128)(2,1)S(1)} copy-done((bf16[768,384]{1,0:T(8,128)(2,1)S(1)}, bf16[768,384]{1,0:T(8,128)(2,1)}, u32[]{:S(2)}) %copy-start.1) | copy-done | bytes 589848
  22.3 8.2 %shard_map.95 = (bf16[64,384]{1,0:T(8,128)(2,1)S(1)}, f32[768,384]{1,0:T(8,128)S(1)}, bf16[832,384]{1,0:T(8,128)(2,1)S(1)}) custom-call(s32[1]{0:T(128)} %bitcast.me_ref, bf16[32,16,192]{2,1,0:T(8,128)(2,1)S(1)} %all-to-all-done.both_ref, bf16[384,768]{1,0:T(8,128)(2,1)S(1)} %copy-done, f32[1,768]{1,0:T(1,128)S(1)} %reshape.19.bias_ref, ...), custom_call_target="tpu_custom_call" | custom-call | tf_op jit(solution)/shard_map/pallas_call | solution.py:343
  30.6 2.1 %collective-permute-done.refs_2_ = bf16[832,384]{1,0:T(8,128)(2,1)S(1)} collective-permute-done((bf16[832,384]{1,0:T(8,128)(2,1)S(1)}, bf16[832,384]{1,0:T(8,128)(2,1)S(1)}, u32[]{:S(2)}, u32[]{:S(2)}) %collective-permute-start) | collective-permute-done | bytes 639008 | tf_op jit(solution)/shard_map/ppermute | solution.py:276
  33.3 1.3 %collective-permute-start.2 = (bf16[224,384]{1,0:T(8,128)(2,1)S(1)}, bf16[224,384]{1,0:T(8,128)(2,1)S(1)}, u32[]{:S(2)}, u32[]{:S(2)}) collective-permute-start(bf16[224,384]{1,0:T(8,128)(2,1)S(1)} %get-tuple-element.24), channel_id=1, source_target_pairs={{0,4},{1,5},{2,6},{3,7},{4,0},{5,1},{6,2},{7,3},{8,12},{9,13},{10,... | collective-permute-start | bytes 516104 | tf_op jit(solution)/shard_map/ppermute | solution.py:276
  34.6 1.7 %collective-permute-start.3 = (bf16[224,384]{1,0:T(8,128)(2,1)S(1)}, bf16[224,384]{1,0:T(8,128)(2,1)S(1)}, u32[]{:S(2)}, u32[]{:S(2)}) collective-permute-start(bf16[224,384]{1,0:T(8,128)(2,1)S(1)} %get-tuple-element.25), channel_id=1, source_target_pairs={{0,6},{1,7},{2,4},{3,5},{4,2},{5,3},{6,0},{7,1},{8,14},{9,15},{10,... | collective-permute-start | bytes 516104 | tf_op jit(solution)/shard_map/ppermute | solution.py:276
  36.3 3.7 %collective-permute-done.1.refs_2_ = bf16[224,384]{1,0:T(8,128)(2,1)S(1)} collective-permute-done((bf16[224,384]{1,0:T(8,128)(2,1)S(1)}, bf16[224,384]{1,0:T(8,128)(2,1)S(1)}, u32[]{:S(2)}, u32[]{:S(2)}) %collective-permute-start.1) | collective-permute-done | bytes 172064 | tf_op jit(solution)/shard_map/ppermute | solution.py:276
  40.5 2.9 %collective-permute-done.3.refs_4_ = bf16[224,384]{1,0:T(8,128)(2,1)S(1)} collective-permute-done((bf16[224,384]{1,0:T(8,128)(2,1)S(1)}, bf16[224,384]{1,0:T(8,128)(2,1)S(1)}, u32[]{:S(2)}, u32[]{:S(2)}) %collective-permute-start.3) | collective-permute-done | bytes 172064 | tf_op jit(solution)/shard_map/ppermute | solution.py:276
  44.2 1.2 %collective-permute-start.5 = (bf16[80,384]{1,0:T(8,128)(2,1)S(1)}, bf16[80,384]{1,0:T(8,128)(2,1)S(1)}, u32[]{:S(2)}, u32[]{:S(2)}) collective-permute-start(bf16[80,384]{1,0:T(8,128)(2,1)S(1)} %get-tuple-element.28), channel_id=1, source_target_pairs={{0,16},{1,17},{2,18},{3,19},{4,20},{5,21},{6,22},{7,23},{8,24},{9,... | collective-permute-start | bytes 184328 | tf_op jit(solution)/shard_map/ppermute | solution.py:276
  45.4 2.6 %collective-permute-start.6 = (bf16[80,384]{1,0:T(8,128)(2,1)S(1)}, bf16[80,384]{1,0:T(8,128)(2,1)S(1)}, u32[]{:S(2)}, u32[]{:S(2)}) collective-permute-start(bf16[80,384]{1,0:T(8,128)(2,1)S(1)} %get-tuple-element.29), channel_id=1, source_target_pairs={{0,24},{1,25},{2,26},{3,27},{4,28},{5,29},{6,30},{7,31},{8,16},{9,... | collective-permute-start | bytes 184328 | tf_op jit(solution)/shard_map/ppermute | solution.py:276
  48.0 2.6 %collective-permute-done.5.refs_2_ = bf16[80,384]{1,0:T(8,128)(2,1)S(1)} collective-permute-done((bf16[80,384]{1,0:T(8,128)(2,1)S(1)}, bf16[80,384]{1,0:T(8,128)(2,1)S(1)}, u32[]{:S(2)}, u32[]{:S(2)}) %collective-permute-start.5) | collective-permute-done | bytes 61472 | tf_op jit(solution)/shard_map/ppermute | solution.py:276
  50.6 0.9 %collective-permute-done.6.refs_3_ = bf16[80,384]{1,0:T(8,128)(2,1)S(1)} collective-permute-done((bf16[80,384]{1,0:T(8,128)(2,1)S(1)}, bf16[80,384]{1,0:T(8,128)(2,1)S(1)}, u32[]{:S(2)}, u32[]{:S(2)}) %collective-permute-start.6) | collective-permute-done | bytes 61472 | tf_op jit(solution)/shard_map/ppermute | solution.py:276
  51.5 2.5 %collective-permute-start.9 = (bf16[48,384]{1,0:T(8,128)(2,1)S(1)}, bf16[48,384]{1,0:T(8,128)(2,1)S(1)}, u32[]{:S(2)}, u32[]{:S(2)}) collective-permute-start(bf16[48,384]{1,0:T(8,128)(2,1)S(1)} %shard_map.99), channel_id=1, source_target_pairs={{0,24},{1,25},{2,26},{3,27},{4,28},{5,29},{6,30},{7,31},{8,16},{9,... | collective-permute-start | bytes 110600 | tf_op jit(solution)/shard_map/ppermute | solution.py:276
  54.4 1.6 %collective-permute-start.7 = (bf16[48,384]{1,0:T(8,128)(2,1)S(1)}, bf16[48,384]{1,0:T(8,128)(2,1)S(1)}, u32[]{:S(2)}, u32[]{:S(2)}) collective-permute-start(bf16[48,384]{1,0:T(8,128)(2,1)S(1)} %shard_map.99), channel_id=1, source_target_pairs={{0,8},{1,9},{2,10},{3,11},{4,12},{5,13},{6,14},{7,15},{8,0},{9,1},... | collective-permute-start | bytes 110600 | tf_op jit(solution)/shard_map/ppermute | solution.py:276
  56.0 1.4 %collective-permute-done.9 = bf16[48,384]{1,0:T(8,128)(2,1)S(1)} collective-permute-done((bf16[48,384]{1,0:T(8,128)(2,1)S(1)}, bf16[48,384]{1,0:T(8,128)(2,1)S(1)}, u32[]{:S(2)}, u32[]{:S(2)}) %collective-permute-start.9) | collective-permute-done | bytes 36896 | tf_op jit(solution)/shard_map/ppermute | solution.py:276
  57.3 1.6 %collective-permute-done.8 = bf16[48,384]{1,0:T(8,128)(2,1)S(1)} collective-permute-done((bf16[48,384]{1,0:T(8,128)(2,1)S(1)}, bf16[48,384]{1,0:T(8,128)(2,1)S(1)}, u32[]{:S(2)}, u32[]{:S(2)}) %collective-permute-start.8) | collective-permute-done | bytes 36896 | tf_op jit(solution)/shard_map/ppermute | solution.py:276
  58.9 1.8 %collective-permute-start.12 = (bf16[192,384]{1,0:T(8,128)(2,1)S(1)}, bf16[192,384]{1,0:T(8,128)(2,1)S(1)}, u32[]{:S(2)}, u32[]{:S(2)}) collective-permute-start(bf16[192,384]{1,0:T(8,128)(2,1)S(1)} %pad_maximum_fusion), channel_id=1, source_target_pairs={{0,6},{1,7},{2,4},{3,5},{4,2},{5,3},{6,0},{7,1},{8,14},{9,15},{10,... | collective-permute-start | bytes 442376 | tf_op jit(solution)/shard_map/ppermute | solution.py:276
  60.8 1.0 %collective-permute-start.11 = (bf16[192,384]{1,0:T(8,128)(2,1)S(1)}, bf16[192,384]{1,0:T(8,128)(2,1)S(1)}, u32[]{:S(2)}, u32[]{:S(2)}) collective-permute-start(bf16[192,384]{1,0:T(8,128)(2,1)S(1)} %pad_maximum_fusion), channel_id=1, source_target_pairs={{0,4},{1,5},{2,6},{3,7},{4,0},{5,1},{6,2},{7,3},{8,12},{9,13},{10,... | collective-permute-start | bytes 442376 | tf_op jit(solution)/shard_map/ppermute | solution.py:276
  62.5 4.4 %collective-permute-done.10 = bf16[192,384]{1,0:T(8,128)(2,1)S(1)} collective-permute-done((bf16[192,384]{1,0:T(8,128)(2,1)S(1)}, bf16[192,384]{1,0:T(8,128)(2,1)S(1)}, u32[]{:S(2)}, u32[]{:S(2)}) %collective-permute-start.10) | collective-permute-done | bytes 147488 | tf_op jit(solution)/shard_map/ppermute | solution.py:276
  68.0 1.2 %collective-permute-done.13.other_ref = bf16[768,384]{1,0:T(8,128)(2,1)S(1)} collective-permute-done((bf16[768,384]{1,0:T(8,128)(2,1)S(1)}, bf16[768,384]{1,0:T(8,128)(2,1)S(1)}, u32[]{:S(2)}, u32[]{:S(2)}) %collective-permute-start.13) | collective-permute-done | bytes 589856 | tf_op jit(solution)/shard_map/ppermute | solution.py:276
  69.1 1.6 %shard_map.100 = (f32[384,768]{1,0:T(8,128)}, f32[768,384]{1,0:T(8,128)}) custom-call(s32[1]{0:T(128)} %bitcast.me_ref, bf16[768,384]{1,0:T(8,128)(2,1)S(1)} %constant_dynamic-update-slice_fusion.mine_ref, bf16[768,384]{1,0:T(8,128)(2,1)S(1)} %collective-permute-done.13.other_ref), custom_call_target="tpu_custom_call" | custom-call | tf_op jit(solution)/shard_map/pallas_call | solution.py:376
  (32 shorter events, 7.1 us)
Async XLA Ops:
  0.6 20.6 %copy-start = (bf16[384,768]{1,0:T(8,128)(2,1)S(1)}, bf16[384,768]{1,0:T(8,128)(2,1)}, u32[]{:S(2)}) copy-start(bf16[384,768]{1,0:T(8,128)(2,1)} %w_in_ref.1) | copy-start | bytes 1769476
  0.6 1.0 %copy-start.2 = (bf16[256,192]{0,1:T(8,128)(2,1)S(1)}, bf16[256,192]{0,1:T(8,128)(2,1)}, u32[]{:S(2)}) copy-start(bf16[256,192]{0,1:T(8,128)(2,1)} %param.7) | copy-start | bytes 294916
  1.6 0.9 %copy-start.3 = (bf16[256,192]{0,1:T(8,128)(2,1)S(1)}, bf16[256,192]{0,1:T(8,128)(2,1)}, u32[]{:S(2)}) copy-start(bf16[256,192]{0,1:T(8,128)(2,1)} %param.8) | copy-start | bytes 294916
  3.3 17.9 %all-to-all-start = ((bf16[32,16,192]{2,1,0:T(8,128)(2,1)}), bf16[32,16,192]{2,1,0:T(8,128)(2,1)S(1)}, u32[]{:S(2)}, u32[]{:S(2)}) async-start(bf16[32,16,192]{2,1,0:T(8,128)(2,1)} %shard_map.94), calls=%async_computation | async-start | bytes 524288 | tf_op jit(solution)/shard_map/all_to_all | solution.py:338
  21.2 1.1 %copy-start.1 = (bf16[768,384]{1,0:T(8,128)(2,1)S(1)}, bf16[768,384]{1,0:T(8,128)(2,1)}, u32[]{:S(2)}) copy-start(bf16[768,384]{1,0:T(8,128)(2,1)} %w_out_ref.1) | copy-start | bytes 1769476
  30.5 2.1 %collective-permute-start = (bf16[832,384]{1,0:T(8,128)(2,1)S(1)}, bf16[832,384]{1,0:T(8,128)(2,1)S(1)}, u32[]{:S(2)}, u32[]{:S(2)}) collective-permute-start(bf16[832,384]{1,0:T(8,128)(2,1)S(1)} %get-tuple-element.20), channel_id=1, source_target_pairs={{0,1},{1,0},{2,3},{3,2},{4,5},{5,4},{6,7},{7,6},{8,9},{9,8},{10,11... | collective-permute-start | bytes 1916936 | tf_op jit(solution)/shard_map/ppermute | solution.py:276
  32.8 7.3 %collective-permute-start.1 = (bf16[224,384]{1,0:T(8,128)(2,1)S(1)}, bf16[224,384]{1,0:T(8,128)(2,1)S(1)}, u32[]{:S(2)}, u32[]{:S(2)}) collective-permute-start(bf16[224,384]{1,0:T(8,128)(2,1)S(1)} %get-tuple-element.23), channel_id=1, source_target_pairs={{0,2},{1,3},{2,0},{3,1},{4,6},{5,7},{6,4},{7,5},{8,10},{9,11},{10,... | collective-permute-start | bytes 516104 | tf_op jit(solution)/shard_map/ppermute | solution.py:276
  33.3 7.2 %collective-permute-start.2 = (bf16[224,384]{1,0:T(8,128)(2,1)S(1)}, bf16[224,384]{1,0:T(8,128)(2,1)S(1)}, u32[]{:S(2)}, u32[]{:S(2)}) collective-permute-start(bf16[224,384]{1,0:T(8,128)(2,1)S(1)} %get-tuple-element.24), channel_id=1, source_target_pairs={{0,4},{1,5},{2,6},{3,7},{4,0},{5,1},{6,2},{7,3},{8,12},{9,13},{10,... | collective-permute-start | bytes 516104 | tf_op jit(solution)/shard_map/ppermute | solution.py:276
  34.6 8.8 %collective-permute-start.3 = (bf16[224,384]{1,0:T(8,128)(2,1)S(1)}, bf16[224,384]{1,0:T(8,128)(2,1)S(1)}, u32[]{:S(2)}, u32[]{:S(2)}) collective-permute-start(bf16[224,384]{1,0:T(8,128)(2,1)S(1)} %get-tuple-element.25), channel_id=1, source_target_pairs={{0,6},{1,7},{2,4},{3,5},{4,2},{5,3},{6,0},{7,1},{8,14},{9,15},{10,... | collective-permute-start | bytes 516104 | tf_op jit(solution)/shard_map/ppermute | solution.py:276
  43.5 4.4 %collective-permute-start.4 = (bf16[80,384]{1,0:T(8,128)(2,1)S(1)}, bf16[80,384]{1,0:T(8,128)(2,1)S(1)}, u32[]{:S(2)}, u32[]{:S(2)}) collective-permute-start(bf16[80,384]{1,0:T(8,128)(2,1)S(1)} %get-tuple-element.27), channel_id=1, source_target_pairs={{0,8},{1,9},{2,10},{3,11},{4,12},{5,13},{6,14},{7,15},{8,0},{9,1},... | collective-permute-start | bytes 184328 | tf_op jit(solution)/shard_map/ppermute | solution.py:276
  44.2 6.4 %collective-permute-start.5 = (bf16[80,384]{1,0:T(8,128)(2,1)S(1)}, bf16[80,384]{1,0:T(8,128)(2,1)S(1)}, u32[]{:S(2)}, u32[]{:S(2)}) collective-permute-start(bf16[80,384]{1,0:T(8,128)(2,1)S(1)} %get-tuple-element.28), channel_id=1, source_target_pairs={{0,16},{1,17},{2,18},{3,19},{4,20},{5,21},{6,22},{7,23},{8,24},{9,... | collective-permute-start | bytes 184328 | tf_op jit(solution)/shard_map/ppermute | solution.py:276
  45.4 6.1 %collective-permute-start.6 = (bf16[80,384]{1,0:T(8,128)(2,1)S(1)}, bf16[80,384]{1,0:T(8,128)(2,1)S(1)}, u32[]{:S(2)}, u32[]{:S(2)}) collective-permute-start(bf16[80,384]{1,0:T(8,128)(2,1)S(1)} %get-tuple-element.29), channel_id=1, source_target_pairs={{0,24},{1,25},{2,26},{3,27},{4,28},{5,29},{6,30},{7,31},{8,16},{9,... | collective-permute-start | bytes 184328 | tf_op jit(solution)/shard_map/ppermute | solution.py:276
  51.5 5.8 %collective-permute-start.9 = (bf16[48,384]{1,0:T(8,128)(2,1)S(1)}, bf16[48,384]{1,0:T(8,128)(2,1)S(1)}, u32[]{:S(2)}, u32[]{:S(2)}) collective-permute-start(bf16[48,384]{1,0:T(8,128)(2,1)S(1)} %shard_map.99), channel_id=1, source_target_pairs={{0,24},{1,25},{2,26},{3,27},{4,28},{5,29},{6,30},{7,31},{8,16},{9,... | collective-permute-start | bytes 110600 | tf_op jit(solution)/shard_map/ppermute | solution.py:276
  54.0 4.9 %collective-permute-start.8 = (bf16[48,384]{1,0:T(8,128)(2,1)S(1)}, bf16[48,384]{1,0:T(8,128)(2,1)S(1)}, u32[]{:S(2)}, u32[]{:S(2)}) collective-permute-start(bf16[48,384]{1,0:T(8,128)(2,1)S(1)} %shard_map.99), channel_id=1, source_target_pairs={{0,16},{1,17},{2,18},{3,19},{4,20},{5,21},{6,22},{7,23},{8,24},{9,... | collective-permute-start | bytes 110600 | tf_op jit(solution)/shard_map/ppermute | solution.py:276
  54.4 4.5 %collective-permute-start.7 = (bf16[48,384]{1,0:T(8,128)(2,1)S(1)}, bf16[48,384]{1,0:T(8,128)(2,1)S(1)}, u32[]{:S(2)}, u32[]{:S(2)}) collective-permute-start(bf16[48,384]{1,0:T(8,128)(2,1)S(1)} %shard_map.99), channel_id=1, source_target_pairs={{0,8},{1,9},{2,10},{3,11},{4,12},{5,13},{6,14},{7,15},{8,0},{9,1},... | collective-permute-start | bytes 110600 | tf_op jit(solution)/shard_map/ppermute | solution.py:276
  58.9 8.1 %collective-permute-start.12 = (bf16[192,384]{1,0:T(8,128)(2,1)S(1)}, bf16[192,384]{1,0:T(8,128)(2,1)S(1)}, u32[]{:S(2)}, u32[]{:S(2)}) collective-permute-start(bf16[192,384]{1,0:T(8,128)(2,1)S(1)} %pad_maximum_fusion), channel_id=1, source_target_pairs={{0,6},{1,7},{2,4},{3,5},{4,2},{5,3},{6,0},{7,1},{8,14},{9,15},{10,... | collective-permute-start | bytes 442376 | tf_op jit(solution)/shard_map/ppermute | solution.py:276
  60.8 6.2 %collective-permute-start.11 = (bf16[192,384]{1,0:T(8,128)(2,1)S(1)}, bf16[192,384]{1,0:T(8,128)(2,1)S(1)}, u32[]{:S(2)}, u32[]{:S(2)}) collective-permute-start(bf16[192,384]{1,0:T(8,128)(2,1)S(1)} %pad_maximum_fusion), channel_id=1, source_target_pairs={{0,4},{1,5},{2,6},{3,7},{4,0},{5,1},{6,2},{7,3},{8,12},{9,13},{10,... | collective-permute-start | bytes 442376 | tf_op jit(solution)/shard_map/ppermute | solution.py:276
  61.8 5.1 %collective-permute-start.10 = (bf16[192,384]{1,0:T(8,128)(2,1)S(1)}, bf16[192,384]{1,0:T(8,128)(2,1)S(1)}, u32[]{:S(2)}, u32[]{:S(2)}) collective-permute-start(bf16[192,384]{1,0:T(8,128)(2,1)S(1)} %pad_maximum_fusion), channel_id=1, source_target_pairs={{0,2},{1,3},{2,0},{3,1},{4,6},{5,7},{6,4},{7,5},{8,10},{9,11},{10,... | collective-permute-start | bytes 442376 | tf_op jit(solution)/shard_map/ppermute | solution.py:276
  67.0 2.1 %collective-permute-start.13 = (bf16[768,384]{1,0:T(8,128)(2,1)S(1)}, bf16[768,384]{1,0:T(8,128)(2,1)S(1)}, u32[]{:S(2)}, u32[]{:S(2)}) collective-permute-start(bf16[768,384]{1,0:T(8,128)(2,1)S(1)} %constant_dynamic-update-slice_fusion.mine_ref), channel_id=1, source_target_pairs={{0,1},{1,0},{2,3},{3,2},{4,5},{5,4},{6,7},{7,6},{8,9},{9,8},{10,11... | collective-permute-start | bytes 1769480 | tf_op jit(solution)/shard_map/ppermute | solution.py:276

commit v4 on v3

--- a/solution.py
+++ b/solution.py
@@ -14,6 +14,7 @@
 bf16 = jnp.bfloat16
 VMEM = pl.BlockSpec(memory_space=pltpu.VMEM)
 SMEM = pl.BlockSpec(memory_space=pltpu.SMEM)
+HBM = pl.BlockSpec(memory_space=pltpu.HBM)
 tile = 16
 
 
@@ -54,14 +55,19 @@
     return total
 
 
-def pack_kernel(x_ref, g_ref, out_ref):
+def pack_kernel(x_ref, g_ref, out_ref, x_s, g_s, sem):
     size, both, width = out_ref.shape
-    for side, ref in enumerate((x_ref, g_ref)):
-        rows = ref[...].astype(f32).T.reshape(size, both // 2, width)
-        if side == 0:
-            first = rows
-        else:
-            out_ref[...] = jnp.concatenate([first, rows], axis=1).astype(bf16)
+    copies = [
+        pltpu.make_async_copy(ref, scratch, sem.at[side])
+        for side, (ref, scratch) in enumerate(((x_ref, x_s), (g_ref, g_s)))
+    ]
+    for copy in copies:
+        copy.start()
+    parts = []
+    for copy, scratch in zip(copies, (x_s, g_s)):
+        copy.wait()
+        parts.append(scratch[...].astype(f32).T.reshape(size, both // 2, width))
+    out_ref[...] = jnp.concatenate(parts, axis=1).astype(bf16)
 
 
 def switch_kernel(
@@ -139,14 +145,10 @@
         grad_ref[...] = grad.astype(bf16)
     grad_in = dot(low_s[...], pre_s[...], (0, 0))
     grad_out = dot(act_s[...], bg_s[...], (0, 0))
-    step = units // 16
 
     def put_in(ref):
-        for piece in range(16):
-            row, lane = (piece // 2) * step, (piece % 2) * double
-            ref[piece * step : (piece + 1) * step, :] = grad_in[row : row + step, lane : lane + double].astype(
-                ref.dtype
-            )
+        for first in range(0, units, double):
+            ref[first : first + double, :] = grad_in[:, first : first + double].astype(ref.dtype)
 
     def put_out(ref):
         ref[0:units, :] = grad_out.astype(ref.dtype)
@@ -162,36 +164,32 @@
         put_out(keep_ref)
 
 
-def split_kernel(radix, shift, cut, me_ref, *refs):
-    count = len(refs) - radix - (cut is not None)
+def split_kernel(radix, shift, riding, me_ref, *refs):
+    count = 2 + riding
     parts, outs = refs[:count], refs[count:]
     rows = outs[0].shape[0]
-    if cut is not None:
+    if riding:
         ride_ref, parts = parts[0], parts[1:]
-        riders = cut(ride_ref, [part.at[rows * radix :, :] for part in parts[1:]])
-        outs[-1][...] = riders[0]
-        for other in range(1, radix):
-            outs[other][rows:, :] = riders[other]
+        sources = [ride_ref[...], parts[1][rows * radix :, :]]
+        each = ride_ref.shape[0] // radix
+        for other in range(radix):
+            riders = jnp.concatenate([source[other * each : (other + 1) * each] for source in sources], axis=0)
+            if other == 0:
+                outs[-1][...] = riders
+            else:
+                outs[other][rows:, :] = riders
     place = (me_ref[0] >> shift) & (radix - 1)
     for other in range(radix):
         at = pl.ds(pl.multiple_of((place ^ other) * rows, tile), rows)
-        total = parts[0][at, :].astype(f32)
-        for part in parts[1:]:
-            total = total + part[at, :].astype(f32)
+        total = parts[0][at, :].astype(f32) + parts[1][at, :].astype(f32)
         outs[other][0:rows, :] = total.astype(outs[other].dtype)
 
 
-def cut_planes(kept_ref, arrived):
-    rows = kept_ref.shape[0] // 4
-    sources = [kept_ref[...], arrived[0][...]]
-    return [jnp.concatenate([source[m * rows : (m + 1) * rows] for source in sources], axis=0) for m in range(4)]
-
-
-def cut_lines(kept_ref, arrived):
-    sources = [ref[...].astype(f32) for ref in [kept_ref] + arrived]
-    rows, double = sources[0].shape
+def lines_kernel(*refs):
+    parts, outs = refs[:4], refs[4:]
+    rows, double = parts[0].shape
+    sources = [part[part.shape[0] - rows :, :].astype(f32) for part in parts]
     width, block = double // 2, rows // 4
-    pieces = []
     for high in range(2):
         for low in range(2):
             sides = []
@@ -202,8 +200,7 @@
                         first = (core * 2 + low) * block
                         blocks.append(source[first : first + block, high * width : (high + 1) * width])
                 sides.append(jnp.concatenate(blocks, axis=0))
-            pieces.append(jnp.concatenate(sides, axis=1).astype(bf16))
-    return pieces
+            outs[high * 2 + low][...] = jnp.concatenate(sides, axis=1).astype(bf16)
 
 
 def unpack_kernel(block, me_ref, *refs):
@@ -230,41 +227,50 @@
     refs[-1][...] = (total * factor).astype(refs[-1].dtype)
 
 
-def place_kernel(phases, step, me_ref, mine_ref, other_ref, in_ref, out_ref):
+def place_kernel(phases, step, other, me_ref, half_ref, *refs):
+    in_ref, out_ref, wide_s, sem = refs[-4:]
     me = me_ref[0]
-    core = me % 2
-    double = mine_ref.shape[1]
-    pieces = mine_ref.shape[0] // step
+    double = half_ref.shape[1]
+    pieces = half_ref.shape[0] // step
     base = 0
     for bit, radix in phases:
         base = base * radix + ((me >> bit) & (radix - 1))
 
-    def write(first_ref, second_ref):
+    def targets(side):
         for slot in range(pieces):
-            piece = slot ^ base
+            first = (slot ^ base) * step
             rows = pl.ds(slot * step, step)
-            to = pl.ds(pl.multiple_of((piece // 2) * step, tile), step)
-            lane = pl.ds(pl.multiple_of((piece % 2) * double, 128), double)
-            in_ref[to, lane] = first_ref[rows, :].astype(f32)
-            out_ref[pl.ds(pl.multiple_of(piece * step, tile), step), :] = second_ref[rows, :].astype(f32)
-
-    @pl.when(core == 0)
-    def _():
-        write(mine_ref, other_ref)
-
-    @pl.when(core == 1)
-    def _():
-        write(other_ref, mine_ref)
-
-
-def call(kernel, outs, scratch=(), specs=None, count=0):
+            if side == 0:
+                lane = (first // double) * double
+                to = in_ref.at[
+                    pl.ds(pl.multiple_of(first - lane, tile), step), pl.ds(pl.multiple_of(lane, 128), double)
+                ]
+            else:
+                to = out_ref.at[pl.ds(pl.multiple_of(first, tile), step), :]
+            yield slot, rows, pltpu.make_async_copy(wide_s.at[rows, :], to, sem.at[slot])
+
+    for side in range(2):
+
+        @pl.when(me % 2 == (side ^ other))
+        def _():
+            copies = []
+            for slot, rows, copy in targets(side):
+                wide_s[rows, :] = half_ref[rows, :].astype(f32)
+                copy.start()
+                copies.append(copy)
+            for copy in copies:
+                copy.wait()
+
+
+def call(kernel, outs, scratch=(), specs=None, count=0, grant=8, **more):
     return pl.pallas_call(
         kernel,
         out_shape=outs,
         in_specs=specs if specs is not None else [VMEM] * count,
-        out_specs=jax.tree.map(lambda _: VMEM, outs),
+        out_specs=more.pop("out_specs", jax.tree.map(lambda _: VMEM, outs)),
         scratch_shapes=list(scratch),
-        compiler_params=pltpu.CompilerParams(vmem_limit_bytes=40 * 2**20),
+        compiler_params=pltpu.CompilerParams(vmem_limit_bytes=grant * 2**20),
+        **more,
     )
 
 
@@ -277,48 +283,39 @@
                          [(d, d ^ mask) for d in range(size)]) for i, mask in enumerate(masks)]
 
 
-def phases_of(size, units):
-    bits = size.bit_length() - 1
-    phases, bit, rows = [], 1, units
-    while bit < bits and rows % (2 * tile) == 0:
-        radix = 4 if bit + 1 < bits and rows % (4 * tile) == 0 else 2
-        phases.append((bit, radix))
-        rows //= radix
-        bit += radix.bit_length() - 1
-    return phases, bit
-
-
 def sum_over_devices(me, ride, keep, send, size, factor, riding):
     bits = size.bit_length() - 1
     rows, double = keep.shape
-    phases, bit = phases_of(size, rows)
-    riding_rows = ride.shape[0] // 2
+    radix = min(4, size // 2)
+    masks = [m << 1 for m in range(1, radix)]
+    rows = rows // radix
     parts = [keep] + exchange([send], [1], size)
-    for phase, (low, radix) in enumerate(phases):
-        rows = rows // radix
-        cut = (cut_planes, cut_lines)[phase] if riding else None
-        extra = riding_rows if riding else 0
-        outs = [struct((rows, double), f32)] + [struct((rows + extra, double), bf16)] * (radix - 1)
-        if riding:
-            outs.append(struct((extra, double), bf16))
-            parts = [ride] + parts
-        pieces = call(
-            functools.partial(split_kernel, radix, low, cut), outs, specs=[SMEM] + [VMEM] * len(parts)
-        )(me, *parts)
-        ride = pieces[-1] if riding else ride
-        parts = [pieces[0]] + exchange(list(pieces[1:radix]), [m << low for m in range(1, radix)], size)
-    riders = [ride] + parts[1:]
-    for rest in range(bit, bits):
+    extra = ride.shape[0] // 2 if riding else 0
+    outs = [struct((rows, double), f32)] + [struct((rows + extra, double), bf16)] * (radix - 1)
+    if riding:
+        outs.append(struct((extra, double), bf16))
+        parts = [ride] + parts
+    pieces = call(
+        functools.partial(split_kernel, radix, 1, riding), outs, specs=[SMEM] + [VMEM] * len(parts)
+    )(me, *parts)
+    arrived = exchange(list(pieces[1:radix]), masks, size)
+    parts = [pieces[0]] + arrived
+    if riding:
+        riders = call(lines_kernel, [struct((extra, double), bf16)] * 4, count=4)(pieces[-1], *arrived)
+    for rest in range(radix.bit_length(), bits):
         total = call(functools.partial(total_kernel, 1.0), struct((rows, double), bf16), count=len(parts))(*parts)
         parts = [total] + exchange([total], [1 << rest], size)
     mine = call(functools.partial(total_kernel, factor), struct((rows, double), bf16), count=len(parts))(*parts)
-    if not riding:
+    if riding:
+        mine, *riders = lax.optimization_barrier((mine, *riders))
+    else:
         mine, ride = lax.optimization_barrier((mine, ride))
-    for low, radix in reversed(phases):
-        got = exchange([mine] * (radix - 1), [m << low for m in range(1, radix)], size)
-        mine = jnp.concatenate([mine] + got, axis=0)
+    got = exchange([mine] * (radix - 1), masks, size)
+    if riding:
+        ride = [riders[0]] + exchange(list(riders[1:]), [m << 3 for m in range(1, 4)], size)
+    mine = jnp.concatenate([mine] + got, axis=0)
     (other,) = exchange([mine], [1], size)
-    return mine, other, rows, phases, riders if riding else ride
+    return mine, other, rows, [(1, radix)], ride
 
 
 def shards(saved_input, cotangent, w_in, bias_in, w_out, residual_logit, branch_scale):
@@ -330,15 +327,19 @@
     half = rows // 2
     me = lax.axis_index("seq").astype(jnp.int32).reshape(1)
     if block % 8 == 0:
-        both = call(pack_kernel, struct((size, 2 * block, width), bf16), count=2)(saved_input.T, cotangent.T)
+        both = call(
+            pack_kernel,
+            struct((size, 2 * block, width), bf16),
+            scratch=[pltpu.VMEM((width, rows), bf16)] * 2 + [pltpu.SemaphoreType.DMA((2,))],
+            specs=[HBM] * 2,
+        )(saved_input.T, cotangent.T)
     else:
         both = jnp.concatenate(
             [saved_input.reshape(size, block, width), cotangent.reshape(size, block, width)], axis=1
         )
     both = lax.all_to_all(both, "seq", split_axis=0, concat_axis=0, tiled=True)
     total = levels * half
-    phases, bit = phases_of(size, units)
-    riding = block % 8 == 0 and [radix for _, radix in phases] == [4, 4] and bit == levels
+    riding = block % 8 == 0 and levels == 5
     rider = struct((rows // 4, double), bf16)
     grad_state, keep, send = call(
         functools.partial(switch_kernel, levels, block),
@@ -358,6 +359,7 @@
             pltpu.VMEM((half, double), f32),
         ],
         specs=[SMEM] + [VMEM] * 6,
+        grant=20,
     )(me, both, w_in, bias_in.reshape(1, units), w_out, residual_logit.reshape(1, double),
       branch_scale.reshape(1, double))
     factor = float(rows * size) ** (-0.5)
@@ -373,11 +375,17 @@
             scratch=[pltpu.VMEM((rows, width), f32)],
             specs=[SMEM] + [VMEM] * len(grad_state),
         )(me, *grad_state).T
+    shapes = [struct((double, units), f32), struct((units, double), f32)]
+    scratch = [pltpu.VMEM((units, double), f32), pltpu.SemaphoreType.DMA((units // step,))]
+    placed = call(
+        functools.partial(place_kernel, phases, step, 0),
+        shapes, scratch=scratch, specs=[SMEM, VMEM], out_specs=[HBM] * 2,
+    )(me, mine)
     grad_in, grad_out = call(
-        functools.partial(place_kernel, phases, step),
-        [struct((double, units), f32), struct((units, double), f32)],
-        specs=[SMEM, VMEM, VMEM],
-    )(me, mine, other)
+        functools.partial(place_kernel, phases, step, 1),
+        shapes, scratch=scratch, specs=[SMEM, VMEM, HBM, HBM], out_specs=[HBM] * 2,
+        input_output_aliases={2: 0, 3: 1},
+    )(me, other, *placed)
     return (grad_state, grad_in, grad_out)
 
 

time: 71 us -> 77.9 us (1.097)
  waiting for transfers between devices: 29.7 us -> 38.6 us
  starting transfers between devices: 23.4 us -> 20.5 us
  Pallas kernels: 11.8 us -> 12.7 us
    ppermute x14 -> x13, waiting for transfers between devices: 21.1 us -> 30 us  [exchange(): lax.ppermute(value if not isinstance(value, list) else value[i], 'seq', [...]
    ppermute x14 -> x13, starting transfers between devices: 16.1 us -> 13.2 us  [exchange(): lax.ppermute(value if not isinstance(value, list) else value[i], 'seq', [...]
    pallas_call x4 -> x7, Pallas kernels: 2.72 us -> 3.63 us  [the longest x1 1.15 us: shards(): call(pack_kernel, struct((size, 2 * block, width), bf16), scratch=[pltpu....]
    unnamed x14 -> x11, local copies, waits for them, and re-layouts: 3 us -> 2.97 us
  transfers between devices with their start and end apart: 15 -> 14, of which waited for: 11 -> 11; matrix products, arithmetic and copies ran while one was open for 3% -> 3% of each run, Pallas kernels for 1% -> 3%
where the time goes in v4:
time: 77.9 us; the launch traced here: 77.6 us
  waiting for transfers between devices  38.6 us (50%)
  starting transfers between devices  20.5 us (26%)
  Pallas kernels  12.7 us (16%)
  local copies, waits for them, and re-layouts  5.06 us (6%)
  between operations  0.78 us (1%)
    ppermute x13, waiting for transfers between devices, exchange(): lax.ppermute(value if not isinstance(value, list) else value[i], 'seq', [...  30 us
    ppermute x13, starting transfers between devices, exchange(): lax.ppermute(value if not isinstance(value, list) else value[i], 'seq', [...  13.2 us
    all_to_all x1, waiting for transfers between devices, shards(): both = lax.all_to_all(both, 'seq', split_axis=0, concat_axis=0, tiled=True)  8.53 us
    pallas_call x1, Pallas kernels, shards(): call(functools.partial(switch_kernel, levels, block), [rider if riding el...  8.18 us
    all_to_all x1, starting transfers between devices, shards(): both = lax.all_to_all(both, 'seq', split_axis=0, concat_axis=0, tiled=True)  7.3 us
    unnamed x11, local copies, waits for them, and re-layouts  2.97 us
  transfers between devices with their start and end apart: 14, of which 11 were waited for; matrix products, arithmetic and copies ran while one was open for 3% of the time, Pallas kernels for 3%

profile of v4, /device:TPU:0, one launch (start us, length us, event | category | flops | bytes accessed | tf_op | source)
XLA Modules:
  0.0 77.6 jit_solution(17793361379398364962)
XLA Ops:
  0.7 0.9 %copy-done.2 = bf16[256,192]{0,1:T(8,128)(2,1)S(1)} copy-done((bf16[256,192]{0,1:T(8,128)(2,1)S(1)}, bf16[256,192]{0,1:T(8,128)(2,1)}, u32[]{:S(2)}) %copy-start.2) | copy-done | bytes 98328
  1.6 0.9 %copy-done.3 = bf16[256,192]{0,1:T(8,128)(2,1)S(1)} copy-done((bf16[256,192]{0,1:T(8,128)(2,1)S(1)}, bf16[256,192]{0,1:T(8,128)(2,1)}, u32[]{:S(2)}) %copy-start.3) | copy-done | bytes 98328
  2.5 1.1 %shard_map.94 = bf16[32,16,192]{2,1,0:T(8,128)(2,1)} custom-call(bf16[192,256]{1,0:T(8,128)(2,1)S(1)} %bitcast.4, bf16[192,256]{1,0:T(8,128)(2,1)S(1)} %bitcast.5), custom_call_target="tpu_custom_call" | custom-call | tf_op jit(solution)/shard_map/pallas_call | solution.py:330
  3.6 7.3 %all-to-all-start = ((bf16[32,16,192]{2,1,0:T(8,128)(2,1)}), bf16[32,16,192]{2,1,0:T(8,128)(2,1)S(1)}, u32[]{:S(2)}, u32[]{:S(2)}) async-start(bf16[32,16,192]{2,1,0:T(8,128)(2,1)} %shard_map.94), calls=%async_computation | async-start | bytes 524288 | tf_op jit(solution)/shard_map/all_to_all | solution.py:340
  13.0 8.5 %all-to-all-done.both_ref = bf16[32,16,192]{2,1,0:T(8,128)(2,1)S(1)} async-done(((bf16[32,16,192]{2,1,0:T(8,128)(2,1)}), bf16[32,16,192]{2,1,0:T(8,128)(2,1)S(1)}, u32[]{:S(2)}, u32[]{:S(2)}) %all-to-all-start) | async-done | bytes 196640 | tf_op jit(solution)/shard_map/all_to_all | solution.py:340
  21.6 1.1 %copy-done.1 = bf16[768,384]{1,0:T(8,128)(2,1)S(1)} copy-done((bf16[768,384]{1,0:T(8,128)(2,1)S(1)}, bf16[768,384]{1,0:T(8,128)(2,1)}, u32[]{:S(2)}) %copy-start.1) | copy-done | bytes 589848
  22.6 8.2 %shard_map.95 = (bf16[64,384]{1,0:T(8,128)(2,1)S(1)}, f32[768,384]{1,0:T(8,128)S(1)}, bf16[832,384]{1,0:T(8,128)(2,1)S(1)}) custom-call(s32[1]{0:T(128)} %bitcast.me_ref, bf16[32,16,192]{2,1,0:T(8,128)(2,1)S(1)} %all-to-all-done.both_ref, bf16[384,768]{1,0:T(8,128)(2,1)S(1)} %copy-done, f32[1,768]{1,0:T(1,128)S(1)} %reshape.19.bias_ref, ...), custom_call_target="tpu_custom_call" | custom-call | tf_op jit(solution)/shard_map/pallas_call | solution.py:344
  30.9 2.1 %collective-permute-done.refs_2_ = bf16[832,384]{1,0:T(8,128)(2,1)S(1)} collective-permute-done((bf16[832,384]{1,0:T(8,128)(2,1)S(1)}, bf16[832,384]{1,0:T(8,128)(2,1)S(1)}, u32[]{:S(2)}, u32[]{:S(2)}) %collective-permute-start) | collective-permute-done | bytes 639008 | tf_op jit(solution)/shard_map/ppermute | solution.py:282
  33.6 1.3 %collective-permute-start.2 = (bf16[224,384]{1,0:T(8,128)(2,1)S(1)}, bf16[224,384]{1,0:T(8,128)(2,1)S(1)}, u32[]{:S(2)}, u32[]{:S(2)}) collective-permute-start(bf16[224,384]{1,0:T(8,128)(2,1)S(1)} %get-tuple-element.29), channel_id=1, source_target_pairs={{0,4},{1,5},{2,6},{3,7},{4,0},{5,1},{6,2},{7,3},{8,12},{9,13},{10,... | collective-permute-start | bytes 516104 | tf_op jit(solution)/shard_map/ppermute | solution.py:282
  34.9 1.8 %collective-permute-start.3 = (bf16[224,384]{1,0:T(8,128)(2,1)S(1)}, bf16[224,384]{1,0:T(8,128)(2,1)S(1)}, u32[]{:S(2)}, u32[]{:S(2)}) collective-permute-start(bf16[224,384]{1,0:T(8,128)(2,1)S(1)} %get-tuple-element.30), channel_id=1, source_target_pairs={{0,6},{1,7},{2,4},{3,5},{4,2},{5,3},{6,0},{7,1},{8,14},{9,15},{10,... | collective-permute-start | bytes 516104 | tf_op jit(solution)/shard_map/ppermute | solution.py:282
  36.7 3.7 %collective-permute-done.1.refs_1_ = bf16[224,384]{1,0:T(8,128)(2,1)S(1)} collective-permute-done((bf16[224,384]{1,0:T(8,128)(2,1)S(1)}, bf16[224,384]{1,0:T(8,128)(2,1)S(1)}, u32[]{:S(2)}, u32[]{:S(2)}) %collective-permute-start.1) | collective-permute-done | bytes 172064 | tf_op jit(solution)/shard_map/ppermute | solution.py:282
  40.8 2.9 %collective-permute-done.3.refs_3_ = bf16[224,384]{1,0:T(8,128)(2,1)S(1)} collective-permute-done((bf16[224,384]{1,0:T(8,128)(2,1)S(1)}, bf16[224,384]{1,0:T(8,128)(2,1)S(1)}, u32[]{:S(2)}, u32[]{:S(2)}) %collective-permute-start.3) | collective-permute-done | bytes 172064 | tf_op jit(solution)/shard_map/ppermute | solution.py:282
  44.5 4.5 %collective-permute-done.4.refs_1_ = bf16[192,384]{1,0:T(8,128)(2,1)S(1)} collective-permute-done((bf16[192,384]{1,0:T(8,128)(2,1)S(1)}, bf16[192,384]{1,0:T(8,128)(2,1)S(1)}, u32[]{:S(2)}, u32[]{:S(2)}) %collective-permute-start.4) | collective-permute-done | bytes 147488 | tf_op jit(solution)/shard_map/ppermute | solution.py:282
  49.8 7.1 %collective-permute-done.5.refs_1_ = bf16[192,384]{1,0:T(8,128)(2,1)S(1)} collective-permute-done((bf16[192,384]{1,0:T(8,128)(2,1)S(1)}, bf16[192,384]{1,0:T(8,128)(2,1)S(1)}, u32[]{:S(2)}, u32[]{:S(2)}) %collective-permute-start.5) | collective-permute-done | bytes 147488 | tf_op jit(solution)/shard_map/ppermute | solution.py:282
  57.0 1.1 %collective-permute-start.9 = (bf16[192,384]{1,0:T(8,128)(2,1)S(1)}, bf16[192,384]{1,0:T(8,128)(2,1)S(1)}, u32[]{:S(2)}, u32[]{:S(2)}) collective-permute-start(bf16[192,384]{1,0:T(8,128)(2,1)S(1)} %shard_map.99), channel_id=1, source_target_pairs={{0,2},{1,3},{2,0},{3,1},{4,6},{5,7},{6,4},{7,5},{8,10},{9,11},{10,... | collective-permute-start | bytes 442376 | tf_op jit(solution)/shard_map/ppermute | solution.py:282
  58.2 1.5 %collective-permute-start.11 = (bf16[192,384]{1,0:T(8,128)(2,1)S(1)}, bf16[192,384]{1,0:T(8,128)(2,1)S(1)}, u32[]{:S(2)}, u32[]{:S(2)}) collective-permute-start(bf16[192,384]{1,0:T(8,128)(2,1)S(1)} %shard_map.99), channel_id=1, source_target_pairs={{0,6},{1,7},{2,4},{3,5},{4,2},{5,3},{6,0},{7,1},{8,14},{9,15},{10,... | collective-permute-start | bytes 442376 | tf_op jit(solution)/shard_map/ppermute | solution.py:282
  59.7 0.9 %collective-permute-start.10 = (bf16[192,384]{1,0:T(8,128)(2,1)S(1)}, bf16[192,384]{1,0:T(8,128)(2,1)S(1)}, u32[]{:S(2)}, u32[]{:S(2)}) collective-permute-start(bf16[192,384]{1,0:T(8,128)(2,1)S(1)} %shard_map.99), channel_id=1, source_target_pairs={{0,4},{1,5},{2,6},{3,7},{4,0},{5,1},{6,2},{7,3},{8,12},{9,13},{10,... | collective-permute-start | bytes 442376 | tf_op jit(solution)/shard_map/ppermute | solution.py:282
  60.6 2.6 %collective-permute-done.9 = bf16[192,384]{1,0:T(8,128)(2,1)S(1)} collective-permute-done((bf16[192,384]{1,0:T(8,128)(2,1)S(1)}, bf16[192,384]{1,0:T(8,128)(2,1)S(1)}, u32[]{:S(2)}, u32[]{:S(2)}) %collective-permute-start.9) | collective-permute-done | bytes 147488 | tf_op jit(solution)/shard_map/ppermute | solution.py:282
  63.2 3.6 %collective-permute-done.10 = bf16[192,384]{1,0:T(8,128)(2,1)S(1)} collective-permute-done((bf16[192,384]{1,0:T(8,128)(2,1)S(1)}, bf16[192,384]{1,0:T(8,128)(2,1)S(1)}, u32[]{:S(2)}, u32[]{:S(2)}) %collective-permute-start.10) | collective-permute-done | bytes 147488 | tf_op jit(solution)/shard_map/ppermute | solution.py:282
  67.1 1.9 %collective-permute-start.7 = (bf16[32,384]{1,0:T(8,128)(2,1)S(1)}, bf16[32,384]{1,0:T(8,128)(2,1)S(1)}, u32[]{:S(2)}, u32[]{:S(2)}) collective-permute-start(bf16[32,384]{1,0:T(8,128)(2,1)S(1)} %get-tuple-element.38), channel_id=1, source_target_pairs={{0,16},{1,17},{2,18},{3,19},{4,20},{5,21},{6,22},{7,23},{8,24},{9,... | collective-permute-start | bytes 73736 | tf_op jit(solution)/shard_map/ppermute | solution.py:282
  68.9 2.5 %collective-permute-start.8 = (bf16[32,384]{1,0:T(8,128)(2,1)S(1)}, bf16[32,384]{1,0:T(8,128)(2,1)S(1)}, u32[]{:S(2)}, u32[]{:S(2)}) collective-permute-start(bf16[32,384]{1,0:T(8,128)(2,1)S(1)} %get-tuple-element.39), channel_id=1, source_target_pairs={{0,24},{1,25},{2,26},{3,27},{4,28},{5,29},{6,30},{7,31},{8,16},{9,... | collective-permute-start | bytes 73736 | tf_op jit(solution)/shard_map/ppermute | solution.py:282
  71.9 2.7 %collective-permute-done.8.refs_3_ = bf16[32,384]{1,0:T(8,128)(2,1)S(1)} collective-permute-done((bf16[32,384]{1,0:T(8,128)(2,1)S(1)}, bf16[32,384]{1,0:T(8,128)(2,1)S(1)}, u32[]{:S(2)}, u32[]{:S(2)}) %collective-permute-start.8) | collective-permute-done | bytes 24608 | tf_op jit(solution)/shard_map/ppermute | solution.py:282
  75.4 1.1 %shard_map.102 = (f32[384,768]{1,0:T(8,128)}, f32[768,384]{1,0:T(8,128)}) custom-call(s32[1]{0:T(128)} %bitcast.me_ref, bf16[768,384]{1,0:T(8,128)(2,1)S(1)} %constant_dynamic-update-slice_fusion.half_ref), custom_call_target="tpu_custom_call" | custom-call | tf_op jit(solution)/shard_map/pallas_call | solution.py:380
  76.5 1.1 %shard_map.103 = (f32[384,768]{1,0:T(8,128)}, f32[768,384]{1,0:T(8,128)}) custom-call(s32[1]{0:T(128)} %bitcast.me_ref, bf16[768,384]{1,0:T(8,128)(2,1)S(1)} %collective-permute-done.12.half_ref, f32[384,768]{1,0:T(8,128)} %get-tuple-element.41.refs_0_, f32[768,384]{1,0:T(8,128)} %get-tuple-element.42.refs_1_), custom_call_target="tpu_custom_call", output_to_operand_aliasing={{0}: (2, {}), {1}: (3, {})} | custom-call | tf_op jit(solution)/shard_map/pallas_call | solution.py:384
  (29 shorter events, 6.4 us)
Async XLA Ops:
  0.6 20.9 %copy-start = (bf16[384,768]{1,0:T(8,128)(2,1)S(1)}, bf16[384,768]{1,0:T(8,128)(2,1)}, u32[]{:S(2)}) copy-start(bf16[384,768]{1,0:T(8,128)(2,1)} %w_in_ref.1) | copy-start | bytes 1769476
  0.6 1.0 %copy-start.2 = (bf16[256,192]{0,1:T(8,128)(2,1)S(1)}, bf16[256,192]{0,1:T(8,128)(2,1)}, u32[]{:S(2)}) copy-start(bf16[256,192]{0,1:T(8,128)(2,1)} %param.7) | copy-start | bytes 294916
  1.6 0.9 %copy-start.3 = (bf16[256,192]{0,1:T(8,128)(2,1)S(1)}, bf16[256,192]{0,1:T(8,128)(2,1)}, u32[]{:S(2)}) copy-start(bf16[256,192]{0,1:T(8,128)(2,1)} %param.8) | copy-start | bytes 294916
  3.6 17.9 %all-to-all-start = ((bf16[32,16,192]{2,1,0:T(8,128)(2,1)}), bf16[32,16,192]{2,1,0:T(8,128)(2,1)S(1)}, u32[]{:S(2)}, u32[]{:S(2)}) async-start(bf16[32,16,192]{2,1,0:T(8,128)(2,1)} %shard_map.94), calls=%async_computation | async-start | bytes 524288 | tf_op jit(solution)/shard_map/all_to_all | solution.py:340
  21.6 1.1 %copy-start.1 = (bf16[768,384]{1,0:T(8,128)(2,1)S(1)}, bf16[768,384]{1,0:T(8,128)(2,1)}, u32[]{:S(2)}) copy-start(bf16[768,384]{1,0:T(8,128)(2,1)} %w_out_ref.1) | copy-start | bytes 1769476
  30.8 2.1 %collective-permute-start = (bf16[832,384]{1,0:T(8,128)(2,1)S(1)}, bf16[832,384]{1,0:T(8,128)(2,1)S(1)}, u32[]{:S(2)}, u32[]{:S(2)}) collective-permute-start(bf16[832,384]{1,0:T(8,128)(2,1)S(1)} %get-tuple-element.26), channel_id=1, source_target_pairs={{0,1},{1,0},{2,3},{3,2},{4,5},{5,4},{6,7},{7,6},{8,9},{9,8},{10,11... | collective-permute-start | bytes 1916936 | tf_op jit(solution)/shard_map/ppermute | solution.py:282
  33.1 7.3 %collective-permute-start.1 = (bf16[224,384]{1,0:T(8,128)(2,1)S(1)}, bf16[224,384]{1,0:T(8,128)(2,1)S(1)}, u32[]{:S(2)}, u32[]{:S(2)}) collective-permute-start(bf16[224,384]{1,0:T(8,128)(2,1)S(1)} %get-tuple-element.28), channel_id=1, source_target_pairs={{0,2},{1,3},{2,0},{3,1},{4,6},{5,7},{6,4},{7,5},{8,10},{9,11},{10,... | collective-permute-start | bytes 516104 | tf_op jit(solution)/shard_map/ppermute | solution.py:282
  33.6 7.2 %collective-permute-start.2 = (bf16[224,384]{1,0:T(8,128)(2,1)S(1)}, bf16[224,384]{1,0:T(8,128)(2,1)S(1)}, u32[]{:S(2)}, u32[]{:S(2)}) collective-permute-start(bf16[224,384]{1,0:T(8,128)(2,1)S(1)} %get-tuple-element.29), channel_id=1, source_target_pairs={{0,4},{1,5},{2,6},{3,7},{4,0},{5,1},{6,2},{7,3},{8,12},{9,13},{10,... | collective-permute-start | bytes 516104 | tf_op jit(solution)/shard_map/ppermute | solution.py:282
  34.9 8.8 %collective-permute-start.3 = (bf16[224,384]{1,0:T(8,128)(2,1)S(1)}, bf16[224,384]{1,0:T(8,128)(2,1)S(1)}, u32[]{:S(2)}, u32[]{:S(2)}) collective-permute-start(bf16[224,384]{1,0:T(8,128)(2,1)S(1)} %get-tuple-element.30), channel_id=1, source_target_pairs={{0,6},{1,7},{2,4},{3,5},{4,2},{5,3},{6,0},{7,1},{8,14},{9,15},{10,... | collective-permute-start | bytes 516104 | tf_op jit(solution)/shard_map/ppermute | solution.py:282
  43.8 5.2 %collective-permute-start.4 = (bf16[192,384]{1,0:T(8,128)(2,1)S(1)}, bf16[192,384]{1,0:T(8,128)(2,1)S(1)}, u32[]{:S(2)}, u32[]{:S(2)}) collective-permute-start(bf16[192,384]{1,0:T(8,128)(2,1)S(1)} %shard_map.97.refs_0_), channel_id=1, source_target_pairs={{0,8},{1,9},{2,10},{3,11},{4,12},{5,13},{6,14},{7,15},{8,0},{9,1},... | collective-permute-start | bytes 442376 | tf_op jit(solution)/shard_map/ppermute | solution.py:282
  49.0 8.0 %collective-permute-start.5 = (bf16[192,384]{1,0:T(8,128)(2,1)S(1)}, bf16[192,384]{1,0:T(8,128)(2,1)S(1)}, u32[]{:S(2)}, u32[]{:S(2)}) collective-permute-start(bf16[192,384]{1,0:T(8,128)(2,1)S(1)} %shard_map.98.refs_0_), channel_id=1, source_target_pairs={{0,16},{1,17},{2,18},{3,19},{4,20},{5,21},{6,22},{7,23},{8,24},{9,... | collective-permute-start | bytes 442376 | tf_op jit(solution)/shard_map/ppermute | solution.py:282
  57.0 6.2 %collective-permute-start.9 = (bf16[192,384]{1,0:T(8,128)(2,1)S(1)}, bf16[192,384]{1,0:T(8,128)(2,1)S(1)}, u32[]{:S(2)}, u32[]{:S(2)}) collective-permute-start(bf16[192,384]{1,0:T(8,128)(2,1)S(1)} %shard_map.99), channel_id=1, source_target_pairs={{0,2},{1,3},{2,0},{3,1},{4,6},{5,7},{6,4},{7,5},{8,10},{9,11},{10,... | collective-permute-start | bytes 442376 | tf_op jit(solution)/shard_map/ppermute | solution.py:282
  58.2 8.7 %collective-permute-start.11 = (bf16[192,384]{1,0:T(8,128)(2,1)S(1)}, bf16[192,384]{1,0:T(8,128)(2,1)S(1)}, u32[]{:S(2)}, u32[]{:S(2)}) collective-permute-start(bf16[192,384]{1,0:T(8,128)(2,1)S(1)} %shard_map.99), channel_id=1, source_target_pairs={{0,6},{1,7},{2,4},{3,5},{4,2},{5,3},{6,0},{7,1},{8,14},{9,15},{10,... | collective-permute-start | bytes 442376 | tf_op jit(solution)/shard_map/ppermute | solution.py:282
  59.7 7.2 %collective-permute-start.10 = (bf16[192,384]{1,0:T(8,128)(2,1)S(1)}, bf16[192,384]{1,0:T(8,128)(2,1)S(1)}, u32[]{:S(2)}, u32[]{:S(2)}) collective-permute-start(bf16[192,384]{1,0:T(8,128)(2,1)S(1)} %shard_map.99), channel_id=1, source_target_pairs={{0,4},{1,5},{2,6},{3,7},{4,0},{5,1},{6,2},{7,3},{8,12},{9,13},{10,... | collective-permute-start | bytes 442376 | tf_op jit(solution)/shard_map/ppermute | solution.py:282
  66.9 9.6 %collective-permute-start.12 = (bf16[768,384]{1,0:T(8,128)(2,1)S(1)}, bf16[768,384]{1,0:T(8,128)(2,1)S(1)}, u32[]{:S(2)}, u32[]{:S(2)}) collective-permute-start(bf16[768,384]{1,0:T(8,128)(2,1)S(1)} %constant_dynamic-update-slice_fusion.half_ref), channel_id=1, source_target_pairs={{0,1},{1,0},{2,3},{3,2},{4,5},{5,4},{6,7},{7,6},{8,9},{9,8},{10,11... | collective-permute-start | bytes 1769480 | tf_op jit(solution)/shard_map/ppermute | solution.py:282
  67.0 4.5 %collective-permute-start.6 = (bf16[32,384]{1,0:T(8,128)(2,1)S(1)}, bf16[32,384]{1,0:T(8,128)(2,1)S(1)}, u32[]{:S(2)}, u32[]{:S(2)}) collective-permute-start(bf16[32,384]{1,0:T(8,128)(2,1)S(1)} %get-tuple-element.37), channel_id=1, source_target_pairs={{0,8},{1,9},{2,10},{3,11},{4,12},{5,13},{6,14},{7,15},{8,0},{9,1},... | collective-permute-start | bytes 73736 | tf_op jit(solution)/shard_map/ppermute | solution.py:282
  67.1 4.8 %collective-permute-start.7 = (bf16[32,384]{1,0:T(8,128)(2,1)S(1)}, bf16[32,384]{1,0:T(8,128)(2,1)S(1)}, u32[]{:S(2)}, u32[]{:S(2)}) collective-permute-start(bf16[32,384]{1,0:T(8,128)(2,1)S(1)} %get-tuple-element.38), channel_id=1, source_target_pairs={{0,16},{1,17},{2,18},{3,19},{4,20},{5,21},{6,22},{7,23},{8,24},{9,... | collective-permute-start | bytes 73736 | tf_op jit(solution)/shard_map/ppermute | solution.py:282
  68.9 5.6 %collective-permute-start.8 = (bf16[32,384]{1,0:T(8,128)(2,1)S(1)}, bf16[32,384]{1,0:T(8,128)(2,1)S(1)}, u32[]{:S(2)}, u32[]{:S(2)}) collective-permute-start(bf16[32,384]{1,0:T(8,128)(2,1)S(1)} %get-tuple-element.39), channel_id=1, source_target_pairs={{0,24},{1,25},{2,26},{3,27},{4,28},{5,29},{6,30},{7,31},{8,16},{9,... | collective-permute-start | bytes 73736 | tf_op jit(solution)/shard_map/ppermute | solution.py:282

commit v5 on v4

--- a/solution.py
+++ b/solution.py
@@ -68,6 +68,15 @@
         copy.wait()
         parts.append(scratch[...].astype(f32).T.reshape(size, both // 2, width))
     out_ref[...] = jnp.concatenate(parts, axis=1).astype(bf16)
+
+
+def fetch_kernel(*refs):
+    count = len(refs) // 2
+    copies = [pltpu.make_async_copy(refs[i], refs[count + i], refs[-1].at[i]) for i in range(count)]
+    for copy in copies:
+        copy.start()
+    for copy in copies:
+        copy.wait()
 
 
 def switch_kernel(
@@ -131,8 +140,8 @@
         paired_s[...] = jnp.where(core == 0, result, turned)
         pairs = half // block
         kept, sent = [], []
-        for plane in range(4):
-            for low in range(pairs // 8):
+        for low in range(pairs // 8):
+            for plane in range(4):
                 sides = []
                 for high in range(2):
                     chip = ((high * (pairs // 8) + low) * 4 + plane) ^ (me_ref[0] >> 1)
@@ -165,66 +174,82 @@
 
 
 def split_kernel(radix, shift, riding, me_ref, *refs):
-    count = 2 + riding
-    parts, outs = refs[:count], refs[count:]
+    parts, outs = refs[: 2 + riding], refs[2 + riding :]
     rows = outs[0].shape[0]
     if riding:
         ride_ref, parts = parts[0], parts[1:]
-        sources = [ride_ref[...], parts[1][rows * radix :, :]]
-        each = ride_ref.shape[0] // radix
-        for other in range(radix):
-            riders = jnp.concatenate([source[other * each : (other + 1) * each] for source in sources], axis=0)
-            if other == 0:
-                outs[-1][...] = riders
-            else:
-                outs[other][rows:, :] = riders
+        width = ride_ref.shape[1] // 2
+        sources = [ride_ref[...].astype(f32), parts[1][rows * radix :, :].astype(f32)]
+        for high in range(2):
+            lanes = [source[:, high * width : (high + 1) * width] for source in sources]
+            outs[radix + high][...] = jnp.concatenate(lanes, axis=1).astype(bf16)
     place = (me_ref[0] >> shift) & (radix - 1)
     for other in range(radix):
         at = pl.ds(pl.multiple_of((place ^ other) * rows, tile), rows)
         total = parts[0][at, :].astype(f32) + parts[1][at, :].astype(f32)
-        outs[other][0:rows, :] = total.astype(outs[other].dtype)
-
-
-def lines_kernel(*refs):
-    parts, outs = refs[:4], refs[4:]
-    rows, double = parts[0].shape
-    sources = [part[part.shape[0] - rows :, :].astype(f32) for part in parts]
-    width, block = double // 2, rows // 4
-    for high in range(2):
-        for low in range(2):
-            sides = []
-            for side in range(2):
-                blocks = []
-                for source in sources[2 * side : 2 * side + 2]:
-                    for core in range(2):
-                        first = (core * 2 + low) * block
-                        blocks.append(source[first : first + block, high * width : (high + 1) * width])
-                sides.append(jnp.concatenate(blocks, axis=0))
-            outs[high * 2 + low][...] = jnp.concatenate(sides, axis=1).astype(bf16)
+        outs[other][...] = total.astype(outs[other].dtype)
+
+
+def total_of(refs):
+    rows = refs[-1].shape[0]
+    total = refs[0][0:rows, :].astype(f32)
+    for ref in refs[1:-1]:
+        total = total + ref[0:rows, :].astype(f32)
+    return total
+
+
+def total_kernel(factor, *refs):
+    refs[-1][...] = (total_of(refs) * factor).astype(refs[-1].dtype)
+
+
+def line_kernel(*refs):
+    parts, sources, (out_ref, kept_ref) = refs[:-4], refs[-4:-2], refs[-2:]
+    rows = parts[0].shape[0]
+    out_ref[0:rows, :] = total_of([*parts, parts[0]]).astype(bf16)
+    half = sources[0].shape[0] // 2
+    for first, ref, at in ((0, kept_ref, 0), (half, out_ref, rows)):
+        for source in sources:
+            ref[at : at + half, :] = source[first : first + half, :]
+            at += half
+
+
+def plane_kernel(factor, *refs):
+    parts, (kept_ref, came_ref), outs = refs[:2], refs[2:4], refs[4:]
+    rows = outs[0].shape[0]
+    mine = (total_of([*parts, outs[0]]) * factor).astype(bf16)
+    outs[0][...] = mine
+    sources = [kept_ref[...].astype(f32), came_ref[rows:, :].astype(f32)]
+    block = sources[0].shape[0] // 8
+    for plane in range(4):
+        riders = jnp.concatenate(
+            [
+                source[(high * 4 + plane) * block : (high * 4 + plane + 1) * block]
+                for source in sources
+                for high in range(2)
+            ],
+            axis=0,
+        ).astype(bf16)
+        if plane == 0:
+            outs[4][...] = riders
+        else:
+            outs[plane][0:rows, :] = mine
+            outs[plane][rows:, :] = riders
 
 
 def unpack_kernel(block, me_ref, *refs):
     parts, out_ref, rows_s = refs[:-2], refs[-2], refs[-1]
     width = rows_s.shape[1]
-    for line, part in enumerate(parts):
+    for plane, part in enumerate(parts):
         values = part[part.shape[0] - 4 * block :, :].astype(f32)
-        for plane in range(4):
-            for core in range(2):
-                source = me_ref[0] ^ (line * 8 + plane * 2 + core)
-                first = ((plane % 2) * 2 + core) * block
-                side = plane // 2
-                rows_s[pl.ds(pl.multiple_of(source * block, 8), block), :] = values[
-                    first : first + block, side * width : (side + 1) * width
-                ]
+        for low in range(2):
+            for high in range(2):
+                for core in range(2):
+                    source = me_ref[0] ^ (high * 16 + low * 8 + plane * 2 + core)
+                    first = (low * 2 + high) * block
+                    rows_s[pl.ds(pl.multiple_of(source * block, 8), block), :] = values[
+                        first : first + block, core * width : (core + 1) * width
+                    ]
     out_ref[...] = rows_s[...].T.astype(bf16)
-
-
-def total_kernel(factor, *refs):
-    rows = refs[0].shape[0]
-    total = refs[0][...].astype(f32)
-    for part in refs[1:-1]:
-        total = total + part[0:rows, :].astype(f32)
-    refs[-1][...] = (total * factor).astype(refs[-1].dtype)
 
 
 def place_kernel(phases, step, other, me_ref, half_ref, *refs):
@@ -269,7 +294,7 @@
         in_specs=specs if specs is not None else [VMEM] * count,
         out_specs=more.pop("out_specs", jax.tree.map(lambda _: VMEM, outs)),
         scratch_shapes=list(scratch),
-        compiler_params=pltpu.CompilerParams(vmem_limit_bytes=grant * 2**20),
+        compiler_params=pltpu.CompilerParams(vmem_limit_bytes=grant and grant * 2**20),
         **more,
     )
 
@@ -289,30 +314,39 @@
     radix = min(4, size // 2)
     masks = [m << 1 for m in range(1, radix)]
     rows = rows // radix
+    piece, rider = struct((rows, double), bf16), struct(ride.shape, bf16)
     parts = [keep] + exchange([send], [1], size)
-    extra = ride.shape[0] // 2 if riding else 0
-    outs = [struct((rows, double), f32)] + [struct((rows + extra, double), bf16)] * (radix - 1)
+    outs = [struct((rows, double), f32)] + [piece] * (radix - 1) + [rider] * 2 * riding
+    operands = [ride] * riding + parts
+    pieces = call(
+        functools.partial(split_kernel, radix, 1, riding), outs, specs=[SMEM] + [VMEM] * len(operands)
+    )(me, *operands)
+    parts = [pieces[0]] + exchange(list(pieces[1:radix]), masks, size)
     if riding:
-        outs.append(struct((extra, double), bf16))
-        parts = [ride] + parts
-    pieces = call(
-        functools.partial(split_kernel, radix, 1, riding), outs, specs=[SMEM] + [VMEM] * len(parts)
-    )(me, *parts)
-    arrived = exchange(list(pieces[1:radix]), masks, size)
-    parts = [pieces[0]] + arrived
-    if riding:
-        riders = call(lines_kernel, [struct((extra, double), bf16)] * 4, count=4)(pieces[-1], *arrived)
-    for rest in range(radix.bit_length(), bits):
-        total = call(functools.partial(total_kernel, 1.0), struct((rows, double), bf16), count=len(parts))(*parts)
-        parts = [total] + exchange([total], [1 << rest], size)
-    mine = call(functools.partial(total_kernel, factor), struct((rows, double), bf16), count=len(parts))(*parts)
-    if riding:
-        mine, *riders = lax.optimization_barrier((mine, *riders))
+        riders = [pieces[radix]] + exchange([pieces[radix + 1]], [16], size)
+        total, kept = call(
+            line_kernel, [struct((rows + ride.shape[0], double), bf16), rider], count=len(parts) + 2
+        )(*parts, *riders)
+        (came,) = exchange([total], [8], size)
+        second = call(functools.partial(total_kernel, 1.0), piece, count=2)
+        total = second(total, came)
+        (last,) = exchange([total], [24], size)
+        joined = struct((rows + ride.shape[0] // 2, double), bf16)
+        mine, *sends, ride = call(
+            functools.partial(plane_kernel, factor),
+            [piece] + [joined] * 3 + [struct((ride.shape[0] // 2, double), bf16)],
+            count=4,
+        )(total, last, kept, came)
+        got = exchange(sends, masks, size)
+        ride = [ride] + got
+        got = [part[:rows] for part in got]
     else:
+        for rest in range(radix.bit_length(), bits):
+            total = call(functools.partial(total_kernel, 1.0), piece, count=len(parts))(*parts)
+            parts = [total] + exchange([total], [1 << rest], size)
+        mine = call(functools.partial(total_kernel, factor), piece, count=len(parts))(*parts)
         mine, ride = lax.optimization_barrier((mine, ride))
-    got = exchange([mine] * (radix - 1), masks, size)
-    if riding:
-        ride = [riders[0]] + exchange(list(riders[1:]), [m << 3 for m in range(1, 4)], size)
+        got = exchange([mine] * (radix - 1), masks, size)
     mine = jnp.concatenate([mine] + got, axis=0)
     (other,) = exchange([mine], [1], size)
     return mine, other, rows, [(1, radix)], ride
@@ -332,12 +366,20 @@
             struct((size, 2 * block, width), bf16),
             scratch=[pltpu.VMEM((width, rows), bf16)] * 2 + [pltpu.SemaphoreType.DMA((2,))],
             specs=[HBM] * 2,
+            grant=None,
         )(saved_input.T, cotangent.T)
     else:
         both = jnp.concatenate(
             [saved_input.reshape(size, block, width), cotangent.reshape(size, block, width)], axis=1
         )
     both = lax.all_to_all(both, "seq", split_axis=0, concat_axis=0, tiled=True)
+    w_in, w_out = call(
+        fetch_kernel,
+        [struct(w_in.shape, bf16), struct(w_out.shape, bf16)],
+        scratch=[pltpu.SemaphoreType.DMA((2,))],
+        specs=[HBM] * 2,
+        grant=None,
+    )(w_in, w_out)
     total = levels * half
     riding = block % 8 == 0 and levels == 5
     rider = struct((rows // 4, double), bf16)

time: 77.9 us -> 68 us (0.87)
  waiting for transfers between devices: 38.6 us -> 30 us
  starting transfers between devices: 20.5 us -> 17.1 us
  Pallas kernels: 12.7 us -> 15.5 us
  local copies, waits for them, and re-layouts: 5.06 us -> 4.23 us
    ppermute x13 -> x11, waiting for transfers between devices: 30 us -> 23.7 us  [exchange(): lax.ppermute(value if not isinstance(value, list) else value[i], 'seq', [...]
    ppermute x13 -> x11, starting transfers between devices: 13.2 us -> 9.76 us  [exchange(): lax.ppermute(value if not isinstance(value, list) else value[i], 'seq', [...]
    all_to_all x1, waiting for transfers between devices: 8.53 us -> 6.26 us  [shards(): both = lax.all_to_all(both, 'seq', split_axis=0, concat_axis=0, tiled=True)]
    pallas_call x4, Pallas kernels: 0.26 us -> 2.44 us  [the longest x1 2.27 us: shards(): call(fetch_kernel, [struct(w_in.shape, bf16), struct(w_out.shape, bf16)],...]
    unnamed x11 -> x4, local copies, waits for them, and re-layouts: 2.97 us -> 2.13 us
  transfers between devices with their start and end apart: 14 -> 12, of which waited for: 11 -> 10; matrix products, arithmetic and copies ran while one was open for 3% -> 3% of each run, Pallas kernels for 3% -> 6%
where the time goes in v5:
time: 68 us; the launch traced here: 67.6 us
  waiting for transfers between devices  30 us (44%)
  starting transfers between devices  17.1 us (25%)
  Pallas kernels  15.5 us (23%)
  local copies, waits for them, and re-layouts  4.23 us (6%)
  between operations  0.74 us (1%)
    ppermute x11, waiting for transfers between devices, exchange(): lax.ppermute(value if not isinstance(value, list) else value[i], 'seq', [...  23.7 us
    ppermute x11, starting transfers between devices, exchange(): lax.ppermute(value if not isinstance(value, list) else value[i], 'seq', [...  9.76 us
    pallas_call x1, Pallas kernels, shards(): call(functools.partial(switch_kernel, levels, block), [rider if riding el...  8.14 us
    all_to_all x1, starting transfers between devices, shards(): both = lax.all_to_all(both, 'seq', split_axis=0, concat_axis=0, tiled=True)  7.3 us
    all_to_all x1, waiting for transfers between devices, shards(): both = lax.all_to_all(both, 'seq', split_axis=0, concat_axis=0, tiled=True)  6.26 us
    pallas_call x1, Pallas kernels, shards(): call(fetch_kernel, [struct(w_in.shape, bf16), struct(w_out.shape, bf16)],...  2.27 us
    unnamed x4, local copies, waits for them, and re-layouts  2.13 us
    pallas_call x1, Pallas kernels, shards(): call(pack_kernel, struct((size, 2 * block, width), bf16), scratch=[pltpu....  1.81 us
  transfers between devices with their start and end apart: 12, of which 10 were waited for; matrix products, arithmetic and copies ran while one was open for 3% of the time, Pallas kernels for 6%

profile of v5, /device:TPU:0, one launch (start us, length us, event | category | flops | bytes accessed | tf_op | source)
XLA Modules:
  0.0 67.6 jit_solution(15479255300178224139)
XLA Ops:
  0.6 1.8 %shard_map.94 = bf16[32,16,192]{2,1,0:T(8,128)(2,1)} custom-call(bf16[192,256]{1,0:T(8,128)(2,1)} %bitcast.4, bf16[192,256]{1,0:T(8,128)(2,1)} %bitcast.5), custom_call_target="tpu_custom_call" | custom-call | tf_op jit(solution)/shard_map/pallas_call | solution.py:364
  2.5 7.3 %all-to-all-start = ((bf16[32,16,192]{2,1,0:T(8,128)(2,1)}), bf16[32,16,192]{2,1,0:T(8,128)(2,1)S(1)}, u32[]{:S(2)}, u32[]{:S(2)}) async-start(bf16[32,16,192]{2,1,0:T(8,128)(2,1)} %shard_map.94), calls=%async_computation | async-start | bytes 524288 | tf_op jit(solution)/shard_map/all_to_all | solution.py:375
  11.8 2.3 %shard_map.95 = (bf16[384,768]{1,0:T(8,128)(2,1)}, bf16[768,384]{1,0:T(8,128)(2,1)}) custom-call(bf16[384,768]{1,0:T(8,128)(2,1)} %refs_0_.1, bf16[768,384]{1,0:T(8,128)(2,1)} %refs_1_.1), custom_call_target="tpu_custom_call" | custom-call | tf_op jit(solution)/shard_map/pallas_call | solution.py:376
  14.1 6.3 %all-to-all-done.both_ref = bf16[32,16,192]{2,1,0:T(8,128)(2,1)S(1)} async-done(((bf16[32,16,192]{2,1,0:T(8,128)(2,1)}), bf16[32,16,192]{2,1,0:T(8,128)(2,1)S(1)}, u32[]{:S(2)}, u32[]{:S(2)}) %all-to-all-start) | async-done | bytes 196640 | tf_op jit(solution)/shard_map/all_to_all | solution.py:375
  20.4 1.1 %copy-done = bf16[384,768]{1,0:T(8,128)(2,1)S(1)} copy-done((bf16[384,768]{1,0:T(8,128)(2,1)S(1)}, bf16[384,768]{1,0:T(8,128)(2,1)}, u32[]{:S(2)}) %copy-start) | copy-done | bytes 589848
  21.4 1.1 %copy-done.1 = bf16[768,384]{1,0:T(8,128)(2,1)S(1)} copy-done((bf16[768,384]{1,0:T(8,128)(2,1)S(1)}, bf16[768,384]{1,0:T(8,128)(2,1)}, u32[]{:S(2)}) %copy-start.1) | copy-done | bytes 589848
  22.5 8.1 %shard_map.96 = (bf16[64,384]{1,0:T(8,128)(2,1)S(1)}, f32[768,384]{1,0:T(8,128)S(1)}, bf16[832,384]{1,0:T(8,128)(2,1)S(1)}) custom-call(s32[1]{0:T(128)} %bitcast.me_ref, bf16[32,16,192]{2,1,0:T(8,128)(2,1)S(1)} %all-to-all-done.both_ref, bf16[384,768]{1,0:T(8,128)(2,1)S(1)} %copy-done, f32[1,768]{1,0:T(1,128)S(1)} %reshape.19.bias_ref, ...), custom_call_target="tpu_custom_call" | custom-call | tf_op jit(solution)/shard_map/pallas_call | solution.py:386
  30.7 2.1 %collective-permute-done.refs_2_ = bf16[832,384]{1,0:T(8,128)(2,1)S(1)} collective-permute-done((bf16[832,384]{1,0:T(8,128)(2,1)S(1)}, bf16[832,384]{1,0:T(8,128)(2,1)S(1)}, u32[]{:S(2)}, u32[]{:S(2)}) %collective-permute-start) | collective-permute-done | bytes 639008 | tf_op jit(solution)/shard_map/ppermute | solution.py:307
  33.5 1.3 %collective-permute-start.2 = (bf16[192,384]{1,0:T(8,128)(2,1)S(1)}, bf16[192,384]{1,0:T(8,128)(2,1)S(1)}, u32[]{:S(2)}, u32[]{:S(2)}) collective-permute-start(bf16[192,384]{1,0:T(8,128)(2,1)S(1)} %get-tuple-element.32), channel_id=1, source_target_pairs={{0,4},{1,5},{2,6},{3,7},{4,0},{5,1},{6,2},{7,3},{8,12},{9,13},{10,... | collective-permute-start | bytes 442376 | tf_op jit(solution)/shard_map/ppermute | solution.py:307
  34.8 1.7 %collective-permute-start.3 = (bf16[192,384]{1,0:T(8,128)(2,1)S(1)}, bf16[192,384]{1,0:T(8,128)(2,1)S(1)}, u32[]{:S(2)}, u32[]{:S(2)}) collective-permute-start(bf16[192,384]{1,0:T(8,128)(2,1)S(1)} %get-tuple-element.33), channel_id=1, source_target_pairs={{0,6},{1,7},{2,4},{3,5},{4,2},{5,3},{6,0},{7,1},{8,14},{9,15},{10,... | collective-permute-start | bytes 442376 | tf_op jit(solution)/shard_map/ppermute | solution.py:307
  37.0 5.0 %collective-permute-done.4.refs_5_ = bf16[64,384]{1,0:T(8,128)(2,1)S(1)} collective-permute-done((bf16[64,384]{1,0:T(8,128)(2,1)S(1)}, bf16[64,384]{1,0:T(8,128)(2,1)S(1)}, u32[]{:S(2)}, u32[]{:S(2)}) %collective-permute-start.4) | collective-permute-done | bytes 49184 | tf_op jit(solution)/shard_map/ppermute | solution.py:307
  42.5 0.7 %collective-permute-start.5 = (bf16[256,384]{1,0:T(8,128)(2,1)S(1)}, bf16[256,384]{1,0:T(8,128)(2,1)S(1)}, u32[]{:S(2)}, u32[]{:S(2)}) collective-permute-start(bf16[256,384]{1,0:T(8,128)(2,1)S(1)} %get-tuple-element.36.refs_0_), channel_id=1, source_target_pairs={{0,8},{1,9},{2,10},{3,11},{4,12},{5,13},{6,14},{7,15},{8,0},{9,1},... | collective-permute-start | bytes 589832 | tf_op jit(solution)/shard_map/ppermute | solution.py:307
  43.3 5.4 %collective-permute-done.5.refs_1_.refs_3_ = bf16[256,384]{1,0:T(8,128)(2,1)S(1)} collective-permute-done((bf16[256,384]{1,0:T(8,128)(2,1)S(1)}, bf16[256,384]{1,0:T(8,128)(2,1)S(1)}, u32[]{:S(2)}, u32[]{:S(2)}) %collective-permute-start.5) | collective-permute-done | bytes 196640 | tf_op jit(solution)/shard_map/ppermute | solution.py:307
  48.7 1.3 %collective-permute-start.6 = (bf16[192,384]{1,0:T(8,128)(2,1)S(1)}, bf16[192,384]{1,0:T(8,128)(2,1)S(1)}, u32[]{:S(2)}, u32[]{:S(2)}) collective-permute-start(bf16[192,384]{1,0:T(8,128)(2,1)S(1)} %shard_map.99.refs_0_), channel_id=1, source_target_pairs={{0,24},{1,25},{2,26},{3,27},{4,28},{5,29},{6,30},{7,31},{8,16},{9,... | collective-permute-start | bytes 442376 | tf_op jit(solution)/shard_map/ppermute | solution.py:307
  50.0 5.8 %collective-permute-done.6.refs_1_ = bf16[192,384]{1,0:T(8,128)(2,1)S(1)} collective-permute-done((bf16[192,384]{1,0:T(8,128)(2,1)S(1)}, bf16[192,384]{1,0:T(8,128)(2,1)S(1)}, u32[]{:S(2)}, u32[]{:S(2)}) %collective-permute-start.6) | collective-permute-done | bytes 147488 | tf_op jit(solution)/shard_map/ppermute | solution.py:307
  55.9 1.0 %collective-permute-start.7 = (bf16[224,384]{1,0:T(8,128)(2,1)S(1)}, bf16[224,384]{1,0:T(8,128)(2,1)S(1)}, u32[]{:S(2)}, u32[]{:S(2)}) collective-permute-start(bf16[224,384]{1,0:T(8,128)(2,1)S(1)} %get-tuple-element.39), channel_id=1, source_target_pairs={{0,2},{1,3},{2,0},{3,1},{4,6},{5,7},{6,4},{7,5},{8,10},{9,11},{10,... | collective-permute-start | bytes 516104 | tf_op jit(solution)/shard_map/ppermute | solution.py:307
  56.9 1.1 %collective-permute-start.8 = (bf16[224,384]{1,0:T(8,128)(2,1)S(1)}, bf16[224,384]{1,0:T(8,128)(2,1)S(1)}, u32[]{:S(2)}, u32[]{:S(2)}) collective-permute-start(bf16[224,384]{1,0:T(8,128)(2,1)S(1)} %get-tuple-element.40), channel_id=1, source_target_pairs={{0,4},{1,5},{2,6},{3,7},{4,0},{5,1},{6,2},{7,3},{8,12},{9,13},{10,... | collective-permute-start | bytes 516104 | tf_op jit(solution)/shard_map/ppermute | solution.py:307
  58.1 1.4 %collective-permute-start.9 = (bf16[224,384]{1,0:T(8,128)(2,1)S(1)}, bf16[224,384]{1,0:T(8,128)(2,1)S(1)}, u32[]{:S(2)}, u32[]{:S(2)}) collective-permute-start(bf16[224,384]{1,0:T(8,128)(2,1)S(1)} %get-tuple-element.41), channel_id=1, source_target_pairs={{0,6},{1,7},{2,4},{3,5},{4,2},{5,3},{6,0},{7,1},{8,14},{9,15},{10,... | collective-permute-start | bytes 516104 | tf_op jit(solution)/shard_map/ppermute | solution.py:307
  59.5 1.9 %collective-permute-done.7.refs_1_ = bf16[224,384]{1,0:T(8,128)(2,1)S(1)} collective-permute-done((bf16[224,384]{1,0:T(8,128)(2,1)S(1)}, bf16[224,384]{1,0:T(8,128)(2,1)S(1)}, u32[]{:S(2)}, u32[]{:S(2)}) %collective-permute-start.7) | collective-permute-done | bytes 172064 | tf_op jit(solution)/shard_map/ppermute | solution.py:307
  61.4 0.9 %collective-permute-done.8.refs_2_ = bf16[224,384]{1,0:T(8,128)(2,1)S(1)} collective-permute-done((bf16[224,384]{1,0:T(8,128)(2,1)S(1)}, bf16[224,384]{1,0:T(8,128)(2,1)S(1)}, u32[]{:S(2)}, u32[]{:S(2)}) %collective-permute-start.8) | collective-permute-done | bytes 172064 | tf_op jit(solution)/shard_map/ppermute | solution.py:307
  62.3 2.0 %collective-permute-done.9.refs_3_ = bf16[224,384]{1,0:T(8,128)(2,1)S(1)} collective-permute-done((bf16[224,384]{1,0:T(8,128)(2,1)S(1)}, bf16[224,384]{1,0:T(8,128)(2,1)S(1)}, u32[]{:S(2)}, u32[]{:S(2)}) %collective-permute-start.9) | collective-permute-done | bytes 172064 | tf_op jit(solution)/shard_map/ppermute | solution.py:307
  64.5 1.1 %shard_map.102 = (f32[384,768]{1,0:T(8,128)}, f32[768,384]{1,0:T(8,128)}) custom-call(s32[1]{0:T(128)} %bitcast.me_ref, bf16[768,384]{1,0:T(8,128)(2,1)S(1)} %pad_maximum_fusion.half_ref), custom_call_target="tpu_custom_call" | custom-call | tf_op jit(solution)/shard_map/pallas_call | solution.py:422
  65.6 0.8 %shard_map.101 = bf16[192,256]{1,0:T(8,128)(2,1)} custom-call(s32[1]{0:T(128)} %bitcast.me_ref, bf16[32,384]{1,0:T(8,128)(2,1)S(1)} %get-tuple-element.38.refs_0_, bf16[224,384]{1,0:T(8,128)(2,1)S(1)} %collective-permute-done.7.refs_1_, bf16[224,384]{1,0:T(8,128)(2,1)S(1)} %collective-permute-done.8.refs_2_, bf16[224,384]{1,0:T(8,128)(2,1)S(1)} %collective-permute-done.9.refs_3_), custom_call_target="tpu_custom_call" | custom-call | tf_op jit(solution)/shard_map/pallas_call | solution.py:414
  66.5 1.1 %shard_map.103 = (f32[384,768]{1,0:T(8,128)}, f32[768,384]{1,0:T(8,128)}) custom-call(s32[1]{0:T(128)} %bitcast.me_ref, bf16[768,384]{1,0:T(8,128)(2,1)S(1)} %collective-permute-done.10.half_ref, f32[384,768]{1,0:T(8,128)} %get-tuple-element.43.refs_0_, f32[768,384]{1,0:T(8,128)} %get-tuple-element.44.refs_1_), custom_call_target="tpu_custom_call", output_to_operand_aliasing={{0}: (2, {}), {1}: (3, {})} | custom-call | tf_op jit(solution)/shard_map/pallas_call | solution.py:426
  (21 shorter events, 4.2 us)
Async XLA Ops:
  2.5 17.9 %all-to-all-start = ((bf16[32,16,192]{2,1,0:T(8,128)(2,1)}), bf16[32,16,192]{2,1,0:T(8,128)(2,1)S(1)}, u32[]{:S(2)}, u32[]{:S(2)}) async-start(bf16[32,16,192]{2,1,0:T(8,128)(2,1)} %shard_map.94), calls=%async_computation | async-start | bytes 524288 | tf_op jit(solution)/shard_map/all_to_all | solution.py:375
  20.4 1.1 %copy-start = (bf16[384,768]{1,0:T(8,128)(2,1)S(1)}, bf16[384,768]{1,0:T(8,128)(2,1)}, u32[]{:S(2)}) copy-start(bf16[384,768]{1,0:T(8,128)(2,1)} %get-tuple-element.25.w_in_ref) | copy-start | bytes 1769476
  21.4 1.1 %copy-start.1 = (bf16[768,384]{1,0:T(8,128)(2,1)S(1)}, bf16[768,384]{1,0:T(8,128)(2,1)}, u32[]{:S(2)}) copy-start(bf16[768,384]{1,0:T(8,128)(2,1)} %get-tuple-element.26.w_out_ref) | copy-start | bytes 1769476
  30.6 2.1 %collective-permute-start = (bf16[832,384]{1,0:T(8,128)(2,1)S(1)}, bf16[832,384]{1,0:T(8,128)(2,1)S(1)}, u32[]{:S(2)}, u32[]{:S(2)}) collective-permute-start(bf16[832,384]{1,0:T(8,128)(2,1)S(1)} %get-tuple-element.29), channel_id=1, source_target_pairs={{0,1},{1,0},{2,3},{3,2},{4,5},{5,4},{6,7},{7,6},{8,9},{9,8},{10,11... | collective-permute-start | bytes 1916936 | tf_op jit(solution)/shard_map/ppermute | solution.py:307
  32.9 9.1 %collective-permute-start.1 = (bf16[192,384]{1,0:T(8,128)(2,1)S(1)}, bf16[192,384]{1,0:T(8,128)(2,1)S(1)}, u32[]{:S(2)}, u32[]{:S(2)}) collective-permute-start(bf16[192,384]{1,0:T(8,128)(2,1)S(1)} %get-tuple-element.31), channel_id=1, source_target_pairs={{0,2},{1,3},{2,0},{3,1},{4,6},{5,7},{6,4},{7,5},{8,10},{9,11},{10,... | collective-permute-start | bytes 442376 | tf_op jit(solution)/shard_map/ppermute | solution.py:307
  33.5 8.5 %collective-permute-start.2 = (bf16[192,384]{1,0:T(8,128)(2,1)S(1)}, bf16[192,384]{1,0:T(8,128)(2,1)S(1)}, u32[]{:S(2)}, u32[]{:S(2)}) collective-permute-start(bf16[192,384]{1,0:T(8,128)(2,1)S(1)} %get-tuple-element.32), channel_id=1, source_target_pairs={{0,4},{1,5},{2,6},{3,7},{4,0},{5,1},{6,2},{7,3},{8,12},{9,13},{10,... | collective-permute-start | bytes 442376 | tf_op jit(solution)/shard_map/ppermute | solution.py:307
  34.8 7.7 %collective-permute-start.3 = (bf16[192,384]{1,0:T(8,128)(2,1)S(1)}, bf16[192,384]{1,0:T(8,128)(2,1)S(1)}, u32[]{:S(2)}, u32[]{:S(2)}) collective-permute-start(bf16[192,384]{1,0:T(8,128)(2,1)S(1)} %get-tuple-element.33), channel_id=1, source_target_pairs={{0,6},{1,7},{2,4},{3,5},{4,2},{5,3},{6,0},{7,1},{8,14},{9,15},{10,... | collective-permute-start | bytes 442376 | tf_op jit(solution)/shard_map/ppermute | solution.py:307
  36.5 5.5 %collective-permute-start.4 = (bf16[64,384]{1,0:T(8,128)(2,1)S(1)}, bf16[64,384]{1,0:T(8,128)(2,1)S(1)}, u32[]{:S(2)}, u32[]{:S(2)}) collective-permute-start(bf16[64,384]{1,0:T(8,128)(2,1)S(1)} %get-tuple-element.35), channel_id=1, source_target_pairs={{0,16},{1,17},{2,18},{3,19},{4,20},{5,21},{6,22},{7,23},{8,24},{9,... | collective-permute-start | bytes 147464 | tf_op jit(solution)/shard_map/ppermute | solution.py:307
  42.5 6.1 %collective-permute-start.5 = (bf16[256,384]{1,0:T(8,128)(2,1)S(1)}, bf16[256,384]{1,0:T(8,128)(2,1)S(1)}, u32[]{:S(2)}, u32[]{:S(2)}) collective-permute-start(bf16[256,384]{1,0:T(8,128)(2,1)S(1)} %get-tuple-element.36.refs_0_), channel_id=1, source_target_pairs={{0,8},{1,9},{2,10},{3,11},{4,12},{5,13},{6,14},{7,15},{8,0},{9,1},... | collective-permute-start | bytes 589832 | tf_op jit(solution)/shard_map/ppermute | solution.py:307
  48.7 7.1 %collective-permute-start.6 = (bf16[192,384]{1,0:T(8,128)(2,1)S(1)}, bf16[192,384]{1,0:T(8,128)(2,1)S(1)}, u32[]{:S(2)}, u32[]{:S(2)}) collective-permute-start(bf16[192,384]{1,0:T(8,128)(2,1)S(1)} %shard_map.99.refs_0_), channel_id=1, source_target_pairs={{0,24},{1,25},{2,26},{3,27},{4,28},{5,29},{6,30},{7,31},{8,16},{9,... | collective-permute-start | bytes 442376 | tf_op jit(solution)/shard_map/ppermute | solution.py:307
  55.9 5.5 %collective-permute-start.7 = (bf16[224,384]{1,0:T(8,128)(2,1)S(1)}, bf16[224,384]{1,0:T(8,128)(2,1)S(1)}, u32[]{:S(2)}, u32[]{:S(2)}) collective-permute-start(bf16[224,384]{1,0:T(8,128)(2,1)S(1)} %get-tuple-element.39), channel_id=1, source_target_pairs={{0,2},{1,3},{2,0},{3,1},{4,6},{5,7},{6,4},{7,5},{8,10},{9,11},{10,... | collective-permute-start | bytes 516104 | tf_op jit(solution)/shard_map/ppermute | solution.py:307
  56.9 5.4 %collective-permute-start.8 = (bf16[224,384]{1,0:T(8,128)(2,1)S(1)}, bf16[224,384]{1,0:T(8,128)(2,1)S(1)}, u32[]{:S(2)}, u32[]{:S(2)}) collective-permute-start(bf16[224,384]{1,0:T(8,128)(2,1)S(1)} %get-tuple-element.40), channel_id=1, source_target_pairs={{0,4},{1,5},{2,6},{3,7},{4,0},{5,1},{6,2},{7,3},{8,12},{9,13},{10,... | collective-permute-start | bytes 516104 | tf_op jit(solution)/shard_map/ppermute | solution.py:307
  58.1 6.3 %collective-permute-start.9 = (bf16[224,384]{1,0:T(8,128)(2,1)S(1)}, bf16[224,384]{1,0:T(8,128)(2,1)S(1)}, u32[]{:S(2)}, u32[]{:S(2)}) collective-permute-start(bf16[224,384]{1,0:T(8,128)(2,1)S(1)} %get-tuple-element.41), channel_id=1, source_target_pairs={{0,6},{1,7},{2,4},{3,5},{4,2},{5,3},{6,0},{7,1},{8,14},{9,15},{10,... | collective-permute-start | bytes 516104 | tf_op jit(solution)/shard_map/ppermute | solution.py:307
  64.5 2.1 %collective-permute-start.10 = (bf16[768,384]{1,0:T(8,128)(2,1)S(1)}, bf16[768,384]{1,0:T(8,128)(2,1)S(1)}, u32[]{:S(2)}, u32[]{:S(2)}) collective-permute-start(bf16[768,384]{1,0:T(8,128)(2,1)S(1)} %pad_maximum_fusion.half_ref), channel_id=1, source_target_pairs={{0,1},{1,0},{2,3},{3,2},{4,5},{5,4},{6,7},{7,6},{8,9},{9,8},{10,11... | collective-permute-start | bytes 1769480 | tf_op jit(solution)/shard_map/ppermute | solution.py:307

commit v6 on v5

--- a/solution.py
+++ b/solution.py
@@ -27,27 +27,23 @@
     groups = rows // (2 * stride)
     if stride >= 8:
         viewed = state.reshape(groups, 2, stride, width)
-        halves = [viewed[:, side].reshape(rows // 2, width) for side in (0, 1)]
-    else:
-        halves = []
-        for side in (0, 1):
-            row = lax.broadcasted_iota(jnp.int32, (rows // 2, rows), 0)
-            col = lax.broadcasted_iota(jnp.int32, (rows // 2, rows), 1)
-            pick = (row // stride) * (2 * stride) + row % stride + side * stride
-            halves.append(dot((col == pick).astype(bf16), state.astype(bf16), (1, 0)))
-    return jnp.concatenate(halves, axis=1)
-
-
-def unpair_rows(paired, stride):
-    half, double = paired.shape
-    width = double // 2
-    groups = half // stride
-    first, second = paired[:, :width], paired[:, width:]
+        return [viewed[:, side].reshape(rows // 2, width) for side in (0, 1)]
+    halves = []
+    for side in (0, 1):
+        row = lax.broadcasted_iota(jnp.int32, (rows // 2, rows), 0)
+        col = lax.broadcasted_iota(jnp.int32, (rows // 2, rows), 1)
+        pick = (row // stride) * (2 * stride) + row % stride + side * stride
+        halves.append(dot((col == pick).astype(bf16), state.astype(bf16), (1, 0)))
+    return halves
+
+
+def unpair_rows(halves, stride):
+    half, width = halves[0].shape
     if stride >= 8:
-        parts = [part.reshape(groups, 1, stride, width) for part in (first, second)]
+        parts = [part.reshape(half // stride, 1, stride, width) for part in halves]
         return jnp.concatenate(parts, axis=1).reshape(2 * half, width)
     total = jnp.zeros((2 * half, width), f32)
-    for side, part in enumerate((first, second)):
+    for side, part in enumerate(halves):
         row = lax.broadcasted_iota(jnp.int32, (2 * half, half), 0)
         col = lax.broadcasted_iota(jnp.int32, (2 * half, half), 1)
         place = (col // stride) * (2 * stride) + col % stride + side * stride
@@ -55,8 +51,16 @@
     return total
 
 
+def mean_of(halves, count):
+    return jnp.sum(halves[0] + halves[1], axis=-1, keepdims=True) * (1.0 / count)
+
+
+def widen(part, lanes):
+    rows, width = part.shape
+    return part if width == lanes else jnp.concatenate([part, jnp.zeros((rows, lanes - width), part.dtype)], axis=1)
+
+
 def pack_kernel(x_ref, g_ref, out_ref, x_s, g_s, sem):
-    size, both, width = out_ref.shape
     copies = [
         pltpu.make_async_copy(ref, scratch, sem.at[side])
         for side, (ref, scratch) in enumerate(((x_ref, x_s), (g_ref, g_s)))
@@ -66,21 +70,36 @@
     parts = []
     for copy, scratch in zip(copies, (x_s, g_s)):
         copy.wait()
-        parts.append(scratch[...].astype(f32).T.reshape(size, both // 2, width))
-    out_ref[...] = jnp.concatenate(parts, axis=1).astype(bf16)
-
-
-def fetch_kernel(*refs):
-    count = len(refs) // 2
-    copies = [pltpu.make_async_copy(refs[i], refs[count + i], refs[-1].at[i]) for i in range(count)]
+        parts.append(scratch[...].astype(f32).T)
+    out_ref[...] = jnp.concatenate(parts, axis=1).reshape(out_ref.shape).astype(bf16)
+
+
+def fetch_kernel(w_in_ref, w_out_ref, bias_ref, logit_ref, scale_ref, *refs):
+    w_in_o, w_out_o, bias_o, gate_o, scale_o, w_in_s, w_out_s, sem = refs
+    copies = [
+        pltpu.make_async_copy(ref, to, sem.at[i])
+        for i, (ref, to) in enumerate(((w_in_ref, w_in_s), (w_out_ref, w_out_s)))
+    ]
     for copy in copies:
         copy.start()
+    width, lanes = w_in_ref.shape[0] // 2, w_in_o.shape[0] // 2
+    bias_o[...] = bias_ref[...].reshape(bias_o.shape)
+    gate = jax.nn.sigmoid(logit_ref[...].reshape(1, 2 * width))
+    scale = scale_ref[...].reshape(1, 2 * width)
     for copy in copies:
         copy.wait()
+    for side in range(2):
+        first, at = side * width, side * lanes
+        gate_o[:, at : at + lanes] = widen(gate[:, first : first + width], lanes)
+        scale_o[:, at : at + lanes] = widen(scale[:, first : first + width], lanes)
+        w_out_o[:, at : at + lanes] = widen(w_out_s[:, first : first + width], lanes)
+        w_in_o[at : at + width, :] = w_in_s[first : first + width, :]
+        if lanes > width:
+            w_in_o[at + width : at + lanes, :] = jnp.zeros((lanes - width, w_in_o.shape[1]), bf16)
 
 
 def switch_kernel(
-    levels, block, me_ref, both_ref, w_in_ref, bias_ref, w_out_ref, logit_ref, scale_ref,
+    levels, block, me_ref, both_ref, w_in_ref, w_out_ref, bias_ref, gate_ref, scale_ref,
     grad_ref, keep_ref, send_ref,
     low_s, act_s, slope_s, normed_s, inverse_s, pre_s, bg_s, paired_s,
 ):
@@ -89,70 +108,84 @@
     units = bias_ref.shape[1]
     riding = send_ref.shape[0] > units
     core = me_ref[0] % 2
-    both = both_ref[...].astype(f32)
-    gate = jax.nn.sigmoid(logit_ref[...])
-    scale = scale_ref[...]
-    state = both[:, :block].reshape(rows, width)
+    sides = range(2)
+    lanes = w_in_ref.shape[0] // 2
+    gate = [gate_ref[:, side * lanes : (side + 1) * lanes] for side in sides]
+    scale = [scale_ref[:, side * lanes : (side + 1) * lanes] for side in sides]
+    both = both_ref[...].astype(f32).reshape(rows, double)
+    state = widen(both[:, :width], lanes)
+    inside = lax.broadcasted_iota(jnp.int32, (half, lanes), 1) < width
     for level in range(levels):
         at = pl.ds(level * half, half)
         paired = pair_rows(state, block * 2**level)
-        centered = paired - jnp.mean(paired, axis=-1, keepdims=True)
-        inverse = lax.rsqrt(jnp.mean(centered * centered, axis=-1, keepdims=True) + epsilon)
-        normed = centered * inverse
-        low = normed.astype(bf16)
-        normed_s[at, :] = normed
+        average = mean_of(paired, double)
+        centered = [jnp.where(inside, part - average, 0.0) for part in paired]
+        inverse = lax.rsqrt(mean_of([part * part for part in centered], double) + epsilon)
+        normed = [part * inverse for part in centered]
+        low = jnp.concatenate([part.astype(bf16) for part in normed], axis=1)
+        low_s[at, :] = low
         inverse_s[at, :] = inverse
-        low_s[at, :] = low
+        for side in sides:
+            normed_s[side, at, :] = normed[side]
         u = dot(low, w_in_ref[...], (1, 0)) + bias_ref[...]
         square = u * u
-        tangent = jnp.tanh(tanh_scale * (u + cubic_coef * square * u))
-        rise = 0.5 * (1.0 + tangent)
-        act = (u * rise).astype(bf16)
-        slope_s[at, :] = rise + 0.5 * u * (1.0 - tangent * tangent) * tanh_scale * (
-            1.0 + 3.0 * cubic_coef * square
-        )
+        tangent = jnp.tanh(u * (tanh_scale + tanh_scale * cubic_coef * square))
+        rise = 0.5 + 0.5 * tangent
+        value = u * rise
+        act = value.astype(bf16)
+        slope_s[at, :] = rise + value * (1.0 - tangent) * (tanh_scale + 3.0 * tanh_scale * cubic_coef * square)
         act_s[at, :] = act
         if level < levels - 1:
             branch = dot(act, w_out_ref[...], (1, 0))
-            result = (gate * paired + scale * branch).astype(bf16).astype(f32)
+            result = [
+                (gate[side] * paired[side] + scale[side] * branch[:, side * lanes : (side + 1) * lanes])
+                .astype(bf16)
+                .astype(f32)
+                for side in sides
+            ]
             state = unpair_rows(result, block * 2**level)
-    grad = both[:, block:].reshape(rows, width)
+    grad = widen(both[:, width:], lanes)
     for level in reversed(range(levels)):
         at = pl.ds(level * half, half)
         upstream = pair_rows(grad, block * 2**level)
-        branch_grad = (scale * upstream).astype(bf16)
-        bg_s[at, :] = branch_grad
-        act_grad = dot(branch_grad, w_out_ref[...], (1, 1))
+        branch_grad = [(scale[side] * upstream[side]).astype(bf16) for side in sides]
+        bg_s[at, :] = jnp.concatenate([part[:, :width] for part in branch_grad], axis=1)
+        act_grad = dot(jnp.concatenate(branch_grad, axis=1), w_out_ref[...], (1, 1))
         pre_grad = (act_grad * slope_s[at, :]).astype(bf16)
         pre_s[at, :] = pre_grad
         normed_grad = dot(pre_grad, w_in_ref[...], (1, 1))
-        normed = normed_s[at, :]
-        moved = (
-            normed_grad
-            - jnp.mean(normed_grad, axis=-1, keepdims=True)
-            - normed * jnp.mean(normed_grad * normed, axis=-1, keepdims=True)
-        )
-        result = (gate * upstream + inverse_s[at, :] * moved).astype(bf16).astype(f32)
+        normed_grad = [normed_grad[:, side * lanes : (side + 1) * lanes] for side in sides]
+        normed = [normed_s[side, at, :] for side in sides]
+        average = mean_of(normed_grad, double)
+        product = mean_of([normed_grad[side] * normed[side] for side in sides], double)
+        inverse = inverse_s[at, :]
+        result = [
+            (gate[side] * upstream[side] + inverse * (normed_grad[side] - average - normed[side] * product))
+            .astype(bf16)
+            .astype(f32)
+            for side in sides
+        ]
         if level > 0 or not riding:
             grad = unpair_rows(result, block * 2**level)
     if riding:
-        turned = jnp.concatenate([result[:, width:], result[:, :width]], axis=1)
-        paired_s[...] = jnp.where(core == 0, result, turned)
+        paired_s[:, :width] = jnp.where(core == 0, result[0], result[1])[:, :width]
+        paired_s[:, width:] = jnp.where(core == 0, result[1], result[0])[:, :width]
         pairs = half // block
         kept, sent = [], []
         for low in range(pairs // 8):
             for plane in range(4):
-                sides = []
+                found = []
                 for high in range(2):
                     chip = ((high * (pairs // 8) + low) * 4 + plane) ^ (me_ref[0] >> 1)
-                    sides.append(paired_s[pl.ds(pl.multiple_of(chip * block, 8), block), :])
-                kept.append(jnp.concatenate([side[:, :width] for side in sides], axis=1))
-                sent.append(jnp.concatenate([side[:, width:] for side in sides], axis=1))
+                    found.append(paired_s[pl.ds(pl.multiple_of(chip * block, 8), block), :])
+                kept.append(jnp.concatenate([part[:, :width] for part in found], axis=1))
+                sent.append(jnp.concatenate([part[:, width:] for part in found], axis=1))
         grad_ref[...] = jnp.concatenate(kept, axis=0).astype(bf16)
         send_ref[units:, :] = jnp.concatenate(sent, axis=0).astype(bf16)
     else:
-        grad_ref[...] = grad.astype(bf16)
+        grad_ref[...] = grad[:, :width].astype(bf16)
     grad_in = dot(low_s[...], pre_s[...], (0, 0))
+    grad_in = jnp.concatenate([grad_in[side * lanes : side * lanes + width] for side in sides], axis=0)
     grad_out = dot(act_s[...], bg_s[...], (0, 0))
 
     def put_in(ref):
@@ -252,39 +285,38 @@
     out_ref[...] = rows_s[...].T.astype(bf16)
 
 
-def place_kernel(phases, step, other, me_ref, half_ref, *refs):
+def place_kernel(bit, me_ref, *refs):
     in_ref, out_ref, wide_s, sem = refs[-4:]
+    count, step, double = wide_s.shape
     me = me_ref[0]
-    double = half_ref.shape[1]
-    pieces = half_ref.shape[0] // step
-    base = 0
-    for bit, radix in phases:
-        base = base * radix + ((me >> bit) & (radix - 1))
-
-    def targets(side):
-        for slot in range(pieces):
-            first = (slot ^ base) * step
-            rows = pl.ds(slot * step, step)
-            if side == 0:
+    pieces = count // 2
+    base = (me >> bit) & (pieces - 1)
+
+    def write(parts):
+        copies = []
+        for i, part in enumerate(parts):
+            first = ((i % pieces) ^ base) * step
+            if i < pieces:
                 lane = (first // double) * double
                 to = in_ref.at[
                     pl.ds(pl.multiple_of(first - lane, tile), step), pl.ds(pl.multiple_of(lane, 128), double)
                 ]
             else:
                 to = out_ref.at[pl.ds(pl.multiple_of(first, tile), step), :]
-            yield slot, rows, pltpu.make_async_copy(wide_s.at[rows, :], to, sem.at[slot])
-
-    for side in range(2):
-
-        @pl.when(me % 2 == (side ^ other))
-        def _():
-            copies = []
-            for slot, rows, copy in targets(side):
-                wide_s[rows, :] = half_ref[rows, :].astype(f32)
-                copy.start()
-                copies.append(copy)
-            for copy in copies:
-                copy.wait()
+            wide_s[i] = part[0:step, :].astype(f32)
+            copy = pltpu.make_async_copy(wide_s.at[i], to, sem.at[i])
+            copy.start()
+            copies.append(copy)
+        for copy in copies:
+            copy.wait()
+
+    @pl.when(me % 2 == 0)
+    def _():
+        write(refs[:count])
+
+    @pl.when(me % 2 == 1)
+    def _():
+        write(refs[pieces:count] + refs[:pieces])
 
 
 def call(kernel, outs, scratch=(), specs=None, count=0, grant=8, **more):
@@ -339,7 +371,6 @@
         )(total, last, kept, came)
         got = exchange(sends, masks, size)
         ride = [ride] + got
-        got = [part[:rows] for part in got]
     else:
         for rest in range(radix.bit_length(), bits):
             total = call(functools.partial(total_kernel, 1.0), piece, count=len(parts))(*parts)
@@ -347,9 +378,8 @@
         mine = call(functools.partial(total_kernel, factor), piece, count=len(parts))(*parts)
         mine, ride = lax.optimization_barrier((mine, ride))
         got = exchange([mine] * (radix - 1), masks, size)
-    mine = jnp.concatenate([mine] + got, axis=0)
-    (other,) = exchange([mine], [1], size)
-    return mine, other, rows, [(1, radix)], ride
+    mine = [mine] + got
+    return mine, exchange(mine, [1] * radix, size), rows, ride
 
 
 def shards(saved_input, cotangent, w_in, bias_in, w_out, residual_logit, branch_scale):
@@ -363,23 +393,23 @@
     if block % 8 == 0:
         both = call(
             pack_kernel,
-            struct((size, 2 * block, width), bf16),
+            struct((size, block, double), bf16),
             scratch=[pltpu.VMEM((width, rows), bf16)] * 2 + [pltpu.SemaphoreType.DMA((2,))],
             specs=[HBM] * 2,
             grant=None,
+            cost_estimate=pl.CostEstimate(flops=0, bytes_accessed=7 * 10**6, transcendentals=0),
         )(saved_input.T, cotangent.T)
     else:
-        both = jnp.concatenate(
-            [saved_input.reshape(size, block, width), cotangent.reshape(size, block, width)], axis=1
-        )
+        both = jnp.concatenate([saved_input, cotangent], axis=1).reshape(size, block, double)
     both = lax.all_to_all(both, "seq", split_axis=0, concat_axis=0, tiled=True)
-    w_in, w_out = call(
+    lanes = -(-width // 128) * 128
+    parameters = call(
         fetch_kernel,
-        [struct(w_in.shape, bf16), struct(w_out.shape, bf16)],
-        scratch=[pltpu.SemaphoreType.DMA((2,))],
-        specs=[HBM] * 2,
-        grant=None,
-    )(w_in, w_out)
+        [struct((2 * lanes, units), bf16), struct((units, 2 * lanes), bf16)]
+        + [struct((1, count), f32) for count in (units, 2 * lanes, 2 * lanes)],
+        scratch=[pltpu.VMEM(w_in.shape, bf16), pltpu.VMEM(w_out.shape, bf16), pltpu.SemaphoreType.DMA((2,))],
+        specs=[HBM] * 2 + [VMEM] * 3,
+    )(w_in, w_out, bias_in, residual_logit, branch_scale)
     total = levels * half
     riding = block % 8 == 0 and levels == 5
     rider = struct((rows // 4, double), bf16)
@@ -391,10 +421,10 @@
             struct((units + rider.shape[0] * riding, double), bf16),
         ],
         scratch=[
-            pltpu.VMEM((total, double), bf16),
+            pltpu.VMEM((total, 2 * lanes), bf16),
             pltpu.VMEM((total, units), bf16),
             pltpu.VMEM((total, units), f32),
-            pltpu.VMEM((total, double), f32),
+            pltpu.VMEM((2, total, lanes), f32),
             pltpu.VMEM((total, 1), f32),
             pltpu.VMEM((total, units), bf16),
             pltpu.VMEM((total, double), bf16),
@@ -402,14 +432,13 @@
         ],
         specs=[SMEM] + [VMEM] * 6,
         grant=20,
-    )(me, both, w_in, bias_in.reshape(1, units), w_out, residual_logit.reshape(1, double),
-      branch_scale.reshape(1, double))
+    )(me, both, *parameters)
     factor = float(rows * size) ** (-0.5)
     if not riding:
         grad_state = lax.all_to_all(
             grad_state.reshape(size, block, width), "seq", split_axis=0, concat_axis=0, tiled=True
         ).reshape(rows, width)
-    mine, other, step, phases, grad_state = sum_over_devices(me, grad_state, keep, send, size, factor, riding)
+    mine, other, step, grad_state = sum_over_devices(me, grad_state, keep, send, size, factor, riding)
     if riding:
         grad_state = call(
             functools.partial(unpack_kernel, block),
@@ -418,16 +447,14 @@
             specs=[SMEM] + [VMEM] * len(grad_state),
         )(me, *grad_state).T
     shapes = [struct((double, units), f32), struct((units, double), f32)]
-    scratch = [pltpu.VMEM((units, double), f32), pltpu.SemaphoreType.DMA((units // step,))]
-    placed = call(
-        functools.partial(place_kernel, phases, step, 0),
-        shapes, scratch=scratch, specs=[SMEM, VMEM], out_specs=[HBM] * 2,
-    )(me, mine)
+    count = 2 * len(mine)
     grad_in, grad_out = call(
-        functools.partial(place_kernel, phases, step, 1),
-        shapes, scratch=scratch, specs=[SMEM, VMEM, HBM, HBM], out_specs=[HBM] * 2,
-        input_output_aliases={2: 0, 3: 1},
-    )(me, other, *placed)
+        functools.partial(place_kernel, 1),
+        shapes,
+        scratch=[pltpu.VMEM((count, step, double), f32), pltpu.SemaphoreType.DMA((count,))],
+        specs=[SMEM] + [VMEM] * count,
+        out_specs=[HBM] * 2,
+    )(me, *mine, *other)
     return (grad_state, grad_in, grad_out)
 
 

time: 68 us -> 63.8 us (0.938)
  Pallas kernels: 15.5 us -> 12.6 us
  waiting for transfers between devices: 30 us -> 28.1 us
  starting transfers between devices: 17.1 us -> 18.9 us
  local copies, waits for them, and re-layouts: 4.23 us -> 3.11 us
    pallas_call x4 -> x3, Pallas kernels: 6.21 us -> 3.94 us  [the longest x1 1.93 us: shards(): call(pack_kernel, struct((size, block, double), bf16), scratch=[pltpu.VME...]
    reshape x3 -> x0, local copies, waits for them, and re-layouts: 2.06 us -> none  [the longest x1 0.69 us: shards(): bias_in.reshape(1, units)]
    ppermute x11 -> x14, starting transfers between devices: 9.76 us -> 11.6 us  [exchange(): lax.ppermute(value if not isinstance(value, list) else value[i], 'seq', [...]
    all_to_all x1, waiting for transfers between devices: 6.26 us -> 5.23 us  [shards(): both = lax.all_to_all(both, 'seq', split_axis=0, concat_axis=0, tiled=True)]
    unnamed x4 -> x10, local copies, waits for them, and re-layouts: 2.13 us -> 3.11 us
    ppermute x11 -> x14, waiting for transfers between devices: 23.7 us -> 22.8 us  [exchange(): lax.ppermute(value if not isinstance(value, list) else value[i], 'seq', [...]
  transfers between devices with their start and end apart: 12 -> 15, of which waited for: 10 -> 10; matrix products, arithmetic and copies ran while one was open for 3% -> 0% of each run, Pallas kernels for 6% -> 2%
where the time goes in v6:
time: 63.8 us; the launch traced here: 63.5 us
  waiting for transfers between devices  28.1 us (44%)
  starting transfers between devices  18.9 us (30%)
  Pallas kernels  12.6 us (20%)
  local copies, waits for them, and re-layouts  3.11 us (5%)
  between operations  0.73 us (1%)
    ppermute x14, waiting for transfers between devices, exchange(): lax.ppermute(value if not isinstance(value, list) else value[i], 'seq', [...  22.8 us
    ppermute x14, starting transfers between devices, exchange(): lax.ppermute(value if not isinstance(value, list) else value[i], 'seq', [...  11.6 us
    pallas_call x1, Pallas kernels, shards(): call(functools.partial(switch_kernel, levels, block), [rider if riding el...  7.52 us
    all_to_all x1, starting transfers between devices, shards(): both = lax.all_to_all(both, 'seq', split_axis=0, concat_axis=0, tiled=True)  7.3 us
    all_to_all x1, waiting for transfers between devices, shards(): both = lax.all_to_all(both, 'seq', split_axis=0, concat_axis=0, tiled=True)  5.23 us
    unnamed x10, local copies, waits for them, and re-layouts  3.11 us
    pallas_call x1, Pallas kernels, shards(): call(pack_kernel, struct((size, block, double), bf16), scratch=[pltpu.VME...  1.93 us
    pallas_call x1, Pallas kernels, shards(): call(functools.partial(place_kernel, 1), shapes, scratch=[pltpu.VMEM((cou...  1.5 us
  transfers between devices with their start and end apart: 15, of which 10 were waited for; matrix products, arithmetic and copies ran while one was open for 0% of the time, Pallas kernels for 2%

profile of v6, /device:TPU:0, one launch (start us, length us, event | category | flops | bytes accessed | tf_op | source)
XLA Modules:
  0.0 63.5 jit_solution(4339233183514366260)
XLA Ops:
  0.6 1.9 %shard_map.94 = bf16[32,8,384]{2,1,0:T(8,128)(2,1)} custom-call(bf16[192,256]{1,0:T(8,128)(2,1)} %bitcast.4, bf16[192,256]{1,0:T(8,128)(2,1)} %bitcast.5), custom_call_target="tpu_custom_call" | custom-call | bytes 7000000 | tf_op jit(solution)/shard_map/pallas_call | solution.py:394
  2.6 7.3 %all-to-all-start = ((bf16[32,8,384]{2,1,0:T(8,128)(2,1)}), bf16[32,8,384]{2,1,0:T(8,128)(2,1)S(1)}, u32[]{:S(2)}, u32[]{:S(2)}) async-start(bf16[32,8,384]{2,1,0:T(8,128)(2,1)} %shard_map.94), calls=%async_computation | async-start | bytes 393216 | tf_op jit(solution)/shard_map/all_to_all | solution.py:404
  9.9 1.1 %copy-done.1 = bf16[768,384]{1,0:T(8,128)(2,1)S(1)} copy-done((bf16[768,384]{1,0:T(8,128)(2,1)S(1)}, bf16[768,384]{1,0:T(8,128)(2,1)}, u32[]{:S(2)}) %copy-start.1) | copy-done | bytes 589848
  11.0 0.7 %copy-done.2 = f32[768]{0:T(1024)S(1)} copy-done((f32[768]{0:T(1024)S(1)}, f32[768]{0:T(1024)}, u32[]{:S(2)}) %copy-start.2) | copy-done | bytes 3096
  12.3 0.7 %copy-done.4 = f32[384]{0:T(512)S(1)} copy-done((f32[384]{0:T(512)S(1)}, f32[384]{0:T(512)}, u32[]{:S(2)}) %copy-start.4) | copy-done | bytes 1560
  13.5 5.2 %all-to-all-done.both_ref = bf16[32,8,384]{2,1,0:T(8,128)(2,1)S(1)} async-done(((bf16[32,8,384]{2,1,0:T(8,128)(2,1)}), bf16[32,8,384]{2,1,0:T(8,128)(2,1)S(1)}, u32[]{:S(2)}, u32[]{:S(2)}) %all-to-all-start) | async-done | bytes 196640 | tf_op jit(solution)/shard_map/all_to_all | solution.py:404
  18.8 7.5 %shard_map.96 = (bf16[64,384]{1,0:T(8,128)(2,1)S(1)}, f32[768,384]{1,0:T(8,128)S(1)}, bf16[832,384]{1,0:T(8,128)(2,1)S(1)}) custom-call(s32[1]{0:T(128)} %bitcast.me_ref, bf16[32,8,384]{2,1,0:T(8,128)(2,1)S(1)} %all-to-all-done.both_ref, bf16[512,768]{1,0:T(8,128)(2,1)S(1)} %get-tuple-element.26.w_in_ref, bf16[768,512]{1,0:T(8,128)(2,1)S(1)} %get-tuple-element.27.w_out_ref, ...), custom_call_target="tpu_custom_call" | custom-call | tf_op jit(solution)/shard_map/pallas_call | solution.py:416
  27.0 1.7 %collective-permute-done.refs_2_ = bf16[832,384]{1,0:T(8,128)(2,1)S(1)} collective-permute-done((bf16[832,384]{1,0:T(8,128)(2,1)S(1)}, bf16[832,384]{1,0:T(8,128)(2,1)S(1)}, u32[]{:S(2)}, u32[]{:S(2)}) %collective-permute-start) | collective-permute-done | bytes 639008 | tf_op jit(solution)/shard_map/ppermute | solution.py:339
  29.5 1.3 %collective-permute-start.2 = (bf16[192,384]{1,0:T(8,128)(2,1)S(1)}, bf16[192,384]{1,0:T(8,128)(2,1)S(1)}, u32[]{:S(2)}, u32[]{:S(2)}) collective-permute-start(bf16[192,384]{1,0:T(8,128)(2,1)S(1)} %get-tuple-element.36), channel_id=1, source_target_pairs={{0,4},{1,5},{2,6},{3,7},{4,0},{5,1},{6,2},{7,3},{8,12},{9,13},{10,... | collective-permute-start | bytes 442376 | tf_op jit(solution)/shard_map/ppermute | solution.py:339
  30.7 1.7 %collective-permute-start.3 = (bf16[192,384]{1,0:T(8,128)(2,1)S(1)}, bf16[192,384]{1,0:T(8,128)(2,1)S(1)}, u32[]{:S(2)}, u32[]{:S(2)}) collective-permute-start(bf16[192,384]{1,0:T(8,128)(2,1)S(1)} %get-tuple-element.37), channel_id=1, source_target_pairs={{0,6},{1,7},{2,4},{3,5},{4,2},{5,3},{6,0},{7,1},{8,14},{9,15},{10,... | collective-permute-start | bytes 442376 | tf_op jit(solution)/shard_map/ppermute | solution.py:339
  32.4 0.8 %collective-permute-start.4 = (bf16[64,384]{1,0:T(8,128)(2,1)S(1)}, bf16[64,384]{1,0:T(8,128)(2,1)S(1)}, u32[]{:S(2)}, u32[]{:S(2)}) collective-permute-start(bf16[64,384]{1,0:T(8,128)(2,1)S(1)} %get-tuple-element.39), channel_id=1, source_target_pairs={{0,16},{1,17},{2,18},{3,19},{4,20},{5,21},{6,22},{7,23},{8,24},{9,... | collective-permute-start | bytes 147464 | tf_op jit(solution)/shard_map/ppermute | solution.py:339
  33.2 4.7 %collective-permute-done.4.refs_5_ = bf16[64,384]{1,0:T(8,128)(2,1)S(1)} collective-permute-done((bf16[64,384]{1,0:T(8,128)(2,1)S(1)}, bf16[64,384]{1,0:T(8,128)(2,1)S(1)}, u32[]{:S(2)}, u32[]{:S(2)}) %collective-permute-start.4) | collective-permute-done | bytes 49184 | tf_op jit(solution)/shard_map/ppermute | solution.py:339
  38.4 0.8 %collective-permute-start.5 = (bf16[256,384]{1,0:T(8,128)(2,1)S(1)}, bf16[256,384]{1,0:T(8,128)(2,1)S(1)}, u32[]{:S(2)}, u32[]{:S(2)}) collective-permute-start(bf16[256,384]{1,0:T(8,128)(2,1)S(1)} %get-tuple-element.40.refs_0_), channel_id=1, source_target_pairs={{0,8},{1,9},{2,10},{3,11},{4,12},{5,13},{6,14},{7,15},{8,0},{9,1},... | collective-permute-start | bytes 589832 | tf_op jit(solution)/shard_map/ppermute | solution.py:339
  39.2 5.2 %collective-permute-done.5.refs_1_.refs_3_ = bf16[256,384]{1,0:T(8,128)(2,1)S(1)} collective-permute-done((bf16[256,384]{1,0:T(8,128)(2,1)S(1)}, bf16[256,384]{1,0:T(8,128)(2,1)S(1)}, u32[]{:S(2)}, u32[]{:S(2)}) %collective-permute-start.5) | collective-permute-done | bytes 196640 | tf_op jit(solution)/shard_map/ppermute | solution.py:339
  44.4 1.7 %collective-permute-start.6 = (bf16[192,384]{1,0:T(8,128)(2,1)S(1)}, bf16[192,384]{1,0:T(8,128)(2,1)S(1)}, u32[]{:S(2)}, u32[]{:S(2)}) collective-permute-start(bf16[192,384]{1,0:T(8,128)(2,1)S(1)} %shard_map.99.refs_0_), channel_id=1, source_target_pairs={{0,24},{1,25},{2,26},{3,27},{4,28},{5,29},{6,30},{7,31},{8,16},{9,... | collective-permute-start | bytes 442376 | tf_op jit(solution)/shard_map/ppermute | solution.py:339
  46.1 5.5 %collective-permute-done.6.refs_1_ = bf16[192,384]{1,0:T(8,128)(2,1)S(1)} collective-permute-done((bf16[192,384]{1,0:T(8,128)(2,1)S(1)}, bf16[192,384]{1,0:T(8,128)(2,1)S(1)}, u32[]{:S(2)}, u32[]{:S(2)}) %collective-permute-start.6) | collective-permute-done | bytes 147488 | tf_op jit(solution)/shard_map/ppermute | solution.py:339
  51.6 1.3 %collective-permute-start.7 = (bf16[224,384]{1,0:T(8,128)(2,1)S(1)}, bf16[224,384]{1,0:T(8,128)(2,1)S(1)}, u32[]{:S(2)}, u32[]{:S(2)}) collective-permute-start(bf16[224,384]{1,0:T(8,128)(2,1)S(1)} %get-tuple-element.43), channel_id=1, source_target_pairs={{0,2},{1,3},{2,0},{3,1},{4,6},{5,7},{6,4},{7,5},{8,10},{9,11},{10,... | collective-permute-start | bytes 516104 | tf_op jit(solution)/shard_map/ppermute | solution.py:339
  52.9 0.9 %collective-permute-start.8 = (bf16[224,384]{1,0:T(8,128)(2,1)S(1)}, bf16[224,384]{1,0:T(8,128)(2,1)S(1)}, u32[]{:S(2)}, u32[]{:S(2)}) collective-permute-start(bf16[224,384]{1,0:T(8,128)(2,1)S(1)} %get-tuple-element.44), channel_id=1, source_target_pairs={{0,4},{1,5},{2,6},{3,7},{4,0},{5,1},{6,2},{7,3},{8,12},{9,13},{10,... | collective-permute-start | bytes 516104 | tf_op jit(solution)/shard_map/ppermute | solution.py:339
  53.9 1.3 %collective-permute-start.9 = (bf16[224,384]{1,0:T(8,128)(2,1)S(1)}, bf16[224,384]{1,0:T(8,128)(2,1)S(1)}, u32[]{:S(2)}, u32[]{:S(2)}) collective-permute-start(bf16[224,384]{1,0:T(8,128)(2,1)S(1)} %get-tuple-element.45), channel_id=1, source_target_pairs={{0,6},{1,7},{2,4},{3,5},{4,2},{5,3},{6,0},{7,1},{8,14},{9,15},{10,... | collective-permute-start | bytes 516104 | tf_op jit(solution)/shard_map/ppermute | solution.py:339
  55.2 1.9 %collective-permute-done.7.refs_1_ = bf16[224,384]{1,0:T(8,128)(2,1)S(1)} collective-permute-done((bf16[224,384]{1,0:T(8,128)(2,1)S(1)}, bf16[224,384]{1,0:T(8,128)(2,1)S(1)}, u32[]{:S(2)}, u32[]{:S(2)}) %collective-permute-start.7) | collective-permute-done | bytes 172064 | tf_op jit(solution)/shard_map/ppermute | solution.py:339
  57.1 1.4 %collective-permute-done.8.refs_2_ = bf16[224,384]{1,0:T(8,128)(2,1)S(1)} collective-permute-done((bf16[224,384]{1,0:T(8,128)(2,1)S(1)}, bf16[224,384]{1,0:T(8,128)(2,1)S(1)}, u32[]{:S(2)}, u32[]{:S(2)}) %collective-permute-start.8) | collective-permute-done | bytes 172064 | tf_op jit(solution)/shard_map/ppermute | solution.py:339
  58.5 1.8 %collective-permute-done.9.refs_3_ = bf16[224,384]{1,0:T(8,128)(2,1)S(1)} collective-permute-done((bf16[224,384]{1,0:T(8,128)(2,1)S(1)}, bf16[224,384]{1,0:T(8,128)(2,1)S(1)}, u32[]{:S(2)}, u32[]{:S(2)}) %collective-permute-start.9) | collective-permute-done | bytes 172064 | tf_op jit(solution)/shard_map/ppermute | solution.py:339
  60.8 0.8 %shard_map.101 = bf16[192,256]{1,0:T(8,128)(2,1)} custom-call(s32[1]{0:T(128)} %bitcast.me_ref, bf16[32,384]{1,0:T(8,128)(2,1)S(1)} %get-tuple-element.42.refs_0_, bf16[224,384]{1,0:T(8,128)(2,1)S(1)} %collective-permute-done.7.refs_1_, bf16[224,384]{1,0:T(8,128)(2,1)S(1)} %collective-permute-done.8.refs_2_, bf16[224,384]{1,0:T(8,128)(2,1)S(1)} %collective-permute-done.9.refs_3_), custom_call_target="tpu_custom_call" | custom-call | tf_op jit(solution)/shard_map/pallas_call | solution.py:443
  62.0 1.5 %shard_map.102 = (f32[384,768]{1,0:T(8,128)}, f32[768,384]{1,0:T(8,128)}) custom-call(s32[1]{0:T(128)} %bitcast.me_ref, bf16[192,384]{1,0:T(8,128)(2,1)S(1)} %get-tuple-element.46.refs_0_, bf16[224,384]{1,0:T(8,128)(2,1)S(1)} %collective-permute-done.7.refs_1_, bf16[224,384]{1,0:T(8,128)(2,1)S(1)} %collective-permute-done.8.refs_2_, ...), custom_call_target="tpu_custom_call" | custom-call | tf_op jit(solution)/shard_map/pallas_call | solution.py:451
  (25 shorter events, 4.1 us)
Async XLA Ops:
  0.6 9.3 %copy-start = (bf16[384,768]{1,0:T(8,128)(2,1)S(1)}, bf16[384,768]{1,0:T(8,128)(2,1)}, u32[]{:S(2)}) copy-start(bf16[384,768]{1,0:T(8,128)(2,1)} %w_in_ref.1) | copy-start | bytes 1769476
  2.6 16.2 %all-to-all-start = ((bf16[32,8,384]{2,1,0:T(8,128)(2,1)}), bf16[32,8,384]{2,1,0:T(8,128)(2,1)S(1)}, u32[]{:S(2)}, u32[]{:S(2)}) async-start(bf16[32,8,384]{2,1,0:T(8,128)(2,1)} %shard_map.94), calls=%async_computation | async-start | bytes 393216 | tf_op jit(solution)/shard_map/all_to_all | solution.py:404
  9.9 1.1 %copy-start.1 = (bf16[768,384]{1,0:T(8,128)(2,1)S(1)}, bf16[768,384]{1,0:T(8,128)(2,1)}, u32[]{:S(2)}) copy-start(bf16[768,384]{1,0:T(8,128)(2,1)} %w_out_ref.1) | copy-start | bytes 1769476
  11.0 0.7 %copy-start.2 = (f32[768]{0:T(1024)S(1)}, f32[768]{0:T(1024)}, u32[]{:S(2)}) copy-start(f32[768]{0:T(1024)} %bias_ref.1) | copy-start | bytes 9220
  11.7 0.7 %copy-start.3 = (f32[384]{0:T(512)S(1)}, f32[384]{0:T(512)}, u32[]{:S(2)}) copy-start(f32[384]{0:T(512)} %logit_ref.1) | copy-start | bytes 4612
  12.3 0.7 %copy-start.4 = (f32[384]{0:T(512)S(1)}, f32[384]{0:T(512)}, u32[]{:S(2)}) copy-start(f32[384]{0:T(512)} %scale_ref.1) | copy-start | bytes 4612
  26.3 2.4 %collective-permute-start = (bf16[832,384]{1,0:T(8,128)(2,1)S(1)}, bf16[832,384]{1,0:T(8,128)(2,1)S(1)}, u32[]{:S(2)}, u32[]{:S(2)}) collective-permute-start(bf16[832,384]{1,0:T(8,128)(2,1)S(1)} %get-tuple-element.33), channel_id=1, source_target_pairs={{0,1},{1,0},{2,3},{3,2},{4,5},{5,4},{6,7},{7,6},{8,9},{9,8},{10,11... | collective-permute-start | bytes 1916936 | tf_op jit(solution)/shard_map/ppermute | solution.py:339
  28.8 9.1 %collective-permute-start.1 = (bf16[192,384]{1,0:T(8,128)(2,1)S(1)}, bf16[192,384]{1,0:T(8,128)(2,1)S(1)}, u32[]{:S(2)}, u32[]{:S(2)}) collective-permute-start(bf16[192,384]{1,0:T(8,128)(2,1)S(1)} %get-tuple-element.35), channel_id=1, source_target_pairs={{0,2},{1,3},{2,0},{3,1},{4,6},{5,7},{6,4},{7,5},{8,10},{9,11},{10,... | collective-permute-start | bytes 442376 | tf_op jit(solution)/shard_map/ppermute | solution.py:339
  29.5 8.9 %collective-permute-start.2 = (bf16[192,384]{1,0:T(8,128)(2,1)S(1)}, bf16[192,384]{1,0:T(8,128)(2,1)S(1)}, u32[]{:S(2)}, u32[]{:S(2)}) collective-permute-start(bf16[192,384]{1,0:T(8,128)(2,1)S(1)} %get-tuple-element.36), channel_id=1, source_target_pairs={{0,4},{1,5},{2,6},{3,7},{4,0},{5,1},{6,2},{7,3},{8,12},{9,13},{10,... | collective-permute-start | bytes 442376 | tf_op jit(solution)/shard_map/ppermute | solution.py:339
  30.7 7.6 %collective-permute-start.3 = (bf16[192,384]{1,0:T(8,128)(2,1)S(1)}, bf16[192,384]{1,0:T(8,128)(2,1)S(1)}, u32[]{:S(2)}, u32[]{:S(2)}) collective-permute-start(bf16[192,384]{1,0:T(8,128)(2,1)S(1)} %get-tuple-element.37), channel_id=1, source_target_pairs={{0,6},{1,7},{2,4},{3,5},{4,2},{5,3},{6,0},{7,1},{8,14},{9,15},{10,... | collective-permute-start | bytes 442376 | tf_op jit(solution)/shard_map/ppermute | solution.py:339
  32.4 5.5 %collective-permute-start.4 = (bf16[64,384]{1,0:T(8,128)(2,1)S(1)}, bf16[64,384]{1,0:T(8,128)(2,1)S(1)}, u32[]{:S(2)}, u32[]{:S(2)}) collective-permute-start(bf16[64,384]{1,0:T(8,128)(2,1)S(1)} %get-tuple-element.39), channel_id=1, source_target_pairs={{0,16},{1,17},{2,18},{3,19},{4,20},{5,21},{6,22},{7,23},{8,24},{9,... | collective-permute-start | bytes 147464 | tf_op jit(solution)/shard_map/ppermute | solution.py:339
  38.4 6.0 %collective-permute-start.5 = (bf16[256,384]{1,0:T(8,128)(2,1)S(1)}, bf16[256,384]{1,0:T(8,128)(2,1)S(1)}, u32[]{:S(2)}, u32[]{:S(2)}) collective-permute-start(bf16[256,384]{1,0:T(8,128)(2,1)S(1)} %get-tuple-element.40.refs_0_), channel_id=1, source_target_pairs={{0,8},{1,9},{2,10},{3,11},{4,12},{5,13},{6,14},{7,15},{8,0},{9,1},... | collective-permute-start | bytes 589832 | tf_op jit(solution)/shard_map/ppermute | solution.py:339
  44.4 7.1 %collective-permute-start.6 = (bf16[192,384]{1,0:T(8,128)(2,1)S(1)}, bf16[192,384]{1,0:T(8,128)(2,1)S(1)}, u32[]{:S(2)}, u32[]{:S(2)}) collective-permute-start(bf16[192,384]{1,0:T(8,128)(2,1)S(1)} %shard_map.99.refs_0_), channel_id=1, source_target_pairs={{0,24},{1,25},{2,26},{3,27},{4,28},{5,29},{6,30},{7,31},{8,16},{9,... | collective-permute-start | bytes 442376 | tf_op jit(solution)/shard_map/ppermute | solution.py:339
  51.6 5.5 %collective-permute-start.7 = (bf16[224,384]{1,0:T(8,128)(2,1)S(1)}, bf16[224,384]{1,0:T(8,128)(2,1)S(1)}, u32[]{:S(2)}, u32[]{:S(2)}) collective-permute-start(bf16[224,384]{1,0:T(8,128)(2,1)S(1)} %get-tuple-element.43), channel_id=1, source_target_pairs={{0,2},{1,3},{2,0},{3,1},{4,6},{5,7},{6,4},{7,5},{8,10},{9,11},{10,... | collective-permute-start | bytes 516104 | tf_op jit(solution)/shard_map/ppermute | solution.py:339
  52.9 5.6 %collective-permute-start.8 = (bf16[224,384]{1,0:T(8,128)(2,1)S(1)}, bf16[224,384]{1,0:T(8,128)(2,1)S(1)}, u32[]{:S(2)}, u32[]{:S(2)}) collective-permute-start(bf16[224,384]{1,0:T(8,128)(2,1)S(1)} %get-tuple-element.44), channel_id=1, source_target_pairs={{0,4},{1,5},{2,6},{3,7},{4,0},{5,1},{6,2},{7,3},{8,12},{9,13},{10,... | collective-permute-start | bytes 516104 | tf_op jit(solution)/shard_map/ppermute | solution.py:339
  53.9 6.5 %collective-permute-start.9 = (bf16[224,384]{1,0:T(8,128)(2,1)S(1)}, bf16[224,384]{1,0:T(8,128)(2,1)S(1)}, u32[]{:S(2)}, u32[]{:S(2)}) collective-permute-start(bf16[224,384]{1,0:T(8,128)(2,1)S(1)} %get-tuple-element.45), channel_id=1, source_target_pairs={{0,6},{1,7},{2,4},{3,5},{4,2},{5,3},{6,0},{7,1},{8,14},{9,15},{10,... | collective-permute-start | bytes 516104 | tf_op jit(solution)/shard_map/ppermute | solution.py:339
  57.1 4.9 %collective-permute-start.11 = (bf16[224,384]{1,0:T(8,128)(2,1)S(1)}, bf16[224,384]{1,0:T(8,128)(2,1)S(1)}, u32[]{:S(2)}, u32[]{:S(2)}) collective-permute-start(bf16[224,384]{1,0:T(8,128)(2,1)S(1)} %collective-permute-done.7.refs_1_), channel_id=1, source_target_pairs={{0,1},{1,0},{2,3},{3,2},{4,5},{5,4},{6,7},{7,6},{8,9},{9,8},{10,11... | collective-permute-start | bytes 516104 | tf_op jit(solution)/shard_map/ppermute | solution.py:339
  58.5 3.5 %collective-permute-start.12 = (bf16[224,384]{1,0:T(8,128)(2,1)S(1)}, bf16[224,384]{1,0:T(8,128)(2,1)S(1)}, u32[]{:S(2)}, u32[]{:S(2)}) collective-permute-start(bf16[224,384]{1,0:T(8,128)(2,1)S(1)} %collective-permute-done.8.refs_2_), channel_id=1, source_target_pairs={{0,1},{1,0},{2,3},{3,2},{4,5},{5,4},{6,7},{7,6},{8,9},{9,8},{10,11... | collective-permute-start | bytes 516104 | tf_op jit(solution)/shard_map/ppermute | solution.py:339
  60.3 1.6 %collective-permute-start.13 = (bf16[224,384]{1,0:T(8,128)(2,1)S(1)}, bf16[224,384]{1,0:T(8,128)(2,1)S(1)}, u32[]{:S(2)}, u32[]{:S(2)}) collective-permute-start(bf16[224,384]{1,0:T(8,128)(2,1)S(1)} %collective-permute-done.9.refs_3_), channel_id=1, source_target_pairs={{0,1},{1,0},{2,3},{3,2},{4,5},{5,4},{6,7},{7,6},{8,9},{9,8},{10,11... | collective-permute-start | bytes 516104 | tf_op jit(solution)/shard_map/ppermute | solution.py:339
  60.3 1.6 %collective-permute-start.10 = (bf16[192,384]{1,0:T(8,128)(2,1)S(1)}, bf16[192,384]{1,0:T(8,128)(2,1)S(1)}, u32[]{:S(2)}, u32[]{:S(2)}) collective-permute-start(bf16[192,384]{1,0:T(8,128)(2,1)S(1)} %get-tuple-element.46.refs_0_), channel_id=1, source_target_pairs={{0,1},{1,0},{2,3},{3,2},{4,5},{5,4},{6,7},{7,6},{8,9},{9,8},{10,11... | collective-permute-start | bytes 442376 | tf_op jit(solution)/shard_map/ppermute | solution.py:339

commit v7 on v6

--- a/solution.py
+++ b/solution.py
@@ -67,11 +67,10 @@
     ]
     for copy in copies:
         copy.start()
-    parts = []
-    for copy, scratch in zip(copies, (x_s, g_s)):
+    for copy in copies:
         copy.wait()
-        parts.append(scratch[...].astype(f32).T)
-    out_ref[...] = jnp.concatenate(parts, axis=1).reshape(out_ref.shape).astype(bf16)
+    both = jnp.concatenate([x_s[...], g_s[...]], axis=0).T
+    out_ref[...] = both.astype(f32).reshape(out_ref.shape).astype(bf16)
 
 
 def fetch_kernel(w_in_ref, w_out_ref, bias_ref, logit_ref, scale_ref, *refs):
@@ -100,8 +99,8 @@
 
 def switch_kernel(
     levels, block, me_ref, both_ref, w_in_ref, w_out_ref, bias_ref, gate_ref, scale_ref,
-    grad_ref, keep_ref, send_ref,
-    low_s, act_s, slope_s, normed_s, inverse_s, pre_s, bg_s, paired_s,
+    grad_ref, send_ref, low_s, pre_s, act_s, bg_s,
+    slope_s, normed_s, inverse_s, paired_s,
 ):
     half, double = paired_s.shape
     rows, width = 2 * half, double // 2
@@ -184,26 +183,27 @@
         send_ref[units:, :] = jnp.concatenate(sent, axis=0).astype(bf16)
     else:
         grad_ref[...] = grad[:, :width].astype(bf16)
-    grad_in = dot(low_s[...], pre_s[...], (0, 0))
-    grad_in = jnp.concatenate([grad_in[side * lanes : side * lanes + width] for side in sides], axis=0)
-    grad_out = dot(act_s[...], bg_s[...], (0, 0))
-
-    def put_in(ref):
+    put_products(core == 0, send_ref, low_s, pre_s, act_s, bg_s)
+
+
+def put_products(out_first, half_ref, low_ref, pre_ref, act_ref, bg_ref):
+    units, double = pre_ref.shape[1], bg_ref.shape[1]
+    width, lanes = double // 2, low_ref.shape[1] // 2
+
+    @pl.when(out_first)
+    def _():
+        half_ref[0:units, :] = dot(act_ref[...], bg_ref[...], (0, 0)).astype(half_ref.dtype)
+
+    @pl.when(jnp.logical_not(out_first))
+    def _():
+        grad_in = dot(low_ref[...], pre_ref[...], (0, 0))
+        grad_in = jnp.concatenate([grad_in[side * lanes : side * lanes + width] for side in range(2)], axis=0)
         for first in range(0, units, double):
-            ref[first : first + double, :] = grad_in[:, first : first + double].astype(ref.dtype)
-
-    def put_out(ref):
-        ref[0:units, :] = grad_out.astype(ref.dtype)
-
-    @pl.when(core == 0)
-    def _():
-        put_in(keep_ref)
-        put_out(send_ref)
-
-    @pl.when(core == 1)
-    def _():
-        put_in(send_ref)
-        put_out(keep_ref)
+            half_ref[first : first + double, :] = grad_in[:, first : first + double].astype(half_ref.dtype)
+
+
+def keep_kernel(me_ref, *refs):
+    put_products(me_ref[0] % 2 == 1, refs[-1], *refs[:-1])
 
 
 def split_kernel(radix, shift, riding, me_ref, *refs):
@@ -378,8 +378,9 @@
         mine = call(functools.partial(total_kernel, factor), piece, count=len(parts))(*parts)
         mine, ride = lax.optimization_barrier((mine, ride))
         got = exchange([mine] * (radix - 1), masks, size)
-    mine = [mine] + got
-    return mine, exchange(mine, [1] * radix, size), rows, ride
+    (first,) = exchange([mine], [1], size)
+    got[0], first = lax.optimization_barrier((got[0], first))
+    return [mine] + got, [first] + exchange(got, [1] * (radix - 1), size), rows, ride
 
 
 def shards(saved_input, cotangent, w_in, bias_in, w_out, residual_logit, branch_scale):
@@ -413,26 +414,34 @@
     total = levels * half
     riding = block % 8 == 0 and levels == 5
     rider = struct((rows // 4, double), bf16)
-    grad_state, keep, send = call(
+    grad_state, send, *factors = call(
         functools.partial(switch_kernel, levels, block),
         [
             rider if riding else struct((rows, width), bf16),
-            struct((units, double), f32),
             struct((units + rider.shape[0] * riding, double), bf16),
+            struct((total, 2 * lanes), bf16),
+            struct((total, units), bf16),
+            struct((total, units), bf16),
+            struct((total, double), bf16),
         ],
         scratch=[
-            pltpu.VMEM((total, 2 * lanes), bf16),
-            pltpu.VMEM((total, units), bf16),
             pltpu.VMEM((total, units), f32),
             pltpu.VMEM((2, total, lanes), f32),
             pltpu.VMEM((total, 1), f32),
-            pltpu.VMEM((total, units), bf16),
-            pltpu.VMEM((total, double), bf16),
             pltpu.VMEM((half, double), f32),
         ],
         specs=[SMEM] + [VMEM] * 6,
         grant=20,
     )(me, both, *parameters)
+    keep = call(
+        keep_kernel,
+        struct((units, double), f32),
+        specs=[SMEM] + [VMEM] * 4,
+        grant=16,
+        cost_estimate=pl.CostEstimate(
+            flops=2 * total * units * double, bytes_accessed=8 * total * units, transcendentals=0
+        ),
+    )(me, *factors)
     factor = float(rows * size) ** (-0.5)
     if not riding:
         grad_state = lax.all_to_all(

time: 63.8 us -> 63.2 us (level)
    pallas_call x0 -> x1, Pallas kernels: none -> 0.82 us  [shards(): call(keep_kernel, struct((units, double), f32), specs=[SMEM] + [VMEM] * 4...]
  transfers between devices with their start and end apart: 15 -> 15, of which waited for: 10 -> 11; matrix products, arithmetic and copies ran while one was open for 0% -> 0% of each run, Pallas kernels for 2% -> 3%
where the time goes in v7:
time: 63.2 us; the launch traced here: 62.9 us
  waiting for transfers between devices  27.5 us (44%)
  starting transfers between devices  18.5 us (29%)
  Pallas kernels  13 us (21%)
  local copies, waits for them, and re-layouts  3.11 us (5%)
  between operations  0.74 us (1%)
    ppermute x14, waiting for transfers between devices, exchange(): lax.ppermute(value if not isinstance(value, list) else value[i], 'seq', [...  22.3 us
    ppermute x14, starting transfers between devices, exchange(): lax.ppermute(value if not isinstance(value, list) else value[i], 'seq', [...  11.2 us
    all_to_all x1, starting transfers between devices, shards(): both = lax.all_to_all(both, 'seq', split_axis=0, concat_axis=0, tiled=True)  7.3 us
    pallas_call x1, Pallas kernels, shards(): call(functools.partial(switch_kernel, levels, block), [rider if riding el...  7.23 us
    all_to_all x1, waiting for transfers between devices, shards(): both = lax.all_to_all(both, 'seq', split_axis=0, concat_axis=0, tiled=True)  5.23 us
    unnamed x10, local copies, waits for them, and re-layouts  3.11 us
    pallas_call x1, Pallas kernels, shards(): call(pack_kernel, struct((size, block, double), bf16), scratch=[pltpu.VME...  1.8 us
    pallas_call x1, Pallas kernels, shards(): call(functools.partial(place_kernel, 1), shapes, scratch=[pltpu.VMEM((cou...  1.48 us
  transfers between devices with their start and end apart: 15, of which 11 were waited for; matrix products, arithmetic and copies ran while one was open for 0% of the time, Pallas kernels for 3%

profile of v7, /device:TPU:0, one launch (start us, length us, event | category | flops | bytes accessed | tf_op | source)
XLA Modules:
  0.0 62.9 jit_solution(4866868770157487041)
XLA Ops:
  0.6 1.8 %shard_map.94 = bf16[32,8,384]{2,1,0:T(8,128)(2,1)} custom-call(bf16[192,256]{1,0:T(8,128)(2,1)} %bitcast.4, bf16[192,256]{1,0:T(8,128)(2,1)} %bitcast.5), custom_call_target="tpu_custom_call" | custom-call | bytes 7000000 | tf_op jit(solution)/shard_map/pallas_call | solution.py:395
  2.4 7.3 %all-to-all-start = ((bf16[32,8,384]{2,1,0:T(8,128)(2,1)}), bf16[32,8,384]{2,1,0:T(8,128)(2,1)S(1)}, u32[]{:S(2)}, u32[]{:S(2)}) async-start(bf16[32,8,384]{2,1,0:T(8,128)(2,1)} %shard_map.94), calls=%async_computation | async-start | bytes 393216 | tf_op jit(solution)/shard_map/all_to_all | solution.py:405
  9.8 1.1 %copy-done.1 = bf16[768,384]{1,0:T(8,128)(2,1)S(1)} copy-done((bf16[768,384]{1,0:T(8,128)(2,1)S(1)}, bf16[768,384]{1,0:T(8,128)(2,1)}, u32[]{:S(2)}) %copy-start.1) | copy-done | bytes 589848
  13.4 5.2 %all-to-all-done.both_ref = bf16[32,8,384]{2,1,0:T(8,128)(2,1)S(1)} async-done(((bf16[32,8,384]{2,1,0:T(8,128)(2,1)}), bf16[32,8,384]{2,1,0:T(8,128)(2,1)S(1)}, u32[]{:S(2)}, u32[]{:S(2)}) %all-to-all-start) | async-done | bytes 196640 | tf_op jit(solution)/shard_map/all_to_all | solution.py:405
  18.6 7.2 %shard_map.96 = (bf16[64,384]{1,0:T(8,128)(2,1)S(1)}, bf16[832,384]{1,0:T(8,128)(2,1)S(1)}, bf16[640,512]{1,0:T(8,128)(2,1)S(1)}, bf16[640,768]{1,0:T(8,128)(2,1...) custom-call(s32[1]{0:T(128)} %bitcast.me_ref, bf16[32,8,384]{2,1,0:T(8,128)(2,1)S(1)} %all-to-all-done.both_ref, ...), custom_call_target="tpu_custom_call" | custom-call | tf_op jit(solution)/shard_map/pallas_call | solution.py:417
  25.9 0.7 %collective-permute-start = (bf16[832,384]{1,0:T(8,128)(2,1)S(1)}, bf16[832,384]{1,0:T(8,128)(2,1)S(1)}, u32[]{:S(2)}, u32[]{:S(2)}) collective-permute-start(bf16[832,384]{1,0:T(8,128)(2,1)S(1)} %get-tuple-element.41), channel_id=1, source_target_pairs={{0,1},{1,0},{2,3},{3,2},{4,5},{5,4},{6,7},{7,6},{8,9},{9,8},{10,11... | collective-permute-start | bytes 1916936 | tf_op jit(solution)/shard_map/ppermute | solution.py:339
  26.6 0.8 %shard_map.97.refs_1_ = f32[768,384]{1,0:T(8,128)S(1)} custom-call(s32[1]{0:T(128)} %bitcast.me_ref, bf16[640,512]{1,0:T(8,128)(2,1)S(1)} %get-tuple-element.37.refs_0_, bf16[640,768]{1,0:T(8,128)(2,1)S(1)} %get-tuple-element.38.refs_1_, bf16[640,768]{1,0:T(8,128)(2,1)S(1)} %get-tuple-element.39.refs_2_, bf16[640,384]{1,0:T(8,128)(2,1)S(1)} %get-tuple-element.40.refs_3_), custom_call_target="tpu_custom_call" | custom-call | flops 377487360 | bytes 3932160 | tf_op jit(solution)/shard_map/pallas_call | solution.py:436
  27.4 0.9 %collective-permute-done.refs_2_ = bf16[832,384]{1,0:T(8,128)(2,1)S(1)} collective-permute-done((bf16[832,384]{1,0:T(8,128)(2,1)S(1)}, bf16[832,384]{1,0:T(8,128)(2,1)S(1)}, u32[]{:S(2)}, u32[]{:S(2)}) %collective-permute-start) | collective-permute-done | bytes 639008 | tf_op jit(solution)/shard_map/ppermute | solution.py:339
  29.1 1.3 %collective-permute-start.2 = (bf16[192,384]{1,0:T(8,128)(2,1)S(1)}, bf16[192,384]{1,0:T(8,128)(2,1)S(1)}, u32[]{:S(2)}, u32[]{:S(2)}) collective-permute-start(bf16[192,384]{1,0:T(8,128)(2,1)S(1)} %get-tuple-element.44), channel_id=1, source_target_pairs={{0,4},{1,5},{2,6},{3,7},{4,0},{5,1},{6,2},{7,3},{8,12},{9,13},{10,... | collective-permute-start | bytes 442376 | tf_op jit(solution)/shard_map/ppermute | solution.py:339
  30.3 1.7 %collective-permute-start.3 = (bf16[192,384]{1,0:T(8,128)(2,1)S(1)}, bf16[192,384]{1,0:T(8,128)(2,1)S(1)}, u32[]{:S(2)}, u32[]{:S(2)}) collective-permute-start(bf16[192,384]{1,0:T(8,128)(2,1)S(1)} %get-tuple-element.45), channel_id=1, source_target_pairs={{0,6},{1,7},{2,4},{3,5},{4,2},{5,3},{6,0},{7,1},{8,14},{9,15},{10,... | collective-permute-start | bytes 442376 | tf_op jit(solution)/shard_map/ppermute | solution.py:339
  32.0 0.8 %collective-permute-start.4 = (bf16[64,384]{1,0:T(8,128)(2,1)S(1)}, bf16[64,384]{1,0:T(8,128)(2,1)S(1)}, u32[]{:S(2)}, u32[]{:S(2)}) collective-permute-start(bf16[64,384]{1,0:T(8,128)(2,1)S(1)} %get-tuple-element.47), channel_id=1, source_target_pairs={{0,16},{1,17},{2,18},{3,19},{4,20},{5,21},{6,22},{7,23},{8,24},{9,... | collective-permute-start | bytes 147464 | tf_op jit(solution)/shard_map/ppermute | solution.py:339
  32.8 4.7 %collective-permute-done.4.refs_5_ = bf16[64,384]{1,0:T(8,128)(2,1)S(1)} collective-permute-done((bf16[64,384]{1,0:T(8,128)(2,1)S(1)}, bf16[64,384]{1,0:T(8,128)(2,1)S(1)}, u32[]{:S(2)}, u32[]{:S(2)}) %collective-permute-start.4) | collective-permute-done | bytes 49184 | tf_op jit(solution)/shard_map/ppermute | solution.py:339
  38.1 0.8 %collective-permute-start.5 = (bf16[256,384]{1,0:T(8,128)(2,1)S(1)}, bf16[256,384]{1,0:T(8,128)(2,1)S(1)}, u32[]{:S(2)}, u32[]{:S(2)}) collective-permute-start(bf16[256,384]{1,0:T(8,128)(2,1)S(1)} %get-tuple-element.48.refs_0_), channel_id=1, source_target_pairs={{0,8},{1,9},{2,10},{3,11},{4,12},{5,13},{6,14},{7,15},{8,0},{9,1},... | collective-permute-start | bytes 589832 | tf_op jit(solution)/shard_map/ppermute | solution.py:339
  38.9 5.1 %collective-permute-done.5.refs_1_.refs_3_ = bf16[256,384]{1,0:T(8,128)(2,1)S(1)} collective-permute-done((bf16[256,384]{1,0:T(8,128)(2,1)S(1)}, bf16[256,384]{1,0:T(8,128)(2,1)S(1)}, u32[]{:S(2)}, u32[]{:S(2)}) %collective-permute-start.5) | collective-permute-done | bytes 196640 | tf_op jit(solution)/shard_map/ppermute | solution.py:339
  44.0 1.7 %collective-permute-start.6 = (bf16[192,384]{1,0:T(8,128)(2,1)S(1)}, bf16[192,384]{1,0:T(8,128)(2,1)S(1)}, u32[]{:S(2)}, u32[]{:S(2)}) collective-permute-start(bf16[192,384]{1,0:T(8,128)(2,1)S(1)} %shard_map.100.refs_0_), channel_id=1, source_target_pairs={{0,24},{1,25},{2,26},{3,27},{4,28},{5,29},{6,30},{7,31},{8,16},{9,... | collective-permute-start | bytes 442376 | tf_op jit(solution)/shard_map/ppermute | solution.py:339
  45.7 5.4 %collective-permute-done.6.refs_1_ = bf16[192,384]{1,0:T(8,128)(2,1)S(1)} collective-permute-done((bf16[192,384]{1,0:T(8,128)(2,1)S(1)}, bf16[192,384]{1,0:T(8,128)(2,1)S(1)}, u32[]{:S(2)}, u32[]{:S(2)}) %collective-permute-start.6) | collective-permute-done | bytes 147488 | tf_op jit(solution)/shard_map/ppermute | solution.py:339
  51.2 1.4 %collective-permute-start.7 = (bf16[224,384]{1,0:T(8,128)(2,1)S(1)}, bf16[224,384]{1,0:T(8,128)(2,1)S(1)}, u32[]{:S(2)}, u32[]{:S(2)}) collective-permute-start(bf16[224,384]{1,0:T(8,128)(2,1)S(1)} %get-tuple-element.51), channel_id=1, source_target_pairs={{0,2},{1,3},{2,0},{3,1},{4,6},{5,7},{6,4},{7,5},{8,10},{9,11},{10,... | collective-permute-start | bytes 516104 | tf_op jit(solution)/shard_map/ppermute | solution.py:339
  52.6 1.0 %collective-permute-start.8 = (bf16[224,384]{1,0:T(8,128)(2,1)S(1)}, bf16[224,384]{1,0:T(8,128)(2,1)S(1)}, u32[]{:S(2)}, u32[]{:S(2)}) collective-permute-start(bf16[224,384]{1,0:T(8,128)(2,1)S(1)} %get-tuple-element.52), channel_id=1, source_target_pairs={{0,4},{1,5},{2,6},{3,7},{4,0},{5,1},{6,2},{7,3},{8,12},{9,13},{10,... | collective-permute-start | bytes 516104 | tf_op jit(solution)/shard_map/ppermute | solution.py:339
  53.5 1.2 %collective-permute-start.9 = (bf16[224,384]{1,0:T(8,128)(2,1)S(1)}, bf16[224,384]{1,0:T(8,128)(2,1)S(1)}, u32[]{:S(2)}, u32[]{:S(2)}) collective-permute-start(bf16[224,384]{1,0:T(8,128)(2,1)S(1)} %get-tuple-element.53), channel_id=1, source_target_pairs={{0,6},{1,7},{2,4},{3,5},{4,2},{5,3},{6,0},{7,1},{8,14},{9,15},{10,... | collective-permute-start | bytes 516104 | tf_op jit(solution)/shard_map/ppermute | solution.py:339
  54.8 1.4 %collective-permute-done.10.refs_4_ = bf16[192,384]{1,0:T(8,128)(2,1)S(1)} collective-permute-done((bf16[192,384]{1,0:T(8,128)(2,1)S(1)}, bf16[192,384]{1,0:T(8,128)(2,1)S(1)}, u32[]{:S(2)}, u32[]{:S(2)}) %collective-permute-start.10) | collective-permute-done | bytes 147488 | tf_op jit(solution)/shard_map/ppermute | solution.py:339
  56.7 1.4 %collective-permute-done.8.refs_2_ = bf16[224,384]{1,0:T(8,128)(2,1)S(1)} collective-permute-done((bf16[224,384]{1,0:T(8,128)(2,1)S(1)}, bf16[224,384]{1,0:T(8,128)(2,1)S(1)}, u32[]{:S(2)}, u32[]{:S(2)}) %collective-permute-start.8) | collective-permute-done | bytes 172064 | tf_op jit(solution)/shard_map/ppermute | solution.py:339
  58.1 1.8 %collective-permute-done.9.refs_3_ = bf16[224,384]{1,0:T(8,128)(2,1)S(1)} collective-permute-done((bf16[224,384]{1,0:T(8,128)(2,1)S(1)}, bf16[224,384]{1,0:T(8,128)(2,1)S(1)}, u32[]{:S(2)}, u32[]{:S(2)}) %collective-permute-start.9) | collective-permute-done | bytes 172064 | tf_op jit(solution)/shard_map/ppermute | solution.py:339
  60.0 0.8 %shard_map.102 = bf16[192,256]{1,0:T(8,128)(2,1)} custom-call(s32[1]{0:T(128)} %bitcast.me_ref, bf16[32,384]{1,0:T(8,128)(2,1)S(1)} %get-tuple-element.50.refs_0_, bf16[224,384]{1,0:T(8,128)(2,1)S(1)} %collective-permute-done.7.refs_1_, bf16[224,384]{1,0:T(8,128)(2,1)S(1)} %collective-permute-done.8.refs_2_, bf16[224,384]{1,0:T(8,128)(2,1)S(1)} %collective-permute-done.9.refs_3_), custom_call_target="tpu_custom_call" | custom-call | tf_op jit(solution)/shard_map/pallas_call | solution.py:452
  61.4 1.5 %shard_map.103 = (f32[384,768]{1,0:T(8,128)}, f32[768,384]{1,0:T(8,128)}) custom-call(s32[1]{0:T(128)} %bitcast.me_ref, bf16[192,384]{1,0:T(8,128)(2,1)S(1)} %get-tuple-element.54.refs_0_, bf16[224,384]{1,0:T(8,128)(2,1)S(1)} %collective-permute-done.7.refs_1_, bf16[224,384]{1,0:T(8,128)(2,1)S(1)} %collective-permute-done.8.refs_2_, ...), custom_call_target="tpu_custom_call" | custom-call | tf_op jit(solution)/shard_map/pallas_call | solution.py:460
  (26 shorter events, 5.1 us)
Async XLA Ops:
  0.6 9.1 %copy-start = (bf16[384,768]{1,0:T(8,128)(2,1)S(1)}, bf16[384,768]{1,0:T(8,128)(2,1)}, u32[]{:S(2)}) copy-start(bf16[384,768]{1,0:T(8,128)(2,1)} %w_in_ref.1) | copy-start | bytes 1769476
  2.4 16.2 %all-to-all-start = ((bf16[32,8,384]{2,1,0:T(8,128)(2,1)}), bf16[32,8,384]{2,1,0:T(8,128)(2,1)S(1)}, u32[]{:S(2)}, u32[]{:S(2)}) async-start(bf16[32,8,384]{2,1,0:T(8,128)(2,1)} %shard_map.94), calls=%async_computation | async-start | bytes 393216 | tf_op jit(solution)/shard_map/all_to_all | solution.py:405
  9.8 1.1 %copy-start.1 = (bf16[768,384]{1,0:T(8,128)(2,1)S(1)}, bf16[768,384]{1,0:T(8,128)(2,1)}, u32[]{:S(2)}) copy-start(bf16[768,384]{1,0:T(8,128)(2,1)} %w_out_ref.1) | copy-start | bytes 1769476
  10.8 0.7 %copy-start.2 = (f32[768]{0:T(1024)S(1)}, f32[768]{0:T(1024)}, u32[]{:S(2)}) copy-start(f32[768]{0:T(1024)} %bias_ref.1) | copy-start | bytes 9220
  11.5 0.7 %copy-start.3 = (f32[384]{0:T(512)S(1)}, f32[384]{0:T(512)}, u32[]{:S(2)}) copy-start(f32[384]{0:T(512)} %logit_ref.1) | copy-start | bytes 4612
  12.2 0.7 %copy-start.4 = (f32[384]{0:T(512)S(1)}, f32[384]{0:T(512)}, u32[]{:S(2)}) copy-start(f32[384]{0:T(512)} %scale_ref.1) | copy-start | bytes 4612
  25.9 2.4 %collective-permute-start = (bf16[832,384]{1,0:T(8,128)(2,1)S(1)}, bf16[832,384]{1,0:T(8,128)(2,1)S(1)}, u32[]{:S(2)}, u32[]{:S(2)}) collective-permute-start(bf16[832,384]{1,0:T(8,128)(2,1)S(1)} %get-tuple-element.41), channel_id=1, source_target_pairs={{0,1},{1,0},{2,3},{3,2},{4,5},{5,4},{6,7},{7,6},{8,9},{9,8},{10,11... | collective-permute-start | bytes 1916936 | tf_op jit(solution)/shard_map/ppermute | solution.py:339
  28.5 9.1 %collective-permute-start.1 = (bf16[192,384]{1,0:T(8,128)(2,1)S(1)}, bf16[192,384]{1,0:T(8,128)(2,1)S(1)}, u32[]{:S(2)}, u32[]{:S(2)}) collective-permute-start(bf16[192,384]{1,0:T(8,128)(2,1)S(1)} %get-tuple-element.43), channel_id=1, source_target_pairs={{0,2},{1,3},{2,0},{3,1},{4,6},{5,7},{6,4},{7,5},{8,10},{9,11},{10,... | collective-permute-start | bytes 442376 | tf_op jit(solution)/shard_map/ppermute | solution.py:339
  29.1 8.9 %collective-permute-start.2 = (bf16[192,384]{1,0:T(8,128)(2,1)S(1)}, bf16[192,384]{1,0:T(8,128)(2,1)S(1)}, u32[]{:S(2)}, u32[]{:S(2)}) collective-permute-start(bf16[192,384]{1,0:T(8,128)(2,1)S(1)} %get-tuple-element.44), channel_id=1, source_target_pairs={{0,4},{1,5},{2,6},{3,7},{4,0},{5,1},{6,2},{7,3},{8,12},{9,13},{10,... | collective-permute-start | bytes 442376 | tf_op jit(solution)/shard_map/ppermute | solution.py:339
  30.3 7.7 %collective-permute-start.3 = (bf16[192,384]{1,0:T(8,128)(2,1)S(1)}, bf16[192,384]{1,0:T(8,128)(2,1)S(1)}, u32[]{:S(2)}, u32[]{:S(2)}) collective-permute-start(bf16[192,384]{1,0:T(8,128)(2,1)S(1)} %get-tuple-element.45), channel_id=1, source_target_pairs={{0,6},{1,7},{2,4},{3,5},{4,2},{5,3},{6,0},{7,1},{8,14},{9,15},{10,... | collective-permute-start | bytes 442376 | tf_op jit(solution)/shard_map/ppermute | solution.py:339
  32.0 5.5 %collective-permute-start.4 = (bf16[64,384]{1,0:T(8,128)(2,1)S(1)}, bf16[64,384]{1,0:T(8,128)(2,1)S(1)}, u32[]{:S(2)}, u32[]{:S(2)}) collective-permute-start(bf16[64,384]{1,0:T(8,128)(2,1)S(1)} %get-tuple-element.47), channel_id=1, source_target_pairs={{0,16},{1,17},{2,18},{3,19},{4,20},{5,21},{6,22},{7,23},{8,24},{9,... | collective-permute-start | bytes 147464 | tf_op jit(solution)/shard_map/ppermute | solution.py:339
  38.1 5.9 %collective-permute-start.5 = (bf16[256,384]{1,0:T(8,128)(2,1)S(1)}, bf16[256,384]{1,0:T(8,128)(2,1)S(1)}, u32[]{:S(2)}, u32[]{:S(2)}) collective-permute-start(bf16[256,384]{1,0:T(8,128)(2,1)S(1)} %get-tuple-element.48.refs_0_), channel_id=1, source_target_pairs={{0,8},{1,9},{2,10},{3,11},{4,12},{5,13},{6,14},{7,15},{8,0},{9,1},... | collective-permute-start | bytes 589832 | tf_op jit(solution)/shard_map/ppermute | solution.py:339
  44.0 7.1 %collective-permute-start.6 = (bf16[192,384]{1,0:T(8,128)(2,1)S(1)}, bf16[192,384]{1,0:T(8,128)(2,1)S(1)}, u32[]{:S(2)}, u32[]{:S(2)}) collective-permute-start(bf16[192,384]{1,0:T(8,128)(2,1)S(1)} %shard_map.100.refs_0_), channel_id=1, source_target_pairs={{0,24},{1,25},{2,26},{3,27},{4,28},{5,29},{6,30},{7,31},{8,16},{9,... | collective-permute-start | bytes 442376 | tf_op jit(solution)/shard_map/ppermute | solution.py:339
  51.2 5.5 %collective-permute-start.7 = (bf16[224,384]{1,0:T(8,128)(2,1)S(1)}, bf16[224,384]{1,0:T(8,128)(2,1)S(1)}, u32[]{:S(2)}, u32[]{:S(2)}) collective-permute-start(bf16[224,384]{1,0:T(8,128)(2,1)S(1)} %get-tuple-element.51), channel_id=1, source_target_pairs={{0,2},{1,3},{2,0},{3,1},{4,6},{5,7},{6,4},{7,5},{8,10},{9,11},{10,... | collective-permute-start | bytes 516104 | tf_op jit(solution)/shard_map/ppermute | solution.py:339
  52.6 5.6 %collective-permute-start.8 = (bf16[224,384]{1,0:T(8,128)(2,1)S(1)}, bf16[224,384]{1,0:T(8,128)(2,1)S(1)}, u32[]{:S(2)}, u32[]{:S(2)}) collective-permute-start(bf16[224,384]{1,0:T(8,128)(2,1)S(1)} %get-tuple-element.52), channel_id=1, source_target_pairs={{0,4},{1,5},{2,6},{3,7},{4,0},{5,1},{6,2},{7,3},{8,12},{9,13},{10,... | collective-permute-start | bytes 516104 | tf_op jit(solution)/shard_map/ppermute | solution.py:339
  53.5 6.5 %collective-permute-start.9 = (bf16[224,384]{1,0:T(8,128)(2,1)S(1)}, bf16[224,384]{1,0:T(8,128)(2,1)S(1)}, u32[]{:S(2)}, u32[]{:S(2)}) collective-permute-start(bf16[224,384]{1,0:T(8,128)(2,1)S(1)} %get-tuple-element.53), channel_id=1, source_target_pairs={{0,6},{1,7},{2,4},{3,5},{4,2},{5,3},{6,0},{7,1},{8,14},{9,15},{10,... | collective-permute-start | bytes 516104 | tf_op jit(solution)/shard_map/ppermute | solution.py:339
  54.8 1.4 %collective-permute-start.10 = (bf16[192,384]{1,0:T(8,128)(2,1)S(1)}, bf16[192,384]{1,0:T(8,128)(2,1)S(1)}, u32[]{:S(2)}, u32[]{:S(2)}) collective-permute-start(bf16[192,384]{1,0:T(8,128)(2,1)S(1)} %get-tuple-element.54.refs_0_), channel_id=1, source_target_pairs={{0,1},{1,0},{2,3},{3,2},{4,5},{5,4},{6,7},{7,6},{8,9},{9,8},{10,11... | collective-permute-start | bytes 442376 | tf_op jit(solution)/shard_map/ppermute | solution.py:339
  56.7 4.1 %collective-permute-start.11 = (bf16[224,384]{1,0:T(8,128)(2,1)S(1)}, bf16[224,384]{1,0:T(8,128)(2,1)S(1)}, u32[]{:S(2)}, u32[]{:S(2)}) collective-permute-start(bf16[224,384]{1,0:T(8,128)(2,1)S(1)} %collective-permute-done.7.refs_1_), channel_id=1, source_target_pairs={{0,1},{1,0},{2,3},{3,2},{4,5},{5,4},{6,7},{7,6},{8,9},{9,8},{10,11... | collective-permute-start | bytes 516104 | tf_op jit(solution)/shard_map/ppermute | solution.py:339
  58.1 2.7 %collective-permute-start.12 = (bf16[224,384]{1,0:T(8,128)(2,1)S(1)}, bf16[224,384]{1,0:T(8,128)(2,1)S(1)}, u32[]{:S(2)}, u32[]{:S(2)}) collective-permute-start(bf16[224,384]{1,0:T(8,128)(2,1)S(1)} %collective-permute-done.8.refs_2_), channel_id=1, source_target_pairs={{0,1},{1,0},{2,3},{3,2},{4,5},{5,4},{6,7},{7,6},{8,9},{9,8},{10,11... | collective-permute-start | bytes 516104 | tf_op jit(solution)/shard_map/ppermute | solution.py:339
  60.0 1.4 %collective-permute-start.13 = (bf16[224,384]{1,0:T(8,128)(2,1)S(1)}, bf16[224,384]{1,0:T(8,128)(2,1)S(1)}, u32[]{:S(2)}, u32[]{:S(2)}) collective-permute-start(bf16[224,384]{1,0:T(8,128)(2,1)S(1)} %collective-permute-done.9.refs_3_), channel_id=1, source_target_pairs={{0,1},{1,0},{2,3},{3,2},{4,5},{5,4},{6,7},{7,6},{8,9},{9,8},{10,11... | collective-permute-start | bytes 516104 | tf_op jit(solution)/shard_map/ppermute | solution.py:339

commit v8 on v7

--- a/solution.py
+++ b/solution.py
@@ -74,7 +74,7 @@
 
 
 def fetch_kernel(w_in_ref, w_out_ref, bias_ref, logit_ref, scale_ref, *refs):
-    w_in_o, w_out_o, bias_o, gate_o, scale_o, w_in_s, w_out_s, sem = refs
+    w_in_o, w_out_o, w_in_turned_o, w_out_turned_o, bias_o, gate_o, scale_o, w_in_s, w_out_s, sem = refs
     copies = [
         pltpu.make_async_copy(ref, to, sem.at[i])
         for i, (ref, to) in enumerate(((w_in_ref, w_in_s), (w_out_ref, w_out_s)))
@@ -95,10 +95,12 @@
         w_in_o[at : at + width, :] = w_in_s[first : first + width, :]
         if lanes > width:
             w_in_o[at + width : at + lanes, :] = jnp.zeros((lanes - width, w_in_o.shape[1]), bf16)
+    w_in_turned_o[...] = w_in_o[...].astype(f32).T.astype(bf16)
+    w_out_turned_o[...] = w_out_o[...].astype(f32).T.astype(bf16)
 
 
 def switch_kernel(
-    levels, block, me_ref, both_ref, w_in_ref, w_out_ref, bias_ref, gate_ref, scale_ref,
+    levels, block, me_ref, both_ref, w_in_ref, w_out_ref, w_in_turned_ref, w_out_turned_ref, bias_ref, gate_ref, scale_ref,
     grad_ref, send_ref, low_s, pre_s, act_s, bg_s,
     slope_s, normed_s, inverse_s, paired_s,
 ):
@@ -149,10 +151,10 @@
         upstream = pair_rows(grad, block * 2**level)
         branch_grad = [(scale[side] * upstream[side]).astype(bf16) for side in sides]
         bg_s[at, :] = jnp.concatenate([part[:, :width] for part in branch_grad], axis=1)
-        act_grad = dot(jnp.concatenate(branch_grad, axis=1), w_out_ref[...], (1, 1))
+        act_grad = dot(jnp.concatenate(branch_grad, axis=1), w_out_turned_ref[...], (1, 0))
         pre_grad = (act_grad * slope_s[at, :]).astype(bf16)
         pre_s[at, :] = pre_grad
-        normed_grad = dot(pre_grad, w_in_ref[...], (1, 1))
+        normed_grad = dot(pre_grad, w_in_turned_ref[...], (1, 0))
         normed_grad = [normed_grad[:, side * lanes : (side + 1) * lanes] for side in sides]
         normed = [normed_s[side, at, :] for side in sides]
         average = mean_of(normed_grad, double)
@@ -285,38 +287,44 @@
     out_ref[...] = rows_s[...].T.astype(bf16)
 
 
-def place_kernel(bit, me_ref, *refs):
-    in_ref, out_ref, wide_s, sem = refs[-4:]
-    count, step, double = wide_s.shape
+def place_kernel(bit, pieces, slots, placed, me_ref, *refs):
+    parts, (in_ref, out_ref, wide_s, sem) = refs[: len(slots)], refs[len(slots) + placed :]
+    step, double = wide_s.shape[1:]
     me = me_ref[0]
-    pieces = count // 2
     base = (me >> bit) & (pieces - 1)
-
-    def write(parts):
-        copies = []
-        for i, part in enumerate(parts):
-            first = ((i % pieces) ^ base) * step
-            if i < pieces:
-                lane = (first // double) * double
-                to = in_ref.at[
-                    pl.ds(pl.multiple_of(first - lane, tile), step), pl.ds(pl.multiple_of(lane, 128), double)
-                ]
-            else:
-                to = out_ref.at[pl.ds(pl.multiple_of(first, tile), step), :]
-            wide_s[i] = part[0:step, :].astype(f32)
-            copy = pltpu.make_async_copy(wide_s.at[i], to, sem.at[i])
-            copy.start()
-            copies.append(copy)
-        for copy in copies:
-            copy.wait()
-
-    @pl.when(me % 2 == 0)
-    def _():
-        write(refs[:count])
-
-    @pl.when(me % 2 == 1)
-    def _():
-        write(refs[pieces:count] + refs[:pieces])
+    for core in range(2):
+
+        @pl.when(me % 2 == core)
+        def _():
+            copies = []
+            for i, slot in enumerate(slots):
+                first = ((slot % pieces) ^ base) * step
+                if (slot >= pieces) == (core == 1):
+                    lane = (first // double) * double
+                    to = in_ref.at[
+                        pl.ds(pl.multiple_of(first - lane, tile), step), pl.ds(pl.multiple_of(lane, 128), double)
+                    ]
+                else:
+                    to = out_ref.at[pl.ds(pl.multiple_of(first, tile), step), :]
+                wide_s[i] = parts[i][0:step, :].astype(f32)
+                copy = pltpu.make_async_copy(wide_s.at[i], to, sem.at[i])
+                copy.start()
+                copies.append(copy)
+            for copy in copies:
+                copy.wait()
+
+
+def place(me, shapes, quarters, slots, placed):
+    pieces = len(quarters) // 2
+    step, double = min(quarter.shape for quarter in quarters if quarter is not None)
+    return call(
+        functools.partial(place_kernel, 1, pieces, slots, len(placed)),
+        shapes,
+        scratch=[pltpu.VMEM((len(slots), step, double), f32), pltpu.SemaphoreType.DMA((len(slots),))],
+        specs=[SMEM] + [VMEM] * len(slots) + [HBM] * len(placed),
+        out_specs=[HBM] * 2,
+        input_output_aliases={1 + len(slots) + i: i for i in range(len(placed))},
+    )(me, *[quarters[slot] for slot in slots], *placed)
 
 
 def call(kernel, outs, scratch=(), specs=None, count=0, grant=8, **more):
@@ -340,7 +348,7 @@
                          [(d, d ^ mask) for d in range(size)]) for i, mask in enumerate(masks)]
 
 
-def sum_over_devices(me, ride, keep, send, size, factor, riding):
+def sum_over_devices(me, ride, keep, send, size, factor, riding, shapes):
     bits = size.bit_length() - 1
     rows, double = keep.shape
     radix = min(4, size // 2)
@@ -380,7 +388,14 @@
         got = exchange([mine] * (radix - 1), masks, size)
     (first,) = exchange([mine], [1], size)
     got[0], first = lax.optimization_barrier((got[0], first))
-    return [mine] + got, [first] + exchange(got, [1] * (radix - 1), size), rows, ride
+    quarters = [mine] + got + [first] + [None] * (radix - 1)
+    early = [slot for slot in (0, radix, 1) if riding]
+    placed = place(me, shapes, quarters, early, []) if early else []
+    if early:
+        *got[1:], placed = lax.optimization_barrier((*got[1:], placed))
+    quarters = [mine] + got + [first] + exchange(got, [1] * (radix - 1), size)
+    placed = place(me, shapes, quarters, [slot for slot in range(2 * radix) if slot not in early], placed)
+    return placed, ride
 
 
 def shards(saved_input, cotangent, w_in, bias_in, w_out, residual_logit, branch_scale):
@@ -406,7 +421,7 @@
     lanes = -(-width // 128) * 128
     parameters = call(
         fetch_kernel,
-        [struct((2 * lanes, units), bf16), struct((units, 2 * lanes), bf16)]
+        [struct(shape, bf16) for shape in ((2 * lanes, units), (units, 2 * lanes)) + ((units, 2 * lanes), (2 * lanes, units))]
         + [struct((1, count), f32) for count in (units, 2 * lanes, 2 * lanes)],
         scratch=[pltpu.VMEM(w_in.shape, bf16), pltpu.VMEM(w_out.shape, bf16), pltpu.SemaphoreType.DMA((2,))],
         specs=[HBM] * 2 + [VMEM] * 3,
@@ -430,7 +445,7 @@
             pltpu.VMEM((total, 1), f32),
             pltpu.VMEM((half, double), f32),
         ],
-        specs=[SMEM] + [VMEM] * 6,
+        specs=[SMEM] + [VMEM] * 8,
         grant=20,
     )(me, both, *parameters)
     keep = call(
@@ -447,7 +462,8 @@
         grad_state = lax.all_to_all(
             grad_state.reshape(size, block, width), "seq", split_axis=0, concat_axis=0, tiled=True
         ).reshape(rows, width)
-    mine, other, step, grad_state = sum_over_devices(me, grad_state, keep, send, size, factor, riding)
+    shapes = [struct((double, units), f32), struct((units, double), f32)]
+    (grad_in, grad_out), grad_state = sum_over_devices(me, grad_state, keep, send, size, factor, riding, shapes)
     if riding:
         grad_state = call(
             functools.partial(unpack_kernel, block),
@@ -455,15 +471,6 @@
             scratch=[pltpu.VMEM((rows, width), f32)],
             specs=[SMEM] + [VMEM] * len(grad_state),
         )(me, *grad_state).T
-    shapes = [struct((double, units), f32), struct((units, double), f32)]
-    count = 2 * len(mine)
-    grad_in, grad_out = call(
-        functools.partial(place_kernel, 1),
-        shapes,
-        scratch=[pltpu.VMEM((count, step, double), f32), pltpu.SemaphoreType.DMA((count,))],
-        specs=[SMEM] + [VMEM] * count,
-        out_specs=[HBM] * 2,
-    )(me, *mine, *other)
     return (grad_state, grad_in, grad_out)
 
 

time: 63.2 us -> 62.3 us (0.986)
  waiting for transfers between devices: 27.5 us -> 24.9 us
  local copies, waits for them, and re-layouts: 3.11 us -> 4.17 us
    all_to_all x1, waiting for transfers between devices: 5.23 us -> 3.83 us  [shards(): both = lax.all_to_all(both, 'seq', split_axis=0, concat_axis=0, tiled=True)]
    ppermute x14, waiting for transfers between devices: 22.3 us -> 21.1 us  [exchange(): lax.ppermute(value if not isinstance(value, list) else value[i], 'seq', [...]
    unnamed x10, local copies, waits for them, and re-layouts: 3.11 us -> 4.17 us
    pallas_call x2 -> x3, Pallas kernels: 2 us -> 2.98 us  [the longest x2 2.12 us: place(): call(functools.partial(place_kernel, 1, pieces, slots, len(placed)), shap...]
    pallas_call x1, Pallas kernels: 7.23 us -> 6.42 us  [shards(): call(functools.partial(switch_kernel, levels, block), [rider if riding el...]
  transfers between devices with their start and end apart: 15 -> 15, of which waited for: 11 -> 12; matrix products, arithmetic and copies ran while one was open for 0% -> 0% of each run, Pallas kernels for 3% -> 6%
where the time goes in v8:
time: 62.3 us; the launch traced here: 61.9 us
  waiting for transfers between devices  24.9 us (40%)
  starting transfers between devices  19 us (30%)
  Pallas kernels  13.1 us (21%)
  local copies, waits for them, and re-layouts  4.17 us (7%)
  between operations  0.73 us (1%)
    ppermute x14, waiting for transfers between devices, exchange(): lax.ppermute(value if not isinstance(value, list) else value[i], 'seq', [...  21.1 us
    ppermute x14, starting transfers between devices, exchange(): lax.ppermute(value if not isinstance(value, list) else value[i], 'seq', [...  11.7 us
    all_to_all x1, starting transfers between devices, shards(): both = lax.all_to_all(both, 'seq', split_axis=0, concat_axis=0, tiled=True)  7.3 us
    pallas_call x1, Pallas kernels, shards(): call(functools.partial(switch_kernel, levels, block), [rider if riding el...  6.42 us
    unnamed x10, local copies, waits for them, and re-layouts  4.17 us
    all_to_all x1, waiting for transfers between devices, shards(): both = lax.all_to_all(both, 'seq', split_axis=0, concat_axis=0, tiled=True)  3.83 us
    pallas_call x2, Pallas kernels, place(): call(functools.partial(place_kernel, 1, pieces, slots, len(placed)), shap...  2.12 us
    pallas_call x1, Pallas kernels, shards(): call(pack_kernel, struct((size, block, double), bf16), scratch=[pltpu.VME...  1.74 us
  transfers between devices with their start and end apart: 15, of which 12 were waited for; matrix products, arithmetic and copies ran while one was open for 0% of the time, Pallas kernels for 6%

profile of v8, /device:TPU:0, one launch (start us, length us, event | category | flops | bytes accessed | tf_op | source)
XLA Modules:
  0.0 61.9 jit_solution(8273354656284295855)
XLA Ops:
  0.6 1.7 %shard_map.94 = bf16[32,8,384]{2,1,0:T(8,128)(2,1)} custom-call(bf16[192,256]{1,0:T(8,128)(2,1)} %bitcast.4, bf16[192,256]{1,0:T(8,128)(2,1)} %bitcast.5), custom_call_target="tpu_custom_call" | custom-call | bytes 7000000 | tf_op jit(solution)/shard_map/pallas_call | solution.py:410
  2.4 7.3 %all-to-all-start = ((bf16[32,8,384]{2,1,0:T(8,128)(2,1)}), bf16[32,8,384]{2,1,0:T(8,128)(2,1)S(1)}, u32[]{:S(2)}, u32[]{:S(2)}) async-start(bf16[32,8,384]{2,1,0:T(8,128)(2,1)} %shard_map.94), calls=%async_computation | async-start | bytes 393216 | tf_op jit(solution)/shard_map/all_to_all | solution.py:420
  9.7 1.1 %copy-done = bf16[384,768]{1,0:T(8,128)(2,1)S(1)} copy-done((bf16[384,768]{1,0:T(8,128)(2,1)S(1)}, bf16[384,768]{1,0:T(8,128)(2,1)}, u32[]{:S(2)}) %copy-start) | copy-done | bytes 589848
  10.8 1.1 %copy-done.1 = bf16[768,384]{1,0:T(8,128)(2,1)S(1)} copy-done((bf16[768,384]{1,0:T(8,128)(2,1)S(1)}, bf16[768,384]{1,0:T(8,128)(2,1)}, u32[]{:S(2)}) %copy-start.1) | copy-done | bytes 589848
  13.9 0.9 %shard_map.95 = (bf16[512,768]{1,0:T(8,128)(2,1)S(1)}, bf16[768,512]{1,0:T(8,128)(2,1)S(1)}, bf16[768,512]{1,0:T(8,128)(2,1)S(1)}, bf16[512,768]{1,0:T(8,128)(2,...) custom-call(bf16[384,768]{1,0:T(8,128)(2,1)S(1)} %copy-done, ...), custom_call_target="tpu_custom_call" | custom-call | tf_op jit(solution)/shard_map/pallas_call | solution.py:422
  14.7 3.8 %all-to-all-done.both_ref = bf16[32,8,384]{2,1,0:T(8,128)(2,1)S(1)} async-done(((bf16[32,8,384]{2,1,0:T(8,128)(2,1)}), bf16[32,8,384]{2,1,0:T(8,128)(2,1)S(1)}, u32[]{:S(2)}, u32[]{:S(2)}) %all-to-all-start) | async-done | bytes 196640 | tf_op jit(solution)/shard_map/all_to_all | solution.py:420
  18.6 6.4 %shard_map.96 = (bf16[64,384]{1,0:T(8,128)(2,1)S(1)}, bf16[832,384]{1,0:T(8,128)(2,1)S(1)}, bf16[640,512]{1,0:T(8,128)(2,1)S(1)}, bf16[640,768]{1,0:T(8,128)(2,1...) custom-call(s32[1]{0:T(128)} %bitcast.me_ref, bf16[32,8,384]{2,1,0:T(8,128)(2,1)S(1)} %all-to-all-done.both_ref, ...), custom_call_target="tpu_custom_call" | custom-call | tf_op jit(solution)/shard_map/pallas_call | solution.py:432
  25.7 0.8 %shard_map.97.refs_1_ = f32[768,384]{1,0:T(8,128)S(1)} custom-call(s32[1]{0:T(128)} %bitcast.me_ref, bf16[640,512]{1,0:T(8,128)(2,1)S(1)} %get-tuple-element.47.refs_0_, bf16[640,768]{1,0:T(8,128)(2,1)S(1)} %get-tuple-element.48.refs_1_, bf16[640,768]{1,0:T(8,128)(2,1)S(1)} %get-tuple-element.49.refs_2_, bf16[640,384]{1,0:T(8,128)(2,1)S(1)} %get-tuple-element.50.refs_3_), custom_call_target="tpu_custom_call" | custom-call | flops 377487360 | bytes 3932160 | tf_op jit(solution)/shard_map/pallas_call | solution.py:451
  26.5 0.9 %collective-permute-done.refs_2_ = bf16[832,384]{1,0:T(8,128)(2,1)S(1)} collective-permute-done((bf16[832,384]{1,0:T(8,128)(2,1)S(1)}, bf16[832,384]{1,0:T(8,128)(2,1)S(1)}, u32[]{:S(2)}, u32[]{:S(2)}) %collective-permute-start) | collective-permute-done | bytes 639008 | tf_op jit(solution)/shard_map/ppermute | solution.py:347
  28.2 1.3 %collective-permute-start.2 = (bf16[192,384]{1,0:T(8,128)(2,1)S(1)}, bf16[192,384]{1,0:T(8,128)(2,1)S(1)}, u32[]{:S(2)}, u32[]{:S(2)}) collective-permute-start(bf16[192,384]{1,0:T(8,128)(2,1)S(1)} %get-tuple-element.54), channel_id=1, source_target_pairs={{0,4},{1,5},{2,6},{3,7},{4,0},{5,1},{6,2},{7,3},{8,12},{9,13},{10,... | collective-permute-start | bytes 442376 | tf_op jit(solution)/shard_map/ppermute | solution.py:347
  29.4 1.7 %collective-permute-start.3 = (bf16[192,384]{1,0:T(8,128)(2,1)S(1)}, bf16[192,384]{1,0:T(8,128)(2,1)S(1)}, u32[]{:S(2)}, u32[]{:S(2)}) collective-permute-start(bf16[192,384]{1,0:T(8,128)(2,1)S(1)} %get-tuple-element.55), channel_id=1, source_target_pairs={{0,6},{1,7},{2,4},{3,5},{4,2},{5,3},{6,0},{7,1},{8,14},{9,15},{10,... | collective-permute-start | bytes 442376 | tf_op jit(solution)/shard_map/ppermute | solution.py:347
  31.9 4.7 %collective-permute-done.4.refs_5_ = bf16[64,384]{1,0:T(8,128)(2,1)S(1)} collective-permute-done((bf16[64,384]{1,0:T(8,128)(2,1)S(1)}, bf16[64,384]{1,0:T(8,128)(2,1)S(1)}, u32[]{:S(2)}, u32[]{:S(2)}) %collective-permute-start.4) | collective-permute-done | bytes 49184 | tf_op jit(solution)/shard_map/ppermute | solution.py:347
  37.2 0.8 %collective-permute-start.5 = (bf16[256,384]{1,0:T(8,128)(2,1)S(1)}, bf16[256,384]{1,0:T(8,128)(2,1)S(1)}, u32[]{:S(2)}, u32[]{:S(2)}) collective-permute-start(bf16[256,384]{1,0:T(8,128)(2,1)S(1)} %get-tuple-element.58.refs_0_), channel_id=1, source_target_pairs={{0,8},{1,9},{2,10},{3,11},{4,12},{5,13},{6,14},{7,15},{8,0},{9,1},... | collective-permute-start | bytes 589832 | tf_op jit(solution)/shard_map/ppermute | solution.py:347
  38.0 5.1 %collective-permute-done.5.refs_1_.refs_3_ = bf16[256,384]{1,0:T(8,128)(2,1)S(1)} collective-permute-done((bf16[256,384]{1,0:T(8,128)(2,1)S(1)}, bf16[256,384]{1,0:T(8,128)(2,1)S(1)}, u32[]{:S(2)}, u32[]{:S(2)}) %collective-permute-start.5) | collective-permute-done | bytes 196640 | tf_op jit(solution)/shard_map/ppermute | solution.py:347
  43.1 1.7 %collective-permute-start.6 = (bf16[192,384]{1,0:T(8,128)(2,1)S(1)}, bf16[192,384]{1,0:T(8,128)(2,1)S(1)}, u32[]{:S(2)}, u32[]{:S(2)}) collective-permute-start(bf16[192,384]{1,0:T(8,128)(2,1)S(1)} %shard_map.100.refs_0_), channel_id=1, source_target_pairs={{0,24},{1,25},{2,26},{3,27},{4,28},{5,29},{6,30},{7,31},{8,16},{9,... | collective-permute-start | bytes 442376 | tf_op jit(solution)/shard_map/ppermute | solution.py:347
  44.8 5.4 %collective-permute-done.6.refs_1_ = bf16[192,384]{1,0:T(8,128)(2,1)S(1)} collective-permute-done((bf16[192,384]{1,0:T(8,128)(2,1)S(1)}, bf16[192,384]{1,0:T(8,128)(2,1)S(1)}, u32[]{:S(2)}, u32[]{:S(2)}) %collective-permute-start.6) | collective-permute-done | bytes 147488 | tf_op jit(solution)/shard_map/ppermute | solution.py:347
  50.3 1.3 %collective-permute-start.7 = (bf16[224,384]{1,0:T(8,128)(2,1)S(1)}, bf16[224,384]{1,0:T(8,128)(2,1)S(1)}, u32[]{:S(2)}, u32[]{:S(2)}) collective-permute-start(bf16[224,384]{1,0:T(8,128)(2,1)S(1)} %get-tuple-element.61), channel_id=1, source_target_pairs={{0,2},{1,3},{2,0},{3,1},{4,6},{5,7},{6,4},{7,5},{8,10},{9,11},{10,... | collective-permute-start | bytes 516104 | tf_op jit(solution)/shard_map/ppermute | solution.py:347
  51.7 1.0 %collective-permute-start.8 = (bf16[224,384]{1,0:T(8,128)(2,1)S(1)}, bf16[224,384]{1,0:T(8,128)(2,1)S(1)}, u32[]{:S(2)}, u32[]{:S(2)}) collective-permute-start(bf16[224,384]{1,0:T(8,128)(2,1)S(1)} %get-tuple-element.62), channel_id=1, source_target_pairs={{0,4},{1,5},{2,6},{3,7},{4,0},{5,1},{6,2},{7,3},{8,12},{9,13},{10,... | collective-permute-start | bytes 516104 | tf_op jit(solution)/shard_map/ppermute | solution.py:347
  52.6 1.2 %collective-permute-start.9 = (bf16[224,384]{1,0:T(8,128)(2,1)S(1)}, bf16[224,384]{1,0:T(8,128)(2,1)S(1)}, u32[]{:S(2)}, u32[]{:S(2)}) collective-permute-start(bf16[224,384]{1,0:T(8,128)(2,1)S(1)} %get-tuple-element.63), channel_id=1, source_target_pairs={{0,6},{1,7},{2,4},{3,5},{4,2},{5,3},{6,0},{7,1},{8,14},{9,15},{10,... | collective-permute-start | bytes 516104 | tf_op jit(solution)/shard_map/ppermute | solution.py:347
  53.9 1.4 %collective-permute-done.10.refs_1_ = bf16[192,384]{1,0:T(8,128)(2,1)S(1)} collective-permute-done((bf16[192,384]{1,0:T(8,128)(2,1)S(1)}, bf16[192,384]{1,0:T(8,128)(2,1)S(1)}, u32[]{:S(2)}, u32[]{:S(2)}) %collective-permute-start.10) | collective-permute-done | bytes 147488 | tf_op jit(solution)/shard_map/ppermute | solution.py:347
  55.8 1.0 %shard_map.103 = (f32[384,768]{1,0:T(8,128)}, f32[768,384]{1,0:T(8,128)}) custom-call(s32[1]{0:T(128)} %bitcast.me_ref, bf16[192,384]{1,0:T(8,128)(2,1)S(1)} %get-tuple-element.64.refs_0_, bf16[192,384]{1,0:T(8,128)(2,1)S(1)} %collective-permute-done.10.refs_1_, bf16[224,384]{1,0:T(8,128)(2,1)S(1)} %collective-permute-done.7.refs_1_.refs_2_), custom_call_target="tpu_custom_call" | custom-call | tf_op jit(solution)/shard_map/pallas_call | solution.py:320
  57.2 1.8 %collective-permute-done.9.refs_3_.refs_1_ = bf16[224,384]{1,0:T(8,128)(2,1)S(1)} collective-permute-done((bf16[224,384]{1,0:T(8,128)(2,1)S(1)}, bf16[224,384]{1,0:T(8,128)(2,1)S(1)}, u32[]{:S(2)}, u32[]{:S(2)}) %collective-permute-start.9) | collective-permute-done | bytes 172064 | tf_op jit(solution)/shard_map/ppermute | solution.py:347
  59.6 0.8 %shard_map.102 = bf16[192,256]{1,0:T(8,128)(2,1)} custom-call(s32[1]{0:T(128)} %bitcast.me_ref, bf16[32,384]{1,0:T(8,128)(2,1)S(1)} %get-tuple-element.60.refs_0_, bf16[224,384]{1,0:T(8,128)(2,1)S(1)} %collective-permute-done.7.refs_1_.refs_2_, bf16[224,384]{1,0:T(8,128)(2,1)S(1)} %collective-permute-done.8.refs_2_.refs_0_, ...), custom_call_target="tpu_custom_call" | custom-call | tf_op jit(solution)/shard_map/pallas_call | solution.py:468
  60.7 1.2 %shard_map.104 = (f32[384,768]{1,0:T(8,128)}, f32[768,384]{1,0:T(8,128)}) custom-call(s32[1]{0:T(128)} %bitcast.me_ref, bf16[224,384]{1,0:T(8,128)(2,1)S(1)} %collective-permute-done.8.refs_2_.refs_0_, bf16[224,384]{1,0:T(8,128)(2,1)S(1)} %collective-permute-done.9.refs_3_.refs_1_, ...), custom_call_target="tpu_custom_call", output_to_operand_aliasing={{0}: (6, {}), {1}: (7, {})} | custom-call | tf_op jit(solution)/shard_map/pallas_call | solution.py:320
  (27 shorter events, 6.8 us)
Async XLA Ops:
  2.4 16.2 %all-to-all-start = ((bf16[32,8,384]{2,1,0:T(8,128)(2,1)}), bf16[32,8,384]{2,1,0:T(8,128)(2,1)S(1)}, u32[]{:S(2)}, u32[]{:S(2)}) async-start(bf16[32,8,384]{2,1,0:T(8,128)(2,1)} %shard_map.94), calls=%async_computation | async-start | bytes 393216 | tf_op jit(solution)/shard_map/all_to_all | solution.py:420
  9.7 1.1 %copy-start = (bf16[384,768]{1,0:T(8,128)(2,1)S(1)}, bf16[384,768]{1,0:T(8,128)(2,1)}, u32[]{:S(2)}) copy-start(bf16[384,768]{1,0:T(8,128)(2,1)} %w_in_ref.1) | copy-start | bytes 1769476
  10.8 1.1 %copy-start.1 = (bf16[768,384]{1,0:T(8,128)(2,1)S(1)}, bf16[768,384]{1,0:T(8,128)(2,1)}, u32[]{:S(2)}) copy-start(bf16[768,384]{1,0:T(8,128)(2,1)} %w_out_ref.1) | copy-start | bytes 1769476
  11.8 0.7 %copy-start.2 = (f32[768]{0:T(1024)S(1)}, f32[768]{0:T(1024)}, u32[]{:S(2)}) copy-start(f32[768]{0:T(1024)} %bias_ref.1) | copy-start | bytes 9220
  12.5 0.7 %copy-start.3 = (f32[384]{0:T(512)S(1)}, f32[384]{0:T(512)}, u32[]{:S(2)}) copy-start(f32[384]{0:T(512)} %logit_ref.1) | copy-start | bytes 4612
  13.2 0.7 %copy-start.4 = (f32[384]{0:T(512)S(1)}, f32[384]{0:T(512)}, u32[]{:S(2)}) copy-start(f32[384]{0:T(512)} %scale_ref.1) | copy-start | bytes 4612
  25.0 2.4 %collective-permute-start = (bf16[832,384]{1,0:T(8,128)(2,1)S(1)}, bf16[832,384]{1,0:T(8,128)(2,1)S(1)}, u32[]{:S(2)}, u32[]{:S(2)}) collective-permute-start(bf16[832,384]{1,0:T(8,128)(2,1)S(1)} %get-tuple-element.51), channel_id=1, source_target_pairs={{0,1},{1,0},{2,3},{3,2},{4,5},{5,4},{6,7},{7,6},{8,9},{9,8},{10,11... | collective-permute-start | bytes 1916936 | tf_op jit(solution)/shard_map/ppermute | solution.py:347
  27.6 9.1 %collective-permute-start.1 = (bf16[192,384]{1,0:T(8,128)(2,1)S(1)}, bf16[192,384]{1,0:T(8,128)(2,1)S(1)}, u32[]{:S(2)}, u32[]{:S(2)}) collective-permute-start(bf16[192,384]{1,0:T(8,128)(2,1)S(1)} %get-tuple-element.53), channel_id=1, source_target_pairs={{0,2},{1,3},{2,0},{3,1},{4,6},{5,7},{6,4},{7,5},{8,10},{9,11},{10,... | collective-permute-start | bytes 442376 | tf_op jit(solution)/shard_map/ppermute | solution.py:347
  28.2 8.9 %collective-permute-start.2 = (bf16[192,384]{1,0:T(8,128)(2,1)S(1)}, bf16[192,384]{1,0:T(8,128)(2,1)S(1)}, u32[]{:S(2)}, u32[]{:S(2)}) collective-permute-start(bf16[192,384]{1,0:T(8,128)(2,1)S(1)} %get-tuple-element.54), channel_id=1, source_target_pairs={{0,4},{1,5},{2,6},{3,7},{4,0},{5,1},{6,2},{7,3},{8,12},{9,13},{10,... | collective-permute-start | bytes 442376 | tf_op jit(solution)/shard_map/ppermute | solution.py:347
  29.4 7.7 %collective-permute-start.3 = (bf16[192,384]{1,0:T(8,128)(2,1)S(1)}, bf16[192,384]{1,0:T(8,128)(2,1)S(1)}, u32[]{:S(2)}, u32[]{:S(2)}) collective-permute-start(bf16[192,384]{1,0:T(8,128)(2,1)S(1)} %get-tuple-element.55), channel_id=1, source_target_pairs={{0,6},{1,7},{2,4},{3,5},{4,2},{5,3},{6,0},{7,1},{8,14},{9,15},{10,... | collective-permute-start | bytes 442376 | tf_op jit(solution)/shard_map/ppermute | solution.py:347
  31.1 5.5 %collective-permute-start.4 = (bf16[64,384]{1,0:T(8,128)(2,1)S(1)}, bf16[64,384]{1,0:T(8,128)(2,1)S(1)}, u32[]{:S(2)}, u32[]{:S(2)}) collective-permute-start(bf16[64,384]{1,0:T(8,128)(2,1)S(1)} %get-tuple-element.57), channel_id=1, source_target_pairs={{0,16},{1,17},{2,18},{3,19},{4,20},{5,21},{6,22},{7,23},{8,24},{9,... | collective-permute-start | bytes 147464 | tf_op jit(solution)/shard_map/ppermute | solution.py:347
  37.2 5.9 %collective-permute-start.5 = (bf16[256,384]{1,0:T(8,128)(2,1)S(1)}, bf16[256,384]{1,0:T(8,128)(2,1)S(1)}, u32[]{:S(2)}, u32[]{:S(2)}) collective-permute-start(bf16[256,384]{1,0:T(8,128)(2,1)S(1)} %get-tuple-element.58.refs_0_), channel_id=1, source_target_pairs={{0,8},{1,9},{2,10},{3,11},{4,12},{5,13},{6,14},{7,15},{8,0},{9,1},... | collective-permute-start | bytes 589832 | tf_op jit(solution)/shard_map/ppermute | solution.py:347
  43.1 7.1 %collective-permute-start.6 = (bf16[192,384]{1,0:T(8,128)(2,1)S(1)}, bf16[192,384]{1,0:T(8,128)(2,1)S(1)}, u32[]{:S(2)}, u32[]{:S(2)}) collective-permute-start(bf16[192,384]{1,0:T(8,128)(2,1)S(1)} %shard_map.100.refs_0_), channel_id=1, source_target_pairs={{0,24},{1,25},{2,26},{3,27},{4,28},{5,29},{6,30},{7,31},{8,16},{9,... | collective-permute-start | bytes 442376 | tf_op jit(solution)/shard_map/ppermute | solution.py:347
  50.3 5.5 %collective-permute-start.7 = (bf16[224,384]{1,0:T(8,128)(2,1)S(1)}, bf16[224,384]{1,0:T(8,128)(2,1)S(1)}, u32[]{:S(2)}, u32[]{:S(2)}) collective-permute-start(bf16[224,384]{1,0:T(8,128)(2,1)S(1)} %get-tuple-element.61), channel_id=1, source_target_pairs={{0,2},{1,3},{2,0},{3,1},{4,6},{5,7},{6,4},{7,5},{8,10},{9,11},{10,... | collective-permute-start | bytes 516104 | tf_op jit(solution)/shard_map/ppermute | solution.py:347
  51.7 5.6 %collective-permute-start.8 = (bf16[224,384]{1,0:T(8,128)(2,1)S(1)}, bf16[224,384]{1,0:T(8,128)(2,1)S(1)}, u32[]{:S(2)}, u32[]{:S(2)}) collective-permute-start(bf16[224,384]{1,0:T(8,128)(2,1)S(1)} %get-tuple-element.62), channel_id=1, source_target_pairs={{0,4},{1,5},{2,6},{3,7},{4,0},{5,1},{6,2},{7,3},{8,12},{9,13},{10,... | collective-permute-start | bytes 516104 | tf_op jit(solution)/shard_map/ppermute | solution.py:347
  52.6 6.4 %collective-permute-start.9 = (bf16[224,384]{1,0:T(8,128)(2,1)S(1)}, bf16[224,384]{1,0:T(8,128)(2,1)S(1)}, u32[]{:S(2)}, u32[]{:S(2)}) collective-permute-start(bf16[224,384]{1,0:T(8,128)(2,1)S(1)} %get-tuple-element.63), channel_id=1, source_target_pairs={{0,6},{1,7},{2,4},{3,5},{4,2},{5,3},{6,0},{7,1},{8,14},{9,15},{10,... | collective-permute-start | bytes 516104 | tf_op jit(solution)/shard_map/ppermute | solution.py:347
  53.9 1.4 %collective-permute-start.10 = (bf16[192,384]{1,0:T(8,128)(2,1)S(1)}, bf16[192,384]{1,0:T(8,128)(2,1)S(1)}, u32[]{:S(2)}, u32[]{:S(2)}) collective-permute-start(bf16[192,384]{1,0:T(8,128)(2,1)S(1)} %get-tuple-element.64.refs_0_), channel_id=1, source_target_pairs={{0,1},{1,0},{2,3},{3,2},{4,5},{5,4},{6,7},{7,6},{8,9},{9,8},{10,11... | collective-permute-start | bytes 442376 | tf_op jit(solution)/shard_map/ppermute | solution.py:347
  55.8 4.6 %collective-permute-start.11 = (bf16[224,384]{1,0:T(8,128)(2,1)S(1)}, bf16[224,384]{1,0:T(8,128)(2,1)S(1)}, u32[]{:S(2)}, u32[]{:S(2)}) collective-permute-start(bf16[224,384]{1,0:T(8,128)(2,1)S(1)} %collective-permute-done.7.refs_1_.refs_2_), channel_id=1, source_target_pairs={{0,1},{1,0},{2,3},{3,2},{4,5},{5,4},{6,7},{7,6},{8,9},{9,8},{10,11... | collective-permute-start | bytes 516104 | tf_op jit(solution)/shard_map/ppermute | solution.py:347
  59.1 1.4 %collective-permute-start.12 = (bf16[224,384]{1,0:T(8,128)(2,1)S(1)}, bf16[224,384]{1,0:T(8,128)(2,1)S(1)}, u32[]{:S(2)}, u32[]{:S(2)}) collective-permute-start(bf16[224,384]{1,0:T(8,128)(2,1)S(1)} %collective-permute-done.8.refs_2_.refs_0_), channel_id=1, source_target_pairs={{0,1},{1,0},{2,3},{3,2},{4,5},{5,4},{6,7},{7,6},{8,9},{9,8},{10,11... | collective-permute-start | bytes 516104 | tf_op jit(solution)/shard_map/ppermute | solution.py:347
  59.1 1.6 %collective-permute-start.13 = (bf16[224,384]{1,0:T(8,128)(2,1)S(1)}, bf16[224,384]{1,0:T(8,128)(2,1)S(1)}, u32[]{:S(2)}, u32[]{:S(2)}) collective-permute-start(bf16[224,384]{1,0:T(8,128)(2,1)S(1)} %collective-permute-done.9.refs_3_.refs_1_), channel_id=1, source_target_pairs={{0,1},{1,0},{2,3},{3,2},{4,5},{5,4},{6,7},{7,6},{8,9},{9,8},{10,11... | collective-permute-start | bytes 516104 | tf_op jit(solution)/shard_map/ppermute | solution.py:347

commit v9 on v8

--- a/solution.py
+++ b/solution.py
@@ -101,14 +101,11 @@
 
 def switch_kernel(
     levels, block, me_ref, both_ref, w_in_ref, w_out_ref, w_in_turned_ref, w_out_turned_ref, bias_ref, gate_ref, scale_ref,
-    grad_ref, send_ref, low_s, pre_s, act_s, bg_s,
-    slope_s, normed_s, inverse_s, paired_s,
+    send_ref, low_s, pre_s, act_s, bg_s, upstream_ref, normed_ref, inverse_ref,
+    slope_s, normed_s, inverse_s,
 ):
-    half, double = paired_s.shape
+    half, double = upstream_ref.shape[1], bg_s.shape[1]
     rows, width = 2 * half, double // 2
-    units = bias_ref.shape[1]
-    riding = send_ref.shape[0] > units
-    core = me_ref[0] % 2
     sides = range(2)
     lanes = w_in_ref.shape[0] // 2
     gate = [gate_ref[:, side * lanes : (side + 1) * lanes] for side in sides]
@@ -154,21 +151,46 @@
         act_grad = dot(jnp.concatenate(branch_grad, axis=1), w_out_turned_ref[...], (1, 0))
         pre_grad = (act_grad * slope_s[at, :]).astype(bf16)
         pre_s[at, :] = pre_grad
-        normed_grad = dot(pre_grad, w_in_turned_ref[...], (1, 0))
-        normed_grad = [normed_grad[:, side * lanes : (side + 1) * lanes] for side in sides]
         normed = [normed_s[side, at, :] for side in sides]
-        average = mean_of(normed_grad, double)
-        product = mean_of([normed_grad[side] * normed[side] for side in sides], double)
-        inverse = inverse_s[at, :]
-        result = [
-            (gate[side] * upstream[side] + inverse * (normed_grad[side] - average - normed[side] * product))
-            .astype(bf16)
-            .astype(f32)
-            for side in sides
-        ]
-        if level > 0 or not riding:
+        if level > 0:
+            result = input_grad(pre_grad, w_in_turned_ref, gate, upstream, normed, inverse_s[at, :], double)
             grad = unpair_rows(result, block * 2**level)
-    if riding:
+    for side in sides:
+        upstream_ref[side] = upstream[side]
+        normed_ref[side] = normed[side]
+    inverse_ref[...] = inverse_s[0:half, :]
+    put_products(me_ref[0] % 2 == 0, send_ref, low_s, pre_s, act_s, bg_s)
+
+
+def input_grad(pre_grad, w_in_turned_ref, gate, upstream, normed, inverse, double):
+    sides, lanes = range(2), w_in_turned_ref.shape[1] // 2
+    normed_grad = dot(pre_grad, w_in_turned_ref[...], (1, 0))
+    normed_grad = [normed_grad[:, side * lanes : (side + 1) * lanes] for side in sides]
+    average = mean_of(normed_grad, double)
+    product = mean_of([normed_grad[side] * normed[side] for side in sides], double)
+    return [
+        (gate[side] * upstream[side] + inverse * (normed_grad[side] - average - normed[side] * product))
+        .astype(bf16)
+        .astype(f32)
+        for side in sides
+    ]
+
+
+def keep_kernel(me_ref, *refs):
+    put_products(me_ref[0] % 2 == 1, refs[-1], *refs[:-1])
+
+
+def first_kernel(
+    block, me_ref, pre_ref, upstream_ref, normed_ref, inverse_ref, w_in_turned_ref, gate_ref, *refs
+):
+    *riders, paired_s = refs
+    half, double = paired_s.shape
+    width, lanes, sides = double // 2, upstream_ref.shape[2], range(2)
+    gate = [gate_ref[:, side * lanes : (side + 1) * lanes] for side in sides]
+    upstream, normed = [upstream_ref[side] for side in sides], [normed_ref[side] for side in sides]
+    result = input_grad(pre_ref[0:half, :], w_in_turned_ref, gate, upstream, normed, inverse_ref[...], double)
+    if len(riders) == 2:
+        core = me_ref[0] % 2
         paired_s[:, :width] = jnp.where(core == 0, result[0], result[1])[:, :width]
         paired_s[:, width:] = jnp.where(core == 0, result[1], result[0])[:, :width]
         pairs = half // block
@@ -181,11 +203,10 @@
                     found.append(paired_s[pl.ds(pl.multiple_of(chip * block, 8), block), :])
                 kept.append(jnp.concatenate([part[:, :width] for part in found], axis=1))
                 sent.append(jnp.concatenate([part[:, width:] for part in found], axis=1))
-        grad_ref[...] = jnp.concatenate(kept, axis=0).astype(bf16)
-        send_ref[units:, :] = jnp.concatenate(sent, axis=0).astype(bf16)
+        riders[0][...] = jnp.concatenate(kept, axis=0).astype(bf16)
+        riders[1][...] = jnp.concatenate(sent, axis=0).astype(bf16)
     else:
-        grad_ref[...] = grad[:, :width].astype(bf16)
-    put_products(core == 0, send_ref, low_s, pre_s, act_s, bg_s)
+        riders[0][...] = unpair_rows(result, block)[:, :width].astype(bf16)
 
 
 def put_products(out_first, half_ref, low_ref, pre_ref, act_ref, bg_ref):
@@ -204,25 +225,21 @@
             half_ref[first : first + double, :] = grad_in[:, first : first + double].astype(half_ref.dtype)
 
 
-def keep_kernel(me_ref, *refs):
-    put_products(me_ref[0] % 2 == 1, refs[-1], *refs[:-1])
-
-
-def split_kernel(radix, shift, riding, me_ref, *refs):
-    parts, outs = refs[: 2 + riding], refs[2 + riding :]
+def split_kernel(radix, shift, me_ref, keep_ref, arrived_ref, *outs):
     rows = outs[0].shape[0]
-    if riding:
-        ride_ref, parts = parts[0], parts[1:]
-        width = ride_ref.shape[1] // 2
-        sources = [ride_ref[...].astype(f32), parts[1][rows * radix :, :].astype(f32)]
-        for high in range(2):
-            lanes = [source[:, high * width : (high + 1) * width] for source in sources]
-            outs[radix + high][...] = jnp.concatenate(lanes, axis=1).astype(bf16)
     place = (me_ref[0] >> shift) & (radix - 1)
     for other in range(radix):
         at = pl.ds(pl.multiple_of((place ^ other) * rows, tile), rows)
-        total = parts[0][at, :].astype(f32) + parts[1][at, :].astype(f32)
+        total = keep_ref[at, :].astype(f32) + arrived_ref[at, :].astype(f32)
         outs[other][...] = total.astype(outs[other].dtype)
+
+
+def cores_kernel(kept_ref, arrived_ref, *outs):
+    width = kept_ref.shape[1] // 2
+    sources = [kept_ref[...].astype(f32), arrived_ref[...].astype(f32)]
+    for high in range(2):
+        lanes = [source[:, high * width : (high + 1) * width] for source in sources]
+        outs[high][...] = jnp.concatenate(lanes, axis=1).astype(bf16)
 
 
 def total_of(refs):
@@ -348,22 +365,26 @@
                          [(d, d ^ mask) for d in range(size)]) for i, mask in enumerate(masks)]
 
 
-def sum_over_devices(me, ride, keep, send, size, factor, riding, shapes):
+def sum_over_devices(me, ride, ride_send, keep, send, size, factor, riding, shapes):
     bits = size.bit_length() - 1
     rows, double = keep.shape
     radix = min(4, size // 2)
     masks = [m << 1 for m in range(1, radix)]
     rows = rows // radix
     piece, rider = struct((rows, double), bf16), struct(ride.shape, bf16)
-    parts = [keep] + exchange([send], [1], size)
-    outs = [struct((rows, double), f32)] + [piece] * (radix - 1) + [rider] * 2 * riding
-    operands = [ride] * riding + parts
+    (arrived,) = exchange([send], [1], size)
+    if riding:
+        (came,) = exchange([ride_send], [1], size)
+        arrived, came = lax.optimization_barrier((arrived, came))
     pieces = call(
-        functools.partial(split_kernel, radix, 1, riding), outs, specs=[SMEM] + [VMEM] * len(operands)
-    )(me, *operands)
-    parts = [pieces[0]] + exchange(list(pieces[1:radix]), masks, size)
+        functools.partial(split_kernel, radix, 1),
+        [struct((rows, double), f32)] + [piece] * (radix - 1),
+        specs=[SMEM, VMEM, VMEM],
+    )(me, keep, arrived)
+    parts = [pieces[0]] + exchange(list(pieces[1:]), masks, size)
     if riding:
-        riders = [pieces[radix]] + exchange([pieces[radix + 1]], [16], size)
+        high = call(cores_kernel, [rider] * 2, count=2)(ride, came)
+        riders = [high[0]] + exchange([high[1]], [16], size)
         total, kept = call(
             line_kernel, [struct((rows + ride.shape[0], double), bf16), rider], count=len(parts) + 2
         )(*parts, *riders)
@@ -429,25 +450,34 @@
     total = levels * half
     riding = block % 8 == 0 and levels == 5
     rider = struct((rows // 4, double), bf16)
-    grad_state, send, *factors = call(
+    send, *factors = call(
         functools.partial(switch_kernel, levels, block),
         [
-            rider if riding else struct((rows, width), bf16),
-            struct((units + rider.shape[0] * riding, double), bf16),
+            struct((units, double), bf16),
             struct((total, 2 * lanes), bf16),
             struct((total, units), bf16),
             struct((total, units), bf16),
             struct((total, double), bf16),
+            struct((2, half, lanes), f32),
+            struct((2, half, lanes), f32),
+            struct((half, 1), f32),
         ],
         scratch=[
             pltpu.VMEM((total, units), f32),
             pltpu.VMEM((2, total, lanes), f32),
             pltpu.VMEM((total, 1), f32),
-            pltpu.VMEM((half, double), f32),
         ],
         specs=[SMEM] + [VMEM] * 8,
         grant=20,
     )(me, both, *parameters)
+    factors, rest = factors[:4], factors[4:]
+    grad_state, *ride_send = call(
+        functools.partial(first_kernel, block),
+        [rider] * 2 if riding else [struct((rows, width), bf16)],
+        scratch=[pltpu.VMEM((half, double), f32)],
+        specs=[SMEM] + [VMEM] * 6,
+        cost_estimate=pl.CostEstimate(flops=rows * units * double, bytes_accessed=rows * units, transcendentals=0),
+    )(me, factors[1], *rest, parameters[2], parameters[5])
     keep = call(
         keep_kernel,
         struct((units, double), f32),
@@ -457,13 +487,14 @@
             flops=2 * total * units * double, bytes_accessed=8 * total * units, transcendentals=0
         ),
     )(me, *factors)
+    ride_send = ride_send[0] if riding else None
     factor = float(rows * size) ** (-0.5)
     if not riding:
         grad_state = lax.all_to_all(
             grad_state.reshape(size, block, width), "seq", split_axis=0, concat_axis=0, tiled=True
         ).reshape(rows, width)
     shapes = [struct((double, units), f32), struct((units, double), f32)]
-    (grad_in, grad_out), grad_state = sum_over_devices(me, grad_state, keep, send, size, factor, riding, shapes)
+    (grad_in, grad_out), grad_state = sum_over_devices(me, grad_state, ride_send, keep, send, size, factor, riding, shapes)
     if riding:
         grad_state = call(
             functools.partial(unpack_kernel, block),

time: 62.3 us -> 61.8 us (level)
  waiting for transfers between devices: 24.9 us -> 24.2 us
    ppermute x14 -> x15, waiting for transfers between devices: 21.1 us -> 20.4 us  [exchange(): lax.ppermute(value if not isinstance(value, list) else value[i], 'seq', [...]
    pallas_call x2 -> x4, Pallas kernels: 6.58 us -> 6.79 us  [the longest x1 6.05 us: shards(): call(functools.partial(switch_kernel, levels, block), [struct((units, dou...]
    ppermute x14 -> x15, starting transfers between devices: 11.7 us -> 11.6 us  [exchange(): lax.ppermute(value if not isinstance(value, list) else value[i], 'seq', [...]
  transfers between devices with their start and end apart: 15 -> 16, of which waited for: 12 -> 11; matrix products, arithmetic and copies ran while one was open for 0% -> 0% of each run, Pallas kernels for 6% -> 7%
where the time goes in v9:
time: 61.8 us; the launch traced here: 61.4 us
  waiting for transfers between devices  24.2 us (39%)
  starting transfers between devices  18.9 us (31%)
  Pallas kernels  13.4 us (22%)
  local copies, waits for them, and re-layouts  4.17 us (7%)
  between operations  0.74 us (1%)
    ppermute x15, waiting for transfers between devices, exchange(): lax.ppermute(value if not isinstance(value, list) else value[i], 'seq', [...  20.4 us
    ppermute x15, starting transfers between devices, exchange(): lax.ppermute(value if not isinstance(value, list) else value[i], 'seq', [...  11.6 us
    all_to_all x1, starting transfers between devices, shards(): both = lax.all_to_all(both, 'seq', split_axis=0, concat_axis=0, tiled=True)  7.3 us
    pallas_call x1, Pallas kernels, shards(): call(functools.partial(switch_kernel, levels, block), [struct((units, dou...  6.05 us
    unnamed x10, local copies, waits for them, and re-layouts  4.17 us
    all_to_all x1, waiting for transfers between devices, shards(): both = lax.all_to_all(both, 'seq', split_axis=0, concat_axis=0, tiled=True)  3.82 us
    pallas_call x2, Pallas kernels, place(): call(functools.partial(place_kernel, 1, pieces, slots, len(placed)), shap...  2.12 us
    pallas_call x1, Pallas kernels, shards(): call(pack_kernel, struct((size, block, double), bf16), scratch=[pltpu.VME...  1.74 us
  transfers between devices with their start and end apart: 16, of which 11 were waited for; matrix products, arithmetic and copies ran while one was open for 0% of the time, Pallas kernels for 7%

profile of v9, /device:TPU:0, one launch (start us, length us, event | category | flops | bytes accessed | tf_op | source)
XLA Modules:
  0.0 61.4 jit_solution(1607124604504150476)
XLA Ops:
  0.6 1.7 %shard_map.94 = bf16[32,8,384]{2,1,0:T(8,128)(2,1)} custom-call(bf16[192,256]{1,0:T(8,128)(2,1)} %bitcast.4, bf16[192,256]{1,0:T(8,128)(2,1)} %bitcast.5), custom_call_target="tpu_custom_call" | custom-call | bytes 7000000 | tf_op jit(solution)/shard_map/pallas_call | solution.py:431
  2.4 7.3 %all-to-all-start = ((bf16[32,8,384]{2,1,0:T(8,128)(2,1)}), bf16[32,8,384]{2,1,0:T(8,128)(2,1)S(1)}, u32[]{:S(2)}, u32[]{:S(2)}) async-start(bf16[32,8,384]{2,1,0:T(8,128)(2,1)} %shard_map.94), calls=%async_computation | async-start | bytes 393216 | tf_op jit(solution)/shard_map/all_to_all | solution.py:441
  9.7 1.1 %copy-done = bf16[384,768]{1,0:T(8,128)(2,1)S(1)} copy-done((bf16[384,768]{1,0:T(8,128)(2,1)S(1)}, bf16[384,768]{1,0:T(8,128)(2,1)}, u32[]{:S(2)}) %copy-start) | copy-done | bytes 589848
  10.8 1.1 %copy-done.1 = bf16[768,384]{1,0:T(8,128)(2,1)S(1)} copy-done((bf16[768,384]{1,0:T(8,128)(2,1)S(1)}, bf16[768,384]{1,0:T(8,128)(2,1)}, u32[]{:S(2)}) %copy-start.1) | copy-done | bytes 589848
  13.9 0.9 %shard_map.95 = (bf16[512,768]{1,0:T(8,128)(2,1)S(1)}, bf16[768,512]{1,0:T(8,128)(2,1)S(1)}, bf16[768,512]{1,0:T(8,128)(2,1)S(1)}, bf16[512,768]{1,0:T(8,128)(2,...) custom-call(bf16[384,768]{1,0:T(8,128)(2,1)S(1)} %copy-done, ...), custom_call_target="tpu_custom_call" | custom-call | tf_op jit(solution)/shard_map/pallas_call | solution.py:443
  14.8 3.8 %all-to-all-done.both_ref = bf16[32,8,384]{2,1,0:T(8,128)(2,1)S(1)} async-done(((bf16[32,8,384]{2,1,0:T(8,128)(2,1)}), bf16[32,8,384]{2,1,0:T(8,128)(2,1)S(1)}, u32[]{:S(2)}, u32[]{:S(2)}) %all-to-all-start) | async-done | bytes 196640 | tf_op jit(solution)/shard_map/all_to_all | solution.py:441
  18.6 6.0 %shard_map.96 = (bf16[768,384]{1,0:T(8,128)(2,1)S(1)}, bf16[640,512]{1,0:T(8,128)(2,1)S(1)}, bf16[640,768]{1,0:T(8,128)(2,1)S(1)}, bf16[640,768]{1,0:T(8,128)(2,...) custom-call(s32[1]{0:T(128)} %bitcast.me_ref, ...), custom_call_target="tpu_custom_call" | custom-call | tf_op jit(solution)/shard_map/pallas_call | solution.py:453
  24.6 0.7 %collective-permute-start = (bf16[768,384]{1,0:T(8,128)(2,1)S(1)}, bf16[768,384]{1,0:T(8,128)(2,1)S(1)}, u32[]{:S(2)}, u32[]{:S(2)}) collective-permute-start(bf16[768,384]{1,0:T(8,128)(2,1)S(1)} %get-tuple-element.56), channel_id=1, source_target_pairs={{0,1},{1,0},{2,3},{3,2},{4,5},{5,4},{6,7},{7,6},{8,9},{9,8},{10,11... | collective-permute-start | bytes 1769480 | tf_op jit(solution)/shard_map/ppermute | solution.py:364
  26.0 0.8 %shard_map.97.keep_ref = f32[768,384]{1,0:T(8,128)S(1)} custom-call(s32[1]{0:T(128)} %bitcast.me_ref, bf16[640,512]{1,0:T(8,128)(2,1)S(1)} %get-tuple-element.52.refs_0_, bf16[640,768]{1,0:T(8,128)(2,1)S(1)} %get-tuple-element.53.refs_1_.pre_ref, bf16[640,768]{1,0:T(8,128)(2,1)S(1)} %get-tuple-element.54.refs_2_, bf16[640,384]{1,0:T(8,128)(2,1)S(1)} %get-tuple-element.55.refs_3_), custom_call_target="tpu_custom_call" | custom-call | flops 377487360 | bytes 3932160 | tf_op jit(solution)/shard_map/pallas_call | solution.py:481
  27.8 1.2 %collective-permute-start.3 = (bf16[192,384]{1,0:T(8,128)(2,1)S(1)}, bf16[192,384]{1,0:T(8,128)(2,1)S(1)}, u32[]{:S(2)}, u32[]{:S(2)}) collective-permute-start(bf16[192,384]{1,0:T(8,128)(2,1)S(1)} %get-tuple-element.64), channel_id=1, source_target_pairs={{0,4},{1,5},{2,6},{3,7},{4,0},{5,1},{6,2},{7,3},{8,12},{9,13},{10,... | collective-permute-start | bytes 442376 | tf_op jit(solution)/shard_map/ppermute | solution.py:364
  29.0 1.9 %collective-permute-start.4 = (bf16[192,384]{1,0:T(8,128)(2,1)S(1)}, bf16[192,384]{1,0:T(8,128)(2,1)S(1)}, u32[]{:S(2)}, u32[]{:S(2)}) collective-permute-start(bf16[192,384]{1,0:T(8,128)(2,1)S(1)} %get-tuple-element.65), channel_id=1, source_target_pairs={{0,6},{1,7},{2,4},{3,5},{4,2},{5,3},{6,0},{7,1},{8,14},{9,15},{10,... | collective-permute-start | bytes 442376 | tf_op jit(solution)/shard_map/ppermute | solution.py:364
  31.7 4.9 %collective-permute-done.5.refs_5_ = bf16[64,384]{1,0:T(8,128)(2,1)S(1)} collective-permute-done((bf16[64,384]{1,0:T(8,128)(2,1)S(1)}, bf16[64,384]{1,0:T(8,128)(2,1)S(1)}, u32[]{:S(2)}, u32[]{:S(2)}) %collective-permute-start.5) | collective-permute-done | bytes 49184 | tf_op jit(solution)/shard_map/ppermute | solution.py:364
  36.7 0.8 %collective-permute-start.6 = (bf16[256,384]{1,0:T(8,128)(2,1)S(1)}, bf16[256,384]{1,0:T(8,128)(2,1)S(1)}, u32[]{:S(2)}, u32[]{:S(2)}) collective-permute-start(bf16[256,384]{1,0:T(8,128)(2,1)S(1)} %get-tuple-element.70.refs_0_), channel_id=1, source_target_pairs={{0,8},{1,9},{2,10},{3,11},{4,12},{5,13},{6,14},{7,15},{8,0},{9,1},... | collective-permute-start | bytes 589832 | tf_op jit(solution)/shard_map/ppermute | solution.py:364
  37.6 5.4 %collective-permute-done.6.refs_1_.refs_3_ = bf16[256,384]{1,0:T(8,128)(2,1)S(1)} collective-permute-done((bf16[256,384]{1,0:T(8,128)(2,1)S(1)}, bf16[256,384]{1,0:T(8,128)(2,1)S(1)}, u32[]{:S(2)}, u32[]{:S(2)}) %collective-permute-start.6) | collective-permute-done | bytes 196640 | tf_op jit(solution)/shard_map/ppermute | solution.py:364
  43.0 1.7 %collective-permute-start.7 = (bf16[192,384]{1,0:T(8,128)(2,1)S(1)}, bf16[192,384]{1,0:T(8,128)(2,1)S(1)}, u32[]{:S(2)}, u32[]{:S(2)}) collective-permute-start(bf16[192,384]{1,0:T(8,128)(2,1)S(1)} %shard_map.102.refs_0_), channel_id=1, source_target_pairs={{0,24},{1,25},{2,26},{3,27},{4,28},{5,29},{6,30},{7,31},{8,16},{9,... | collective-permute-start | bytes 442376 | tf_op jit(solution)/shard_map/ppermute | solution.py:364
  44.7 5.4 %collective-permute-done.7.refs_1_ = bf16[192,384]{1,0:T(8,128)(2,1)S(1)} collective-permute-done((bf16[192,384]{1,0:T(8,128)(2,1)S(1)}, bf16[192,384]{1,0:T(8,128)(2,1)S(1)}, u32[]{:S(2)}, u32[]{:S(2)}) %collective-permute-start.7) | collective-permute-done | bytes 147488 | tf_op jit(solution)/shard_map/ppermute | solution.py:364
  50.2 1.1 %collective-permute-start.8 = (bf16[224,384]{1,0:T(8,128)(2,1)S(1)}, bf16[224,384]{1,0:T(8,128)(2,1)S(1)}, u32[]{:S(2)}, u32[]{:S(2)}) collective-permute-start(bf16[224,384]{1,0:T(8,128)(2,1)S(1)} %get-tuple-element.73), channel_id=1, source_target_pairs={{0,2},{1,3},{2,0},{3,1},{4,6},{5,7},{6,4},{7,5},{8,10},{9,11},{10,... | collective-permute-start | bytes 516104 | tf_op jit(solution)/shard_map/ppermute | solution.py:364
  51.3 0.8 %collective-permute-start.9 = (bf16[224,384]{1,0:T(8,128)(2,1)S(1)}, bf16[224,384]{1,0:T(8,128)(2,1)S(1)}, u32[]{:S(2)}, u32[]{:S(2)}) collective-permute-start(bf16[224,384]{1,0:T(8,128)(2,1)S(1)} %get-tuple-element.74), channel_id=1, source_target_pairs={{0,4},{1,5},{2,6},{3,7},{4,0},{5,1},{6,2},{7,3},{8,12},{9,13},{10,... | collective-permute-start | bytes 516104 | tf_op jit(solution)/shard_map/ppermute | solution.py:364
  52.1 1.7 %collective-permute-start.10 = (bf16[224,384]{1,0:T(8,128)(2,1)S(1)}, bf16[224,384]{1,0:T(8,128)(2,1)S(1)}, u32[]{:S(2)}, u32[]{:S(2)}) collective-permute-start(bf16[224,384]{1,0:T(8,128)(2,1)S(1)} %get-tuple-element.75), channel_id=1, source_target_pairs={{0,6},{1,7},{2,4},{3,5},{4,2},{5,3},{6,0},{7,1},{8,14},{9,15},{10,... | collective-permute-start | bytes 516104 | tf_op jit(solution)/shard_map/ppermute | solution.py:364
  53.8 1.4 %collective-permute-done.11.refs_1_ = bf16[192,384]{1,0:T(8,128)(2,1)S(1)} collective-permute-done((bf16[192,384]{1,0:T(8,128)(2,1)S(1)}, bf16[192,384]{1,0:T(8,128)(2,1)S(1)}, u32[]{:S(2)}, u32[]{:S(2)}) %collective-permute-start.11) | collective-permute-done | bytes 147488 | tf_op jit(solution)/shard_map/ppermute | solution.py:364
  55.7 1.0 %shard_map.105 = (f32[384,768]{1,0:T(8,128)}, f32[768,384]{1,0:T(8,128)}) custom-call(s32[1]{0:T(128)} %bitcast.me_ref, bf16[192,384]{1,0:T(8,128)(2,1)S(1)} %get-tuple-element.76.refs_0_, bf16[192,384]{1,0:T(8,128)(2,1)S(1)} %collective-permute-done.11.refs_1_, bf16[224,384]{1,0:T(8,128)(2,1)S(1)} %collective-permute-done.8.refs_1_.refs_2_), custom_call_target="tpu_custom_call" | custom-call | tf_op jit(solution)/shard_map/pallas_call | solution.py:337
  56.7 1.9 %collective-permute-done.9.refs_2_.refs_0_ = bf16[224,384]{1,0:T(8,128)(2,1)S(1)} collective-permute-done((bf16[224,384]{1,0:T(8,128)(2,1)S(1)}, bf16[224,384]{1,0:T(8,128)(2,1)S(1)}, u32[]{:S(2)}, u32[]{:S(2)}) %collective-permute-start.9) | collective-permute-done | bytes 172064 | tf_op jit(solution)/shard_map/ppermute | solution.py:364
  59.1 0.8 %shard_map.104 = bf16[192,256]{1,0:T(8,128)(2,1)} custom-call(s32[1]{0:T(128)} %bitcast.me_ref, bf16[32,384]{1,0:T(8,128)(2,1)S(1)} %get-tuple-element.72.refs_0_, bf16[224,384]{1,0:T(8,128)(2,1)S(1)} %collective-permute-done.8.refs_1_.refs_2_, bf16[224,384]{1,0:T(8,128)(2,1)S(1)} %collective-permute-done.9.refs_2_.refs_0_, ...), custom_call_target="tpu_custom_call" | custom-call | tf_op jit(solution)/shard_map/pallas_call | solution.py:499
  60.2 1.2 %shard_map.106 = (f32[384,768]{1,0:T(8,128)}, f32[768,384]{1,0:T(8,128)}) custom-call(s32[1]{0:T(128)} %bitcast.me_ref, bf16[224,384]{1,0:T(8,128)(2,1)S(1)} %collective-permute-done.9.refs_2_.refs_0_, bf16[224,384]{1,0:T(8,128)(2,1)S(1)} %collective-permute-done.10.refs_3_.refs_1_, ...), custom_call_target="tpu_custom_call", output_to_operand_aliasing={{0}: (6, {}), {1}: (7, {})} | custom-call | tf_op jit(solution)/shard_map/pallas_call | solution.py:337
  (31 shorter events, 6.1 us)
Async XLA Ops:
  2.4 16.2 %all-to-all-start = ((bf16[32,8,384]{2,1,0:T(8,128)(2,1)}), bf16[32,8,384]{2,1,0:T(8,128)(2,1)S(1)}, u32[]{:S(2)}, u32[]{:S(2)}) async-start(bf16[32,8,384]{2,1,0:T(8,128)(2,1)} %shard_map.94), calls=%async_computation | async-start | bytes 393216 | tf_op jit(solution)/shard_map/all_to_all | solution.py:441
  9.7 1.1 %copy-start = (bf16[384,768]{1,0:T(8,128)(2,1)S(1)}, bf16[384,768]{1,0:T(8,128)(2,1)}, u32[]{:S(2)}) copy-start(bf16[384,768]{1,0:T(8,128)(2,1)} %w_in_ref.1) | copy-start | bytes 1769476
  10.8 1.1 %copy-start.1 = (bf16[768,384]{1,0:T(8,128)(2,1)S(1)}, bf16[768,384]{1,0:T(8,128)(2,1)}, u32[]{:S(2)}) copy-start(bf16[768,384]{1,0:T(8,128)(2,1)} %w_out_ref.1) | copy-start | bytes 1769476
  11.8 0.7 %copy-start.2 = (f32[768]{0:T(1024)S(1)}, f32[768]{0:T(1024)}, u32[]{:S(2)}) copy-start(f32[768]{0:T(1024)} %bias_ref.1) | copy-start | bytes 9220
  12.5 0.7 %copy-start.3 = (f32[384]{0:T(512)S(1)}, f32[384]{0:T(512)}, u32[]{:S(2)}) copy-start(f32[384]{0:T(512)} %logit_ref.1) | copy-start | bytes 4612
  13.2 0.7 %copy-start.4 = (f32[384]{0:T(512)S(1)}, f32[384]{0:T(512)}, u32[]{:S(2)}) copy-start(f32[384]{0:T(512)} %scale_ref.1) | copy-start | bytes 4612
  24.6 2.6 %collective-permute-start = (bf16[768,384]{1,0:T(8,128)(2,1)S(1)}, bf16[768,384]{1,0:T(8,128)(2,1)S(1)}, u32[]{:S(2)}, u32[]{:S(2)}) collective-permute-start(bf16[768,384]{1,0:T(8,128)(2,1)S(1)} %get-tuple-element.56), channel_id=1, source_target_pairs={{0,1},{1,0},{2,3},{3,2},{4,5},{5,4},{6,7},{7,6},{8,9},{9,8},{10,11... | collective-permute-start | bytes 1769480 | tf_op jit(solution)/shard_map/ppermute | solution.py:364
  25.9 1.3 %collective-permute-start.1 = (bf16[64,384]{1,0:T(8,128)(2,1)S(1)}, bf16[64,384]{1,0:T(8,128)(2,1)S(1)}, u32[]{:S(2)}, u32[]{:S(2)}) collective-permute-start(bf16[64,384]{1,0:T(8,128)(2,1)S(1)} %get-tuple-element.60), channel_id=1, source_target_pairs={{0,1},{1,0},{2,3},{3,2},{4,5},{5,4},{6,7},{7,6},{8,9},{9,8},{10,11... | collective-permute-start | bytes 147464 | tf_op jit(solution)/shard_map/ppermute | solution.py:364
  27.3 9.2 %collective-permute-start.2 = (bf16[192,384]{1,0:T(8,128)(2,1)S(1)}, bf16[192,384]{1,0:T(8,128)(2,1)S(1)}, u32[]{:S(2)}, u32[]{:S(2)}) collective-permute-start(bf16[192,384]{1,0:T(8,128)(2,1)S(1)} %get-tuple-element.63), channel_id=1, source_target_pairs={{0,2},{1,3},{2,0},{3,1},{4,6},{5,7},{6,4},{7,5},{8,10},{9,11},{10,... | collective-permute-start | bytes 442376 | tf_op jit(solution)/shard_map/ppermute | solution.py:364
  27.8 8.9 %collective-permute-start.3 = (bf16[192,384]{1,0:T(8,128)(2,1)S(1)}, bf16[192,384]{1,0:T(8,128)(2,1)S(1)}, u32[]{:S(2)}, u32[]{:S(2)}) collective-permute-start(bf16[192,384]{1,0:T(8,128)(2,1)S(1)} %get-tuple-element.64), channel_id=1, source_target_pairs={{0,4},{1,5},{2,6},{3,7},{4,0},{5,1},{6,2},{7,3},{8,12},{9,13},{10,... | collective-permute-start | bytes 442376 | tf_op jit(solution)/shard_map/ppermute | solution.py:364
  29.0 7.7 %collective-permute-start.4 = (bf16[192,384]{1,0:T(8,128)(2,1)S(1)}, bf16[192,384]{1,0:T(8,128)(2,1)S(1)}, u32[]{:S(2)}, u32[]{:S(2)}) collective-permute-start(bf16[192,384]{1,0:T(8,128)(2,1)S(1)} %get-tuple-element.65), channel_id=1, source_target_pairs={{0,6},{1,7},{2,4},{3,5},{4,2},{5,3},{6,0},{7,1},{8,14},{9,15},{10,... | collective-permute-start | bytes 442376 | tf_op jit(solution)/shard_map/ppermute | solution.py:364
  31.0 5.6 %collective-permute-start.5 = (bf16[64,384]{1,0:T(8,128)(2,1)S(1)}, bf16[64,384]{1,0:T(8,128)(2,1)S(1)}, u32[]{:S(2)}, u32[]{:S(2)}) collective-permute-start(bf16[64,384]{1,0:T(8,128)(2,1)S(1)} %get-tuple-element.69), channel_id=1, source_target_pairs={{0,16},{1,17},{2,18},{3,19},{4,20},{5,21},{6,22},{7,23},{8,24},{9,... | collective-permute-start | bytes 147464 | tf_op jit(solution)/shard_map/ppermute | solution.py:364
  36.7 6.3 %collective-permute-start.6 = (bf16[256,384]{1,0:T(8,128)(2,1)S(1)}, bf16[256,384]{1,0:T(8,128)(2,1)S(1)}, u32[]{:S(2)}, u32[]{:S(2)}) collective-permute-start(bf16[256,384]{1,0:T(8,128)(2,1)S(1)} %get-tuple-element.70.refs_0_), channel_id=1, source_target_pairs={{0,8},{1,9},{2,10},{3,11},{4,12},{5,13},{6,14},{7,15},{8,0},{9,1},... | collective-permute-start | bytes 589832 | tf_op jit(solution)/shard_map/ppermute | solution.py:364
  43.0 7.1 %collective-permute-start.7 = (bf16[192,384]{1,0:T(8,128)(2,1)S(1)}, bf16[192,384]{1,0:T(8,128)(2,1)S(1)}, u32[]{:S(2)}, u32[]{:S(2)}) collective-permute-start(bf16[192,384]{1,0:T(8,128)(2,1)S(1)} %shard_map.102.refs_0_), channel_id=1, source_target_pairs={{0,24},{1,25},{2,26},{3,27},{4,28},{5,29},{6,30},{7,31},{8,16},{9,... | collective-permute-start | bytes 442376 | tf_op jit(solution)/shard_map/ppermute | solution.py:364
  50.2 5.5 %collective-permute-start.8 = (bf16[224,384]{1,0:T(8,128)(2,1)S(1)}, bf16[224,384]{1,0:T(8,128)(2,1)S(1)}, u32[]{:S(2)}, u32[]{:S(2)}) collective-permute-start(bf16[224,384]{1,0:T(8,128)(2,1)S(1)} %get-tuple-element.73), channel_id=1, source_target_pairs={{0,2},{1,3},{2,0},{3,1},{4,6},{5,7},{6,4},{7,5},{8,10},{9,11},{10,... | collective-permute-start | bytes 516104 | tf_op jit(solution)/shard_map/ppermute | solution.py:364
  51.3 7.2 %collective-permute-start.9 = (bf16[224,384]{1,0:T(8,128)(2,1)S(1)}, bf16[224,384]{1,0:T(8,128)(2,1)S(1)}, u32[]{:S(2)}, u32[]{:S(2)}) collective-permute-start(bf16[224,384]{1,0:T(8,128)(2,1)S(1)} %get-tuple-element.74), channel_id=1, source_target_pairs={{0,4},{1,5},{2,6},{3,7},{4,0},{5,1},{6,2},{7,3},{8,12},{9,13},{10,... | collective-permute-start | bytes 516104 | tf_op jit(solution)/shard_map/ppermute | solution.py:364
  52.1 6.4 %collective-permute-start.10 = (bf16[224,384]{1,0:T(8,128)(2,1)S(1)}, bf16[224,384]{1,0:T(8,128)(2,1)S(1)}, u32[]{:S(2)}, u32[]{:S(2)}) collective-permute-start(bf16[224,384]{1,0:T(8,128)(2,1)S(1)} %get-tuple-element.75), channel_id=1, source_target_pairs={{0,6},{1,7},{2,4},{3,5},{4,2},{5,3},{6,0},{7,1},{8,14},{9,15},{10,... | collective-permute-start | bytes 516104 | tf_op jit(solution)/shard_map/ppermute | solution.py:364
  53.8 1.4 %collective-permute-start.11 = (bf16[192,384]{1,0:T(8,128)(2,1)S(1)}, bf16[192,384]{1,0:T(8,128)(2,1)S(1)}, u32[]{:S(2)}, u32[]{:S(2)}) collective-permute-start(bf16[192,384]{1,0:T(8,128)(2,1)S(1)} %get-tuple-element.76.refs_0_), channel_id=1, source_target_pairs={{0,1},{1,0},{2,3},{3,2},{4,5},{5,4},{6,7},{7,6},{8,9},{9,8},{10,11... | collective-permute-start | bytes 442376 | tf_op jit(solution)/shard_map/ppermute | solution.py:364
  55.7 4.2 %collective-permute-start.12 = (bf16[224,384]{1,0:T(8,128)(2,1)S(1)}, bf16[224,384]{1,0:T(8,128)(2,1)S(1)}, u32[]{:S(2)}, u32[]{:S(2)}) collective-permute-start(bf16[224,384]{1,0:T(8,128)(2,1)S(1)} %collective-permute-done.8.refs_1_.refs_2_), channel_id=1, source_target_pairs={{0,1},{1,0},{2,3},{3,2},{4,5},{5,4},{6,7},{7,6},{8,9},{9,8},{10,11... | collective-permute-start | bytes 516104 | tf_op jit(solution)/shard_map/ppermute | solution.py:364
  58.6 1.4 %collective-permute-start.13 = (bf16[224,384]{1,0:T(8,128)(2,1)S(1)}, bf16[224,384]{1,0:T(8,128)(2,1)S(1)}, u32[]{:S(2)}, u32[]{:S(2)}) collective-permute-start(bf16[224,384]{1,0:T(8,128)(2,1)S(1)} %collective-permute-done.9.refs_2_.refs_0_), channel_id=1, source_target_pairs={{0,1},{1,0},{2,3},{3,2},{4,5},{5,4},{6,7},{7,6},{8,9},{9,8},{10,11... | collective-permute-start | bytes 516104 | tf_op jit(solution)/shard_map/ppermute | solution.py:364
  58.6 1.7 %collective-permute-start.14 = (bf16[224,384]{1,0:T(8,128)(2,1)S(1)}, bf16[224,384]{1,0:T(8,128)(2,1)S(1)}, u32[]{:S(2)}, u32[]{:S(2)}) collective-permute-start(bf16[224,384]{1,0:T(8,128)(2,1)S(1)} %collective-permute-done.10.refs_3_.refs_1_), channel_id=1, source_target_pairs={{0,1},{1,0},{2,3},{3,2},{4,5},{5,4},{6,7},{7,6},{8,9},{9,8},{10,11... | collective-permute-start | bytes 516104 | tf_op jit(solution)/shard_map/ppermute | solution.py:364

commit v10 on v9

--- a/solution.py
+++ b/solution.py
@@ -255,14 +255,12 @@
 
 
 def line_kernel(*refs):
-    parts, sources, (out_ref, kept_ref) = refs[:-4], refs[-4:-2], refs[-2:]
-    rows = parts[0].shape[0]
-    out_ref[0:rows, :] = total_of([*parts, parts[0]]).astype(bf16)
+    parts, sources, (out_ref, kept_ref, sent_ref) = refs[:-5], refs[-5:-3], refs[-3:]
+    out_ref[...] = total_of([*parts, out_ref]).astype(bf16)
     half = sources[0].shape[0] // 2
-    for first, ref, at in ((0, kept_ref, 0), (half, out_ref, rows)):
-        for source in sources:
-            ref[at : at + half, :] = source[first : first + half, :]
-            at += half
+    for first, ref in ((0, kept_ref), (half, sent_ref)):
+        for i, source in enumerate(sources):
+            ref[i * half : (i + 1) * half, :] = source[first : first + half, :]
 
 
 def plane_kernel(factor, *refs):
@@ -270,7 +268,7 @@
     rows = outs[0].shape[0]
     mine = (total_of([*parts, outs[0]]) * factor).astype(bf16)
     outs[0][...] = mine
-    sources = [kept_ref[...].astype(f32), came_ref[rows:, :].astype(f32)]
+    sources = [kept_ref[...].astype(f32), came_ref[...].astype(f32)]
     block = sources[0].shape[0] // 8
     for plane in range(4):
         riders = jnp.concatenate(
@@ -385,13 +383,11 @@
     if riding:
         high = call(cores_kernel, [rider] * 2, count=2)(ride, came)
         riders = [high[0]] + exchange([high[1]], [16], size)
-        total, kept = call(
-            line_kernel, [struct((rows + ride.shape[0], double), bf16), rider], count=len(parts) + 2
-        )(*parts, *riders)
+        parts, riders = lax.optimization_barrier((parts, riders))
+        total = call(functools.partial(total_kernel, 1.0), piece, count=len(parts))(*parts)
         (came,) = exchange([total], [8], size)
-        second = call(functools.partial(total_kernel, 1.0), piece, count=2)
-        total = second(total, came)
-        (last,) = exchange([total], [24], size)
+        total, kept, sent = call(line_kernel, [piece, rider, rider], count=4)(total, came, *riders)
+        last, came = exchange([total, sent], [24, 8], size)
         joined = struct((rows + ride.shape[0] // 2, double), bf16)
         mine, *sends, ride = call(
             functools.partial(plane_kernel, factor),

time: 61.8 us -> 61.4 us (level)
    ppermute x15 -> x16, waiting for transfers between devices: 20.4 us -> 20 us  [exchange(): lax.ppermute(value if not isinstance(value, list) else value[i], 'seq', [...]
    ppermute x15 -> x16, starting transfers between devices: 11.6 us -> 11.6 us  [exchange(): lax.ppermute(value if not isinstance(value, list) else value[i], 'seq', [...]
  transfers between devices with their start and end apart: 16 -> 17, of which waited for: 11 -> 11; matrix products, arithmetic and copies ran while one was open for 0% -> 0% of each run, Pallas kernels for 7% -> 7%
where the time goes in v10:
time: 61.4 us; the launch traced here: 61 us
  waiting for transfers between devices  23.8 us (39%)
  starting transfers between devices  18.9 us (31%)
  Pallas kernels  13.3 us (22%)
  local copies, waits for them, and re-layouts  4.17 us (7%)
  between operations  0.75 us (1%)
    ppermute x16, waiting for transfers between devices, exchange(): lax.ppermute(value if not isinstance(value, list) else value[i], 'seq', [...  20 us
    ppermute x16, starting transfers between devices, exchange(): lax.ppermute(value if not isinstance(value, list) else value[i], 'seq', [...  11.6 us
    all_to_all x1, starting transfers between devices, shards(): both = lax.all_to_all(both, 'seq', split_axis=0, concat_axis=0, tiled=True)  7.3 us
    pallas_call x1, Pallas kernels, shards(): call(functools.partial(switch_kernel, levels, block), [struct((units, dou...  6.05 us
    unnamed x10, local copies, waits for them, and re-layouts  4.17 us
    all_to_all x1, waiting for transfers between devices, shards(): both = lax.all_to_all(both, 'seq', split_axis=0, concat_axis=0, tiled=True)  3.82 us
    pallas_call x2, Pallas kernels, place(): call(functools.partial(place_kernel, 1, pieces, slots, len(placed)), shap...  2.12 us
    pallas_call x1, Pallas kernels, shards(): call(pack_kernel, struct((size, block, double), bf16), scratch=[pltpu.VME...  1.74 us
  transfers between devices with their start and end apart: 17, of which 11 were waited for; matrix products, arithmetic and copies ran while one was open for 0% of the time, Pallas kernels for 7%

profile of v10, /device:TPU:0, one launch (start us, length us, event | category | flops | bytes accessed | tf_op | source)
XLA Modules:
  0.0 61.0 jit_solution(8883806732546623958)
XLA Ops:
  0.6 1.7 %shard_map.94 = bf16[32,8,384]{2,1,0:T(8,128)(2,1)} custom-call(bf16[192,256]{1,0:T(8,128)(2,1)} %bitcast.4, bf16[192,256]{1,0:T(8,128)(2,1)} %bitcast.5), custom_call_target="tpu_custom_call" | custom-call | bytes 7000000 | tf_op jit(solution)/shard_map/pallas_call | solution.py:427
  2.4 7.3 %all-to-all-start = ((bf16[32,8,384]{2,1,0:T(8,128)(2,1)}), bf16[32,8,384]{2,1,0:T(8,128)(2,1)S(1)}, u32[]{:S(2)}, u32[]{:S(2)}) async-start(bf16[32,8,384]{2,1,0:T(8,128)(2,1)} %shard_map.94), calls=%async_computation | async-start | bytes 393216 | tf_op jit(solution)/shard_map/all_to_all | solution.py:437
  9.7 1.1 %copy-done = bf16[384,768]{1,0:T(8,128)(2,1)S(1)} copy-done((bf16[384,768]{1,0:T(8,128)(2,1)S(1)}, bf16[384,768]{1,0:T(8,128)(2,1)}, u32[]{:S(2)}) %copy-start) | copy-done | bytes 589848
  10.8 1.1 %copy-done.1 = bf16[768,384]{1,0:T(8,128)(2,1)S(1)} copy-done((bf16[768,384]{1,0:T(8,128)(2,1)S(1)}, bf16[768,384]{1,0:T(8,128)(2,1)}, u32[]{:S(2)}) %copy-start.1) | copy-done | bytes 589848
  13.9 0.9 %shard_map.95 = (bf16[512,768]{1,0:T(8,128)(2,1)S(1)}, bf16[768,512]{1,0:T(8,128)(2,1)S(1)}, bf16[768,512]{1,0:T(8,128)(2,1)S(1)}, bf16[512,768]{1,0:T(8,128)(2,...) custom-call(bf16[384,768]{1,0:T(8,128)(2,1)S(1)} %copy-done, ...), custom_call_target="tpu_custom_call" | custom-call | tf_op jit(solution)/shard_map/pallas_call | solution.py:439
  14.8 3.8 %all-to-all-done.both_ref = bf16[32,8,384]{2,1,0:T(8,128)(2,1)S(1)} async-done(((bf16[32,8,384]{2,1,0:T(8,128)(2,1)}), bf16[32,8,384]{2,1,0:T(8,128)(2,1)S(1)}, u32[]{:S(2)}, u32[]{:S(2)}) %all-to-all-start) | async-done | bytes 196640 | tf_op jit(solution)/shard_map/all_to_all | solution.py:437
  18.6 6.0 %shard_map.96 = (bf16[768,384]{1,0:T(8,128)(2,1)S(1)}, bf16[640,512]{1,0:T(8,128)(2,1)S(1)}, bf16[640,768]{1,0:T(8,128)(2,1)S(1)}, bf16[640,768]{1,0:T(8,128)(2,...) custom-call(s32[1]{0:T(128)} %bitcast.me_ref, ...), custom_call_target="tpu_custom_call" | custom-call | tf_op jit(solution)/shard_map/pallas_call | solution.py:449
  24.6 0.7 %collective-permute-start = (bf16[768,384]{1,0:T(8,128)(2,1)S(1)}, bf16[768,384]{1,0:T(8,128)(2,1)S(1)}, u32[]{:S(2)}, u32[]{:S(2)}) collective-permute-start(bf16[768,384]{1,0:T(8,128)(2,1)S(1)} %get-tuple-element.63), channel_id=1, source_target_pairs={{0,1},{1,0},{2,3},{3,2},{4,5},{5,4},{6,7},{7,6},{8,9},{9,8},{10,11... | collective-permute-start | bytes 1769480 | tf_op jit(solution)/shard_map/ppermute | solution.py:362
  26.0 0.8 %shard_map.97.keep_ref = f32[768,384]{1,0:T(8,128)S(1)} custom-call(s32[1]{0:T(128)} %bitcast.me_ref, bf16[640,512]{1,0:T(8,128)(2,1)S(1)} %get-tuple-element.59.refs_0_, bf16[640,768]{1,0:T(8,128)(2,1)S(1)} %get-tuple-element.60.refs_1_.pre_ref, bf16[640,768]{1,0:T(8,128)(2,1)S(1)} %get-tuple-element.61.refs_2_, bf16[640,384]{1,0:T(8,128)(2,1)S(1)} %get-tuple-element.62.refs_3_), custom_call_target="tpu_custom_call" | custom-call | flops 377487360 | bytes 3932160 | tf_op jit(solution)/shard_map/pallas_call | solution.py:477
  27.8 1.2 %collective-permute-start.3 = (bf16[192,384]{1,0:T(8,128)(2,1)S(1)}, bf16[192,384]{1,0:T(8,128)(2,1)S(1)}, u32[]{:S(2)}, u32[]{:S(2)}) collective-permute-start(bf16[192,384]{1,0:T(8,128)(2,1)S(1)} %get-tuple-element.71), channel_id=1, source_target_pairs={{0,4},{1,5},{2,6},{3,7},{4,0},{5,1},{6,2},{7,3},{8,12},{9,13},{10,... | collective-permute-start | bytes 442376 | tf_op jit(solution)/shard_map/ppermute | solution.py:362
  29.0 1.9 %collective-permute-start.4 = (bf16[192,384]{1,0:T(8,128)(2,1)S(1)}, bf16[192,384]{1,0:T(8,128)(2,1)S(1)}, u32[]{:S(2)}, u32[]{:S(2)}) collective-permute-start(bf16[192,384]{1,0:T(8,128)(2,1)S(1)} %get-tuple-element.72), channel_id=1, source_target_pairs={{0,6},{1,7},{2,4},{3,5},{4,2},{5,3},{6,0},{7,1},{8,14},{9,15},{10,... | collective-permute-start | bytes 442376 | tf_op jit(solution)/shard_map/ppermute | solution.py:362
  31.7 4.9 %collective-permute-done.5.refs_3_ = bf16[64,384]{1,0:T(8,128)(2,1)S(1)} collective-permute-done((bf16[64,384]{1,0:T(8,128)(2,1)S(1)}, bf16[64,384]{1,0:T(8,128)(2,1)S(1)}, u32[]{:S(2)}, u32[]{:S(2)}) %collective-permute-start.5) | collective-permute-done | bytes 49184 | tf_op jit(solution)/shard_map/ppermute | solution.py:362
  36.7 0.8 %collective-permute-start.6 = (bf16[192,384]{1,0:T(8,128)(2,1)S(1)}, bf16[192,384]{1,0:T(8,128)(2,1)S(1)}, u32[]{:S(2)}, u32[]{:S(2)}) collective-permute-start(bf16[192,384]{1,0:T(8,128)(2,1)S(1)} %shard_map.101.refs_0_), channel_id=1, source_target_pairs={{0,8},{1,9},{2,10},{3,11},{4,12},{5,13},{6,14},{7,15},{8,0},{9,1},... | collective-permute-start | bytes 442376 | tf_op jit(solution)/shard_map/ppermute | solution.py:362
  37.6 4.4 %collective-permute-done.6.refs_1_ = bf16[192,384]{1,0:T(8,128)(2,1)S(1)} collective-permute-done((bf16[192,384]{1,0:T(8,128)(2,1)S(1)}, bf16[192,384]{1,0:T(8,128)(2,1)S(1)}, u32[]{:S(2)}, u32[]{:S(2)}) %collective-permute-start.6) | collective-permute-done | bytes 147488 | tf_op jit(solution)/shard_map/ppermute | solution.py:362
  42.0 1.7 %collective-permute-start.7 = (bf16[192,384]{1,0:T(8,128)(2,1)S(1)}, bf16[192,384]{1,0:T(8,128)(2,1)S(1)}, u32[]{:S(2)}, u32[]{:S(2)}) collective-permute-start(bf16[192,384]{1,0:T(8,128)(2,1)S(1)} %get-tuple-element.83.refs_0_), channel_id=1, source_target_pairs={{0,24},{1,25},{2,26},{3,27},{4,28},{5,29},{6,30},{7,31},{8,16},{9,... | collective-permute-start | bytes 442376 | tf_op jit(solution)/shard_map/ppermute | solution.py:362
  43.7 5.7 %collective-permute-done.8.refs_3_ = bf16[64,384]{1,0:T(8,128)(2,1)S(1)} collective-permute-done((bf16[64,384]{1,0:T(8,128)(2,1)S(1)}, bf16[64,384]{1,0:T(8,128)(2,1)S(1)}, u32[]{:S(2)}, u32[]{:S(2)}) %collective-permute-start.8) | collective-permute-done | bytes 49184 | tf_op jit(solution)/shard_map/ppermute | solution.py:362
  49.4 1.5 %collective-permute-start.9 = (bf16[224,384]{1,0:T(8,128)(2,1)S(1)}, bf16[224,384]{1,0:T(8,128)(2,1)S(1)}, u32[]{:S(2)}, u32[]{:S(2)}) collective-permute-start(bf16[224,384]{1,0:T(8,128)(2,1)S(1)} %get-tuple-element.87), channel_id=1, source_target_pairs={{0,2},{1,3},{2,0},{3,1},{4,6},{5,7},{6,4},{7,5},{8,10},{9,11},{10,... | collective-permute-start | bytes 516104 | tf_op jit(solution)/shard_map/ppermute | solution.py:362
  50.9 0.7 %collective-permute-start.10 = (bf16[224,384]{1,0:T(8,128)(2,1)S(1)}, bf16[224,384]{1,0:T(8,128)(2,1)S(1)}, u32[]{:S(2)}, u32[]{:S(2)}) collective-permute-start(bf16[224,384]{1,0:T(8,128)(2,1)S(1)} %get-tuple-element.88), channel_id=1, source_target_pairs={{0,4},{1,5},{2,6},{3,7},{4,0},{5,1},{6,2},{7,3},{8,12},{9,13},{10,... | collective-permute-start | bytes 516104 | tf_op jit(solution)/shard_map/ppermute | solution.py:362
  51.7 1.3 %collective-permute-start.11 = (bf16[224,384]{1,0:T(8,128)(2,1)S(1)}, bf16[224,384]{1,0:T(8,128)(2,1)S(1)}, u32[]{:S(2)}, u32[]{:S(2)}) collective-permute-start(bf16[224,384]{1,0:T(8,128)(2,1)S(1)} %get-tuple-element.89), channel_id=1, source_target_pairs={{0,6},{1,7},{2,4},{3,5},{4,2},{5,3},{6,0},{7,1},{8,14},{9,15},{10,... | collective-permute-start | bytes 516104 | tf_op jit(solution)/shard_map/ppermute | solution.py:362
  53.0 1.4 %collective-permute-done.12.refs_1_ = bf16[192,384]{1,0:T(8,128)(2,1)S(1)} collective-permute-done((bf16[192,384]{1,0:T(8,128)(2,1)S(1)}, bf16[192,384]{1,0:T(8,128)(2,1)S(1)}, u32[]{:S(2)}, u32[]{:S(2)}) %collective-permute-start.12) | collective-permute-done | bytes 147488 | tf_op jit(solution)/shard_map/ppermute | solution.py:362
  54.9 1.0 %shard_map.105 = (f32[384,768]{1,0:T(8,128)}, f32[768,384]{1,0:T(8,128)}) custom-call(s32[1]{0:T(128)} %bitcast.me_ref, bf16[192,384]{1,0:T(8,128)(2,1)S(1)} %get-tuple-element.90.refs_0_, bf16[192,384]{1,0:T(8,128)(2,1)S(1)} %collective-permute-done.12.refs_1_, bf16[224,384]{1,0:T(8,128)(2,1)S(1)} %collective-permute-done.9.refs_1_.refs_2_), custom_call_target="tpu_custom_call" | custom-call | tf_op jit(solution)/shard_map/pallas_call | solution.py:335
  55.8 2.3 %collective-permute-done.10.refs_2_.refs_0_ = bf16[224,384]{1,0:T(8,128)(2,1)S(1)} collective-permute-done((bf16[224,384]{1,0:T(8,128)(2,1)S(1)}, bf16[224,384]{1,0:T(8,128)(2,1)S(1)}, u32[]{:S(2)}, u32[]{:S(2)}) %collective-permute-start.10) | collective-permute-done | bytes 172064 | tf_op jit(solution)/shard_map/ppermute | solution.py:362
  58.7 0.8 %shard_map.104 = bf16[192,256]{1,0:T(8,128)(2,1)} custom-call(s32[1]{0:T(128)} %bitcast.me_ref, bf16[32,384]{1,0:T(8,128)(2,1)S(1)} %get-tuple-element.86.refs_0_, bf16[224,384]{1,0:T(8,128)(2,1)S(1)} %collective-permute-done.9.refs_1_.refs_2_, bf16[224,384]{1,0:T(8,128)(2,1)S(1)} %collective-permute-done.10.refs_2_.refs_0_, ...), custom_call_target="tpu_custom_call" | custom-call | tf_op jit(solution)/shard_map/pallas_call | solution.py:495
  59.8 1.2 %shard_map.106 = (f32[384,768]{1,0:T(8,128)}, f32[768,384]{1,0:T(8,128)}) custom-call(s32[1]{0:T(128)} %bitcast.me_ref, bf16[224,384]{1,0:T(8,128)(2,1)S(1)} %collective-permute-done.10.refs_2_.refs_0_, bf16[224,384]{1,0:T(8,128)(2,1)S(1)} %collective-permute-done.11.refs_3_.refs_1_, ...), custom_call_target="tpu_custom_call", output_to_operand_aliasing={{0}: (6, {}), {1}: (7, {})} | custom-call | tf_op jit(solution)/shard_map/pallas_call | solution.py:335
  (33 shorter events, 6.1 us)
Async XLA Ops:
  2.4 16.2 %all-to-all-start = ((bf16[32,8,384]{2,1,0:T(8,128)(2,1)}), bf16[32,8,384]{2,1,0:T(8,128)(2,1)S(1)}, u32[]{:S(2)}, u32[]{:S(2)}) async-start(bf16[32,8,384]{2,1,0:T(8,128)(2,1)} %shard_map.94), calls=%async_computation | async-start | bytes 393216 | tf_op jit(solution)/shard_map/all_to_all | solution.py:437
  9.7 1.1 %copy-start = (bf16[384,768]{1,0:T(8,128)(2,1)S(1)}, bf16[384,768]{1,0:T(8,128)(2,1)}, u32[]{:S(2)}) copy-start(bf16[384,768]{1,0:T(8,128)(2,1)} %w_in_ref.1) | copy-start | bytes 1769476
  10.8 1.1 %copy-start.1 = (bf16[768,384]{1,0:T(8,128)(2,1)S(1)}, bf16[768,384]{1,0:T(8,128)(2,1)}, u32[]{:S(2)}) copy-start(bf16[768,384]{1,0:T(8,128)(2,1)} %w_out_ref.1) | copy-start | bytes 1769476
  11.8 0.7 %copy-start.2 = (f32[768]{0:T(1024)S(1)}, f32[768]{0:T(1024)}, u32[]{:S(2)}) copy-start(f32[768]{0:T(1024)} %bias_ref.1) | copy-start | bytes 9220
  12.5 0.7 %copy-start.3 = (f32[384]{0:T(512)S(1)}, f32[384]{0:T(512)}, u32[]{:S(2)}) copy-start(f32[384]{0:T(512)} %logit_ref.1) | copy-start | bytes 4612
  13.2 0.7 %copy-start.4 = (f32[384]{0:T(512)S(1)}, f32[384]{0:T(512)}, u32[]{:S(2)}) copy-start(f32[384]{0:T(512)} %scale_ref.1) | copy-start | bytes 4612
  24.6 2.6 %collective-permute-start = (bf16[768,384]{1,0:T(8,128)(2,1)S(1)}, bf16[768,384]{1,0:T(8,128)(2,1)S(1)}, u32[]{:S(2)}, u32[]{:S(2)}) collective-permute-start(bf16[768,384]{1,0:T(8,128)(2,1)S(1)} %get-tuple-element.63), channel_id=1, source_target_pairs={{0,1},{1,0},{2,3},{3,2},{4,5},{5,4},{6,7},{7,6},{8,9},{9,8},{10,11... | collective-permute-start | bytes 1769480 | tf_op jit(solution)/shard_map/ppermute | solution.py:362
  25.9 1.3 %collective-permute-start.1 = (bf16[64,384]{1,0:T(8,128)(2,1)S(1)}, bf16[64,384]{1,0:T(8,128)(2,1)S(1)}, u32[]{:S(2)}, u32[]{:S(2)}) collective-permute-start(bf16[64,384]{1,0:T(8,128)(2,1)S(1)} %get-tuple-element.67), channel_id=1, source_target_pairs={{0,1},{1,0},{2,3},{3,2},{4,5},{5,4},{6,7},{7,6},{8,9},{9,8},{10,11... | collective-permute-start | bytes 147464 | tf_op jit(solution)/shard_map/ppermute | solution.py:362
  27.3 9.2 %collective-permute-start.2 = (bf16[192,384]{1,0:T(8,128)(2,1)S(1)}, bf16[192,384]{1,0:T(8,128)(2,1)S(1)}, u32[]{:S(2)}, u32[]{:S(2)}) collective-permute-start(bf16[192,384]{1,0:T(8,128)(2,1)S(1)} %get-tuple-element.70), channel_id=1, source_target_pairs={{0,2},{1,3},{2,0},{3,1},{4,6},{5,7},{6,4},{7,5},{8,10},{9,11},{10,... | collective-permute-start | bytes 442376 | tf_op jit(solution)/shard_map/ppermute | solution.py:362
  27.8 8.9 %collective-permute-start.3 = (bf16[192,384]{1,0:T(8,128)(2,1)S(1)}, bf16[192,384]{1,0:T(8,128)(2,1)S(1)}, u32[]{:S(2)}, u32[]{:S(2)}) collective-permute-start(bf16[192,384]{1,0:T(8,128)(2,1)S(1)} %get-tuple-element.71), channel_id=1, source_target_pairs={{0,4},{1,5},{2,6},{3,7},{4,0},{5,1},{6,2},{7,3},{8,12},{9,13},{10,... | collective-permute-start | bytes 442376 | tf_op jit(solution)/shard_map/ppermute | solution.py:362
  29.0 7.7 %collective-permute-start.4 = (bf16[192,384]{1,0:T(8,128)(2,1)S(1)}, bf16[192,384]{1,0:T(8,128)(2,1)S(1)}, u32[]{:S(2)}, u32[]{:S(2)}) collective-permute-start(bf16[192,384]{1,0:T(8,128)(2,1)S(1)} %get-tuple-element.72), channel_id=1, source_target_pairs={{0,6},{1,7},{2,4},{3,5},{4,2},{5,3},{6,0},{7,1},{8,14},{9,15},{10,... | collective-permute-start | bytes 442376 | tf_op jit(solution)/shard_map/ppermute | solution.py:362
  31.0 5.6 %collective-permute-start.5 = (bf16[64,384]{1,0:T(8,128)(2,1)S(1)}, bf16[64,384]{1,0:T(8,128)(2,1)S(1)}, u32[]{:S(2)}, u32[]{:S(2)}) collective-permute-start(bf16[64,384]{1,0:T(8,128)(2,1)S(1)} %get-tuple-element.76), channel_id=1, source_target_pairs={{0,16},{1,17},{2,18},{3,19},{4,20},{5,21},{6,22},{7,23},{8,24},{9,... | collective-permute-start | bytes 147464 | tf_op jit(solution)/shard_map/ppermute | solution.py:362
  36.7 5.2 %collective-permute-start.6 = (bf16[192,384]{1,0:T(8,128)(2,1)S(1)}, bf16[192,384]{1,0:T(8,128)(2,1)S(1)}, u32[]{:S(2)}, u32[]{:S(2)}) collective-permute-start(bf16[192,384]{1,0:T(8,128)(2,1)S(1)} %shard_map.101.refs_0_), channel_id=1, source_target_pairs={{0,8},{1,9},{2,10},{3,11},{4,12},{5,13},{6,14},{7,15},{8,0},{9,1},... | collective-permute-start | bytes 442376 | tf_op jit(solution)/shard_map/ppermute | solution.py:362
  42.0 7.3 %collective-permute-start.7 = (bf16[192,384]{1,0:T(8,128)(2,1)S(1)}, bf16[192,384]{1,0:T(8,128)(2,1)S(1)}, u32[]{:S(2)}, u32[]{:S(2)}) collective-permute-start(bf16[192,384]{1,0:T(8,128)(2,1)S(1)} %get-tuple-element.83.refs_0_), channel_id=1, source_target_pairs={{0,24},{1,25},{2,26},{3,27},{4,28},{5,29},{6,30},{7,31},{8,16},{9,... | collective-permute-start | bytes 442376 | tf_op jit(solution)/shard_map/ppermute | solution.py:362
  43.7 5.7 %collective-permute-start.8 = (bf16[64,384]{1,0:T(8,128)(2,1)S(1)}, bf16[64,384]{1,0:T(8,128)(2,1)S(1)}, u32[]{:S(2)}, u32[]{:S(2)}) collective-permute-start(bf16[64,384]{1,0:T(8,128)(2,1)S(1)} %get-tuple-element.85), channel_id=1, source_target_pairs={{0,8},{1,9},{2,10},{3,11},{4,12},{5,13},{6,14},{7,15},{8,0},{9,1},... | collective-permute-start | bytes 147464 | tf_op jit(solution)/shard_map/ppermute | solution.py:362
  49.4 5.5 %collective-permute-start.9 = (bf16[224,384]{1,0:T(8,128)(2,1)S(1)}, bf16[224,384]{1,0:T(8,128)(2,1)S(1)}, u32[]{:S(2)}, u32[]{:S(2)}) collective-permute-start(bf16[224,384]{1,0:T(8,128)(2,1)S(1)} %get-tuple-element.87), channel_id=1, source_target_pairs={{0,2},{1,3},{2,0},{3,1},{4,6},{5,7},{6,4},{7,5},{8,10},{9,11},{10,... | collective-permute-start | bytes 516104 | tf_op jit(solution)/shard_map/ppermute | solution.py:362
  50.9 7.2 %collective-permute-start.10 = (bf16[224,384]{1,0:T(8,128)(2,1)S(1)}, bf16[224,384]{1,0:T(8,128)(2,1)S(1)}, u32[]{:S(2)}, u32[]{:S(2)}) collective-permute-start(bf16[224,384]{1,0:T(8,128)(2,1)S(1)} %get-tuple-element.88), channel_id=1, source_target_pairs={{0,4},{1,5},{2,6},{3,7},{4,0},{5,1},{6,2},{7,3},{8,12},{9,13},{10,... | collective-permute-start | bytes 516104 | tf_op jit(solution)/shard_map/ppermute | solution.py:362
  51.7 6.5 %collective-permute-start.11 = (bf16[224,384]{1,0:T(8,128)(2,1)S(1)}, bf16[224,384]{1,0:T(8,128)(2,1)S(1)}, u32[]{:S(2)}, u32[]{:S(2)}) collective-permute-start(bf16[224,384]{1,0:T(8,128)(2,1)S(1)} %get-tuple-element.89), channel_id=1, source_target_pairs={{0,6},{1,7},{2,4},{3,5},{4,2},{5,3},{6,0},{7,1},{8,14},{9,15},{10,... | collective-permute-start | bytes 516104 | tf_op jit(solution)/shard_map/ppermute | solution.py:362
  53.0 1.4 %collective-permute-start.12 = (bf16[192,384]{1,0:T(8,128)(2,1)S(1)}, bf16[192,384]{1,0:T(8,128)(2,1)S(1)}, u32[]{:S(2)}, u32[]{:S(2)}) collective-permute-start(bf16[192,384]{1,0:T(8,128)(2,1)S(1)} %get-tuple-element.90.refs_0_), channel_id=1, source_target_pairs={{0,1},{1,0},{2,3},{3,2},{4,5},{5,4},{6,7},{7,6},{8,9},{9,8},{10,11... | collective-permute-start | bytes 442376 | tf_op jit(solution)/shard_map/ppermute | solution.py:362
  54.9 4.7 %collective-permute-start.13 = (bf16[224,384]{1,0:T(8,128)(2,1)S(1)}, bf16[224,384]{1,0:T(8,128)(2,1)S(1)}, u32[]{:S(2)}, u32[]{:S(2)}) collective-permute-start(bf16[224,384]{1,0:T(8,128)(2,1)S(1)} %collective-permute-done.9.refs_1_.refs_2_), channel_id=1, source_target_pairs={{0,1},{1,0},{2,3},{3,2},{4,5},{5,4},{6,7},{7,6},{8,9},{9,8},{10,11... | collective-permute-start | bytes 516104 | tf_op jit(solution)/shard_map/ppermute | solution.py:362
  58.2 1.4 %collective-permute-start.14 = (bf16[224,384]{1,0:T(8,128)(2,1)S(1)}, bf16[224,384]{1,0:T(8,128)(2,1)S(1)}, u32[]{:S(2)}, u32[]{:S(2)}) collective-permute-start(bf16[224,384]{1,0:T(8,128)(2,1)S(1)} %collective-permute-done.10.refs_2_.refs_0_), channel_id=1, source_target_pairs={{0,1},{1,0},{2,3},{3,2},{4,5},{5,4},{6,7},{7,6},{8,9},{9,8},{10,11... | collective-permute-start | bytes 516104 | tf_op jit(solution)/shard_map/ppermute | solution.py:362
  58.2 1.7 %collective-permute-start.15 = (bf16[224,384]{1,0:T(8,128)(2,1)S(1)}, bf16[224,384]{1,0:T(8,128)(2,1)S(1)}, u32[]{:S(2)}, u32[]{:S(2)}) collective-permute-start(bf16[224,384]{1,0:T(8,128)(2,1)S(1)} %collective-permute-done.11.refs_3_.refs_1_), channel_id=1, source_target_pairs={{0,1},{1,0},{2,3},{3,2},{4,5},{5,4},{6,7},{7,6},{8,9},{9,8},{10,11... | collective-permute-start | bytes 516104 | tf_op jit(solution)/shard_map/ppermute | solution.py:362

commit v11 on v10

--- a/solution.py
+++ b/solution.py
@@ -60,17 +60,35 @@
     return part if width == lanes else jnp.concatenate([part, jnp.zeros((rows, lanes - width), part.dtype)], axis=1)
 
 
-def pack_kernel(x_ref, g_ref, out_ref, x_s, g_s, sem):
-    copies = [
-        pltpu.make_async_copy(ref, scratch, sem.at[side])
-        for side, (ref, scratch) in enumerate(((x_ref, x_s), (g_ref, g_s)))
+def pack_kernel(x_ref, g_ref, out_ref, both_s, rows_s, in_sem, out_sem):
+    width, count = x_ref.shape[0], in_sem.shape[1]
+    some = width // count
+    loads = [
+        pltpu.make_async_copy(
+            ref.at[part * some : (part + 1) * some, :],
+            both_s.at[side * width + part * some : side * width + (part + 1) * some, :],
+            in_sem.at[side, part],
+        )
+        for side, ref in enumerate((x_ref, g_ref))
+        for part in range(count)
     ]
-    for copy in copies:
-        copy.start()
-    for copy in copies:
-        copy.wait()
-    both = jnp.concatenate([x_s[...], g_s[...]], axis=0).T
-    out_ref[...] = both.astype(f32).reshape(out_ref.shape).astype(bf16)
+    for load in loads:
+        load.start()
+    for load in loads:
+        load.wait()
+    blocks = rows_s.shape[1]
+    stores = []
+    for part in range(rows_s.shape[0]):
+        positions = blocks * rows_s.shape[2]
+        turned = both_s[:, part * positions : (part + 1) * positions].T
+        rows_s[part] = turned.astype(f32).reshape(rows_s.shape[1:]).astype(bf16)
+        store = pltpu.make_async_copy(
+            rows_s.at[part], out_ref.at[part * blocks : (part + 1) * blocks], out_sem.at[part]
+        )
+        store.start()
+        stores.append(store)
+    for store in stores:
+        store.wait()
 
 
 def fetch_kernel(w_in_ref, w_out_ref, bias_ref, logit_ref, scale_ref, *refs):
@@ -121,7 +139,7 @@
         inverse = lax.rsqrt(mean_of([part * part for part in centered], double) + epsilon)
         normed = [part * inverse for part in centered]
         low = jnp.concatenate([part.astype(bf16) for part in normed], axis=1)
-        low_s[at, :] = low
+        low_s[at, :] = jnp.concatenate([part[:, :width].astype(bf16) for part in normed], axis=1)
         inverse_s[at, :] = inverse
         for side in sides:
             normed_s[side, at, :] = normed[side]
@@ -211,7 +229,6 @@
 
 def put_products(out_first, half_ref, low_ref, pre_ref, act_ref, bg_ref):
     units, double = pre_ref.shape[1], bg_ref.shape[1]
-    width, lanes = double // 2, low_ref.shape[1] // 2
 
     @pl.when(out_first)
     def _():
@@ -220,7 +237,6 @@
     @pl.when(jnp.logical_not(out_first))
     def _():
         grad_in = dot(low_ref[...], pre_ref[...], (0, 0))
-        grad_in = jnp.concatenate([grad_in[side * lanes : side * lanes + width] for side in range(2)], axis=0)
         for first in range(0, units, double):
             half_ref[first : first + double, :] = grad_in[:, first : first + double].astype(half_ref.dtype)
 
@@ -424,11 +440,18 @@
     half = rows // 2
     me = lax.axis_index("seq").astype(jnp.int32).reshape(1)
     if block % 8 == 0:
+        parts = rows // 128
         both = call(
             pack_kernel,
             struct((size, block, double), bf16),
-            scratch=[pltpu.VMEM((width, rows), bf16)] * 2 + [pltpu.SemaphoreType.DMA((2,))],
+            scratch=[
+                pltpu.VMEM((double, rows), bf16),
+                pltpu.VMEM((parts, size // parts, block, double), bf16),
+                pltpu.SemaphoreType.DMA((2, 2)),
+                pltpu.SemaphoreType.DMA((parts,)),
+            ],
             specs=[HBM] * 2,
+            out_specs=HBM,
             grant=None,
             cost_estimate=pl.CostEstimate(flops=0, bytes_accessed=7 * 10**6, transcendentals=0),
         )(saved_input.T, cotangent.T)
@@ -450,7 +473,7 @@
         functools.partial(switch_kernel, levels, block),
         [
             struct((units, double), bf16),
-            struct((total, 2 * lanes), bf16),
+            struct((total, double), bf16),
             struct((total, units), bf16),
             struct((total, units), bf16),
             struct((total, double), bf16),

time: 61.4 us -> 61.4 us (level)
  transfers between devices with their start and end apart: 17 -> 17, of which waited for: 11 -> 11; matrix products, arithmetic and copies ran while one was open for 0% -> 0% of each run, Pallas kernels for 7% -> 6%
where the time goes in v11:
time: 61.4 us; the launch traced here: 61 us
  waiting for transfers between devices  24.1 us (39%)
  starting transfers between devices  18.8 us (31%)
  Pallas kernels  13.1 us (21%)
  local copies, waits for them, and re-layouts  4.17 us (7%)
  between operations  0.75 us (1%)
    ppermute x16, waiting for transfers between devices, exchange(): lax.ppermute(value if not isinstance(value, list) else value[i], 'seq', [...  20.3 us
    ppermute x16, starting transfers between devices, exchange(): lax.ppermute(value if not isinstance(value, list) else value[i], 'seq', [...  11.5 us
    all_to_all x1, starting transfers between devices, shards(): both = lax.all_to_all(both, 'seq', split_axis=0, concat_axis=0, tiled=True)  7.3 us
    pallas_call x1, Pallas kernels, shards(): call(functools.partial(switch_kernel, levels, block), [struct((units, dou...  6.05 us
    unnamed x10, local copies, waits for them, and re-layouts  4.17 us
    all_to_all x1, waiting for transfers between devices, shards(): both = lax.all_to_all(both, 'seq', split_axis=0, concat_axis=0, tiled=True)  3.82 us
    pallas_call x2, Pallas kernels, place(): call(functools.partial(place_kernel, 1, pieces, slots, len(placed)), shap...  2.12 us
    pallas_call x1, Pallas kernels, shards(): call(pack_kernel, struct((size, block, double), bf16), scratch=[pltpu.VME...  1.68 us
  transfers between devices with their start and end apart: 17, of which 11 were waited for; matrix products, arithmetic and copies ran while one was open for 0% of the time, Pallas kernels for 6%

profile of v11, /device:TPU:0, one launch (start us, length us, event | category | flops | bytes accessed | tf_op | source)
XLA Modules:
  0.0 61.0 jit_solution(14074078395830828995)
XLA Ops:
  0.6 1.7 %shard_map.94 = bf16[32,8,384]{2,1,0:T(8,128)(2,1)} custom-call(bf16[192,256]{1,0:T(8,128)(2,1)} %bitcast.4, bf16[192,256]{1,0:T(8,128)(2,1)} %bitcast.5), custom_call_target="tpu_custom_call" | custom-call | bytes 7000000 | tf_op jit(solution)/shard_map/pallas_call | solution.py:444
  2.3 7.3 %all-to-all-start = ((bf16[32,8,384]{2,1,0:T(8,128)(2,1)}), bf16[32,8,384]{2,1,0:T(8,128)(2,1)S(1)}, u32[]{:S(2)}, u32[]{:S(2)}) async-start(bf16[32,8,384]{2,1,0:T(8,128)(2,1)} %shard_map.94), calls=%async_computation | async-start | bytes 393216 | tf_op jit(solution)/shard_map/all_to_all | solution.py:460
  9.6 1.1 %copy-done = bf16[384,768]{1,0:T(8,128)(2,1)S(1)} copy-done((bf16[384,768]{1,0:T(8,128)(2,1)S(1)}, bf16[384,768]{1,0:T(8,128)(2,1)}, u32[]{:S(2)}) %copy-start) | copy-done | bytes 589848
  10.7 1.1 %copy-done.1 = bf16[768,384]{1,0:T(8,128)(2,1)S(1)} copy-done((bf16[768,384]{1,0:T(8,128)(2,1)S(1)}, bf16[768,384]{1,0:T(8,128)(2,1)}, u32[]{:S(2)}) %copy-start.1) | copy-done | bytes 589848
  11.8 0.7 %copy-done.2 = f32[768]{0:T(1024)S(1)} copy-done((f32[768]{0:T(1024)S(1)}, f32[768]{0:T(1024)}, u32[]{:S(2)}) %copy-start.2) | copy-done | bytes 3096
  13.8 0.9 %shard_map.95 = (bf16[512,768]{1,0:T(8,128)(2,1)S(1)}, bf16[768,512]{1,0:T(8,128)(2,1)S(1)}, bf16[768,512]{1,0:T(8,128)(2,1)S(1)}, bf16[512,768]{1,0:T(8,128)(2,...) custom-call(bf16[384,768]{1,0:T(8,128)(2,1)S(1)} %copy-done, ...), custom_call_target="tpu_custom_call" | custom-call | tf_op jit(solution)/shard_map/pallas_call | solution.py:462
  14.7 3.8 %all-to-all-done.both_ref = bf16[32,8,384]{2,1,0:T(8,128)(2,1)S(1)} async-done(((bf16[32,8,384]{2,1,0:T(8,128)(2,1)}), bf16[32,8,384]{2,1,0:T(8,128)(2,1)S(1)}, u32[]{:S(2)}, u32[]{:S(2)}) %all-to-all-start) | async-done | bytes 196640 | tf_op jit(solution)/shard_map/all_to_all | solution.py:460
  18.5 6.1 %shard_map.96 = (bf16[768,384]{1,0:T(8,128)(2,1)S(1)}, bf16[640,384]{1,0:T(8,128)(2,1)S(1)}, bf16[640,768]{1,0:T(8,128)(2,1)S(1)}, bf16[640,768]{1,0:T(8,128)(2,...) custom-call(s32[1]{0:T(128)} %bitcast.me_ref, ...), custom_call_target="tpu_custom_call" | custom-call | tf_op jit(solution)/shard_map/pallas_call | solution.py:472
  27.7 1.3 %collective-permute-start.3 = (bf16[192,384]{1,0:T(8,128)(2,1)S(1)}, bf16[192,384]{1,0:T(8,128)(2,1)S(1)}, u32[]{:S(2)}, u32[]{:S(2)}) collective-permute-start(bf16[192,384]{1,0:T(8,128)(2,1)S(1)} %get-tuple-element.71), channel_id=1, source_target_pairs={{0,4},{1,5},{2,6},{3,7},{4,0},{5,1},{6,2},{7,3},{8,12},{9,13},{10,... | collective-permute-start | bytes 442376 | tf_op jit(solution)/shard_map/ppermute | solution.py:378
  28.9 1.7 %collective-permute-start.4 = (bf16[192,384]{1,0:T(8,128)(2,1)S(1)}, bf16[192,384]{1,0:T(8,128)(2,1)S(1)}, u32[]{:S(2)}, u32[]{:S(2)}) collective-permute-start(bf16[192,384]{1,0:T(8,128)(2,1)S(1)} %get-tuple-element.72), channel_id=1, source_target_pairs={{0,6},{1,7},{2,4},{3,5},{4,2},{5,3},{6,0},{7,1},{8,14},{9,15},{10,... | collective-permute-start | bytes 442376 | tf_op jit(solution)/shard_map/ppermute | solution.py:378
  30.8 0.9 %collective-permute-start.5 = (bf16[64,384]{1,0:T(8,128)(2,1)S(1)}, bf16[64,384]{1,0:T(8,128)(2,1)S(1)}, u32[]{:S(2)}, u32[]{:S(2)}) collective-permute-start(bf16[64,384]{1,0:T(8,128)(2,1)S(1)} %get-tuple-element.76), channel_id=1, source_target_pairs={{0,16},{1,17},{2,18},{3,19},{4,20},{5,21},{6,22},{7,23},{8,24},{9,... | collective-permute-start | bytes 147464 | tf_op jit(solution)/shard_map/ppermute | solution.py:378
  31.6 4.7 %collective-permute-done.5.refs_3_ = bf16[64,384]{1,0:T(8,128)(2,1)S(1)} collective-permute-done((bf16[64,384]{1,0:T(8,128)(2,1)S(1)}, bf16[64,384]{1,0:T(8,128)(2,1)S(1)}, u32[]{:S(2)}, u32[]{:S(2)}) %collective-permute-start.5) | collective-permute-done | bytes 49184 | tf_op jit(solution)/shard_map/ppermute | solution.py:378
  36.7 0.7 %collective-permute-start.6 = (bf16[192,384]{1,0:T(8,128)(2,1)S(1)}, bf16[192,384]{1,0:T(8,128)(2,1)S(1)}, u32[]{:S(2)}, u32[]{:S(2)}) collective-permute-start(bf16[192,384]{1,0:T(8,128)(2,1)S(1)} %shard_map.101.refs_0_), channel_id=1, source_target_pairs={{0,8},{1,9},{2,10},{3,11},{4,12},{5,13},{6,14},{7,15},{8,0},{9,1},... | collective-permute-start | bytes 442376 | tf_op jit(solution)/shard_map/ppermute | solution.py:378
  37.4 4.5 %collective-permute-done.6.refs_1_ = bf16[192,384]{1,0:T(8,128)(2,1)S(1)} collective-permute-done((bf16[192,384]{1,0:T(8,128)(2,1)S(1)}, bf16[192,384]{1,0:T(8,128)(2,1)S(1)}, u32[]{:S(2)}, u32[]{:S(2)}) %collective-permute-start.6) | collective-permute-done | bytes 147488 | tf_op jit(solution)/shard_map/ppermute | solution.py:378
  41.9 1.7 %collective-permute-start.7 = (bf16[192,384]{1,0:T(8,128)(2,1)S(1)}, bf16[192,384]{1,0:T(8,128)(2,1)S(1)}, u32[]{:S(2)}, u32[]{:S(2)}) collective-permute-start(bf16[192,384]{1,0:T(8,128)(2,1)S(1)} %get-tuple-element.83.refs_0_), channel_id=1, source_target_pairs={{0,24},{1,25},{2,26},{3,27},{4,28},{5,29},{6,30},{7,31},{8,16},{9,... | collective-permute-start | bytes 442376 | tf_op jit(solution)/shard_map/ppermute | solution.py:378
  43.6 5.7 %collective-permute-done.8.refs_3_ = bf16[64,384]{1,0:T(8,128)(2,1)S(1)} collective-permute-done((bf16[64,384]{1,0:T(8,128)(2,1)S(1)}, bf16[64,384]{1,0:T(8,128)(2,1)S(1)}, u32[]{:S(2)}, u32[]{:S(2)}) %collective-permute-start.8) | collective-permute-done | bytes 49184 | tf_op jit(solution)/shard_map/ppermute | solution.py:378
  49.4 1.5 %collective-permute-start.9 = (bf16[224,384]{1,0:T(8,128)(2,1)S(1)}, bf16[224,384]{1,0:T(8,128)(2,1)S(1)}, u32[]{:S(2)}, u32[]{:S(2)}) collective-permute-start(bf16[224,384]{1,0:T(8,128)(2,1)S(1)} %get-tuple-element.87), channel_id=1, source_target_pairs={{0,2},{1,3},{2,0},{3,1},{4,6},{5,7},{6,4},{7,5},{8,10},{9,11},{10,... | collective-permute-start | bytes 516104 | tf_op jit(solution)/shard_map/ppermute | solution.py:378
  50.9 0.8 %collective-permute-start.10 = (bf16[224,384]{1,0:T(8,128)(2,1)S(1)}, bf16[224,384]{1,0:T(8,128)(2,1)S(1)}, u32[]{:S(2)}, u32[]{:S(2)}) collective-permute-start(bf16[224,384]{1,0:T(8,128)(2,1)S(1)} %get-tuple-element.88), channel_id=1, source_target_pairs={{0,4},{1,5},{2,6},{3,7},{4,0},{5,1},{6,2},{7,3},{8,12},{9,13},{10,... | collective-permute-start | bytes 516104 | tf_op jit(solution)/shard_map/ppermute | solution.py:378
  51.6 1.3 %collective-permute-start.11 = (bf16[224,384]{1,0:T(8,128)(2,1)S(1)}, bf16[224,384]{1,0:T(8,128)(2,1)S(1)}, u32[]{:S(2)}, u32[]{:S(2)}) collective-permute-start(bf16[224,384]{1,0:T(8,128)(2,1)S(1)} %get-tuple-element.89), channel_id=1, source_target_pairs={{0,6},{1,7},{2,4},{3,5},{4,2},{5,3},{6,0},{7,1},{8,14},{9,15},{10,... | collective-permute-start | bytes 516104 | tf_op jit(solution)/shard_map/ppermute | solution.py:378
  52.9 1.4 %collective-permute-done.12.refs_1_ = bf16[192,384]{1,0:T(8,128)(2,1)S(1)} collective-permute-done((bf16[192,384]{1,0:T(8,128)(2,1)S(1)}, bf16[192,384]{1,0:T(8,128)(2,1)S(1)}, u32[]{:S(2)}, u32[]{:S(2)}) %collective-permute-start.12) | collective-permute-done | bytes 147488 | tf_op jit(solution)/shard_map/ppermute | solution.py:378
  54.8 1.0 %shard_map.105 = (f32[384,768]{1,0:T(8,128)}, f32[768,384]{1,0:T(8,128)}) custom-call(s32[1]{0:T(128)} %bitcast.me_ref, bf16[192,384]{1,0:T(8,128)(2,1)S(1)} %get-tuple-element.90.refs_0_, bf16[192,384]{1,0:T(8,128)(2,1)S(1)} %collective-permute-done.12.refs_1_, bf16[224,384]{1,0:T(8,128)(2,1)S(1)} %collective-permute-done.9.refs_1_.refs_2_), custom_call_target="tpu_custom_call" | custom-call | tf_op jit(solution)/shard_map/pallas_call | solution.py:351
  55.8 2.3 %collective-permute-done.10.refs_2_.refs_0_ = bf16[224,384]{1,0:T(8,128)(2,1)S(1)} collective-permute-done((bf16[224,384]{1,0:T(8,128)(2,1)S(1)}, bf16[224,384]{1,0:T(8,128)(2,1)S(1)}, u32[]{:S(2)}, u32[]{:S(2)}) %collective-permute-start.10) | collective-permute-done | bytes 172064 | tf_op jit(solution)/shard_map/ppermute | solution.py:378
  58.6 0.8 %shard_map.104 = bf16[192,256]{1,0:T(8,128)(2,1)} custom-call(s32[1]{0:T(128)} %bitcast.me_ref, bf16[32,384]{1,0:T(8,128)(2,1)S(1)} %get-tuple-element.86.refs_0_, bf16[224,384]{1,0:T(8,128)(2,1)S(1)} %collective-permute-done.9.refs_1_.refs_2_, bf16[224,384]{1,0:T(8,128)(2,1)S(1)} %collective-permute-done.10.refs_2_.refs_0_, ...), custom_call_target="tpu_custom_call" | custom-call | tf_op jit(solution)/shard_map/pallas_call | solution.py:518
  59.8 1.2 %shard_map.106 = (f32[384,768]{1,0:T(8,128)}, f32[768,384]{1,0:T(8,128)}) custom-call(s32[1]{0:T(128)} %bitcast.me_ref, bf16[224,384]{1,0:T(8,128)(2,1)S(1)} %collective-permute-done.10.refs_2_.refs_0_, bf16[224,384]{1,0:T(8,128)(2,1)S(1)} %collective-permute-done.11.refs_3_.refs_1_, ...), custom_call_target="tpu_custom_call", output_to_operand_aliasing={{0}: (6, {}), {1}: (7, {})} | custom-call | tf_op jit(solution)/shard_map/pallas_call | solution.py:351
  (33 shorter events, 6.4 us)
Async XLA Ops:
  2.3 16.2 %all-to-all-start = ((bf16[32,8,384]{2,1,0:T(8,128)(2,1)}), bf16[32,8,384]{2,1,0:T(8,128)(2,1)S(1)}, u32[]{:S(2)}, u32[]{:S(2)}) async-start(bf16[32,8,384]{2,1,0:T(8,128)(2,1)} %shard_map.94), calls=%async_computation | async-start | bytes 393216 | tf_op jit(solution)/shard_map/all_to_all | solution.py:460
  9.6 1.1 %copy-start = (bf16[384,768]{1,0:T(8,128)(2,1)S(1)}, bf16[384,768]{1,0:T(8,128)(2,1)}, u32[]{:S(2)}) copy-start(bf16[384,768]{1,0:T(8,128)(2,1)} %w_in_ref.1) | copy-start | bytes 1769476
  10.7 1.1 %copy-start.1 = (bf16[768,384]{1,0:T(8,128)(2,1)S(1)}, bf16[768,384]{1,0:T(8,128)(2,1)}, u32[]{:S(2)}) copy-start(bf16[768,384]{1,0:T(8,128)(2,1)} %w_out_ref.1) | copy-start | bytes 1769476
  11.8 0.7 %copy-start.2 = (f32[768]{0:T(1024)S(1)}, f32[768]{0:T(1024)}, u32[]{:S(2)}) copy-start(f32[768]{0:T(1024)} %bias_ref.1) | copy-start | bytes 9220
  12.5 0.7 %copy-start.3 = (f32[384]{0:T(512)S(1)}, f32[384]{0:T(512)}, u32[]{:S(2)}) copy-start(f32[384]{0:T(512)} %logit_ref.1) | copy-start | bytes 4612
  13.1 0.7 %copy-start.4 = (f32[384]{0:T(512)S(1)}, f32[384]{0:T(512)}, u32[]{:S(2)}) copy-start(f32[384]{0:T(512)} %scale_ref.1) | copy-start | bytes 4612
  24.6 2.4 %collective-permute-start = (bf16[768,384]{1,0:T(8,128)(2,1)S(1)}, bf16[768,384]{1,0:T(8,128)(2,1)S(1)}, u32[]{:S(2)}, u32[]{:S(2)}) collective-permute-start(bf16[768,384]{1,0:T(8,128)(2,1)S(1)} %get-tuple-element.63), channel_id=1, source_target_pairs={{0,1},{1,0},{2,3},{3,2},{4,5},{5,4},{6,7},{7,6},{8,9},{9,8},{10,11... | collective-permute-start | bytes 1769480 | tf_op jit(solution)/shard_map/ppermute | solution.py:378
  25.7 1.3 %collective-permute-start.1 = (bf16[64,384]{1,0:T(8,128)(2,1)S(1)}, bf16[64,384]{1,0:T(8,128)(2,1)S(1)}, u32[]{:S(2)}, u32[]{:S(2)}) collective-permute-start(bf16[64,384]{1,0:T(8,128)(2,1)S(1)} %get-tuple-element.67), channel_id=1, source_target_pairs={{0,1},{1,0},{2,3},{3,2},{4,5},{5,4},{6,7},{7,6},{8,9},{9,8},{10,11... | collective-permute-start | bytes 147464 | tf_op jit(solution)/shard_map/ppermute | solution.py:378
  27.1 9.2 %collective-permute-start.2 = (bf16[192,384]{1,0:T(8,128)(2,1)S(1)}, bf16[192,384]{1,0:T(8,128)(2,1)S(1)}, u32[]{:S(2)}, u32[]{:S(2)}) collective-permute-start(bf16[192,384]{1,0:T(8,128)(2,1)S(1)} %get-tuple-element.70), channel_id=1, source_target_pairs={{0,2},{1,3},{2,0},{3,1},{4,6},{5,7},{6,4},{7,5},{8,10},{9,11},{10,... | collective-permute-start | bytes 442376 | tf_op jit(solution)/shard_map/ppermute | solution.py:378
  27.7 8.9 %collective-permute-start.3 = (bf16[192,384]{1,0:T(8,128)(2,1)S(1)}, bf16[192,384]{1,0:T(8,128)(2,1)S(1)}, u32[]{:S(2)}, u32[]{:S(2)}) collective-permute-start(bf16[192,384]{1,0:T(8,128)(2,1)S(1)} %get-tuple-element.71), channel_id=1, source_target_pairs={{0,4},{1,5},{2,6},{3,7},{4,0},{5,1},{6,2},{7,3},{8,12},{9,13},{10,... | collective-permute-start | bytes 442376 | tf_op jit(solution)/shard_map/ppermute | solution.py:378
  28.9 7.7 %collective-permute-start.4 = (bf16[192,384]{1,0:T(8,128)(2,1)S(1)}, bf16[192,384]{1,0:T(8,128)(2,1)S(1)}, u32[]{:S(2)}, u32[]{:S(2)}) collective-permute-start(bf16[192,384]{1,0:T(8,128)(2,1)S(1)} %get-tuple-element.72), channel_id=1, source_target_pairs={{0,6},{1,7},{2,4},{3,5},{4,2},{5,3},{6,0},{7,1},{8,14},{9,15},{10,... | collective-permute-start | bytes 442376 | tf_op jit(solution)/shard_map/ppermute | solution.py:378
  30.8 5.6 %collective-permute-start.5 = (bf16[64,384]{1,0:T(8,128)(2,1)S(1)}, bf16[64,384]{1,0:T(8,128)(2,1)S(1)}, u32[]{:S(2)}, u32[]{:S(2)}) collective-permute-start(bf16[64,384]{1,0:T(8,128)(2,1)S(1)} %get-tuple-element.76), channel_id=1, source_target_pairs={{0,16},{1,17},{2,18},{3,19},{4,20},{5,21},{6,22},{7,23},{8,24},{9,... | collective-permute-start | bytes 147464 | tf_op jit(solution)/shard_map/ppermute | solution.py:378
  36.7 5.2 %collective-permute-start.6 = (bf16[192,384]{1,0:T(8,128)(2,1)S(1)}, bf16[192,384]{1,0:T(8,128)(2,1)S(1)}, u32[]{:S(2)}, u32[]{:S(2)}) collective-permute-start(bf16[192,384]{1,0:T(8,128)(2,1)S(1)} %shard_map.101.refs_0_), channel_id=1, source_target_pairs={{0,8},{1,9},{2,10},{3,11},{4,12},{5,13},{6,14},{7,15},{8,0},{9,1},... | collective-permute-start | bytes 442376 | tf_op jit(solution)/shard_map/ppermute | solution.py:378
  41.9 7.3 %collective-permute-start.7 = (bf16[192,384]{1,0:T(8,128)(2,1)S(1)}, bf16[192,384]{1,0:T(8,128)(2,1)S(1)}, u32[]{:S(2)}, u32[]{:S(2)}) collective-permute-start(bf16[192,384]{1,0:T(8,128)(2,1)S(1)} %get-tuple-element.83.refs_0_), channel_id=1, source_target_pairs={{0,24},{1,25},{2,26},{3,27},{4,28},{5,29},{6,30},{7,31},{8,16},{9,... | collective-permute-start | bytes 442376 | tf_op jit(solution)/shard_map/ppermute | solution.py:378
  43.6 5.7 %collective-permute-start.8 = (bf16[64,384]{1,0:T(8,128)(2,1)S(1)}, bf16[64,384]{1,0:T(8,128)(2,1)S(1)}, u32[]{:S(2)}, u32[]{:S(2)}) collective-permute-start(bf16[64,384]{1,0:T(8,128)(2,1)S(1)} %get-tuple-element.85), channel_id=1, source_target_pairs={{0,8},{1,9},{2,10},{3,11},{4,12},{5,13},{6,14},{7,15},{8,0},{9,1},... | collective-permute-start | bytes 147464 | tf_op jit(solution)/shard_map/ppermute | solution.py:378
  49.4 5.5 %collective-permute-start.9 = (bf16[224,384]{1,0:T(8,128)(2,1)S(1)}, bf16[224,384]{1,0:T(8,128)(2,1)S(1)}, u32[]{:S(2)}, u32[]{:S(2)}) collective-permute-start(bf16[224,384]{1,0:T(8,128)(2,1)S(1)} %get-tuple-element.87), channel_id=1, source_target_pairs={{0,2},{1,3},{2,0},{3,1},{4,6},{5,7},{6,4},{7,5},{8,10},{9,11},{10,... | collective-permute-start | bytes 516104 | tf_op jit(solution)/shard_map/ppermute | solution.py:378
  50.9 7.2 %collective-permute-start.10 = (bf16[224,384]{1,0:T(8,128)(2,1)S(1)}, bf16[224,384]{1,0:T(8,128)(2,1)S(1)}, u32[]{:S(2)}, u32[]{:S(2)}) collective-permute-start(bf16[224,384]{1,0:T(8,128)(2,1)S(1)} %get-tuple-element.88), channel_id=1, source_target_pairs={{0,4},{1,5},{2,6},{3,7},{4,0},{5,1},{6,2},{7,3},{8,12},{9,13},{10,... | collective-permute-start | bytes 516104 | tf_op jit(solution)/shard_map/ppermute | solution.py:378
  51.6 6.5 %collective-permute-start.11 = (bf16[224,384]{1,0:T(8,128)(2,1)S(1)}, bf16[224,384]{1,0:T(8,128)(2,1)S(1)}, u32[]{:S(2)}, u32[]{:S(2)}) collective-permute-start(bf16[224,384]{1,0:T(8,128)(2,1)S(1)} %get-tuple-element.89), channel_id=1, source_target_pairs={{0,6},{1,7},{2,4},{3,5},{4,2},{5,3},{6,0},{7,1},{8,14},{9,15},{10,... | collective-permute-start | bytes 516104 | tf_op jit(solution)/shard_map/ppermute | solution.py:378
  52.9 1.4 %collective-permute-start.12 = (bf16[192,384]{1,0:T(8,128)(2,1)S(1)}, bf16[192,384]{1,0:T(8,128)(2,1)S(1)}, u32[]{:S(2)}, u32[]{:S(2)}) collective-permute-start(bf16[192,384]{1,0:T(8,128)(2,1)S(1)} %get-tuple-element.90.refs_0_), channel_id=1, source_target_pairs={{0,1},{1,0},{2,3},{3,2},{4,5},{5,4},{6,7},{7,6},{8,9},{9,8},{10,11... | collective-permute-start | bytes 442376 | tf_op jit(solution)/shard_map/ppermute | solution.py:378
  54.8 4.7 %collective-permute-start.13 = (bf16[224,384]{1,0:T(8,128)(2,1)S(1)}, bf16[224,384]{1,0:T(8,128)(2,1)S(1)}, u32[]{:S(2)}, u32[]{:S(2)}) collective-permute-start(bf16[224,384]{1,0:T(8,128)(2,1)S(1)} %collective-permute-done.9.refs_1_.refs_2_), channel_id=1, source_target_pairs={{0,1},{1,0},{2,3},{3,2},{4,5},{5,4},{6,7},{7,6},{8,9},{9,8},{10,11... | collective-permute-start | bytes 516104 | tf_op jit(solution)/shard_map/ppermute | solution.py:378
  58.1 1.4 %collective-permute-start.14 = (bf16[224,384]{1,0:T(8,128)(2,1)S(1)}, bf16[224,384]{1,0:T(8,128)(2,1)S(1)}, u32[]{:S(2)}, u32[]{:S(2)}) collective-permute-start(bf16[224,384]{1,0:T(8,128)(2,1)S(1)} %collective-permute-done.10.refs_2_.refs_0_), channel_id=1, source_target_pairs={{0,1},{1,0},{2,3},{3,2},{4,5},{5,4},{6,7},{7,6},{8,9},{9,8},{10,11... | collective-permute-start | bytes 516104 | tf_op jit(solution)/shard_map/ppermute | solution.py:378
  58.1 1.7 %collective-permute-start.15 = (bf16[224,384]{1,0:T(8,128)(2,1)S(1)}, bf16[224,384]{1,0:T(8,128)(2,1)S(1)}, u32[]{:S(2)}, u32[]{:S(2)}) collective-permute-start(bf16[224,384]{1,0:T(8,128)(2,1)S(1)} %collective-permute-done.11.refs_3_.refs_1_), channel_id=1, source_target_pairs={{0,1},{1,0},{2,3},{3,2},{4,5},{5,4},{6,7},{7,6},{8,9},{9,8},{10,11... | collective-permute-start | bytes 516104 | tf_op jit(solution)/shard_map/ppermute | solution.py:378

commit v12 on v11

--- a/solution.py
+++ b/solution.py
@@ -120,7 +120,7 @@
 def switch_kernel(
     levels, block, me_ref, both_ref, w_in_ref, w_out_ref, w_in_turned_ref, w_out_turned_ref, bias_ref, gate_ref, scale_ref,
     send_ref, low_s, pre_s, act_s, bg_s, upstream_ref, normed_ref, inverse_ref,
-    slope_s, normed_s, inverse_s,
+    slope_s, normed_s, inverse_s, early_s,
 ):
     half, double = upstream_ref.shape[1], bg_s.shape[1]
     rows, width = 2 * half, double // 2
@@ -131,6 +131,14 @@
     both = both_ref[...].astype(f32).reshape(rows, double)
     state = widen(both[:, :width], lanes)
     inside = lax.broadcasted_iota(jnp.int32, (half, lanes), 1) < width
+
+    def scaled_pairs(grad, level):
+        upstream = pair_rows(grad, block * 2**level)
+        return upstream, [(scale[side] * upstream[side]).astype(bf16) for side in sides]
+
+    def product_of(branch_grad):
+        return dot(jnp.concatenate(branch_grad, axis=1), w_out_turned_ref[...], (1, 0))
+
     for level in range(levels):
         at = pl.ds(level * half, half)
         paired = pair_rows(state, block * 2**level)
@@ -144,6 +152,8 @@
         for side in sides:
             normed_s[side, at, :] = normed[side]
         u = dot(low, w_in_ref[...], (1, 0)) + bias_ref[...]
+        if level == 0:
+            early_s[...] = product_of(scaled_pairs(widen(both[:, width:], lanes), levels - 1)[1])
         square = u * u
         tangent = jnp.tanh(u * (tanh_scale + tanh_scale * cubic_coef * square))
         rise = 0.5 + 0.5 * tangent
@@ -163,10 +173,9 @@
     grad = widen(both[:, width:], lanes)
     for level in reversed(range(levels)):
         at = pl.ds(level * half, half)
-        upstream = pair_rows(grad, block * 2**level)
-        branch_grad = [(scale[side] * upstream[side]).astype(bf16) for side in sides]
+        upstream, branch_grad = scaled_pairs(grad, level)
         bg_s[at, :] = jnp.concatenate([part[:, :width] for part in branch_grad], axis=1)
-        act_grad = dot(jnp.concatenate(branch_grad, axis=1), w_out_turned_ref[...], (1, 0))
+        act_grad = early_s[...] if level == levels - 1 else product_of(branch_grad)
         pre_grad = (act_grad * slope_s[at, :]).astype(bf16)
         pre_s[at, :] = pre_grad
         normed = [normed_s[side, at, :] for side in sides]
@@ -485,6 +494,7 @@
             pltpu.VMEM((total, units), f32),
             pltpu.VMEM((2, total, lanes), f32),
             pltpu.VMEM((total, 1), f32),
+            pltpu.VMEM((half, units), f32),
         ],
         specs=[SMEM] + [VMEM] * 8,
         grant=20,

time: 61.4 us -> 61.4 us (level)
  transfers between devices with their start and end apart: 17 -> 17, of which waited for: 11 -> 11; matrix products, arithmetic and copies ran while one was open for 0% -> 0% of each run, Pallas kernels for 6% -> 7%
where the time goes in v12:
time: 61.4 us; the launch traced here: 61 us
  waiting for transfers between devices  24.1 us (39%)
  starting transfers between devices  18.8 us (31%)
  Pallas kernels  13.2 us (21%)
  local copies, waits for them, and re-layouts  4.17 us (7%)
  between operations  0.75 us (1%)
    ppermute x16, waiting for transfers between devices, exchange(): lax.ppermute(value if not isinstance(value, list) else value[i], 'seq', [...  20.3 us
    ppermute x16, starting transfers between devices, exchange(): lax.ppermute(value if not isinstance(value, list) else value[i], 'seq', [...  11.5 us
    all_to_all x1, starting transfers between devices, shards(): both = lax.all_to_all(both, 'seq', split_axis=0, concat_axis=0, tiled=True)  7.3 us
    pallas_call x1, Pallas kernels, shards(): call(functools.partial(switch_kernel, levels, block), [struct((units, dou...  6.08 us
    unnamed x10, local copies, waits for them, and re-layouts  4.17 us
    all_to_all x1, waiting for transfers between devices, shards(): both = lax.all_to_all(both, 'seq', split_axis=0, concat_axis=0, tiled=True)  3.82 us
    pallas_call x2, Pallas kernels, place(): call(functools.partial(place_kernel, 1, pieces, slots, len(placed)), shap...  2.12 us
    pallas_call x1, Pallas kernels, shards(): call(pack_kernel, struct((size, block, double), bf16), scratch=[pltpu.VME...  1.68 us
  transfers between devices with their start and end apart: 17, of which 11 were waited for; matrix products, arithmetic and copies ran while one was open for 0% of the time, Pallas kernels for 7%

profile of v12, /device:TPU:0, one launch (start us, length us, event | category | flops | bytes accessed | tf_op | source)
XLA Modules:
  0.0 61.0 jit_solution(11952234470814839437)
XLA Ops:
  0.6 1.7 %shard_map.94 = bf16[32,8,384]{2,1,0:T(8,128)(2,1)} custom-call(bf16[192,256]{1,0:T(8,128)(2,1)} %bitcast.4, bf16[192,256]{1,0:T(8,128)(2,1)} %bitcast.5), custom_call_target="tpu_custom_call" | custom-call | bytes 7000000 | tf_op jit(solution)/shard_map/pallas_call | solution.py:453
  2.3 7.3 %all-to-all-start = ((bf16[32,8,384]{2,1,0:T(8,128)(2,1)}), bf16[32,8,384]{2,1,0:T(8,128)(2,1)S(1)}, u32[]{:S(2)}, u32[]{:S(2)}) async-start(bf16[32,8,384]{2,1,0:T(8,128)(2,1)} %shard_map.94), calls=%async_computation | async-start | bytes 393216 | tf_op jit(solution)/shard_map/all_to_all | solution.py:469
  9.6 1.1 %copy-done = bf16[384,768]{1,0:T(8,128)(2,1)S(1)} copy-done((bf16[384,768]{1,0:T(8,128)(2,1)S(1)}, bf16[384,768]{1,0:T(8,128)(2,1)}, u32[]{:S(2)}) %copy-start) | copy-done | bytes 589848
  10.7 1.1 %copy-done.1 = bf16[768,384]{1,0:T(8,128)(2,1)S(1)} copy-done((bf16[768,384]{1,0:T(8,128)(2,1)S(1)}, bf16[768,384]{1,0:T(8,128)(2,1)}, u32[]{:S(2)}) %copy-start.1) | copy-done | bytes 589848
  11.8 0.7 %copy-done.2 = f32[768]{0:T(1024)S(1)} copy-done((f32[768]{0:T(1024)S(1)}, f32[768]{0:T(1024)}, u32[]{:S(2)}) %copy-start.2) | copy-done | bytes 3096
  13.8 0.9 %shard_map.95 = (bf16[512,768]{1,0:T(8,128)(2,1)S(1)}, bf16[768,512]{1,0:T(8,128)(2,1)S(1)}, bf16[768,512]{1,0:T(8,128)(2,1)S(1)}, bf16[512,768]{1,0:T(8,128)(2,...) custom-call(bf16[384,768]{1,0:T(8,128)(2,1)S(1)} %copy-done, ...), custom_call_target="tpu_custom_call" | custom-call | tf_op jit(solution)/shard_map/pallas_call | solution.py:471
  14.7 3.8 %all-to-all-done.both_ref = bf16[32,8,384]{2,1,0:T(8,128)(2,1)S(1)} async-done(((bf16[32,8,384]{2,1,0:T(8,128)(2,1)}), bf16[32,8,384]{2,1,0:T(8,128)(2,1)S(1)}, u32[]{:S(2)}, u32[]{:S(2)}) %all-to-all-start) | async-done | bytes 196640 | tf_op jit(solution)/shard_map/all_to_all | solution.py:469
  18.5 6.1 %shard_map.96 = (bf16[768,384]{1,0:T(8,128)(2,1)S(1)}, bf16[640,384]{1,0:T(8,128)(2,1)S(1)}, bf16[640,768]{1,0:T(8,128)(2,1)S(1)}, bf16[640,768]{1,0:T(8,128)(2,...) custom-call(s32[1]{0:T(128)} %bitcast.me_ref, ...), custom_call_target="tpu_custom_call" | custom-call | tf_op jit(solution)/shard_map/pallas_call | solution.py:481
  27.7 1.3 %collective-permute-start.3 = (bf16[192,384]{1,0:T(8,128)(2,1)S(1)}, bf16[192,384]{1,0:T(8,128)(2,1)S(1)}, u32[]{:S(2)}, u32[]{:S(2)}) collective-permute-start(bf16[192,384]{1,0:T(8,128)(2,1)S(1)} %get-tuple-element.71), channel_id=1, source_target_pairs={{0,4},{1,5},{2,6},{3,7},{4,0},{5,1},{6,2},{7,3},{8,12},{9,13},{10,... | collective-permute-start | bytes 442376 | tf_op jit(solution)/shard_map/ppermute | solution.py:387
  29.0 1.7 %collective-permute-start.4 = (bf16[192,384]{1,0:T(8,128)(2,1)S(1)}, bf16[192,384]{1,0:T(8,128)(2,1)S(1)}, u32[]{:S(2)}, u32[]{:S(2)}) collective-permute-start(bf16[192,384]{1,0:T(8,128)(2,1)S(1)} %get-tuple-element.72), channel_id=1, source_target_pairs={{0,6},{1,7},{2,4},{3,5},{4,2},{5,3},{6,0},{7,1},{8,14},{9,15},{10,... | collective-permute-start | bytes 442376 | tf_op jit(solution)/shard_map/ppermute | solution.py:387
  30.8 0.9 %collective-permute-start.5 = (bf16[64,384]{1,0:T(8,128)(2,1)S(1)}, bf16[64,384]{1,0:T(8,128)(2,1)S(1)}, u32[]{:S(2)}, u32[]{:S(2)}) collective-permute-start(bf16[64,384]{1,0:T(8,128)(2,1)S(1)} %get-tuple-element.76), channel_id=1, source_target_pairs={{0,16},{1,17},{2,18},{3,19},{4,20},{5,21},{6,22},{7,23},{8,24},{9,... | collective-permute-start | bytes 147464 | tf_op jit(solution)/shard_map/ppermute | solution.py:387
  31.6 4.7 %collective-permute-done.5.refs_3_ = bf16[64,384]{1,0:T(8,128)(2,1)S(1)} collective-permute-done((bf16[64,384]{1,0:T(8,128)(2,1)S(1)}, bf16[64,384]{1,0:T(8,128)(2,1)S(1)}, u32[]{:S(2)}, u32[]{:S(2)}) %collective-permute-start.5) | collective-permute-done | bytes 49184 | tf_op jit(solution)/shard_map/ppermute | solution.py:387
  36.7 0.7 %collective-permute-start.6 = (bf16[192,384]{1,0:T(8,128)(2,1)S(1)}, bf16[192,384]{1,0:T(8,128)(2,1)S(1)}, u32[]{:S(2)}, u32[]{:S(2)}) collective-permute-start(bf16[192,384]{1,0:T(8,128)(2,1)S(1)} %shard_map.101.refs_0_), channel_id=1, source_target_pairs={{0,8},{1,9},{2,10},{3,11},{4,12},{5,13},{6,14},{7,15},{8,0},{9,1},... | collective-permute-start | bytes 442376 | tf_op jit(solution)/shard_map/ppermute | solution.py:387
  37.4 4.5 %collective-permute-done.6.refs_1_ = bf16[192,384]{1,0:T(8,128)(2,1)S(1)} collective-permute-done((bf16[192,384]{1,0:T(8,128)(2,1)S(1)}, bf16[192,384]{1,0:T(8,128)(2,1)S(1)}, u32[]{:S(2)}, u32[]{:S(2)}) %collective-permute-start.6) | collective-permute-done | bytes 147488 | tf_op jit(solution)/shard_map/ppermute | solution.py:387
  42.0 1.7 %collective-permute-start.7 = (bf16[192,384]{1,0:T(8,128)(2,1)S(1)}, bf16[192,384]{1,0:T(8,128)(2,1)S(1)}, u32[]{:S(2)}, u32[]{:S(2)}) collective-permute-start(bf16[192,384]{1,0:T(8,128)(2,1)S(1)} %get-tuple-element.83.refs_0_), channel_id=1, source_target_pairs={{0,24},{1,25},{2,26},{3,27},{4,28},{5,29},{6,30},{7,31},{8,16},{9,... | collective-permute-start | bytes 442376 | tf_op jit(solution)/shard_map/ppermute | solution.py:387
  43.6 5.7 %collective-permute-done.8.refs_3_ = bf16[64,384]{1,0:T(8,128)(2,1)S(1)} collective-permute-done((bf16[64,384]{1,0:T(8,128)(2,1)S(1)}, bf16[64,384]{1,0:T(8,128)(2,1)S(1)}, u32[]{:S(2)}, u32[]{:S(2)}) %collective-permute-start.8) | collective-permute-done | bytes 49184 | tf_op jit(solution)/shard_map/ppermute | solution.py:387
  49.4 1.5 %collective-permute-start.9 = (bf16[224,384]{1,0:T(8,128)(2,1)S(1)}, bf16[224,384]{1,0:T(8,128)(2,1)S(1)}, u32[]{:S(2)}, u32[]{:S(2)}) collective-permute-start(bf16[224,384]{1,0:T(8,128)(2,1)S(1)} %get-tuple-element.87), channel_id=1, source_target_pairs={{0,2},{1,3},{2,0},{3,1},{4,6},{5,7},{6,4},{7,5},{8,10},{9,11},{10,... | collective-permute-start | bytes 516104 | tf_op jit(solution)/shard_map/ppermute | solution.py:387
  50.9 0.7 %collective-permute-start.10 = (bf16[224,384]{1,0:T(8,128)(2,1)S(1)}, bf16[224,384]{1,0:T(8,128)(2,1)S(1)}, u32[]{:S(2)}, u32[]{:S(2)}) collective-permute-start(bf16[224,384]{1,0:T(8,128)(2,1)S(1)} %get-tuple-element.88), channel_id=1, source_target_pairs={{0,4},{1,5},{2,6},{3,7},{4,0},{5,1},{6,2},{7,3},{8,12},{9,13},{10,... | collective-permute-start | bytes 516104 | tf_op jit(solution)/shard_map/ppermute | solution.py:387
  51.7 1.3 %collective-permute-start.11 = (bf16[224,384]{1,0:T(8,128)(2,1)S(1)}, bf16[224,384]{1,0:T(8,128)(2,1)S(1)}, u32[]{:S(2)}, u32[]{:S(2)}) collective-permute-start(bf16[224,384]{1,0:T(8,128)(2,1)S(1)} %get-tuple-element.89), channel_id=1, source_target_pairs={{0,6},{1,7},{2,4},{3,5},{4,2},{5,3},{6,0},{7,1},{8,14},{9,15},{10,... | collective-permute-start | bytes 516104 | tf_op jit(solution)/shard_map/ppermute | solution.py:387
  52.9 1.4 %collective-permute-done.12.refs_1_ = bf16[192,384]{1,0:T(8,128)(2,1)S(1)} collective-permute-done((bf16[192,384]{1,0:T(8,128)(2,1)S(1)}, bf16[192,384]{1,0:T(8,128)(2,1)S(1)}, u32[]{:S(2)}, u32[]{:S(2)}) %collective-permute-start.12) | collective-permute-done | bytes 147488 | tf_op jit(solution)/shard_map/ppermute | solution.py:387
  54.9 1.0 %shard_map.105 = (f32[384,768]{1,0:T(8,128)}, f32[768,384]{1,0:T(8,128)}) custom-call(s32[1]{0:T(128)} %bitcast.me_ref, bf16[192,384]{1,0:T(8,128)(2,1)S(1)} %get-tuple-element.90.refs_0_, bf16[192,384]{1,0:T(8,128)(2,1)S(1)} %collective-permute-done.12.refs_1_, bf16[224,384]{1,0:T(8,128)(2,1)S(1)} %collective-permute-done.9.refs_1_.refs_2_), custom_call_target="tpu_custom_call" | custom-call | tf_op jit(solution)/shard_map/pallas_call | solution.py:360
  55.8 2.3 %collective-permute-done.10.refs_2_.refs_0_ = bf16[224,384]{1,0:T(8,128)(2,1)S(1)} collective-permute-done((bf16[224,384]{1,0:T(8,128)(2,1)S(1)}, bf16[224,384]{1,0:T(8,128)(2,1)S(1)}, u32[]{:S(2)}, u32[]{:S(2)}) %collective-permute-start.10) | collective-permute-done | bytes 172064 | tf_op jit(solution)/shard_map/ppermute | solution.py:387
  58.7 0.8 %shard_map.104 = bf16[192,256]{1,0:T(8,128)(2,1)} custom-call(s32[1]{0:T(128)} %bitcast.me_ref, bf16[32,384]{1,0:T(8,128)(2,1)S(1)} %get-tuple-element.86.refs_0_, bf16[224,384]{1,0:T(8,128)(2,1)S(1)} %collective-permute-done.9.refs_1_.refs_2_, bf16[224,384]{1,0:T(8,128)(2,1)S(1)} %collective-permute-done.10.refs_2_.refs_0_, ...), custom_call_target="tpu_custom_call" | custom-call | tf_op jit(solution)/shard_map/pallas_call | solution.py:528
  59.8 1.2 %shard_map.106 = (f32[384,768]{1,0:T(8,128)}, f32[768,384]{1,0:T(8,128)}) custom-call(s32[1]{0:T(128)} %bitcast.me_ref, bf16[224,384]{1,0:T(8,128)(2,1)S(1)} %collective-permute-done.10.refs_2_.refs_0_, bf16[224,384]{1,0:T(8,128)(2,1)S(1)} %collective-permute-done.11.refs_3_.refs_1_, ...), custom_call_target="tpu_custom_call", output_to_operand_aliasing={{0}: (6, {}), {1}: (7, {})} | custom-call | tf_op jit(solution)/shard_map/pallas_call | solution.py:360
  (33 shorter events, 6.4 us)
Async XLA Ops:
  2.3 16.2 %all-to-all-start = ((bf16[32,8,384]{2,1,0:T(8,128)(2,1)}), bf16[32,8,384]{2,1,0:T(8,128)(2,1)S(1)}, u32[]{:S(2)}, u32[]{:S(2)}) async-start(bf16[32,8,384]{2,1,0:T(8,128)(2,1)} %shard_map.94), calls=%async_computation | async-start | bytes 393216 | tf_op jit(solution)/shard_map/all_to_all | solution.py:469
  9.6 1.1 %copy-start = (bf16[384,768]{1,0:T(8,128)(2,1)S(1)}, bf16[384,768]{1,0:T(8,128)(2,1)}, u32[]{:S(2)}) copy-start(bf16[384,768]{1,0:T(8,128)(2,1)} %w_in_ref.1) | copy-start | bytes 1769476
  10.7 1.1 %copy-start.1 = (bf16[768,384]{1,0:T(8,128)(2,1)S(1)}, bf16[768,384]{1,0:T(8,128)(2,1)}, u32[]{:S(2)}) copy-start(bf16[768,384]{1,0:T(8,128)(2,1)} %w_out_ref.1) | copy-start | bytes 1769476
  11.8 0.7 %copy-start.2 = (f32[768]{0:T(1024)S(1)}, f32[768]{0:T(1024)}, u32[]{:S(2)}) copy-start(f32[768]{0:T(1024)} %bias_ref.1) | copy-start | bytes 9220
  12.5 0.7 %copy-start.3 = (f32[384]{0:T(512)S(1)}, f32[384]{0:T(512)}, u32[]{:S(2)}) copy-start(f32[384]{0:T(512)} %logit_ref.1) | copy-start | bytes 4612
  13.1 0.7 %copy-start.4 = (f32[384]{0:T(512)S(1)}, f32[384]{0:T(512)}, u32[]{:S(2)}) copy-start(f32[384]{0:T(512)} %scale_ref.1) | copy-start | bytes 4612
  24.6 2.4 %collective-permute-start = (bf16[768,384]{1,0:T(8,128)(2,1)S(1)}, bf16[768,384]{1,0:T(8,128)(2,1)S(1)}, u32[]{:S(2)}, u32[]{:S(2)}) collective-permute-start(bf16[768,384]{1,0:T(8,128)(2,1)S(1)} %get-tuple-element.63), channel_id=1, source_target_pairs={{0,1},{1,0},{2,3},{3,2},{4,5},{5,4},{6,7},{7,6},{8,9},{9,8},{10,11... | collective-permute-start | bytes 1769480 | tf_op jit(solution)/shard_map/ppermute | solution.py:387
  25.7 1.3 %collective-permute-start.1 = (bf16[64,384]{1,0:T(8,128)(2,1)S(1)}, bf16[64,384]{1,0:T(8,128)(2,1)S(1)}, u32[]{:S(2)}, u32[]{:S(2)}) collective-permute-start(bf16[64,384]{1,0:T(8,128)(2,1)S(1)} %get-tuple-element.67), channel_id=1, source_target_pairs={{0,1},{1,0},{2,3},{3,2},{4,5},{5,4},{6,7},{7,6},{8,9},{9,8},{10,11... | collective-permute-start | bytes 147464 | tf_op jit(solution)/shard_map/ppermute | solution.py:387
  27.1 9.2 %collective-permute-start.2 = (bf16[192,384]{1,0:T(8,128)(2,1)S(1)}, bf16[192,384]{1,0:T(8,128)(2,1)S(1)}, u32[]{:S(2)}, u32[]{:S(2)}) collective-permute-start(bf16[192,384]{1,0:T(8,128)(2,1)S(1)} %get-tuple-element.70), channel_id=1, source_target_pairs={{0,2},{1,3},{2,0},{3,1},{4,6},{5,7},{6,4},{7,5},{8,10},{9,11},{10,... | collective-permute-start | bytes 442376 | tf_op jit(solution)/shard_map/ppermute | solution.py:387
  27.7 8.9 %collective-permute-start.3 = (bf16[192,384]{1,0:T(8,128)(2,1)S(1)}, bf16[192,384]{1,0:T(8,128)(2,1)S(1)}, u32[]{:S(2)}, u32[]{:S(2)}) collective-permute-start(bf16[192,384]{1,0:T(8,128)(2,1)S(1)} %get-tuple-element.71), channel_id=1, source_target_pairs={{0,4},{1,5},{2,6},{3,7},{4,0},{5,1},{6,2},{7,3},{8,12},{9,13},{10,... | collective-permute-start | bytes 442376 | tf_op jit(solution)/shard_map/ppermute | solution.py:387
  29.0 7.7 %collective-permute-start.4 = (bf16[192,384]{1,0:T(8,128)(2,1)S(1)}, bf16[192,384]{1,0:T(8,128)(2,1)S(1)}, u32[]{:S(2)}, u32[]{:S(2)}) collective-permute-start(bf16[192,384]{1,0:T(8,128)(2,1)S(1)} %get-tuple-element.72), channel_id=1, source_target_pairs={{0,6},{1,7},{2,4},{3,5},{4,2},{5,3},{6,0},{7,1},{8,14},{9,15},{10,... | collective-permute-start | bytes 442376 | tf_op jit(solution)/shard_map/ppermute | solution.py:387
  30.8 5.6 %collective-permute-start.5 = (bf16[64,384]{1,0:T(8,128)(2,1)S(1)}, bf16[64,384]{1,0:T(8,128)(2,1)S(1)}, u32[]{:S(2)}, u32[]{:S(2)}) collective-permute-start(bf16[64,384]{1,0:T(8,128)(2,1)S(1)} %get-tuple-element.76), channel_id=1, source_target_pairs={{0,16},{1,17},{2,18},{3,19},{4,20},{5,21},{6,22},{7,23},{8,24},{9,... | collective-permute-start | bytes 147464 | tf_op jit(solution)/shard_map/ppermute | solution.py:387
  36.7 5.2 %collective-permute-start.6 = (bf16[192,384]{1,0:T(8,128)(2,1)S(1)}, bf16[192,384]{1,0:T(8,128)(2,1)S(1)}, u32[]{:S(2)}, u32[]{:S(2)}) collective-permute-start(bf16[192,384]{1,0:T(8,128)(2,1)S(1)} %shard_map.101.refs_0_), channel_id=1, source_target_pairs={{0,8},{1,9},{2,10},{3,11},{4,12},{5,13},{6,14},{7,15},{8,0},{9,1},... | collective-permute-start | bytes 442376 | tf_op jit(solution)/shard_map/ppermute | solution.py:387
  42.0 7.3 %collective-permute-start.7 = (bf16[192,384]{1,0:T(8,128)(2,1)S(1)}, bf16[192,384]{1,0:T(8,128)(2,1)S(1)}, u32[]{:S(2)}, u32[]{:S(2)}) collective-permute-start(bf16[192,384]{1,0:T(8,128)(2,1)S(1)} %get-tuple-element.83.refs_0_), channel_id=1, source_target_pairs={{0,24},{1,25},{2,26},{3,27},{4,28},{5,29},{6,30},{7,31},{8,16},{9,... | collective-permute-start | bytes 442376 | tf_op jit(solution)/shard_map/ppermute | solution.py:387
  43.6 5.7 %collective-permute-start.8 = (bf16[64,384]{1,0:T(8,128)(2,1)S(1)}, bf16[64,384]{1,0:T(8,128)(2,1)S(1)}, u32[]{:S(2)}, u32[]{:S(2)}) collective-permute-start(bf16[64,384]{1,0:T(8,128)(2,1)S(1)} %get-tuple-element.85), channel_id=1, source_target_pairs={{0,8},{1,9},{2,10},{3,11},{4,12},{5,13},{6,14},{7,15},{8,0},{9,1},... | collective-permute-start | bytes 147464 | tf_op jit(solution)/shard_map/ppermute | solution.py:387
  49.4 5.5 %collective-permute-start.9 = (bf16[224,384]{1,0:T(8,128)(2,1)S(1)}, bf16[224,384]{1,0:T(8,128)(2,1)S(1)}, u32[]{:S(2)}, u32[]{:S(2)}) collective-permute-start(bf16[224,384]{1,0:T(8,128)(2,1)S(1)} %get-tuple-element.87), channel_id=1, source_target_pairs={{0,2},{1,3},{2,0},{3,1},{4,6},{5,7},{6,4},{7,5},{8,10},{9,11},{10,... | collective-permute-start | bytes 516104 | tf_op jit(solution)/shard_map/ppermute | solution.py:387
  50.9 7.2 %collective-permute-start.10 = (bf16[224,384]{1,0:T(8,128)(2,1)S(1)}, bf16[224,384]{1,0:T(8,128)(2,1)S(1)}, u32[]{:S(2)}, u32[]{:S(2)}) collective-permute-start(bf16[224,384]{1,0:T(8,128)(2,1)S(1)} %get-tuple-element.88), channel_id=1, source_target_pairs={{0,4},{1,5},{2,6},{3,7},{4,0},{5,1},{6,2},{7,3},{8,12},{9,13},{10,... | collective-permute-start | bytes 516104 | tf_op jit(solution)/shard_map/ppermute | solution.py:387
  51.7 6.5 %collective-permute-start.11 = (bf16[224,384]{1,0:T(8,128)(2,1)S(1)}, bf16[224,384]{1,0:T(8,128)(2,1)S(1)}, u32[]{:S(2)}, u32[]{:S(2)}) collective-permute-start(bf16[224,384]{1,0:T(8,128)(2,1)S(1)} %get-tuple-element.89), channel_id=1, source_target_pairs={{0,6},{1,7},{2,4},{3,5},{4,2},{5,3},{6,0},{7,1},{8,14},{9,15},{10,... | collective-permute-start | bytes 516104 | tf_op jit(solution)/shard_map/ppermute | solution.py:387
  52.9 1.4 %collective-permute-start.12 = (bf16[192,384]{1,0:T(8,128)(2,1)S(1)}, bf16[192,384]{1,0:T(8,128)(2,1)S(1)}, u32[]{:S(2)}, u32[]{:S(2)}) collective-permute-start(bf16[192,384]{1,0:T(8,128)(2,1)S(1)} %get-tuple-element.90.refs_0_), channel_id=1, source_target_pairs={{0,1},{1,0},{2,3},{3,2},{4,5},{5,4},{6,7},{7,6},{8,9},{9,8},{10,11... | collective-permute-start | bytes 442376 | tf_op jit(solution)/shard_map/ppermute | solution.py:387
  54.9 4.7 %collective-permute-start.13 = (bf16[224,384]{1,0:T(8,128)(2,1)S(1)}, bf16[224,384]{1,0:T(8,128)(2,1)S(1)}, u32[]{:S(2)}, u32[]{:S(2)}) collective-permute-start(bf16[224,384]{1,0:T(8,128)(2,1)S(1)} %collective-permute-done.9.refs_1_.refs_2_), channel_id=1, source_target_pairs={{0,1},{1,0},{2,3},{3,2},{4,5},{5,4},{6,7},{7,6},{8,9},{9,8},{10,11... | collective-permute-start | bytes 516104 | tf_op jit(solution)/shard_map/ppermute | solution.py:387
  58.2 1.4 %collective-permute-start.14 = (bf16[224,384]{1,0:T(8,128)(2,1)S(1)}, bf16[224,384]{1,0:T(8,128)(2,1)S(1)}, u32[]{:S(2)}, u32[]{:S(2)}) collective-permute-start(bf16[224,384]{1,0:T(8,128)(2,1)S(1)} %collective-permute-done.10.refs_2_.refs_0_), channel_id=1, source_target_pairs={{0,1},{1,0},{2,3},{3,2},{4,5},{5,4},{6,7},{7,6},{8,9},{9,8},{10,11... | collective-permute-start | bytes 516104 | tf_op jit(solution)/shard_map/ppermute | solution.py:387
  58.2 1.7 %collective-permute-start.15 = (bf16[224,384]{1,0:T(8,128)(2,1)S(1)}, bf16[224,384]{1,0:T(8,128)(2,1)S(1)}, u32[]{:S(2)}, u32[]{:S(2)}) collective-permute-start(bf16[224,384]{1,0:T(8,128)(2,1)S(1)} %collective-permute-done.11.refs_3_.refs_1_), channel_id=1, source_target_pairs={{0,1},{1,0},{2,3},{3,2},{4,5},{5,4},{6,7},{7,6},{8,9},{9,8},{10,11... | collective-permute-start | bytes 516104 | tf_op jit(solution)/shard_map/ppermute | solution.py:387

commit v13 on v11

--- a/solution.py
+++ b/solution.py
@@ -426,7 +426,7 @@
     placed = place(me, shapes, quarters, early, []) if early else []
     if early:
         *got[1:], placed = lax.optimization_barrier((*got[1:], placed))
-    quarters = [mine] + got + [first] + exchange(got, [1] * (radix - 1), size)
+    quarters = [mine] + got + [first] + exchange([part[:rows] for part in got], [1] * (radix - 1), size)
     placed = place(me, shapes, quarters, [slot for slot in range(2 * radix) if slot not in early], placed)
     return placed, ride
 

time: 61.4 us -> 61.4 us (level)
  transfers between devices with their start and end apart: 17 -> 17, of which waited for: 11 -> 10; matrix products, arithmetic and copies ran while one was open for 0% -> 0% of each run, Pallas kernels for 6% -> 7%
where the time goes in v13:
time: 61.4 us; the launch traced here: 61 us
  waiting for transfers between devices  23.9 us (39%)
  starting transfers between devices  18.9 us (31%)
  Pallas kernels  13.2 us (21%)
  local copies, waits for them, and re-layouts  4.22 us (7%)
  between operations  0.78 us (1%)
    ppermute x16, waiting for transfers between devices, exchange(): lax.ppermute(value if not isinstance(value, list) else value[i], 'seq', [...  20.1 us
    ppermute x16, starting transfers between devices, exchange(): lax.ppermute(value if not isinstance(value, list) else value[i], 'seq', [...  11.6 us
    all_to_all x1, starting transfers between devices, shards(): both = lax.all_to_all(both, 'seq', split_axis=0, concat_axis=0, tiled=True)  7.3 us
    pallas_call x1, Pallas kernels, shards(): call(functools.partial(switch_kernel, levels, block), [struct((units, dou...  6.05 us
    unnamed x10, local copies, waits for them, and re-layouts  4.17 us
    all_to_all x1, waiting for transfers between devices, shards(): both = lax.all_to_all(both, 'seq', split_axis=0, concat_axis=0, tiled=True)  3.82 us
    pallas_call x2, Pallas kernels, place(): call(functools.partial(place_kernel, 1, pieces, slots, len(placed)), shap...  2.13 us
    pallas_call x1, Pallas kernels, shards(): call(pack_kernel, struct((size, block, double), bf16), scratch=[pltpu.VME...  1.68 us
  transfers between devices with their start and end apart: 17, of which 10 were waited for; matrix products, arithmetic and copies ran while one was open for 0% of the time, Pallas kernels for 7%

profile of v13, /device:TPU:0, one launch (start us, length us, event | category | flops | bytes accessed | tf_op | source)
XLA Modules:
  0.0 61.0 jit_solution(10371389847515428454)
XLA Ops:
  0.6 1.7 %shard_map.94 = bf16[32,8,384]{2,1,0:T(8,128)(2,1)} custom-call(bf16[192,256]{1,0:T(8,128)(2,1)} %bitcast.4, bf16[192,256]{1,0:T(8,128)(2,1)} %bitcast.5), custom_call_target="tpu_custom_call" | custom-call | bytes 7000000 | tf_op jit(solution)/shard_map/pallas_call | solution.py:444
  2.3 7.3 %all-to-all-start = ((bf16[32,8,384]{2,1,0:T(8,128)(2,1)}), bf16[32,8,384]{2,1,0:T(8,128)(2,1)S(1)}, u32[]{:S(2)}, u32[]{:S(2)}) async-start(bf16[32,8,384]{2,1,0:T(8,128)(2,1)} %shard_map.94), calls=%async_computation | async-start | bytes 393216 | tf_op jit(solution)/shard_map/all_to_all | solution.py:460
  9.6 1.1 %copy-done = bf16[384,768]{1,0:T(8,128)(2,1)S(1)} copy-done((bf16[384,768]{1,0:T(8,128)(2,1)S(1)}, bf16[384,768]{1,0:T(8,128)(2,1)}, u32[]{:S(2)}) %copy-start) | copy-done | bytes 589848
  10.7 1.1 %copy-done.1 = bf16[768,384]{1,0:T(8,128)(2,1)S(1)} copy-done((bf16[768,384]{1,0:T(8,128)(2,1)S(1)}, bf16[768,384]{1,0:T(8,128)(2,1)}, u32[]{:S(2)}) %copy-start.1) | copy-done | bytes 589848
  11.8 0.7 %copy-done.2 = f32[768]{0:T(1024)S(1)} copy-done((f32[768]{0:T(1024)S(1)}, f32[768]{0:T(1024)}, u32[]{:S(2)}) %copy-start.2) | copy-done | bytes 3096
  13.8 0.9 %shard_map.95 = (bf16[512,768]{1,0:T(8,128)(2,1)S(1)}, bf16[768,512]{1,0:T(8,128)(2,1)S(1)}, bf16[768,512]{1,0:T(8,128)(2,1)S(1)}, bf16[512,768]{1,0:T(8,128)(2,...) custom-call(bf16[384,768]{1,0:T(8,128)(2,1)S(1)} %copy-done, ...), custom_call_target="tpu_custom_call" | custom-call | tf_op jit(solution)/shard_map/pallas_call | solution.py:462
  14.7 3.8 %all-to-all-done.both_ref = bf16[32,8,384]{2,1,0:T(8,128)(2,1)S(1)} async-done(((bf16[32,8,384]{2,1,0:T(8,128)(2,1)}), bf16[32,8,384]{2,1,0:T(8,128)(2,1)S(1)}, u32[]{:S(2)}, u32[]{:S(2)}) %all-to-all-start) | async-done | bytes 196640 | tf_op jit(solution)/shard_map/all_to_all | solution.py:460
  18.5 6.1 %shard_map.96 = (bf16[768,384]{1,0:T(8,128)(2,1)S(1)}, bf16[640,384]{1,0:T(8,128)(2,1)S(1)}, bf16[640,768]{1,0:T(8,128)(2,1)S(1)}, bf16[640,768]{1,0:T(8,128)(2,...) custom-call(s32[1]{0:T(128)} %bitcast.me_ref, ...), custom_call_target="tpu_custom_call" | custom-call | tf_op jit(solution)/shard_map/pallas_call | solution.py:472
  27.7 1.3 %collective-permute-start.3 = (bf16[192,384]{1,0:T(8,128)(2,1)S(1)}, bf16[192,384]{1,0:T(8,128)(2,1)S(1)}, u32[]{:S(2)}, u32[]{:S(2)}) collective-permute-start(bf16[192,384]{1,0:T(8,128)(2,1)S(1)} %get-tuple-element.71), channel_id=1, source_target_pairs={{0,4},{1,5},{2,6},{3,7},{4,0},{5,1},{6,2},{7,3},{8,12},{9,13},{10,... | collective-permute-start | bytes 442376 | tf_op jit(solution)/shard_map/ppermute | solution.py:378
  28.9 1.7 %collective-permute-start.4 = (bf16[192,384]{1,0:T(8,128)(2,1)S(1)}, bf16[192,384]{1,0:T(8,128)(2,1)S(1)}, u32[]{:S(2)}, u32[]{:S(2)}) collective-permute-start(bf16[192,384]{1,0:T(8,128)(2,1)S(1)} %get-tuple-element.72), channel_id=1, source_target_pairs={{0,6},{1,7},{2,4},{3,5},{4,2},{5,3},{6,0},{7,1},{8,14},{9,15},{10,... | collective-permute-start | bytes 442376 | tf_op jit(solution)/shard_map/ppermute | solution.py:378
  30.8 0.9 %collective-permute-start.5 = (bf16[64,384]{1,0:T(8,128)(2,1)S(1)}, bf16[64,384]{1,0:T(8,128)(2,1)S(1)}, u32[]{:S(2)}, u32[]{:S(2)}) collective-permute-start(bf16[64,384]{1,0:T(8,128)(2,1)S(1)} %get-tuple-element.76), channel_id=1, source_target_pairs={{0,16},{1,17},{2,18},{3,19},{4,20},{5,21},{6,22},{7,23},{8,24},{9,... | collective-permute-start | bytes 147464 | tf_op jit(solution)/shard_map/ppermute | solution.py:378
  31.6 4.7 %collective-permute-done.5.refs_3_ = bf16[64,384]{1,0:T(8,128)(2,1)S(1)} collective-permute-done((bf16[64,384]{1,0:T(8,128)(2,1)S(1)}, bf16[64,384]{1,0:T(8,128)(2,1)S(1)}, u32[]{:S(2)}, u32[]{:S(2)}) %collective-permute-start.5) | collective-permute-done | bytes 49184 | tf_op jit(solution)/shard_map/ppermute | solution.py:378
  36.7 0.7 %collective-permute-start.6 = (bf16[192,384]{1,0:T(8,128)(2,1)S(1)}, bf16[192,384]{1,0:T(8,128)(2,1)S(1)}, u32[]{:S(2)}, u32[]{:S(2)}) collective-permute-start(bf16[192,384]{1,0:T(8,128)(2,1)S(1)} %shard_map.101.refs_0_), channel_id=1, source_target_pairs={{0,8},{1,9},{2,10},{3,11},{4,12},{5,13},{6,14},{7,15},{8,0},{9,1},... | collective-permute-start | bytes 442376 | tf_op jit(solution)/shard_map/ppermute | solution.py:378
  37.4 4.5 %collective-permute-done.6.refs_1_ = bf16[192,384]{1,0:T(8,128)(2,1)S(1)} collective-permute-done((bf16[192,384]{1,0:T(8,128)(2,1)S(1)}, bf16[192,384]{1,0:T(8,128)(2,1)S(1)}, u32[]{:S(2)}, u32[]{:S(2)}) %collective-permute-start.6) | collective-permute-done | bytes 147488 | tf_op jit(solution)/shard_map/ppermute | solution.py:378
  41.9 1.7 %collective-permute-start.7 = (bf16[192,384]{1,0:T(8,128)(2,1)S(1)}, bf16[192,384]{1,0:T(8,128)(2,1)S(1)}, u32[]{:S(2)}, u32[]{:S(2)}) collective-permute-start(bf16[192,384]{1,0:T(8,128)(2,1)S(1)} %get-tuple-element.83.refs_0_), channel_id=1, source_target_pairs={{0,24},{1,25},{2,26},{3,27},{4,28},{5,29},{6,30},{7,31},{8,16},{9,... | collective-permute-start | bytes 442376 | tf_op jit(solution)/shard_map/ppermute | solution.py:378
  43.6 5.7 %collective-permute-done.8.refs_3_ = bf16[64,384]{1,0:T(8,128)(2,1)S(1)} collective-permute-done((bf16[64,384]{1,0:T(8,128)(2,1)S(1)}, bf16[64,384]{1,0:T(8,128)(2,1)S(1)}, u32[]{:S(2)}, u32[]{:S(2)}) %collective-permute-start.8) | collective-permute-done | bytes 49184 | tf_op jit(solution)/shard_map/ppermute | solution.py:378
  49.4 1.5 %collective-permute-start.9 = (bf16[224,384]{1,0:T(8,128)(2,1)S(1)}, bf16[224,384]{1,0:T(8,128)(2,1)S(1)}, u32[]{:S(2)}, u32[]{:S(2)}) collective-permute-start(bf16[224,384]{1,0:T(8,128)(2,1)S(1)} %get-tuple-element.87), channel_id=1, source_target_pairs={{0,2},{1,3},{2,0},{3,1},{4,6},{5,7},{6,4},{7,5},{8,10},{9,11},{10,... | collective-permute-start | bytes 516104 | tf_op jit(solution)/shard_map/ppermute | solution.py:378
  50.9 0.8 %collective-permute-start.10 = (bf16[224,384]{1,0:T(8,128)(2,1)S(1)}, bf16[224,384]{1,0:T(8,128)(2,1)S(1)}, u32[]{:S(2)}, u32[]{:S(2)}) collective-permute-start(bf16[224,384]{1,0:T(8,128)(2,1)S(1)} %get-tuple-element.88), channel_id=1, source_target_pairs={{0,4},{1,5},{2,6},{3,7},{4,0},{5,1},{6,2},{7,3},{8,12},{9,13},{10,... | collective-permute-start | bytes 516104 | tf_op jit(solution)/shard_map/ppermute | solution.py:378
  51.6 1.3 %collective-permute-start.11 = (bf16[224,384]{1,0:T(8,128)(2,1)S(1)}, bf16[224,384]{1,0:T(8,128)(2,1)S(1)}, u32[]{:S(2)}, u32[]{:S(2)}) collective-permute-start(bf16[224,384]{1,0:T(8,128)(2,1)S(1)} %get-tuple-element.89), channel_id=1, source_target_pairs={{0,6},{1,7},{2,4},{3,5},{4,2},{5,3},{6,0},{7,1},{8,14},{9,15},{10,... | collective-permute-start | bytes 516104 | tf_op jit(solution)/shard_map/ppermute | solution.py:378
  52.9 1.4 %collective-permute-done.12.refs_1_ = bf16[192,384]{1,0:T(8,128)(2,1)S(1)} collective-permute-done((bf16[192,384]{1,0:T(8,128)(2,1)S(1)}, bf16[192,384]{1,0:T(8,128)(2,1)S(1)}, u32[]{:S(2)}, u32[]{:S(2)}) %collective-permute-start.12) | collective-permute-done | bytes 147488 | tf_op jit(solution)/shard_map/ppermute | solution.py:378
  54.9 1.0 %shard_map.105 = (f32[384,768]{1,0:T(8,128)}, f32[768,384]{1,0:T(8,128)}) custom-call(s32[1]{0:T(128)} %bitcast.me_ref, bf16[192,384]{1,0:T(8,128)(2,1)S(1)} %get-tuple-element.90.refs_0_, bf16[192,384]{1,0:T(8,128)(2,1)S(1)} %collective-permute-done.12.refs_1_, bf16[224,384]{1,0:T(8,128)(2,1)S(1)} %collective-permute-done.9.refs_1_.refs_2_), custom_call_target="tpu_custom_call" | custom-call | tf_op jit(solution)/shard_map/pallas_call | solution.py:351
  55.9 2.2 %collective-permute-done.10.refs_2_.refs_0_ = bf16[224,384]{1,0:T(8,128)(2,1)S(1)} collective-permute-done((bf16[224,384]{1,0:T(8,128)(2,1)S(1)}, bf16[224,384]{1,0:T(8,128)(2,1)S(1)}, u32[]{:S(2)}, u32[]{:S(2)}) %collective-permute-start.10) | collective-permute-done | bytes 172064 | tf_op jit(solution)/shard_map/ppermute | solution.py:378
  58.8 0.8 %shard_map.104 = bf16[192,256]{1,0:T(8,128)(2,1)} custom-call(s32[1]{0:T(128)} %bitcast.me_ref, bf16[32,384]{1,0:T(8,128)(2,1)S(1)} %get-tuple-element.86.refs_0_, bf16[224,384]{1,0:T(8,128)(2,1)S(1)} %collective-permute-done.9.refs_1_.refs_2_, bf16[224,384]{1,0:T(8,128)(2,1)S(1)} %collective-permute-done.10.refs_2_.refs_0_, ...), custom_call_target="tpu_custom_call" | custom-call | tf_op jit(solution)/shard_map/pallas_call | solution.py:518
  59.8 1.2 %shard_map.106 = (f32[384,768]{1,0:T(8,128)}, f32[768,384]{1,0:T(8,128)}) custom-call(s32[1]{0:T(128)} %bitcast.me_ref, bf16[224,384]{1,0:T(8,128)(2,1)S(1)} %collective-permute-done.10.refs_2_.refs_0_, bf16[224,384]{1,0:T(8,128)(2,1)S(1)} %collective-permute-done.11.refs_3_.refs_1_, ...), custom_call_target="tpu_custom_call", output_to_operand_aliasing={{0}: (6, {}), {1}: (7, {})} | custom-call | tf_op jit(solution)/shard_map/pallas_call | solution.py:351
  (36 shorter events, 6.5 us)
Async XLA Ops:
  2.3 16.2 %all-to-all-start = ((bf16[32,8,384]{2,1,0:T(8,128)(2,1)}), bf16[32,8,384]{2,1,0:T(8,128)(2,1)S(1)}, u32[]{:S(2)}, u32[]{:S(2)}) async-start(bf16[32,8,384]{2,1,0:T(8,128)(2,1)} %shard_map.94), calls=%async_computation | async-start | bytes 393216 | tf_op jit(solution)/shard_map/all_to_all | solution.py:460
  9.6 1.1 %copy-start = (bf16[384,768]{1,0:T(8,128)(2,1)S(1)}, bf16[384,768]{1,0:T(8,128)(2,1)}, u32[]{:S(2)}) copy-start(bf16[384,768]{1,0:T(8,128)(2,1)} %w_in_ref.1) | copy-start | bytes 1769476
  10.7 1.1 %copy-start.1 = (bf16[768,384]{1,0:T(8,128)(2,1)S(1)}, bf16[768,384]{1,0:T(8,128)(2,1)}, u32[]{:S(2)}) copy-start(bf16[768,384]{1,0:T(8,128)(2,1)} %w_out_ref.1) | copy-start | bytes 1769476
  11.8 0.7 %copy-start.2 = (f32[768]{0:T(1024)S(1)}, f32[768]{0:T(1024)}, u32[]{:S(2)}) copy-start(f32[768]{0:T(1024)} %bias_ref.1) | copy-start | bytes 9220
  12.5 0.7 %copy-start.3 = (f32[384]{0:T(512)S(1)}, f32[384]{0:T(512)}, u32[]{:S(2)}) copy-start(f32[384]{0:T(512)} %logit_ref.1) | copy-start | bytes 4612
  13.1 0.7 %copy-start.4 = (f32[384]{0:T(512)S(1)}, f32[384]{0:T(512)}, u32[]{:S(2)}) copy-start(f32[384]{0:T(512)} %scale_ref.1) | copy-start | bytes 4612
  24.6 2.4 %collective-permute-start = (bf16[768,384]{1,0:T(8,128)(2,1)S(1)}, bf16[768,384]{1,0:T(8,128)(2,1)S(1)}, u32[]{:S(2)}, u32[]{:S(2)}) collective-permute-start(bf16[768,384]{1,0:T(8,128)(2,1)S(1)} %get-tuple-element.63), channel_id=1, source_target_pairs={{0,1},{1,0},{2,3},{3,2},{4,5},{5,4},{6,7},{7,6},{8,9},{9,8},{10,11... | collective-permute-start | bytes 1769480 | tf_op jit(solution)/shard_map/ppermute | solution.py:378
  25.7 1.3 %collective-permute-start.1 = (bf16[64,384]{1,0:T(8,128)(2,1)S(1)}, bf16[64,384]{1,0:T(8,128)(2,1)S(1)}, u32[]{:S(2)}, u32[]{:S(2)}) collective-permute-start(bf16[64,384]{1,0:T(8,128)(2,1)S(1)} %get-tuple-element.67), channel_id=1, source_target_pairs={{0,1},{1,0},{2,3},{3,2},{4,5},{5,4},{6,7},{7,6},{8,9},{9,8},{10,11... | collective-permute-start | bytes 147464 | tf_op jit(solution)/shard_map/ppermute | solution.py:378
  27.1 9.2 %collective-permute-start.2 = (bf16[192,384]{1,0:T(8,128)(2,1)S(1)}, bf16[192,384]{1,0:T(8,128)(2,1)S(1)}, u32[]{:S(2)}, u32[]{:S(2)}) collective-permute-start(bf16[192,384]{1,0:T(8,128)(2,1)S(1)} %get-tuple-element.70), channel_id=1, source_target_pairs={{0,2},{1,3},{2,0},{3,1},{4,6},{5,7},{6,4},{7,5},{8,10},{9,11},{10,... | collective-permute-start | bytes 442376 | tf_op jit(solution)/shard_map/ppermute | solution.py:378
  27.7 8.9 %collective-permute-start.3 = (bf16[192,384]{1,0:T(8,128)(2,1)S(1)}, bf16[192,384]{1,0:T(8,128)(2,1)S(1)}, u32[]{:S(2)}, u32[]{:S(2)}) collective-permute-start(bf16[192,384]{1,0:T(8,128)(2,1)S(1)} %get-tuple-element.71), channel_id=1, source_target_pairs={{0,4},{1,5},{2,6},{3,7},{4,0},{5,1},{6,2},{7,3},{8,12},{9,13},{10,... | collective-permute-start | bytes 442376 | tf_op jit(solution)/shard_map/ppermute | solution.py:378
  28.9 7.7 %collective-permute-start.4 = (bf16[192,384]{1,0:T(8,128)(2,1)S(1)}, bf16[192,384]{1,0:T(8,128)(2,1)S(1)}, u32[]{:S(2)}, u32[]{:S(2)}) collective-permute-start(bf16[192,384]{1,0:T(8,128)(2,1)S(1)} %get-tuple-element.72), channel_id=1, source_target_pairs={{0,6},{1,7},{2,4},{3,5},{4,2},{5,3},{6,0},{7,1},{8,14},{9,15},{10,... | collective-permute-start | bytes 442376 | tf_op jit(solution)/shard_map/ppermute | solution.py:378
  30.8 5.6 %collective-permute-start.5 = (bf16[64,384]{1,0:T(8,128)(2,1)S(1)}, bf16[64,384]{1,0:T(8,128)(2,1)S(1)}, u32[]{:S(2)}, u32[]{:S(2)}) collective-permute-start(bf16[64,384]{1,0:T(8,128)(2,1)S(1)} %get-tuple-element.76), channel_id=1, source_target_pairs={{0,16},{1,17},{2,18},{3,19},{4,20},{5,21},{6,22},{7,23},{8,24},{9,... | collective-permute-start | bytes 147464 | tf_op jit(solution)/shard_map/ppermute | solution.py:378
  36.7 5.2 %collective-permute-start.6 = (bf16[192,384]{1,0:T(8,128)(2,1)S(1)}, bf16[192,384]{1,0:T(8,128)(2,1)S(1)}, u32[]{:S(2)}, u32[]{:S(2)}) collective-permute-start(bf16[192,384]{1,0:T(8,128)(2,1)S(1)} %shard_map.101.refs_0_), channel_id=1, source_target_pairs={{0,8},{1,9},{2,10},{3,11},{4,12},{5,13},{6,14},{7,15},{8,0},{9,1},... | collective-permute-start | bytes 442376 | tf_op jit(solution)/shard_map/ppermute | solution.py:378
  41.9 7.3 %collective-permute-start.7 = (bf16[192,384]{1,0:T(8,128)(2,1)S(1)}, bf16[192,384]{1,0:T(8,128)(2,1)S(1)}, u32[]{:S(2)}, u32[]{:S(2)}) collective-permute-start(bf16[192,384]{1,0:T(8,128)(2,1)S(1)} %get-tuple-element.83.refs_0_), channel_id=1, source_target_pairs={{0,24},{1,25},{2,26},{3,27},{4,28},{5,29},{6,30},{7,31},{8,16},{9,... | collective-permute-start | bytes 442376 | tf_op jit(solution)/shard_map/ppermute | solution.py:378
  43.6 5.7 %collective-permute-start.8 = (bf16[64,384]{1,0:T(8,128)(2,1)S(1)}, bf16[64,384]{1,0:T(8,128)(2,1)S(1)}, u32[]{:S(2)}, u32[]{:S(2)}) collective-permute-start(bf16[64,384]{1,0:T(8,128)(2,1)S(1)} %get-tuple-element.85), channel_id=1, source_target_pairs={{0,8},{1,9},{2,10},{3,11},{4,12},{5,13},{6,14},{7,15},{8,0},{9,1},... | collective-permute-start | bytes 147464 | tf_op jit(solution)/shard_map/ppermute | solution.py:378
  49.4 5.5 %collective-permute-start.9 = (bf16[224,384]{1,0:T(8,128)(2,1)S(1)}, bf16[224,384]{1,0:T(8,128)(2,1)S(1)}, u32[]{:S(2)}, u32[]{:S(2)}) collective-permute-start(bf16[224,384]{1,0:T(8,128)(2,1)S(1)} %get-tuple-element.87), channel_id=1, source_target_pairs={{0,2},{1,3},{2,0},{3,1},{4,6},{5,7},{6,4},{7,5},{8,10},{9,11},{10,... | collective-permute-start | bytes 516104 | tf_op jit(solution)/shard_map/ppermute | solution.py:378
  50.9 7.2 %collective-permute-start.10 = (bf16[224,384]{1,0:T(8,128)(2,1)S(1)}, bf16[224,384]{1,0:T(8,128)(2,1)S(1)}, u32[]{:S(2)}, u32[]{:S(2)}) collective-permute-start(bf16[224,384]{1,0:T(8,128)(2,1)S(1)} %get-tuple-element.88), channel_id=1, source_target_pairs={{0,4},{1,5},{2,6},{3,7},{4,0},{5,1},{6,2},{7,3},{8,12},{9,13},{10,... | collective-permute-start | bytes 516104 | tf_op jit(solution)/shard_map/ppermute | solution.py:378
  51.6 6.5 %collective-permute-start.11 = (bf16[224,384]{1,0:T(8,128)(2,1)S(1)}, bf16[224,384]{1,0:T(8,128)(2,1)S(1)}, u32[]{:S(2)}, u32[]{:S(2)}) collective-permute-start(bf16[224,384]{1,0:T(8,128)(2,1)S(1)} %get-tuple-element.89), channel_id=1, source_target_pairs={{0,6},{1,7},{2,4},{3,5},{4,2},{5,3},{6,0},{7,1},{8,14},{9,15},{10,... | collective-permute-start | bytes 516104 | tf_op jit(solution)/shard_map/ppermute | solution.py:378
  52.9 1.4 %collective-permute-start.12 = (bf16[192,384]{1,0:T(8,128)(2,1)S(1)}, bf16[192,384]{1,0:T(8,128)(2,1)S(1)}, u32[]{:S(2)}, u32[]{:S(2)}) collective-permute-start(bf16[192,384]{1,0:T(8,128)(2,1)S(1)} %get-tuple-element.90.refs_0_), channel_id=1, source_target_pairs={{0,1},{1,0},{2,3},{3,2},{4,5},{5,4},{6,7},{7,6},{8,9},{9,8},{10,11... | collective-permute-start | bytes 442376 | tf_op jit(solution)/shard_map/ppermute | solution.py:378
  54.9 4.7 %collective-permute-start.13 = (bf16[192,384]{1,0:T(8,128)(2,1)S(1)}, bf16[192,384]{1,0:T(8,128)(2,1)S(1)}, u32[]{:S(2)}, u32[]{:S(2)}) collective-permute-start(bf16[192,384]{1,0:T(8,128)(2,1)S(1)} %slice.9), channel_id=1, source_target_pairs={{0,1},{1,0},{2,3},{3,2},{4,5},{5,4},{6,7},{7,6},{8,9},{9,8},{10,11... | collective-permute-start | bytes 442376 | tf_op jit(solution)/shard_map/ppermute | solution.py:378
  58.2 1.4 %collective-permute-start.15 = (bf16[192,384]{1,0:T(8,128)(2,1)S(1)}, bf16[192,384]{1,0:T(8,128)(2,1)S(1)}, u32[]{:S(2)}, u32[]{:S(2)}) collective-permute-start(bf16[192,384]{1,0:T(8,128)(2,1)S(1)} %slice.11), channel_id=1, source_target_pairs={{0,1},{1,0},{2,3},{3,2},{4,5},{5,4},{6,7},{7,6},{8,9},{9,8},{10,11... | collective-permute-start | bytes 442376 | tf_op jit(solution)/shard_map/ppermute | solution.py:378
  58.3 1.6 %collective-permute-start.14 = (bf16[192,384]{1,0:T(8,128)(2,1)S(1)}, bf16[192,384]{1,0:T(8,128)(2,1)S(1)}, u32[]{:S(2)}, u32[]{:S(2)}) collective-permute-start(bf16[192,384]{1,0:T(8,128)(2,1)S(1)} %slice.10), channel_id=1, source_target_pairs={{0,1},{1,0},{2,3},{3,2},{4,5},{5,4},{6,7},{7,6},{8,9},{9,8},{10,11... | collective-permute-start | bytes 442376 | tf_op jit(solution)/shard_map/ppermute | solution.py:378
